TPU v7x, 32 devices: a whole 2x2x4 slice. The times are simulated.
32 devices in a mesh: grp: 2 (over y), gx: 4 (over z), gy: 2 (over core), shot: 2 (over x).
Axes of the slice: x: 2, y: 2, z: 4, core: 2. Of those that a mesh axis runs over, the one named last changes fastest.
Arguments:
- conductivity: float32 [64, 128, 128], P(('grp', 'gx'), 'gy'), parts along dimension 0, may hold values from 0.2 to 5
- stations: int32 [512], P('grp'), parts along dimension 0, may hold values from 0 to 524287
- currents: float32 [4, 256], P(('grp', 'shot')), parts along dimension 0, may hold values from 0.5 to 2
- receivers: int32 [1024, 2], P('grp'), parts along dimension 0, may hold values from 0 to 255
- observed: float32 [4, 512], P(('grp', 'shot')), parts along dimension 0, may hold values from -4 to 4
Outputs:
- potentials: float32 [4, 32, 128, 128], P(('grp', 'shot'), 'gx', 'gy'), parts along dimension 0
- gradient: float32 [64, 128, 128], P(('grp', 'gx'), ('gy', 'shot')), parts along dimension 0
There are 2 independent parts, one for each index of `grp`. A program takes and returns all parts, laid end to end along the dimension named above; each array names one. Nothing has to cross between parts.
All inputs are finite; a program needn't handle non-finite values.
Results may differ from a plain program's by a relative error of at most 0.00014.
Values sent between devices are 32-bit elements; how exact they have to be, the bound alone decides.
No kernel may reach another device: no remote copies, remote signals or barrier semaphores. Data moves between devices by JAX's collectives and lax.ppermute only.
A program may use at most 128 MiB of HBM per device.

v0:
```python
import jax
import jax.numpy as jnp
from jax import lax
from jax.sharding import PartitionSpec as P

LEVELS = 4
COARSE_SWEEPS = 16


DAMPING = 0.8


def extended(array, sides, width):
    for axis, dim in sides:
        size, length = (lax.axis_size(axis), array.shape[dim])
        up = [(i, (i + 1) % size) for i in range(size - 1)]
        down = [(j, i) for i, j in up]
        last = lax.slice_in_dim(array, length - width, length, axis=dim)
        leading = lax.slice_in_dim(array, 0, width, axis=dim)
        before = lax.ppermute(last, axis, up)
        after = lax.ppermute(leading, axis, down)
        array = jnp.concatenate([before, array, after], axis=dim)
    return array


def upper_z(field):
    return jnp.concatenate([field[..., 1:], jnp.zeros_like(field[..., :1])], axis=-1)


def lower_z(field):
    return jnp.concatenate([jnp.zeros_like(field[..., :1]), field[..., :-1]], axis=-1)


def trim_circle(field, circle_width):
    return field[..., circle_width:-circle_width, circle_width:-circle_width, :]


def pad_plane(field, circle_width):
    spec = [(0, 0)] * (field.ndim - 3) + [
        (circle_width, circle_width),
        (circle_width, circle_width),
        (0, 0),
    ]
    return jnp.pad(field, spec)


def neighbour_list(field_pad):
    centre = trim_circle(field_pad, 1)
    return [
        field_pad[..., 2:, 1:-1, :],
        field_pad[..., :-2, 1:-1, :],
        field_pad[..., 1:-1, 2:, :],
        field_pad[..., 1:-1, :-2, :],
        upper_z(centre),
        lower_z(centre),
    ]


def stencil(field_pad, cond_pad, level_scale):
    centre = trim_circle(field_pad, 1)
    centre_cond = trim_circle(cond_pad, 1)
    summed = jnp.zeros_like(centre)
    for other, other_cond in zip(neighbour_list(field_pad), neighbour_list(cond_pad)):
        summed = summed + level_scale * 0.5 * (centre_cond + other_cond) * (centre - other)
    return summed


def diagonal(cond_pad, level_scale):
    centre_cond = trim_circle(cond_pad, 1)
    summed = jnp.zeros_like(centre_cond)
    for other_cond in neighbour_list(cond_pad):
        summed = summed + level_scale * 0.5 * (centre_cond + other_cond)
    return summed


def relaxed(field_pad, source, cond_pad, diag_level, level_scale):
    return (
        trim_circle(field_pad, 1)
        + DAMPING * (source - stencil(field_pad, cond_pad, level_scale)) / diag_level
    )


def restrict(field):
    leading = field.shape[:-3]
    extent = field.shape[-3:]
    shaped = field.reshape(leading + (extent[0] // 2, 2, extent[1] // 2, 2, extent[2] // 2, 2))
    return shaped.mean(axis=(-5, -3, -1))


def prolong(field):
    return jnp.repeat(jnp.repeat(jnp.repeat(field, 2, axis=-3), 2, axis=-2), 2, axis=-1)


def assemble(blocks, count_x, count_y):
    leading = blocks.shape[1:-3]
    extent = blocks.shape[-3:]
    depth_lead = len(leading)
    shaped = blocks.reshape((count_x, count_y) + leading + extent)
    order = tuple(range(2, 2 + depth_lead)) + (0, 2 + depth_lead, 1, 3 + depth_lead, 4 + depth_lead)
    return shaped.transpose(order).reshape(
        leading + (count_x * extent[0], count_y * extent[1], extent[2])
    )


def field_rim(field):
    return extended(field, (("gx", 1), ("gy", 2)), 1)


def cond_rim(conduct):
    return extended(conduct, (("gx", 0), ("gy", 1)), 1)


def whole_cycle(source, level_index, whole_plans):
    cond_pad, diag_level, level_scale = whole_plans[level_index]
    field = DAMPING * source / diag_level

    def turn(turn_index, iterate):
        return relaxed(pad_plane(iterate, 1), source, cond_pad, diag_level, level_scale)

    return lax.fori_loop(0, COARSE_SWEEPS - 1, turn, field)


def part_cycle(source, level_index, level_plans, whole_plans, gather_level):
    if level_index == gather_level:
        blocks = lax.all_gather(source[None], ("gx", "gy"), axis=0, tiled=True)
        whole = assemble(blocks, lax.axis_size("gx"), lax.axis_size("gy"))
        correction = whole_cycle(whole, level_index, whole_plans)
        extent = source.shape
        starts = (0, lax.axis_index("gx") * extent[1], lax.axis_index("gy") * extent[2], 0)
        return lax.dynamic_slice(correction, starts, extent)
    cond_pad, diag_level, level_scale = level_plans[level_index]
    field = DAMPING * source / diag_level
    field = relaxed(field_rim(field), source, cond_pad, diag_level, level_scale)
    residual = source - stencil(field_rim(field), cond_pad, level_scale)
    field = field + prolong(
        part_cycle(restrict(residual), level_index + 1, level_plans, whole_plans, gather_level)
    )
    field = relaxed(field_rim(field), source, cond_pad, diag_level, level_scale)
    return relaxed(field_rim(field), source, cond_pad, diag_level, level_scale)


def per_device(conductivity, stations, currents, receivers, observed):
    row_count, col_count, z_count = conductivity.shape
    shot_count = currents.shape[0]
    count_x = lax.axis_size("gx")
    count_y = lax.axis_size("gy")
    gather_level = LEVELS - 1
    level_plans = []
    conduct = conductivity
    for level_index in range(gather_level):
        level_scale = 0.25**level_index
        cond_pad = cond_rim(conduct)
        level_plans.append((cond_pad, diagonal(cond_pad, level_scale), level_scale))
        conduct = restrict(conduct)
    blocks = lax.all_gather(conduct[None], ("gx", "gy"), axis=0, tiled=True)
    whole = assemble(blocks, count_x, count_y)
    whole_plans = {}
    level_index = 3
    level_scale = 0.25**level_index
    cond_pad = pad_plane(whole, 1)
    whole_plans[level_index] = (cond_pad, diagonal(cond_pad, level_scale), level_scale)
    total_y = col_count * count_y
    cell_x = stations // (total_y * z_count)
    cell_y = stations // z_count % total_y
    cell_z = stations % z_count
    local_x = cell_x - lax.axis_index("gx") * row_count
    local_y = cell_y - lax.axis_index("gy") * col_count
    owned = (local_x >= 0) & (local_x < row_count) & (local_y >= 0) & (local_y < col_count)
    block_size = row_count * col_count * z_count
    local_cell = jnp.where(owned, (local_x * col_count + local_y) * z_count + cell_z, 0)
    offsets = jnp.arange(shot_count)[:, None] * block_size + local_cell[None, :]
    targets = jnp.where(owned[None, :], offsets, shot_count * block_size).reshape(-1)

    def spread(amounts):
        flat = (
            jnp.zeros((shot_count * block_size,), jnp.float32)
            .at[targets]
            .add(amounts.reshape(-1), mode="drop")
        )
        return flat.reshape(shot_count, row_count, col_count, z_count)

    potentials = part_cycle(spread(currents), 0, level_plans, whole_plans, gather_level)
    local_values = jnp.where(
        owned[None, :], potentials.reshape(shot_count, block_size)[:, local_cell], 0.0
    )
    readings = lax.psum(local_values, ("gx", "gy"))
    positions = jnp.arange(stations.shape[0])[:, None]
    pairs = (receivers[:, 0][None, :] == positions).astype(jnp.float32) - (
        receivers[:, 1][None, :] == positions
    ).astype(jnp.float32)
    misfit = jnp.dot(readings, pairs, precision=lax.Precision.HIGHEST) - observed
    back_source = jnp.dot(misfit, pairs.T, precision=lax.Precision.HIGHEST)
    adjoint = part_cycle(spread(back_source), 0, level_plans, whole_plans, gather_level)
    stacked = jnp.concatenate([potentials, adjoint], axis=0)
    padded = extended(stacked, (("gx", 1), ("gy", 2)), 1)
    potential_pad = padded[:shot_count]
    adjoint_pad = padded[shot_count:]
    gradient = jnp.zeros_like(potentials)
    for other_u, other_w in zip(neighbour_list(potential_pad), neighbour_list(adjoint_pad)):
        gradient = gradient - 0.5 * (potentials - other_u) * (adjoint - other_w)
    summed = lax.psum_scatter(jnp.sum(gradient, axis=0), "shot", scatter_dimension=1, tiled=True)
    return (potentials, summed)


def solution(mesh):
    in_specs = (
        P(("grp", "gx"), "gy", None),
        P("grp"),
        P(("grp", "shot"), None),
        P("grp", None),
        P(("grp", "shot"), None),
    )
    out_specs = (P(("grp", "shot"), "gx", "gy", None), P(("grp", "gx"), ("gy", "shot"), None))
    return jax.shard_map(
        per_device, mesh=mesh, in_specs=in_specs, out_specs=out_specs, check_vma=False
    )
```

profile of v0, /device:TPU:0, one launch (start us, length us, event | category | flops | bytes accessed | tf_op | source)
XLA Modules:
  0.0 556.0 jit_solution(5833461317097818383)
XLA Ops:
  8.0 4.9 collective-permute-start.1
  14.4 18.9 %reshape.330 = f32[4,2,32,2,64,2]{5,4,3,2,1,0:T(8,128)} reshape(f32[8,64,128]{2,1,0:T(8,128)} %param.9) | data formatting | bytes 524288 | tf_op jit(solution)/shard_map/reshape | solution.py:86
  33.2 7.0 %reduce_sum.109 = f32[4,32,64]{2,1,0:T(8,128)S(1)} reduce(f32[4,2,32,2,64,2]{5,4,3,2,1,0:T(8,128)} %reshape.330, f32[]{:T(128)} %constant.152.clone.1), dimensions={1,3,5}, to_apply=%region_2.0 | reduce | flops 57344 | bytes 294916 | tf_op jit(solution)/shard_map/reduce_sum | solution.py:87
  42.2 5.8 %collective-permute-start.13 = (f32[1,32,64]{2,1,0:T(8,128)}, f32[1,32,64]{2,1,0:T(8,128)}, u32[]{:S(2)}, u32[]{:S(2)}) collective-permute-start(f32[1,32,64]{2,1,0:T(8,128)} %get-tuple-element.361), channel_id=1, source_target_pairs={{0,4},{4,8},{8,12},{1,5},{5,9},{9,13},{2,6},{6,10},{10,14},{3,7},{... | collective-permute-start | bytes 24584 | tf_op jit(solution)/shard_map/ppermute | solution.py:20
  61.4 5.2 collective-permute-start.5
  78.5 4.6 collective-permute-start.9
  91.2 18.1 %reshape.329 = f32[4,2,32,2,64,2]{5,4,3,2,1,0:T(8,128)} reshape(f32[1,8,64,128]{3,2,1,0:T(8,128)S(1)} %fusion.159) | data formatting | bytes 524288 | tf_op jit(solution)/shard_map/reshape | solution.py:86
  109.3 7.0 %reduce_sum.108 = f32[4,32,64]{2,1,0:T(8,128)S(1)} reduce(f32[4,2,32,2,64,2]{5,4,3,2,1,0:T(8,128)} %reshape.329, f32[]{:T(128)} %constant.152.clone.1), dimensions={1,3,5}, to_apply=%region_1.0 | reduce | flops 57344 | bytes 294916 | tf_op jit(solution)/shard_map/reduce_sum | solution.py:87
  131.1 4.8 collective-permute-start.21
  162.6 15.5 %all-gather.1 = f32[64,16]{1,0:T(8,128)S(1)} all-gather(f32[8,16]{1,0:T(8,128)S(1)} %broadcast_multiply_fusion.7), channel_id=3, replica_groups=mesh['grp'=2,'gx'=4,'gy'=2,'shot'=2] {'gx','gy'}, dimensions={0}, use_global_device_ids=true | all-gather | bytes 4608 | tf_op jit(solution)/shard_map/all_gather | solution.py:155
  190.8 15.3 %all-gather = f32[64,16]{1,0:T(8,128)S(1)} all-gather(f32[8,16]{1,0:T(8,128)S(1)} %broadcast_multiply_fusion.8), channel_id=2, replica_groups=mesh['grp'=2,'gx'=4,'gy'=2,'shot'=2] {'gx','gy'}, dimensions={0}, use_global_device_ids=true | all-gather | bytes 4608 | tf_op jit(solution)/shard_map/all_gather | solution.py:125
  224.3 4.8 collective-permute-start.41
  237.3 4.8 collective-permute-start.45
  250.1 4.8 collective-permute-start.49
  263.5 4.8 collective-permute-start.53
  276.8 4.9 collective-permute-start.57
  291.1 18.7 %psum.7 = f32[256]{0:T(256)S(1)} all-reduce(f32[256]{0:T(256)S(1)} %broadcast_select_fusion), channel_id=1, replica_groups=mesh['grp'=2,'gx'=4,'gy'=2,'shot'=2] {'gx','gy'}, use_global_device_ids=true, to_apply=%region_11.12 | all-reduce | flops 256 | bytes 2048 | tf_op jit(solution)/shard_map/psum | solution.py:186
  328.1 4.9 collective-permute-start.65
  340.0 18.1 %reshape.336 = f32[4,2,32,2,64,2]{5,4,3,2,1,0:T(8,128)} reshape(f32[1,8,64,128]{3,2,1,0:T(8,128)S(1)} %fusion.94) | data formatting | bytes 524288 | tf_op jit(solution)/shard_map/reshape | solution.py:86
  358.1 7.0 %reduce_sum.118 = f32[4,32,64]{2,1,0:T(8,128)S(1)} reduce(f32[4,2,32,2,64,2]{5,4,3,2,1,0:T(8,128)} %reshape.336, f32[]{:T(128)} %constant.152.clone.1), dimensions={1,3,5}, to_apply=%region_13.14 | reduce | flops 57344 | bytes 294916 | tf_op jit(solution)/shard_map/reduce_sum | solution.py:87
  366.4 4.8 collective-permute-start.69
  379.3 4.8 collective-permute-start.73
  397.4 4.8 collective-permute-start.77
  410.1 4.8 collective-permute-start.81
  421.8 15.7 %all-gather.2 = f32[64,16]{1,0:T(8,128)S(1)} all-gather(f32[8,16]{1,0:T(8,128)S(1)} %broadcast_multiply_fusion.6), channel_id=4, replica_groups=mesh['grp'=2,'gx'=4,'gy'=2,'shot'=2] {'gx','gy'}, dimensions={0}, use_global_device_ids=true | all-gather | bytes 4608 | tf_op jit(solution)/shard_map/all_gather | solution.py:125
  455.6 4.8 collective-permute-start.89
  468.6 4.8 collective-permute-start.93
  481.4 4.8 collective-permute-start.97
  494.8 4.8 collective-permute-start.101
  508.1 4.9 collective-permute-start.105
  521.3 4.9 collective-permute-start.109
  534.4 14.8 %reduce-scatter.2.cloned.1.call-done = f32[8,32,128]{2,1,0:T(8,128)} async-done(((f32[8,64,128]{2,1,0:T(8,128)}), f32[8,32,128]{2,1,0:T(8,128)}) %reduce-scatter.2.cloned.1.call-update) | async-done | bytes 131088 | tf_op jit(solution)/shard_map/reduce_scatter | solution.py:201
  (534 shorter events, 288.7 us)
Async XLA Ops:
  7.2 542.0 %reduce-scatter.2.cloned.1.call-start = ((), (), s32[]{:S(2)}) async-start(), calls=%async_computation.1 | async-start | bytes 393216 | tf_op jit(solution)/shard_map/reduce_scatter | solution.py:201
  8.0 46.6 %collective-permute-start.1 = (f32[1,64,128]{2,1,0:T(8,128)S(1)}, f32[1,64,128]{2,1,0:T(8,128)S(1)}, u32[]{:S(2)}, u32[]{:S(2)}) collective-permute-start(f32[1,64,128]{2,1,0:T(8,128)S(1)} %get-tuple-element.306), channel_id=1, source_target_pairs={{0,4},{4,8},{8,12},{1,5},{5,9},{9,13},{2,6},{6,10},{10,14},{3,7},{... | collective-permute-start | bytes 98312 | tf_op jit(solution)/shard_map/ppermute | solution.py:20
  12.9 41.7 %collective-permute-start = (f32[1,64,128]{2,1,0:T(8,128)S(1)}, f32[1,64,128]{2,1,0:T(8,128)S(1)}, u32[]{:S(2)}, u32[]{:S(2)}) collective-permute-start(f32[1,64,128]{2,1,0:T(8,128)S(1)} %get-tuple-element.307), channel_id=1, source_target_pairs={{4,0},{8,4},{12,8},{5,1},{9,5},{13,9},{6,2},{10,6},{14,10},{7,3},{... | collective-permute-start | bytes 98312 | tf_op jit(solution)/shard_map/ppermute | solution.py:21
  40.9 37.6 %collective-permute-start.12 = (f32[1,32,64]{2,1,0:T(8,128)}, f32[1,32,64]{2,1,0:T(8,128)}, u32[]{:S(2)}, u32[]{:S(2)}) collective-permute-start(f32[1,32,64]{2,1,0:T(8,128)} %get-tuple-element.360), channel_id=1, source_target_pairs={{4,0},{8,4},{12,8},{5,1},{9,5},{13,9},{6,2},{10,6},{14,10},{7,3},{... | collective-permute-start | bytes 24584 | tf_op jit(solution)/shard_map/ppermute | solution.py:21
  42.2 40.9 %collective-permute-start.13 = (f32[1,32,64]{2,1,0:T(8,128)}, f32[1,32,64]{2,1,0:T(8,128)}, u32[]{:S(2)}, u32[]{:S(2)}) collective-permute-start(f32[1,32,64]{2,1,0:T(8,128)} %get-tuple-element.361), channel_id=1, source_target_pairs={{0,4},{4,8},{8,12},{1,5},{5,9},{9,13},{2,6},{6,10},{10,14},{3,7},{... | collective-permute-start | bytes 24584 | tf_op jit(solution)/shard_map/ppermute | solution.py:20
  50.4 85.6 %collective-permute-start.24 = (f32[1,16,32]{2,1,0:T(8,128)S(1)}, f32[1,16,32]{2,1,0:T(8,128)S(1)}, u32[]{:S(2)}, u32[]{:S(2)}) collective-permute-start(f32[1,16,32]{2,1,0:T(8,128)S(1)} %get-tuple-element.421), channel_id=1, source_target_pairs={{4,0},{8,4},{12,8},{5,1},{9,5},{13,9},{6,2},{10,6},{14,10},{7,3},{... | collective-permute-start | bytes 6152 | tf_op jit(solution)/shard_map/ppermute | solution.py:21
  60.1 6.6 %collective-permute-start.4 = (f32[1,1,64,128]{3,2,1,0:T(8,128)S(1)}, f32[1,1,64,128]{3,2,1,0:T(8,128)S(1)}, u32[]{:S(2)}, u32[]{:S(2)}) collective-permute-start(f32[1,1,64,128]{3,2,1,0:T(8,128)S(1)} %get-tuple-element.303), channel_id=1, source_target_pairs={{4,0},{8,4},{12,8},{5,1},{9,5},{13,9},{6,2},{10,6},{14,10},{7,3},{... | collective-permute-start | bytes 98312 | tf_op jit(solution)/shard_map/ppermute | solution.py:21
  61.4 6.8 %collective-permute-start.5 = (f32[1,1,64,128]{3,2,1,0:T(8,128)S(1)}, f32[1,1,64,128]{3,2,1,0:T(8,128)S(1)}, u32[]{:S(2)}, u32[]{:S(2)}) collective-permute-start(f32[1,1,64,128]{3,2,1,0:T(8,128)S(1)} %get-tuple-element.302), channel_id=1, source_target_pairs={{0,4},{4,8},{8,12},{1,5},{5,9},{9,13},{2,6},{6,10},{10,14},{3,7},{... | collective-permute-start | bytes 98312 | tf_op jit(solution)/shard_map/ppermute | solution.py:20
  69.4 7.4 %collective-permute-start.7 = (f32[1,10,1,128]{3,2,1,0:T(1,128)S(1)}, f32[1,10,1,128]{3,2,1,0:T(1,128)S(1)}, u32[]{:S(2)}, u32[]{:S(2)}) collective-permute-start(f32[1,10,1,128]{3,2,1,0:T(1,128)S(1)} %get-tuple-element.265), channel_id=1, source_target_pairs={{0,2},{1,3},{4,6},{5,7},{8,10},{9,11},{12,14},{13,15},{16,18},{17,... | collective-permute-start | bytes 15368 | tf_op jit(solution)/shard_map/ppermute | solution.py:20
  72.6 63.3 %collective-permute-start.25 = (f32[1,16,32]{2,1,0:T(8,128)S(1)}, f32[1,16,32]{2,1,0:T(8,128)S(1)}, u32[]{:S(2)}, u32[]{:S(2)}) collective-permute-start(f32[1,16,32]{2,1,0:T(8,128)S(1)} %get-tuple-element.422), channel_id=1, source_target_pairs={{0,4},{4,8},{8,12},{1,5},{5,9},{9,13},{2,6},{6,10},{10,14},{3,7},{... | collective-permute-start | bytes 6152 | tf_op jit(solution)/shard_map/ppermute | solution.py:20
  77.2 7.9 %collective-permute-start.8 = (f32[1,1,64,128]{3,2,1,0:T(8,128)S(1)}, f32[1,1,64,128]{3,2,1,0:T(8,128)S(1)}, u32[]{:S(2)}, u32[]{:S(2)}) collective-permute-start(f32[1,1,64,128]{3,2,1,0:T(8,128)S(1)} %get-tuple-element.299), channel_id=1, source_target_pairs={{4,0},{8,4},{12,8},{5,1},{9,5},{13,9},{6,2},{10,6},{14,10},{7,3},{... | collective-permute-start | bytes 98312 | tf_op jit(solution)/shard_map/ppermute | solution.py:21
  78.5 6.6 %collective-permute-start.9 = (f32[1,1,64,128]{3,2,1,0:T(8,128)S(1)}, f32[1,1,64,128]{3,2,1,0:T(8,128)S(1)}, u32[]{:S(2)}, u32[]{:S(2)}) collective-permute-start(f32[1,1,64,128]{3,2,1,0:T(8,128)S(1)} %get-tuple-element.298), channel_id=1, source_target_pairs={{0,4},{4,8},{8,12},{1,5},{5,9},{9,13},{2,6},{6,10},{10,14},{3,7},{... | collective-permute-start | bytes 98312 | tf_op jit(solution)/shard_map/ppermute | solution.py:20
  83.8 32.5 %collective-permute-start.14 = (f32[6,1,64]{2,1,0:T(1,128)S(1)}, f32[6,1,64]{2,1,0:T(1,128)S(1)}, u32[]{:S(2)}, u32[]{:S(2)}) collective-permute-start(f32[6,1,64]{2,1,0:T(1,128)S(1)} %get-tuple-element.325), channel_id=1, source_target_pairs={{2,0},{3,1},{6,4},{7,5},{10,8},{11,9},{14,12},{15,13},{18,16},{19,... | collective-permute-start | bytes 4616 | tf_op jit(solution)/shard_map/ppermute | solution.py:21
  89.6 26.7 %collective-permute-start.15 = (f32[6,1,64]{2,1,0:T(1,128)S(1)}, f32[6,1,64]{2,1,0:T(1,128)S(1)}, u32[]{:S(2)}, u32[]{:S(2)}) collective-permute-start(f32[6,1,64]{2,1,0:T(1,128)S(1)} %get-tuple-element.324), channel_id=1, source_target_pairs={{0,2},{1,3},{4,6},{5,7},{8,10},{9,11},{12,14},{13,15},{16,18},{17,... | collective-permute-start | bytes 4616 | tf_op jit(solution)/shard_map/ppermute | solution.py:20
  129.8 10.5 %collective-permute-start.20 = (f32[1,1,32,64]{3,2,1,0:T(8,128)S(1)}, f32[1,1,32,64]{3,2,1,0:T(8,128)S(1)}, u32[]{:S(2)}, u32[]{:S(2)}) collective-permute-start(f32[1,1,32,64]{3,2,1,0:T(8,128)S(1)} %get-tuple-element.353), channel_id=1, source_target_pairs={{4,0},{8,4},{12,8},{5,1},{9,5},{13,9},{6,2},{10,6},{14,10},{7,3},{... | collective-permute-start | bytes 24584 | tf_op jit(solution)/shard_map/ppermute | solution.py:21
  131.1 9.2 %collective-permute-start.21 = (f32[1,1,32,64]{3,2,1,0:T(8,128)S(1)}, f32[1,1,32,64]{3,2,1,0:T(8,128)S(1)}, u32[]{:S(2)}, u32[]{:S(2)}) collective-permute-start(f32[1,1,32,64]{3,2,1,0:T(8,128)S(1)} %get-tuple-element.352), channel_id=1, source_target_pairs={{0,4},{4,8},{8,12},{1,5},{5,9},{9,13},{2,6},{6,10},{10,14},{3,7},{... | collective-permute-start | bytes 24584 | tf_op jit(solution)/shard_map/ppermute | solution.py:20
  136.0 14.9 %collective-permute-start.26 = (f32[4,1,32]{2,1,0:T(1,128)S(1)}, f32[4,1,32]{2,1,0:T(1,128)S(1)}, u32[]{:S(2)}, u32[]{:S(2)}) collective-permute-start(f32[4,1,32]{2,1,0:T(1,128)S(1)} %get-tuple-element.385), channel_id=1, source_target_pairs={{2,0},{3,1},{6,4},{7,5},{10,8},{11,9},{14,12},{15,13},{18,16},{19,... | collective-permute-start | bytes 1544 | tf_op jit(solution)/shard_map/ppermute | solution.py:21
  137.3 13.6 %collective-permute-start.27 = (f32[4,1,32]{2,1,0:T(1,128)S(1)}, f32[4,1,32]{2,1,0:T(1,128)S(1)}, u32[]{:S(2)}, u32[]{:S(2)}) collective-permute-start(f32[4,1,32]{2,1,0:T(1,128)S(1)} %get-tuple-element.384), channel_id=1, source_target_pairs={{0,2},{1,3},{4,6},{5,7},{8,10},{9,11},{12,14},{13,15},{16,18},{17,... | collective-permute-start | bytes 1544 | tf_op jit(solution)/shard_map/ppermute | solution.py:20
  158.3 19.8 %collective-permute-start.30 = (f32[1,4,1,32]{3,2,1,0:T(1,128)S(1)}, f32[1,4,1,32]{3,2,1,0:T(1,128)S(1)}, u32[]{:S(2)}, u32[]{:S(2)}) collective-permute-start(f32[1,4,1,32]{3,2,1,0:T(1,128)S(1)} %get-tuple-element.382), channel_id=1, source_target_pairs={{2,0},{3,1},{6,4},{7,5},{10,8},{11,9},{14,12},{15,13},{18,16},{19,... | collective-permute-start | bytes 1544 | tf_op jit(solution)/shard_map/ppermute | solution.py:21
  159.6 18.5 %collective-permute-start.31 = (f32[1,4,1,32]{3,2,1,0:T(1,128)S(1)}, f32[1,4,1,32]{3,2,1,0:T(1,128)S(1)}, u32[]{:S(2)}, u32[]{:S(2)}) collective-permute-start(f32[1,4,1,32]{3,2,1,0:T(1,128)S(1)} %get-tuple-element.383), channel_id=1, source_target_pairs={{0,2},{1,3},{4,6},{5,7},{8,10},{9,11},{12,14},{13,15},{16,18},{17,... | collective-permute-start | bytes 1544 | tf_op jit(solution)/shard_map/ppermute | solution.py:20
  237.3 6.3 %collective-permute-start.45 = (f32[1,1,32,64]{3,2,1,0:T(8,128)S(1)}, f32[1,1,32,64]{3,2,1,0:T(8,128)S(1)}, u32[]{:S(2)}, u32[]{:S(2)}) collective-permute-start(f32[1,1,32,64]{3,2,1,0:T(8,128)S(1)} %get-tuple-element.348), channel_id=1, source_target_pairs={{0,4},{4,8},{8,12},{1,5},{5,9},{9,13},{2,6},{6,10},{10,14},{3,7},{... | collective-permute-start | bytes 24584 | tf_op jit(solution)/shard_map/ppermute | solution.py:20
  262.2 6.9 %collective-permute-start.52 = (f32[1,1,64,128]{3,2,1,0:T(8,128)S(1)}, f32[1,1,64,128]{3,2,1,0:T(8,128)S(1)}, u32[]{:S(2)}, u32[]{:S(2)}) collective-permute-start(f32[1,1,64,128]{3,2,1,0:T(8,128)S(1)} %get-tuple-element.295), channel_id=1, source_target_pairs={{4,0},{8,4},{12,8},{5,1},{9,5},{13,9},{6,2},{10,6},{14,10},{7,3},{... | collective-permute-start | bytes 98312 | tf_op jit(solution)/shard_map/ppermute | solution.py:21
  263.5 6.4 %collective-permute-start.53 = (f32[1,1,64,128]{3,2,1,0:T(8,128)S(1)}, f32[1,1,64,128]{3,2,1,0:T(8,128)S(1)}, u32[]{:S(2)}, u32[]{:S(2)}) collective-permute-start(f32[1,1,64,128]{3,2,1,0:T(8,128)S(1)} %get-tuple-element.294), channel_id=1, source_target_pairs={{0,4},{4,8},{8,12},{1,5},{5,9},{9,13},{2,6},{6,10},{10,14},{3,7},{... | collective-permute-start | bytes 98312 | tf_op jit(solution)/shard_map/ppermute | solution.py:20
  275.5 6.8 %collective-permute-start.56 = (f32[1,1,64,128]{3,2,1,0:T(8,128)S(1)}, f32[1,1,64,128]{3,2,1,0:T(8,128)S(1)}, u32[]{:S(2)}, u32[]{:S(2)}) collective-permute-start(f32[1,1,64,128]{3,2,1,0:T(8,128)S(1)} %get-tuple-element.291), channel_id=1, source_target_pairs={{4,0},{8,4},{12,8},{5,1},{9,5},{13,9},{6,2},{10,6},{14,10},{7,3},{... | collective-permute-start | bytes 98312 | tf_op jit(solution)/shard_map/ppermute | solution.py:21
  276.8 6.4 %collective-permute-start.57 = (f32[1,1,64,128]{3,2,1,0:T(8,128)S(1)}, f32[1,1,64,128]{3,2,1,0:T(8,128)S(1)}, u32[]{:S(2)}, u32[]{:S(2)}) collective-permute-start(f32[1,1,64,128]{3,2,1,0:T(8,128)S(1)} %get-tuple-element.290), channel_id=1, source_target_pairs={{0,4},{4,8},{8,12},{1,5},{5,9},{9,13},{2,6},{6,10},{10,14},{3,7},{... | collective-permute-start | bytes 98312 | tf_op jit(solution)/shard_map/ppermute | solution.py:20
  328.1 6.4 %collective-permute-start.65 = (f32[1,1,64,128]{3,2,1,0:T(8,128)S(1)}, f32[1,1,64,128]{3,2,1,0:T(8,128)S(1)}, u32[]{:S(2)}, u32[]{:S(2)}) collective-permute-start(f32[1,1,64,128]{3,2,1,0:T(8,128)S(1)} %get-tuple-element.282), channel_id=1, source_target_pairs={{0,4},{4,8},{8,12},{1,5},{5,9},{9,13},{2,6},{6,10},{10,14},{3,7},{... | collective-permute-start | bytes 98312 | tf_op jit(solution)/shard_map/ppermute | solution.py:20
  366.4 6.3 %collective-permute-start.69 = (f32[1,1,32,64]{3,2,1,0:T(8,128)S(1)}, f32[1,1,32,64]{3,2,1,0:T(8,128)S(1)}, u32[]{:S(2)}, u32[]{:S(2)}) collective-permute-start(f32[1,1,32,64]{3,2,1,0:T(8,128)S(1)} %get-tuple-element.340), channel_id=1, source_target_pairs={{0,4},{4,8},{8,12},{1,5},{5,9},{9,13},{2,6},{6,10},{10,14},{3,7},{... | collective-permute-start | bytes 24584 | tf_op jit(solution)/shard_map/ppermute | solution.py:20
  468.6 6.3 %collective-permute-start.93 = (f32[1,1,32,64]{3,2,1,0:T(8,128)S(1)}, f32[1,1,32,64]{3,2,1,0:T(8,128)S(1)}, u32[]{:S(2)}, u32[]{:S(2)}) collective-permute-start(f32[1,1,32,64]{3,2,1,0:T(8,128)S(1)} %get-tuple-element.332), channel_id=1, source_target_pairs={{0,4},{4,8},{8,12},{1,5},{5,9},{9,13},{2,6},{6,10},{10,14},{3,7},{... | collective-permute-start | bytes 24584 | tf_op jit(solution)/shard_map/ppermute | solution.py:20
  494.8 6.4 %collective-permute-start.101 = (f32[1,1,64,128]{3,2,1,0:T(8,128)S(1)}, f32[1,1,64,128]{3,2,1,0:T(8,128)S(1)}, u32[]{:S(2)}, u32[]{:S(2)}) collective-permute-start(f32[1,1,64,128]{3,2,1,0:T(8,128)S(1)} %get-tuple-element.278), channel_id=1, source_target_pairs={{0,4},{4,8},{8,12},{1,5},{5,9},{9,13},{2,6},{6,10},{10,14},{3,7},{... | collective-permute-start | bytes 98312 | tf_op jit(solution)/shard_map/ppermute | solution.py:20
  508.1 6.4 %collective-permute-start.105 = (f32[1,1,64,128]{3,2,1,0:T(8,128)S(1)}, f32[1,1,64,128]{3,2,1,0:T(8,128)S(1)}, u32[]{:S(2)}, u32[]{:S(2)}) collective-permute-start(f32[1,1,64,128]{3,2,1,0:T(8,128)S(1)} %get-tuple-element.274), channel_id=1, source_target_pairs={{0,4},{4,8},{8,12},{1,5},{5,9},{9,13},{2,6},{6,10},{10,14},{3,7},{... | collective-permute-start | bytes 98312 | tf_op jit(solution)/shard_map/ppermute | solution.py:20
  520.0 6.8 %collective-permute-start.108 = (f32[2,1,64,128]{3,2,1,0:T(8,128)S(1)}, f32[2,1,64,128]{3,2,1,0:T(8,128)S(1)}, u32[]{:S(2)}, u32[]{:S(2)}) collective-permute-start(f32[2,1,64,128]{3,2,1,0:T(8,128)S(1)} %get-tuple-element.249), channel_id=1, source_target_pairs={{4,0},{8,4},{12,8},{5,1},{9,5},{13,9},{6,2},{10,6},{14,10},{7,3},{... | collective-permute-start | bytes 196616 | tf_op jit(solution)/shard_map/ppermute | solution.py:21
  521.3 6.7 %collective-permute-start.109 = (f32[2,1,64,128]{3,2,1,0:T(8,128)S(1)}, f32[2,1,64,128]{3,2,1,0:T(8,128)S(1)}, u32[]{:S(2)}, u32[]{:S(2)}) collective-permute-start(f32[2,1,64,128]{3,2,1,0:T(8,128)S(1)} %get-tuple-element.248), channel_id=1, source_target_pairs={{0,4},{4,8},{8,12},{1,5},{5,9},{9,13},{2,6},{6,10},{10,14},{3,7},{... | collective-permute-start | bytes 196616 | tf_op jit(solution)/shard_map/ppermute | solution.py:20
  (88 other events, 774.3 us)
Sparse Core Ops, SparseCore 0:
  534.5 14.5 reduce-scatter.1
where the time goes:
time: 559 us; the launch traced here: 556 us
  starting transfers between devices  290 us (52%)
  local copies, waits for them, and re-layouts  78 us (14%)
  blocking collectives  65.2 us (12%)
  waiting for transfers between devices  62.1 us (11%)
  other arithmetic  42.2 us (8%)
  between operations  16.2 us (3%)
    ppermute x56, starting transfers between devices, extended(): before = lax.ppermute(last, axis, up)  218 us
    ppermute x56, starting transfers between devices, extended(): after = lax.ppermute(leading, axis, down)  72.3 us
    reshape x5, local copies, waits for them, and re-layouts, restrict(): field.reshape(leading + (extent[0] // 2, 2, extent[1] // 2, 2, extent[2]...  62.1 us
    ppermute x56, waiting for transfers between devices, extended(): before = lax.ppermute(last, axis, up)  46.6 us
    all_gather x2, blocking collectives, part_cycle(): blocks = lax.all_gather(source[None], ('gx', 'gy'), axis=0, tiled=True)  31 us
    reduce_sum x11, other arithmetic, restrict(): return shaped.mean(axis=(-5, -3, -1))  25.3 us
    psum x1, blocking collectives, per_device(): readings = lax.psum(local_values, ('gx', 'gy'))  18.7 us
    all_gather x1, blocking collectives, per_device(): blocks = lax.all_gather(conduct[None], ('gx', 'gy'), axis=0, tiled=True)  15.5 us
  transfers between devices with their start and end apart: 113, of which 48 were waited for; matrix products, arithmetic and copies ran while one was open for 12% of the time, Pallas kernels for 0%

commit v1 on v0

--- a/solution.py
+++ b/solution.py
@@ -1,6 +1,10 @@
+import functools
+
 import jax
 import jax.numpy as jnp
 from jax import lax
+from jax.experimental import pallas as pl
+from jax.experimental.pallas import tpu as pltpu
 from jax.sharding import PartitionSpec as P
 
 LEVELS = 4
@@ -8,6 +12,613 @@
 
 
 DAMPING = 0.8
+
+EDGE = 8
+LANES = 128
+REPLICATED_BYTES = 4 * 2**20
+VMEM_BYTES = 56 * 2**20
+
+
+def halves(value):
+    high = value.astype(jnp.bfloat16)
+    return high, (value - high.astype(jnp.float32)).astype(jnp.bfloat16)
+
+
+def product(value, matrix):
+    high, low = halves(value)
+    return jnp.dot(high, matrix, preferred_element_type=jnp.float32) + jnp.dot(
+        low, matrix, preferred_element_type=jnp.float32
+    )
+
+
+def lane_of(shape):
+    return lax.broadcasted_iota(jnp.int32, shape, len(shape) - 1)
+
+
+def row_of(shape):
+    return lax.broadcasted_iota(jnp.int32, shape, len(shape) - 2)
+
+
+def up(field, axis, step=1):
+    return pltpu.roll(field, field.shape[axis] - step, axis)
+
+
+def down(field, axis, step=1):
+    return pltpu.roll(field, step, axis)
+
+
+def masked(keep, field):
+    return jnp.where(keep, field, 0.0)
+
+
+def matrix_of(rows, cols, test, value):
+    shape = (rows, cols)
+    return jnp.where(test(row_of(shape), lane_of(shape)), value, 0.0).astype(jnp.bfloat16)
+
+
+def coarse_coefficients(cond, others, keeps, level_scale):
+    total = 6.0 * cond
+    for other in others:
+        total = total + other
+    total = 0.5 * total
+    valid = cond > 0.0
+    inverse = masked(valid, DAMPING / jnp.where(valid, total, 1.0))
+    links = []
+    for other, keep in zip(others, keeps):
+        link = inverse * (0.5 * (cond + other))
+        links.append(link if keep is None else masked(keep, link))
+    return links, inverse * (1.0 / level_scale), masked(valid, total * (level_scale / DAMPING))
+
+
+def replicated_kernel(
+    dims,
+    blocks_ref,
+    place_ref,
+    cells_ref,
+    stations_ref,
+    currents_ref,
+    receivers_ref,
+    observed_ref,
+    potentials_ref,
+    gradient_ref,
+    cond,
+    link_x,
+    link_y,
+    link_z,
+    weight,
+    diag,
+    source,
+    first,
+    second,
+    forward,
+    pair_rows,
+    cond1,
+    links1,
+    weight1,
+    back1,
+    field1,
+    turned1,
+    other1,
+    turned_other1,
+    base1,
+    links2,
+    weight2,
+    back2,
+    rows2,
+    gathered,
+    sems,
+):
+    nx, ny, rows, cols, count_x, count_y, count_s = dims
+    f32 = jnp.float32
+    electrodes = stations_ref.shape[1]
+    slabs1 = nx // 4
+    rows1 = ny // 2
+    rows2_count = ny // 4
+    rows3 = ny // 8
+    slabs3 = nx // 8
+    inner = pl.ds(EDGE, ny)
+    above = pl.ds(EDGE + 1, ny)
+    below = pl.ds(EDGE - 1, ny)
+
+    part = rows // count_s
+    copies = []
+    for index_x in range(count_x):
+        for index_y in range(count_y):
+            for index_s in range(count_s):
+                block = (index_x * count_y + index_y) * count_s + index_s
+                copies.append(
+                    pltpu.make_async_copy(
+                        blocks_ref.at[block],
+                        cond.at[
+                            pl.ds(1 + index_x * rows + index_s * part, part),
+                            pl.ds(EDGE + index_y * cols, cols),
+                            :,
+                        ],
+                        sems.at[block],
+                    )
+                )
+    for copy in copies:
+        copy.start()
+
+    edge_plane = jnp.zeros((ny + 2 * EDGE, LANES), f32)
+    edge_rows = jnp.zeros((EDGE, LANES), f32)
+    for array in (cond, first, second, forward):
+        array[0] = edge_plane
+        array[nx + 1] = edge_plane
+
+    def clear_edges(x, carry):
+        for array in (cond, first, second, forward):
+            array[x + 1, pl.ds(0, EDGE), :] = edge_rows
+            array[x + 1, pl.ds(EDGE + ny, EDGE), :] = edge_rows
+        link_y[x, pl.ds(0, EDGE), :] = edge_rows
+        return carry
+
+    lax.fori_loop(0, nx, clear_edges, 0)
+    plane1 = jnp.zeros((rows1, LANES), f32)
+    for array in (turned1, turned_other1):
+        array[0] = plane1
+        array[slabs1 + 1] = plane1
+
+    station_row = stations_ref[...]
+    station_line = station_row // LANES
+    station_z = station_row % LANES
+    restrict1 = [
+        matrix_of(LANES, LANES, lambda r, c: c == r // 2 + 64 * p, 0.125) for p in range(2)
+    ]
+    restrict2 = matrix_of(LANES, LANES, lambda r, c: c == r % 64 // 2, 0.125)
+    expand2 = matrix_of(LANES, LANES, lambda r, c: r == c % 64 // 2, 1.0)
+    expand1 = [
+        matrix_of(LANES, LANES, lambda r, c: r == c // 2 + 64 * p, 1.0) for p in range(2)
+    ]
+    restrict3 = [
+        matrix_of(LANES, LANES, lambda r, c: (r < 32) & (c == r // 2 + 16 * x), 0.125)
+        for x in range(slabs3)
+    ]
+    expand3 = [
+        matrix_of(LANES, LANES, lambda r, c: (c < 32) & (r == c // 2 + 16 * x), 1.0)
+        for x in range(slabs3)
+    ]
+
+    for copy in copies:
+        copy.wait()
+
+    lane0 = lane_of((ny, LANES))
+    not_last_z = lane0 < LANES - 1
+    not_first_z = lane0 > 0
+
+    def setup(x, carry):
+        here = cond[x + 1, inner, :]
+        next_x = cond[x + 2, inner, :]
+        next_y = cond[x + 1, above, :]
+        next_z = masked(not_last_z, up(here, 1))
+        link_x[x + 1] = 0.5 * (here + next_x)
+        link_y[x, inner, :] = 0.5 * (here + next_y)
+        link_z[x] = masked(not_last_z, 0.5 * (here + next_z))
+        total = next_x + cond[x, inner, :] + next_y + cond[x + 1, below, :]
+        total = total + next_z + masked(not_first_z, down(here, 1))
+        total = 3.0 * here + 0.5 * total
+        diag[x] = total
+        weight[x] = DAMPING / total
+        return carry
+
+    link_x[0] = jnp.zeros((ny, LANES), f32)
+    lax.fori_loop(0, nx, setup, 0)
+
+    def pairs_in_y(ref, index, count):
+        return ref[index, pl.ds(0, count, stride=2), :] + ref[index, pl.ds(1, count, stride=2), :]
+
+    def restrict_slabs(read, slab):
+        result = None
+        for p in range(2):
+            pair_rows[p] = read(4 * slab + 2 * p) + read(4 * slab + 2 * p + 1)
+        for p in range(2):
+            term = product(pairs_in_y(pair_rows, p, rows1), restrict1[p])
+            result = term if result is None else result + term
+        return result
+
+    def restrict_cond(slab, carry):
+        cond1[slab] = restrict_slabs(lambda x: cond[x + 1, inner, :], slab)
+        return carry
+
+    lax.fori_loop(0, slabs1, restrict_cond, 0)
+
+    lane1 = lane_of((rows1, LANES))
+    row1 = row_of((rows1, LANES))
+    even = lane1 < 64
+    keeps1 = [
+        None,
+        None,
+        row1 < rows1 - 1,
+        row1 > 0,
+        lane1 % 64 < 63,
+        lane1 % 64 > 0,
+    ]
+    for slab in range(slabs1):
+        here = cond1[slab]
+        turned = down(here, 1, 64)
+        before = down(cond1[slab - 1], 1, 64) if slab > 0 else plane1
+        after = down(cond1[slab + 1], 1, 64) if slab < slabs1 - 1 else plane1
+        others = [jnp.where(even, turned, after), jnp.where(even, before, turned)]
+        others += [
+            masked(keeps1[2], up(here, 0)),
+            masked(keeps1[3], down(here, 0)),
+            masked(keeps1[4], up(here, 1)),
+            masked(keeps1[5], down(here, 1)),
+        ]
+        links, inverse, back = coarse_coefficients(here, others, keeps1, 0.25)
+        for index, link in enumerate(links):
+            links1[index, slab] = link
+        weight1[slab] = inverse
+        back1[slab] = back
+
+    def restrict_level2(read, slab):
+        pair_rows[0, pl.ds(0, rows1), :] = read(slab)
+        return product(pairs_in_y(pair_rows, 0, rows2_count), restrict2)
+
+    total2 = slabs1 * rows2_count
+    for slab in range(slabs1):
+        rows2[0, pl.ds(slab * rows2_count, rows2_count), :] = restrict_level2(
+            lambda s: cond1[s], slab
+        )
+    row2 = row_of((total2, LANES))
+    lane2 = lane_of((total2, LANES))
+    here = rows2[0]
+    keeps2 = [
+        row2 < total2 - rows2_count,
+        row2 >= rows2_count,
+        row2 % rows2_count < rows2_count - 1,
+        row2 % rows2_count > 0,
+        lane2 < 31,
+        lane2 > 0,
+    ]
+    shifts2 = [(up, 0, rows2_count), (down, 0, rows2_count), (up, 0, 1), (down, 0, 1), (up, 1, 1), (down, 1, 1)]
+    others = [masked(k, s(here, axis, step)) for k, (s, axis, step) in zip(keeps2, shifts2)]
+    links, inverse, back = coarse_coefficients(here, others, keeps2, 0.25**2)
+    for index, link in enumerate(links):
+        links2[index] = link
+    weight2[...] = inverse
+    back2[...] = back
+
+    def restrict_level3(value):
+        result = None
+        for x in range(slabs3):
+            start = 2 * x * rows2_count
+            pair_rows[0, pl.ds(0, rows2_count), :] = (
+                value[start : start + rows2_count]
+                + value[start + rows2_count : start + 2 * rows2_count]
+            )
+            term = product(pairs_in_y(pair_rows, 0, rows3), restrict3[x])
+            result = term if result is None else result + term
+        return result
+
+    row3 = row_of((rows3, LANES))
+    lane3 = lane_of((rows3, LANES))
+    used3 = lane3 < 16 * slabs3
+    keeps3 = [
+        lane3 < 16 * (slabs3 - 1),
+        (lane3 >= 16) & used3,
+        (row3 < rows3 - 1) & used3,
+        (row3 > 0) & used3,
+        (lane3 % 16 < 15) & used3,
+        (lane3 % 16 > 0) & used3,
+    ]
+    shifts3 = [(up, 1, 16), (down, 1, 16), (up, 0, 1), (down, 0, 1), (up, 1, 1), (down, 1, 1)]
+    here = restrict_level3(here)
+    others = [masked(k, s(here, axis, step)) for k, (s, axis, step) in zip(keeps3, shifts3)]
+    links3, weight3, _ = coarse_coefficients(here, others, keeps3, 0.25**3)
+
+    def neighbour_sum(value, links, shifts, base):
+        for link, (shift, axis, step) in zip(links, shifts):
+            base = base + link * shift(value, axis, step)
+        return base
+
+    def level3(rhs):
+        base = weight3 * rhs
+        value = base
+        for _ in range(COARSE_SWEEPS - 1):
+            value = neighbour_sum(value, links3, shifts3, base + (1.0 - DAMPING) * value)
+        return value
+
+    def level2(rhs):
+        base = weight2[...] * rhs
+        links = [links2.at[index] for index in range(6)]
+
+        def total(value):
+            result = base
+            for link, (shift, axis, step) in zip(links, shifts2):
+                result = result + link[...] * shift(value, axis, step)
+            return result
+
+        value = base
+        value = (1.0 - DAMPING) * value + total(value)
+        residual = (total(value) - DAMPING * value) * back2[...]
+        coarse = level3(restrict_level3(residual))
+        pieces = []
+        for x in range(slabs3):
+            wide = product(coarse, expand3[x])
+            pair_rows[0, pl.ds(0, rows3, stride=2), :] = wide
+            pair_rows[0, pl.ds(1, rows3, stride=2), :] = wide
+            piece = pair_rows[0, pl.ds(0, rows2_count), :]
+            pieces += [piece, piece]
+        value = value + jnp.concatenate(pieces, axis=0)
+        for _ in range(2):
+            value = (1.0 - DAMPING) * value + total(value)
+        return value
+
+    def total1(slab, value, turned):
+        here = value[slab]
+        mine = turned[slab + 1]
+        result = base1[slab]
+        result = result + links1[0, slab] * jnp.where(even, mine, turned[slab + 2])
+        result = result + links1[1, slab] * jnp.where(even, turned[slab], mine)
+        result = result + links1[2, slab] * up(here, 0) + links1[3, slab] * down(here, 0)
+        result = result + links1[4, slab] * up(here, 1) + links1[5, slab] * down(here, 1)
+        return here, result
+
+    def keep1(slab, value, field, turned):
+        field[slab] = value
+        turned[slab + 1] = down(value, 1, 64)
+
+    def sweep1(value, turned, out, turned_out):
+        def one(slab, carry):
+            here, result = total1(slab, value, turned)
+            keep1(slab, (1.0 - DAMPING) * here + result, out, turned_out)
+            return carry
+
+        lax.fori_loop(0, slabs1, one, 0)
+
+    def level1():
+        def begin(slab, carry):
+            keep1(slab, base1[slab], field1, turned1)
+            return carry
+
+        lax.fori_loop(0, slabs1, begin, 0)
+        sweep1(field1, turned1, other1, turned_other1)
+
+        def residual(slab, carry):
+            here, result = total1(slab, other1, turned_other1)
+            field1[slab] = (result - DAMPING * here) * back1[slab]
+            return carry
+
+        lax.fori_loop(0, slabs1, residual, 0)
+        for slab in range(slabs1):
+            rows2[0, pl.ds(slab * rows2_count, rows2_count), :] = restrict_level2(
+                lambda s: field1[s], slab
+            )
+        rows2[1] = level2(rows2[0])
+        for slab in range(slabs1):
+            wide = product(rows2[1, pl.ds(slab * rows2_count, rows2_count), :], expand2)
+            pair_rows[0, pl.ds(0, rows2_count, stride=2), :] = wide
+            pair_rows[0, pl.ds(1, rows2_count, stride=2), :] = wide
+            keep1(slab, other1[slab] + pair_rows[0, pl.ds(0, rows1), :], field1, turned1)
+        sweep1(field1, turned1, other1, turned_other1)
+        sweep1(other1, turned_other1, field1, turned1)
+
+    def total0(x, field):
+        here = field[x + 1, inner, :]
+        along_z = link_z[x]
+        result = source[x]
+        result = result + link_x[x + 1] * field[x + 2, inner, :]
+        result = result + link_x[x] * field[x, inner, :]
+        result = result + link_y[x, inner, :] * field[x + 1, above, :]
+        result = result + link_y[x, below, :] * field[x + 1, below, :]
+        result = result + along_z * up(here, 1) + down(along_z * here, 1)
+        return here, result
+
+    def sweep0(field, out, low, high):
+        def one(x, carry):
+            here, result = total0(x, field)
+            out[x + 1, inner, :] = (1.0 - DAMPING) * here + weight[x] * result
+            return carry
+
+        lax.fori_loop(low, high, one, 0)
+
+    lines = row_of((ny, electrodes))
+
+    def spread(amounts):
+        weighted = masked(row_of((LANES, electrodes)) == station_z, amounts)
+        high, low = halves(weighted)
+        table = jnp.concatenate([high, low], axis=0)
+
+        def one(x, carry):
+            chosen = jnp.where(lines + x * ny == station_line, 1.0, 0.0).astype(jnp.bfloat16)
+            both = lax.dot_general(
+                chosen, table, (((1,), (1,)), ((), ())), preferred_element_type=f32
+            )
+            value = both[:, :LANES] + both[:, LANES:]
+            source[x] = value
+            first[x + 1, inner, :] = weight[x] * value
+            return carry
+
+        lax.fori_loop(0, nx, one, 0)
+
+    def descend():
+        sweep0(first, second, 0, nx)
+
+        def residual(x):
+            here, result = total0(x, second)
+            return result - diag[x] * here
+
+        def one(slab, carry):
+            base1[slab] = weight1[slab] * restrict_slabs(residual, slab)
+            return carry
+
+        lax.fori_loop(0, slabs1, one, 0)
+        level1()
+
+    def ascend(last, low, high, ends):
+        def one(slab, carry):
+            value = field1[slab]
+            for p in range(2):
+                wide = product(value, expand1[p])
+                pair_rows[p, pl.ds(0, rows1, stride=2), :] = wide
+                pair_rows[p, pl.ds(1, rows1, stride=2), :] = wide
+            for p in range(2):
+                for q in range(2):
+                    x = 4 * slab + 2 * p + q
+                    second[x + 1, inner, :] = second[x + 1, inner, :] + pair_rows[p]
+            return carry
+
+        slab_low, slab_high = ends
+        lax.fori_loop(slab_low, slab_high, one, 0)
+        sweep0(second, first, low[0], high[0])
+        sweep0(first, last, low[1], high[1])
+
+    spread(currents_ref[...])
+    descend()
+    ascend(forward, (0, 0), (nx, nx), (0, slabs1))
+
+    def read(electrode, carry):
+        line = cells_ref[electrode] // LANES
+        gathered[pl.ds(electrode, 1), :] = forward[line // ny + 1, pl.ds(EDGE + line % ny, 1), :]
+        return carry
+
+    lax.fori_loop(0, electrodes, read, 0, unroll=8)
+    turned = gathered[...].T
+    readings = jnp.sum(
+        masked(row_of((LANES, electrodes)) == station_z, turned), axis=0, keepdims=True
+    )
+    receivers = receivers_ref[...]
+    numbers = lane_of((receivers.shape[0], electrodes))
+    pairs = jnp.where(numbers == receivers[:, 0:1], 1.0, 0.0) - jnp.where(
+        numbers == receivers[:, 1:2], 1.0, 0.0
+    )
+    pairs = pairs.astype(jnp.bfloat16)
+
+    def exact(row, dims):
+        high = row.astype(jnp.bfloat16)
+        rest = row - high.astype(f32)
+        middle = rest.astype(jnp.bfloat16)
+        low = (rest - middle.astype(f32)).astype(jnp.bfloat16)
+        result = None
+        for piece in (low, middle, high):
+            wide = jnp.broadcast_to(piece, (16, row.shape[1]))
+            term = lax.dot_general(wide, pairs, (dims, ((), ())), preferred_element_type=f32)
+            result = term if result is None else result + term
+        return result[0:1]
+
+    misfit = exact(readings, ((1,), (1,))) - observed_ref[...]
+    spread(exact(misfit, ((1,), (0,))))
+    descend()
+    begin_x = place_ref[0]
+    begin_y = pl.multiple_of(place_ref[1], cols)
+    ascend(
+        second,
+        (jnp.maximum(begin_x - 2, 0), jnp.maximum(begin_x - 1, 0)),
+        (jnp.minimum(begin_x + rows + 2, nx), jnp.minimum(begin_x + rows + 1, nx)),
+        (jnp.maximum(begin_x - 3, 0) // 4, jnp.minimum(begin_x + rows + 3 + 3, nx) // 4),
+    )
+
+    chunk = cols // count_s
+    lane_c = lane_of((chunk, LANES))
+    for k in range(count_s):
+        offset = pl.multiple_of(begin_y + place_ref[2 + k], chunk)
+        mid = pl.ds(EDGE + offset, chunk)
+        nxt = pl.ds(EDGE + offset + 1, chunk)
+        prv = pl.ds(EDGE + offset - 1, chunk)
+
+        def one(x, carry):
+            here_u = forward[begin_x + x + 1, mid, :]
+            here_w = second[begin_x + x + 1, mid, :]
+            total = jnp.zeros_like(here_u)
+            for index, window in ((2, mid), (0, mid), (1, nxt), (1, prv)):
+                total = total + (here_u - forward[begin_x + x + index, window, :]) * (
+                    here_w - second[begin_x + x + index, window, :]
+                )
+            keep = lane_c < LANES - 1
+            ahead = (here_u - masked(keep, up(here_u, 1))) * (here_w - masked(keep, up(here_w, 1)))
+            total = total + ahead + jnp.where(lane_c > 0, down(ahead, 1), here_u * here_w)
+            gradient_ref[k, x] = -0.5 * total
+            return carry
+
+        lax.fori_loop(0, rows, one, 0)
+
+    def give(x, carry):
+        potentials_ref[x] = forward[begin_x + x + 1, pl.ds(EDGE + begin_y, cols), :]
+        return carry
+
+    lax.fori_loop(0, rows, give, 0)
+
+
+def replicated(conductivity, stations, currents, receivers, observed):
+    rows, cols, depth = conductivity.shape
+    count_x = lax.axis_size("gx")
+    count_y = lax.axis_size("gy")
+    count_s = lax.axis_size("shot")
+    nx, ny = rows * count_x, cols * count_y
+    shot = lax.axis_index("shot")
+    part = rows // count_s
+    mine = lax.dynamic_slice_in_dim(conductivity, shot * part, part, axis=0)
+    blocks = lax.all_gather(mine, ("gx", "gy", "shot"), axis=0, tiled=False)
+    chunk = cols // count_s
+    place = jnp.stack(
+        [lax.axis_index("gx") * rows, lax.axis_index("gy") * cols]
+        + [(shot + k) % count_s * chunk for k in range(count_s)]
+    ).astype(jnp.int32)
+    electrodes = stations.shape[0]
+    slabs1, rows1 = nx // 4, ny // 2
+    total2 = slabs1 * ny // 4
+    f32 = jnp.float32
+    padded = pltpu.VMEM((nx + 2, ny + 2 * EDGE, LANES), f32)
+    plain = pltpu.VMEM((nx, ny, LANES), f32)
+    small = pltpu.VMEM((slabs1, rows1, LANES), f32)
+    small_edge = pltpu.VMEM((slabs1 + 2, rows1, LANES), f32)
+    flat2 = pltpu.VMEM((total2, LANES), f32)
+    vmem = pl.BlockSpec(memory_space=pltpu.VMEM)
+    smem = pl.BlockSpec(memory_space=pltpu.SMEM)
+    dims = (nx, ny, rows, cols, count_x, count_y, count_s)
+    potentials, gradient = pl.pallas_call(
+        functools.partial(replicated_kernel, dims),
+        out_shape=(
+            jax.ShapeDtypeStruct((rows, cols, LANES), f32),
+            jax.ShapeDtypeStruct((count_s, rows, chunk, LANES), f32),
+        ),
+        in_specs=[pl.BlockSpec(memory_space=pl.ANY), smem, smem, vmem, vmem, vmem, vmem],
+        out_specs=(vmem, vmem),
+        scratch_shapes=[
+            padded,
+            pltpu.VMEM((nx + 1, ny, LANES), f32),
+            pltpu.VMEM((nx, ny + EDGE, LANES), f32),
+            plain,
+            plain,
+            plain,
+            plain,
+            padded,
+            padded,
+            padded,
+            pltpu.VMEM((2, ny, LANES), f32),
+            small,
+            pltpu.VMEM((6, slabs1, rows1, LANES), f32),
+            small,
+            small,
+            small,
+            small_edge,
+            small,
+            small_edge,
+            small,
+            pltpu.VMEM((6, total2, LANES), f32),
+            flat2,
+            flat2,
+            pltpu.VMEM((2, total2, LANES), f32),
+            pltpu.VMEM((electrodes, LANES), f32),
+            pltpu.SemaphoreType.DMA((count_x * count_y * count_s,)),
+        ],
+        compiler_params=pltpu.CompilerParams(vmem_limit_bytes=VMEM_BYTES),
+        cost_estimate=pl.CostEstimate(flops=200_000_000, bytes_accessed=4_000_000, transcendentals=0),
+    )(
+        blocks,
+        place,
+        stations,
+        stations.reshape(1, electrodes),
+        currents,
+        receivers,
+        observed,
+    )
+    summed = gradient[0]
+    for k in range(1, count_s):
+        pairs = [(i, (i + k) % count_s) for i in range(count_s)]
+        summed = summed + lax.ppermute(gradient[k], "shot", pairs)
+    return potentials[None], summed
 
 
 def extended(array, sides, width):
@@ -139,7 +750,7 @@
     return relaxed(field_rim(field), source, cond_pad, diag_level, level_scale)
 
 
-def per_device(conductivity, stations, currents, receivers, observed):
+def distributed(conductivity, stations, currents, receivers, observed):
     row_count, col_count, z_count = conductivity.shape
     shot_count = currents.shape[0]
     count_x = lax.axis_size("gx")
@@ -202,6 +813,14 @@
     return (potentials, summed)
 
 
+def per_device(conductivity, stations, currents, receivers, observed):
+    count = lax.axis_size("gx") * lax.axis_size("gy")
+    fits = conductivity.size * count * 4 <= REPLICATED_BYTES
+    fits = fits and conductivity.shape[2] == LANES and currents.shape[0] == 1
+    plan = replicated if fits else distributed
+    return plan(conductivity, stations, currents, receivers, observed)
+
+
 def solution(mesh):
     in_specs = (
         P(("grp", "gx"), "gy", None),

time: 559 us -> 139 us (0.25)
  starting transfers between devices: 290 us -> 0.66 us
  local copies, waits for them, and re-layouts: 78 us -> 4.02 us
  Pallas kernels: 0 us -> 68.3 us
  blocking collectives: 65.2 us -> 0 us
  other arithmetic: 42.2 us -> 2.23 us
  waiting for transfers between devices: 62.1 us -> 49 us
    ppermute x112 -> x1, starting transfers between devices: 290 us -> 0.62 us  [replicated(): summed = summed + lax.ppermute(gradient[k], 'shot', pairs)]
    pallas_call x0 -> x1, Pallas kernels: none -> 68.3 us  [replicated(): pl.pallas_call(functools.partial(replicated_kernel, dims), out_shape=(jax...]
    reshape x5 -> x0, local copies, waits for them, and re-layouts: 62.1 us -> none  [restrict(): field.reshape(leading + (extent[0] // 2, 2, extent[1] // 2, 2, extent[2]...]
    all_gather x3 -> x0, blocking collectives: 46.5 us -> none  [the longest x2 31 us: part_cycle(): blocks = lax.all_gather(source[None], ('gx', 'gy'), axis=0, tiled=True)]
    all_gather x0 -> x1, waiting for transfers between devices: none -> 43.8 us  [replicated(): blocks = lax.all_gather(mine, ('gx', 'gy', 'shot'), axis=0, tiled=False)]
    ppermute x112 -> x1, waiting for transfers between devices: 47.3 us -> 5.1 us  [replicated(): summed = summed + lax.ppermute(gradient[k], 'shot', pairs)]
    reduce_sum x12 -> x0, other arithmetic: 26.4 us -> none  [the longest x11 25.3 us: restrict(): return shaped.mean(axis=(-5, -3, -1))]
    psum x1 -> x0, blocking collectives: 18.7 us -> none  [per_device(): readings = lax.psum(local_values, ('gx', 'gy'))]
  transfers between devices with their start and end apart: 113 -> 2, of which waited for: 48 -> 2; matrix products, arithmetic and copies ran while one was open for 12% -> 2% of each run, Pallas kernels for 0% -> 0%
where the time goes in v1:
time: 139 us; the launch traced here: 138 us
  Pallas kernels  68.3 us (49%)
  waiting for transfers between devices  49 us (35%)
  between operations  14.1 us (10%)
  local copies, waits for them, and re-layouts  4.02 us (3%)
  other arithmetic  2.23 us (2%)
    pallas_call x1, Pallas kernels, replicated(): pl.pallas_call(functools.partial(replicated_kernel, dims), out_shape=(jax...  68.3 us
    all_gather x1, waiting for transfers between devices, replicated(): blocks = lax.all_gather(mine, ('gx', 'gy', 'shot'), axis=0, tiled=False)  43.8 us
    ppermute x1, waiting for transfers between devices, replicated(): summed = summed + lax.ppermute(gradient[k], 'shot', pairs)  5.1 us
  transfers between devices with their start and end apart: 2, of which 2 were waited for; matrix products, arithmetic and copies ran while one was open for 2% of the time, Pallas kernels for 0%

profile of v1, /device:TPU:0, one launch (start us, length us, event | category | flops | bytes accessed | tf_op | source)
XLA Modules:
  0.0 138.3 jit_solution(5612474099054952056)
XLA Ops:
  7.2 0.0 copy-start
  7.2 0.0 all-gather.3.cloned.1.call-start
  7.2 0.9 copy-done
  8.1 0.7 constant_dynamic-slice_fusion
  8.8 0.0 all-gather.3.cloned.1.call-update
  8.8 1.5 %copy.8.receivers_ref = s32[512,2]{1,0:T(8,128)} copy(s32[512,2]{0,1:T(2,128)} %param.8) | data formatting | bytes 8192 | tf_op args[3]
  10.4 0.7 pad_add_fusion.place_ref
  11.0 43.8 %all-gather.3.cloned.1.call-done = f32[64,64,128]{2,1,0:T(8,128)} async-done(((f32[4,64,128]{2,1,0:T(8,128)}), f32[64,64,128]{2,1,0:T(8,128)}) %all-gather.3.cloned.1.call-update) | async-done | bytes 2097168 | tf_op jit(solution)/shard_map/all_gather | solution.py:552
  54.9 68.3 %shard_map.68 = (f32[8,64,128]{2,1,0:T(8,128)}, f32[2,8,32,128]{3,2,1,0:T(8,128)}) custom-call(f32[16,4,64,128]{3,2,1,0:T(8,128)} %bitcast.11, s32[4]{0:T(128)} %pad_add_fusion.place_ref, s32[256]{0:T(256)} %cells_ref.1, s32[1,256]{1,0:T(1,128)} %bitcast.12, f32[1,256]{1,0:T(1,128)} %currents_ref.1, s32[512,2]{1,0:T(8,128)} %copy.8.receivers_ref, ...), custom_call_target="tpu_custom_call" | custom-call | flops 200000000 | bytes 4000000 | tf_op jit(solution)/shard_map/pallas_call | solution.py:570
  123.2 0.9 slice_bitcast_fusion
  124.1 0.6 collective-permute-start
  124.8 5.1 %collective-permute-done = f32[8,32,128]{2,1,0:T(8,128)S(1)} collective-permute-done((f32[8,32,128]{2,1,0:T(8,128)S(1)}, f32[8,32,128]{2,1,0:T(8,128)S(1)}, u32[]{:S(2)}, u32[]{:S(2)}) %collective-permute-start) | collective-permute-done | bytes 131104 | tf_op jit(solution)/shard_map/ppermute | solution.py:620
  129.9 1.6 %bitcast_add_fusion = f32[8,32,128]{2,1,0:T(8,128)} fusion(f32[8,32,128]{2,1,0:T(8,128)S(1)} %collective-permute-done, f32[2,8,32,128]{3,2,1,0:T(8,128)} %get-tuple-element.5), kind=kLoop, calls=%fused_computation | loop fusion | flops 32768 | bytes 393216 | tf_op jit(solution)/shard_map/add | solution.py:620
Async XLA Ops:
  7.2 1.0 copy-start
  7.2 47.7 %all-gather.3.cloned.1.call-start = ((), (), s32[]{:S(2)}) async-start(), calls=%async_computation | async-start | bytes 2228224 | tf_op jit(solution)/shard_map/all_gather | solution.py:552
  124.1 5.7 %collective-permute-start = (f32[8,32,128]{2,1,0:T(8,128)S(1)}, f32[8,32,128]{2,1,0:T(8,128)S(1)}, u32[]{:S(2)}, u32[]{:S(2)}) collective-permute-start(f32[8,32,128]{2,1,0:T(8,128)S(1)} %slice_bitcast_fusion), channel_id=1, source_target_pairs={{0,1},{1,0},{2,3},{3,2},{4,5},{5,4},{6,7},{7,6},{8,9},{9,8},{10,11... | collective-permute-start | bytes 393224 | tf_op jit(solution)/shard_map/ppermute | solution.py:620
Sparse Core Ops, SparseCore 0:
  10.8 44.0 all-gather.2

commit v2 on v0

--- a/solution.py
+++ b/solution.py
@@ -1,6 +1,10 @@
+import functools
+
 import jax
 import jax.numpy as jnp
 from jax import lax
+from jax.experimental import pallas as pl
+from jax.experimental.pallas import tpu as pltpu
 from jax.sharding import PartitionSpec as P
 
 LEVELS = 4
@@ -8,6 +12,513 @@
 
 
 DAMPING = 0.8
+
+SIDE = 8
+LANES = 128
+GROUP = 16
+VMEM_BYTES = 56 * 2**20
+
+
+def pieces_of(value, count):
+    pieces = []
+    for _ in range(count):
+        pieces.append(value.astype(jnp.bfloat16))
+        value = value - pieces[-1].astype(jnp.float32)
+    return pieces[::-1]
+
+
+def product(value, matrix, count, dims=((1,), (0,))):
+    result = None
+    for piece in pieces_of(value, count):
+        term = lax.dot_general(
+            piece, matrix, (dims, ((), ())), preferred_element_type=jnp.float32
+        )
+        result = term if result is None else result + term
+    return result
+
+
+def iota(shape, dim):
+    return lax.broadcasted_iota(jnp.int32, shape, dim)
+
+
+def lane_order():
+    row, col = iota((LANES, LANES), 0), iota((LANES, LANES), 1)
+    chosen = row == col % GROUP * SIDE + col // GROUP
+    return jnp.where(chosen, 1.0, 0.0).astype(jnp.bfloat16)
+
+
+def exchange_groups(tiles):
+    tiles = list(tiles)
+    group = iota(tiles[0].shape, 1) // GROUP
+    for bit in range(3):
+        step = 1 << bit
+        keep = (group & step) == 0
+        for low in range(SIDE):
+            if low & step == 0:
+                a, b = tiles[low], tiles[low | step]
+                tiles[low] = jnp.where(keep, a, pltpu.roll(b, step * GROUP, 1))
+                tiles[low | step] = jnp.where(keep, pltpu.roll(a, LANES - step * GROUP, 1), b)
+    return tiles
+
+
+def to_blocks_kernel(natural_ref, blocks_ref):
+    order = lane_order()
+    for x in range(SIDE):
+        tiles = product(natural_ref[x], order, 3)
+        tiles = [tiles[SIDE * k : SIDE * (k + 1)] for k in range(SIDE)]
+        for z, tile in enumerate(exchange_groups(tiles)):
+            blocks_ref[pl.ds((x * SIDE + z) * SIDE, SIDE), :] = tile
+
+
+def from_blocks(tiles, order):
+    natural = jnp.concatenate(exchange_groups(tiles), axis=0)
+    return product(natural, order, 3, ((1,), (1,)))
+
+
+def block_up(field, axis):
+    if axis == 0:
+        return pltpu.roll(field, 6, 1)
+    if axis == 2:
+        return pltpu.roll(field, LANES - 1, 2)
+    turned = pltpu.roll(field, LANES - GROUP, 2)
+    return jnp.where(iota(field.shape, 2) < LANES - GROUP, turned, pltpu.roll(turned, 7, 1))
+
+
+def block_down(field, axis):
+    if axis == 0:
+        return pltpu.roll(field, 2, 1)
+    if axis == 2:
+        return pltpu.roll(field, 1, 2)
+    turned = pltpu.roll(field, GROUP, 2)
+    return jnp.where(iota(field.shape, 2) >= GROUP, turned, pltpu.roll(turned, 1, 1))
+
+
+def inside_up(field, axis):
+    sub, lane = iota(field.shape, 1), iota(field.shape, 2)
+    if axis == 0:
+        keep = sub < 6
+    elif axis == 1:
+        keep = (lane < LANES - GROUP) | (sub % 2 == 0)
+    else:
+        keep = lane % GROUP < GROUP - 1
+    return jnp.where(keep, field, 0.0)
+
+
+def inside_down(field, axis):
+    sub, lane = iota(field.shape, 1), iota(field.shape, 2)
+    if axis == 0:
+        keep = sub >= 2
+    elif axis == 1:
+        keep = (lane >= GROUP) | (sub % 2 == 1)
+    else:
+        keep = lane % GROUP > 0
+    return jnp.where(keep, field, 0.0)
+
+
+def pair_rows(row):
+    count = row.shape[0] // 2
+    return jnp.concatenate([row[2 * i : 2 * i + 1] + row[2 * i + 1 : 2 * i + 2] for i in range(count)])
+
+
+def twice(row):
+    return jnp.concatenate([row[i // 2 : i // 2 + 1] for i in range(2 * row.shape[0])])
+
+
+class Edged:
+    def __init__(self, ref, side):
+        self.ref, self.side = ref, side
+
+    def start(self, x, z, y=0):
+        wide = self.side + 2
+        return (((x + 1) * wide + z + 1) * wide + y + 1) * SIDE
+
+    def __getitem__(self, at):
+        x, z = at
+        rows = self.ref[pl.ds(self.start(x, z), self.side * SIDE), :]
+        return rows.reshape(self.side, SIDE, LANES)
+
+    def __setitem__(self, at, value):
+        x, z = at
+        self.ref[pl.ds(self.start(x, z), self.side * SIDE), :] = value.reshape(-1, LANES)
+
+    def put(self, x, z, value, exact=False):
+        self[x, z] = value
+        n = self.side
+        if z == 0:
+            edge = block_up(value, 2)
+            self[x, n] = inside_up(edge, 2) if exact else edge
+        if z == n - 1:
+            edge = block_down(value, 2)
+            self[x, -1] = inside_down(edge, 2) if exact else edge
+        if exact:
+            after = inside_up(block_up(value[:1], 1), 1)
+            self.ref[pl.ds(self.start(x, z, n), SIDE), :] = after[0]
+            before = inside_down(block_down(value[n - 1 :], 1), 1)
+            self.ref[pl.ds(self.start(x, z, -1), SIDE), :] = before[0]
+
+    def close(self, exact=False):
+        n = self.side
+        for z in range(n):
+            after = block_up(self[0, z], 0)
+            self[n, z] = inside_up(after, 0) if exact else after
+            before = block_down(self[n - 1, z], 0)
+            self[-1, z] = inside_down(before, 0) if exact else before
+
+
+class Plain:
+    def __init__(self, ref, side):
+        self.ref, self.side = ref, side
+
+    def __getitem__(self, at):
+        x, z = at
+        rows = self.side * SIDE
+        return self.ref[pl.ds((x * self.side + z) * rows, rows), :].reshape(self.side, SIDE, LANES)
+
+    def __setitem__(self, at, value):
+        x, z = at
+        rows = self.side * SIDE
+        self.ref[pl.ds((x * self.side + z) * rows, rows), :] = value.reshape(-1, LANES)
+
+
+class Level:
+    def __init__(self, refs, index):
+        self.side = side = SIDE >> index
+        self.scale = 0.25**index
+        self.cond, self.first, self.second = [Edged(ref, side) for ref in refs[:3]]
+        self.links = [Plain(ref, side) for ref in refs[3:9]]
+        self.weight, self.back, self.base, self.half = [Plain(ref, side) for ref in refs[9:13]]
+
+    @staticmethod
+    def scratch(index):
+        side = SIDE >> index
+        edged = pltpu.VMEM(((side + 2) ** 3 * SIDE, LANES), jnp.float32)
+        plain = pltpu.VMEM((side**3 * SIDE, LANES), jnp.float32)
+        return [edged] * 3 + [plain] * 10
+
+    def planes(self, body):
+        if self.side == SIDE:
+
+            def one(x, carry):
+                body(x)
+                return carry
+
+            lax.fori_loop(0, self.side, one, 0)
+        else:
+            for x in range(self.side):
+                body(x)
+
+    def shifted(self, field, x, z, here, exact=False):
+        after = block_up(here[:1], 1)
+        before = block_down(here[-1:], 1)
+        if exact:
+            after, before = inside_up(after, 1), inside_down(before, 1)
+        return [
+            field[x + 1, z],
+            field[x - 1, z],
+            jnp.concatenate([here[1:], after]),
+            jnp.concatenate([before, here[:-1]]),
+            field[x, z + 1],
+            field[x, z - 1],
+        ]
+
+    def prepare(self):
+        n = self.side
+
+        def plane(x):
+            for z in range(n):
+                here = self.cond[x, z]
+                others = self.shifted(self.cond, x, z, here, exact=True)
+                total = others[0]
+                for other in others[1:]:
+                    total = total + other
+                total = 3.0 * here + 0.5 * total
+                inverse = DAMPING / total
+                self.weight[x, z] = inverse * (1.0 / self.scale)
+                self.back[x, z] = total * (self.scale / DAMPING)
+                inverse = 0.5 * inverse
+                for index, other in enumerate(others):
+                    link = inverse * (here + other)
+                    if index == 2:
+                        link = jnp.concatenate([link[:-1], inside_up(link[-1:], 1)])
+                    if index == 3:
+                        link = jnp.concatenate([inside_down(link[:1], 1), link[1:]])
+                    if index == 4 and z == n - 1:
+                        link = inside_up(link, 2)
+                    if index == 5 and z == 0:
+                        link = inside_down(link, 2)
+                    self.links[index][x, z] = link
+
+        self.planes(plane)
+        for z in range(n):
+            self.links[0][n - 1, z] = inside_up(self.links[0][n - 1, z], 0)
+            self.links[1][0, z] = inside_down(self.links[1][0, z], 0)
+
+    def total(self, field, x, z):
+        here = field[x, z]
+        result = self.base[x, z]
+        for link, other in zip(self.links, self.shifted(field, x, z, here)):
+            result = result + link[x, z] * other
+        return here, result
+
+    def sweep(self, field, out, exact=False):
+        def plane(x):
+            for z in range(self.side):
+                here, result = self.total(field, x, z)
+                out.put(x, z, (1.0 - DAMPING) * here + result, exact)
+
+        self.planes(plane)
+        out.close(exact)
+
+    def halve(self, rows, coarse):
+        n = self.side
+
+        def plane(x):
+            for z in range(n // 2):
+                self.half[x, z] = jnp.concatenate([pair_rows(rows(x, 2 * z) + rows(x, 2 * z + 1))] * 2)
+
+        self.planes(plane)
+        for x in range(n // 2):
+            for z in range(n // 2):
+                pair = self.half[2 * x, z][: n // 2] + self.half[2 * x + 1, z][: n // 2]
+                coarse(x, z, 0.125 * pair)
+
+    def descend(self, coarse):
+        self.sweep(self.first, self.second)
+
+        def residual(x, z):
+            here, result = self.total(self.second, x, z)
+            return (result - DAMPING * here) * self.back[x, z]
+
+        self.halve(residual, coarse)
+
+    def ascend(self, correction, out, exact=False):
+        def plane(x):
+            for z in range(self.side):
+                self.second.put(x, z, self.second[x, z] + twice(correction(x, z)))
+
+        self.planes(plane)
+        self.second.close()
+        self.sweep(self.second, self.first)
+        self.sweep(self.first, out, exact)
+
+
+def replicated_kernel(
+    device_ref,
+    cells_ref,
+    blocks_ref,
+    stations_ref,
+    currents_ref,
+    receivers_ref,
+    observed_ref,
+    potentials_ref,
+    gradient_ref,
+    forward_ref,
+    gathered,
+    *level_refs,
+):
+    f32 = jnp.float32
+    electrodes = stations_ref.shape[1]
+    per_level = len(Level.scratch(0))
+    levels = [Level(level_refs[per_level * k : per_level * (k + 1)], k) for k in range(LEVELS - 1)]
+    fine = levels[0]
+    forward = Edged(forward_ref, SIDE)
+    wide = SIDE * SIDE * SIDE
+
+    def collect(x):
+        for z in range(SIDE):
+            rows = []
+            for y in range(SIDE):
+                rows.append(blocks_ref[pl.ds((x * SIDE + z) * SIDE + y, SIDE, stride=wide), :][None])
+            fine.cond.put(x, z, jnp.concatenate(rows), exact=True)
+
+    fine.planes(collect)
+    fine.cond.close(exact=True)
+
+    coarsest = []
+    for level, below in zip(levels, levels[1:] + [None]):
+        level.prepare()
+
+        def coarse(x, z, row, below=below):
+            if below is None:
+                coarsest.append(row)
+            else:
+                below.cond.put(x, z, row, exact=True)
+
+        level.halve(lambda x, z, level=level: level.cond[x, z], coarse)
+        if below is not None:
+            below.cond.close(exact=True)
+
+    last_scale = 0.25 ** (LEVELS - 1)
+    here = coarsest[0]
+    others = [inside(move(here, axis), axis) for axis in range(3) for inside, move in ((inside_up, block_up), (inside_down, block_down))]
+    total = others[0]
+    for other in others[1:]:
+        total = total + other
+    total = 3.0 * here + 0.5 * total
+    inverse = DAMPING / total
+    last_weight = inverse * (1.0 / last_scale)
+    last_links = []
+    for axis in range(3):
+        for inside, other in ((inside_up, others[2 * axis]), (inside_down, others[2 * axis + 1])):
+            last_links.append(inside(0.5 * inverse * (here + other), axis))
+
+    def solve_last(rhs):
+        base = last_weight * rhs
+        value = base
+        for _ in range(COARSE_SWEEPS - 1):
+            parts = []
+            for axis in range(3):
+                parts.append(last_links[2 * axis] * block_up(value, axis))
+                parts.append(last_links[2 * axis + 1] * block_down(value, axis))
+            start = base + (1.0 - DAMPING) * value
+            value = ((start + parts[0]) + (parts[1] + parts[4])) + (parts[5] + (parts[2] + parts[3]))
+        return value
+
+    def cycle(index, out, exact=False):
+        level = levels[index]
+        if index == LEVELS - 2:
+            held = []
+            level.descend(lambda x, z, row: held.append(row))
+            solved = solve_last(held[0])
+            level.ascend(lambda x, z: solved, out, exact)
+            return
+        below = levels[index + 1]
+
+        def coarse(x, z, row):
+            row = below.weight[x, z] * row
+            below.base[x, z] = row
+            below.first.put(x, z, row)
+
+        level.descend(coarse)
+        below.first.close()
+        cycle(index + 1, below.second)
+        level.ascend(lambda x, z: below.second[x // 2, z // 2], out, exact)
+
+    station = stations_ref[...]
+    cell_x, cell_y, cell_z = station >> 14, station >> 7 & 127, station & 127
+    register = ((cell_x & 7) * SIDE + (cell_z & 7)) * SIDE + (cell_y & 7)
+    line = register * SIDE + (cell_x >> 3) * 2 + (cell_y >> 6)
+    spot = (cell_y >> 3 & 7) * GROUP + (cell_z >> 3)
+    at_spot = iota((LANES, electrodes), 0) == spot
+    plane_lines = iota((SIDE * SIDE * SIDE, electrodes), 0)
+
+    def spread(amounts):
+        table = jnp.concatenate(pieces_of(jnp.where(at_spot, amounts, 0.0), 2))
+
+        def plane(x):
+            chosen = plane_lines + x * (SIDE * SIDE * SIDE) == line
+            chosen = jnp.where(chosen, 1.0, 0.0).astype(jnp.bfloat16)
+            both = lax.dot_general(
+                chosen, table, (((1,), (1,)), ((), ())), preferred_element_type=f32
+            )
+            value = (both[:, :LANES] + both[:, LANES:]).reshape(SIDE, SIDE, SIDE, LANES)
+            for z in range(SIDE):
+                row = fine.weight[x, z] * value[z]
+                fine.base[x, z] = row
+                fine.first.put(x, z, row)
+
+        fine.planes(plane)
+        fine.first.close()
+
+    spread(currents_ref[...])
+    cycle(0, forward, exact=True)
+
+    def read(electrode, carry):
+        gathered[pl.ds(electrode, 1), :] = forward_ref[pl.ds(cells_ref[electrode], 1), :]
+        return carry
+
+    lax.fori_loop(0, electrodes, read, 0, unroll=8)
+    readings = jnp.sum(jnp.where(at_spot, gathered[...].T, 0.0), axis=0, keepdims=True)
+    receivers = receivers_ref[...]
+    numbers = iota((receivers.shape[0], electrodes), 1)
+    pairs = jnp.where(numbers == receivers[:, 0:1], 1.0, 0.0) - jnp.where(
+        numbers == receivers[:, 1:2], 1.0, 0.0
+    )
+    pairs = pairs.astype(jnp.bfloat16)
+
+    def exact(row, dims):
+        return product(jnp.broadcast_to(row, (16, row.shape[1])), pairs, 3, dims)[0:1]
+
+    misfit = exact(readings, ((1,), (1,))) - observed_ref[...]
+    spread(exact(misfit, ((1,), (0,))))
+    cycle(0, fine.second, exact=True)
+
+    device = device_ref[0]
+    order = lane_order()
+    adjoint = fine.second
+
+    def own(field, x, z, y=0):
+        return field.ref[pl.ds(field.start(x, z, y) + device, SIDE, stride=SIDE), :]
+
+    for x in range(SIDE):
+        tiles_u, tiles_g = [], []
+        for z in range(SIDE):
+            here_u, here_w = own(forward, x, z), own(adjoint, x, z)
+            total = None
+            for at in ((x + 1, z), (x - 1, z), (x, z, 1), (x, z, -1), (x, z + 1), (x, z - 1)):
+                term = (here_u - own(forward, *at)) * (here_w - own(adjoint, *at))
+                total = term if total is None else total + term
+            tiles_u.append(here_u)
+            tiles_g.append(-0.5 * total)
+        potentials_ref[x] = from_blocks(tiles_u, order)
+        gradient_ref[x] = from_blocks(tiles_g, order)
+
+
+def replicated(conductivity, stations, currents, receivers, observed):
+    rows, cols, depth = conductivity.shape
+    f32 = jnp.float32
+    count_s = lax.axis_size("shot")
+    shot = lax.axis_index("shot")
+    electrodes = stations.shape[0]
+    total = rows * cols
+    vmem = pl.BlockSpec(memory_space=pltpu.VMEM)
+    smem = pl.BlockSpec(memory_space=pltpu.SMEM)
+    params = pltpu.CompilerParams(vmem_limit_bytes=VMEM_BYTES)
+    mine = pl.pallas_call(
+        to_blocks_kernel,
+        out_shape=jax.ShapeDtypeStruct((total, LANES), f32),
+        in_specs=[vmem],
+        out_specs=vmem,
+    )(conductivity)
+    part = total // count_s
+    mine = lax.dynamic_slice_in_dim(mine, shot * part, part, axis=0)
+    blocks = lax.all_gather(mine, ("gx", "gy", "shot"), axis=0, tiled=True)
+    device = (lax.axis_index("gx") * lax.axis_size("gy") + lax.axis_index("gy")).astype(jnp.int32)
+    cell_x, cell_y, cell_z = stations >> 14, stations >> 7 & 127, stations & 127
+    wide = SIDE + 2
+    cells = ((cell_x % 8 + 1) * wide + cell_z % 8 + 1) * wide + cell_y % 8 + 1
+    cells = cells * SIDE + cell_x // 8 * 2 + cell_y // 64
+    levels = [shape for index in range(LEVELS - 1) for shape in Level.scratch(index)]
+    potentials, gradient = pl.pallas_call(
+        replicated_kernel,
+        out_shape=(
+            jax.ShapeDtypeStruct((rows, cols, LANES), f32),
+            jax.ShapeDtypeStruct((rows, cols, LANES), f32),
+        ),
+        in_specs=[smem, smem, vmem, vmem, vmem, vmem, vmem],
+        out_specs=(vmem, vmem),
+        scratch_shapes=[
+            pltpu.VMEM((wide**3 * SIDE, LANES), f32),
+            pltpu.VMEM((electrodes, LANES), f32),
+        ]
+        + levels,
+        compiler_params=params,
+        cost_estimate=pl.CostEstimate(flops=200_000_000, bytes_accessed=4_000_000, transcendentals=0),
+    )(
+        device.reshape(1),
+        cells,
+        blocks,
+        stations.reshape(1, electrodes),
+        currents,
+        receivers,
+        observed,
+    )
+    chunk = cols // count_s
+    summed = lax.dynamic_slice_in_dim(gradient, shot * chunk, chunk, axis=1)
+    for k in range(1, count_s):
+        theirs = lax.dynamic_slice_in_dim(gradient, (shot + k) % count_s * chunk, chunk, axis=1)
+        summed = summed + lax.ppermute(theirs, "shot", [(i, (i + k) % count_s) for i in range(count_s)])
+    return potentials[None], summed
 
 
 def extended(array, sides, width):
@@ -139,7 +650,7 @@
     return relaxed(field_rim(field), source, cond_pad, diag_level, level_scale)
 
 
-def per_device(conductivity, stations, currents, receivers, observed):
+def distributed(conductivity, stations, currents, receivers, observed):
     row_count, col_count, z_count = conductivity.shape
     shot_count = currents.shape[0]
     count_x = lax.axis_size("gx")
@@ -202,6 +713,14 @@
     return (potentials, summed)
 
 
+def per_device(conductivity, stations, currents, receivers, observed):
+    blocks = lax.axis_size("gx") * lax.axis_size("gy")
+    fits = conductivity.shape == (SIDE, SIDE * SIDE, LANES) and blocks == SIDE
+    fits = fits and lax.axis_size("gy") == 2 and currents.shape[0] == 1
+    plan = replicated if fits else distributed
+    return plan(conductivity, stations, currents, receivers, observed)
+
+
 def solution(mesh):
     in_specs = (
         P(("grp", "gx"), "gy", None),

time: 559 us -> 104 us (0.19)
  starting transfers between devices: 290 us -> 0.67 us
  local copies, waits for them, and re-layouts: 78 us -> 4.03 us
  blocking collectives: 65.2 us -> 0 us
  other arithmetic: 42.2 us -> 2.87 us
  Pallas kernels: 0 us -> 35.4 us
  waiting for transfers between devices: 62.1 us -> 46.5 us
    ppermute x112 -> x1, starting transfers between devices: 290 us -> 0.63 us  [replicated(): lax.ppermute(theirs, 'shot', [(i, (i + k) % count_s) for i in range(count...]
    reshape x5 -> x0, local copies, waits for them, and re-layouts: 62.1 us -> none  [restrict(): field.reshape(leading + (extent[0] // 2, 2, extent[1] // 2, 2, extent[2]...]
    all_gather x3 -> x0, blocking collectives: 46.5 us -> none  [the longest x2 31 us: part_cycle(): blocks = lax.all_gather(source[None], ('gx', 'gy'), axis=0, tiled=True)]
    ppermute x112 -> x1, waiting for transfers between devices: 47.3 us -> 5.1 us  [replicated(): lax.ppermute(theirs, 'shot', [(i, (i + k) % count_s) for i in range(count...]
    all_gather x0 -> x1, waiting for transfers between devices: none -> 41.3 us  [replicated(): blocks = lax.all_gather(mine, ('gx', 'gy', 'shot'), axis=0, tiled=True)]
    pallas_call x0 -> x2, Pallas kernels: none -> 35.4 us  [the longest x1 33.1 us: replicated(): pl.pallas_call(replicated_kernel, out_shape=(jax.ShapeDtypeStruct((rows,...]
    reduce_sum x12 -> x0, other arithmetic: 26.4 us -> none  [the longest x11 25.3 us: restrict(): return shaped.mean(axis=(-5, -3, -1))]
    psum x1 -> x0, blocking collectives: 18.7 us -> none  [per_device(): readings = lax.psum(local_values, ('gx', 'gy'))]
  transfers between devices with their start and end apart: 113 -> 2, of which waited for: 48 -> 2; matrix products, arithmetic and copies ran while one was open for 12% -> 3% of each run, Pallas kernels for 0% -> 0%
where the time goes in v2:
time: 104 us; the launch traced here: 103 us
  waiting for transfers between devices  46.5 us (45%)
  Pallas kernels  35.4 us (34%)
  between operations  14 us (13%)
  local copies, waits for them, and re-layouts  4.03 us (4%)
  other arithmetic  2.87 us (3%)
    all_gather x1, waiting for transfers between devices, replicated(): blocks = lax.all_gather(mine, ('gx', 'gy', 'shot'), axis=0, tiled=True)  41.3 us
    pallas_call x1, Pallas kernels, replicated(): pl.pallas_call(replicated_kernel, out_shape=(jax.ShapeDtypeStruct((rows,...  33.1 us
    ppermute x1, waiting for transfers between devices, replicated(): lax.ppermute(theirs, 'shot', [(i, (i + k) % count_s) for i in range(count...  5.1 us
    pallas_call x1, Pallas kernels, replicated(): pl.pallas_call(to_blocks_kernel, out_shape=jax.ShapeDtypeStruct((total, L...  2.23 us
  transfers between devices with their start and end apart: 2, of which 2 were waited for; matrix products, arithmetic and copies ran while one was open for 3% of the time, Pallas kernels for 0%

profile of v2, /device:TPU:0, one launch (start us, length us, event | category | flops | bytes accessed | tf_op | source)
XLA Modules:
  0.0 103.4 jit_solution(14916845051973971439)
XLA Ops:
  7.2 0.0 all-gather.2.cloned.1.call-start
  7.2 2.2 %shard_map.68 = f32[512,128]{1,0:T(8,128)} custom-call(f32[8,64,128]{2,1,0:T(8,128)} %natural_ref.1), custom_call_target="tpu_custom_call" | custom-call | tf_op jit(solution)/shard_map/pallas_call | solution.py:477
  9.4 1.6 %constant_dynamic-slice_fusion.1 = f32[256,128]{1,0:T(8,128)} fusion(f32[512,128]{1,0:T(8,128)} %shard_map.68, s32[]{:T(128)S(6)} %select_n.43), kind=kLoop, calls=%fused_computation.22 | loop fusion | bytes 262148 | tf_op jit(solution)/shard_map/dynamic_slice | solution.py:484
  11.0 0.0 all-gather.2.cloned.1.call-update
  11.1 1.5 %copy.7.receivers_ref = s32[512,2]{1,0:T(8,128)} copy(s32[512,2]{0,1:T(2,128)} %param.8) | data formatting | bytes 8192 | tf_op args[3]
  12.6 1.3 %add_add_fusion.cells_ref = s32[256]{0:T(256)} fusion(s32[256]{0:T(256)} %param.6), kind=kLoop, calls=%fused_computation.19 | loop fusion | flops 17408 | bytes 2048 | tf_op jit(solution)/shard_map/add | solution.py:490
  13.9 41.3 %all-gather.2.cloned.1.call-done.blocks_ref = f32[4096,128]{1,0:T(8,128)} async-done(((f32[256,128]{1,0:T(8,128)}), f32[4096,128]{1,0:T(8,128)}) %all-gather.2.cloned.1.call-update) | async-done | bytes 2097168 | tf_op jit(solution)/shard_map/all_gather | solution.py:485
  55.2 33.1 %shard_map.69 = (f32[8,64,128]{2,1,0:T(8,128)}, f32[8,64,128]{2,1,0:T(8,128)}) custom-call(s32[1]{0:T(128)} %bitcast.device_ref, s32[256]{0:T(256)} %add_add_fusion.cells_ref, f32[4096,128]{1,0:T(8,128)} %all-gather.2.cloned.1.call-done.blocks_ref, s32[1,256]{1,0:T(1,128)} %bitcast.3, f32[1,256]{1,0:T(1,128)} %currents_ref.1, s32[512,2]{1,0:T(8,128)} %copy.7.receivers_ref, ...), custom_call_target="tpu_custom_call" | custom-call | flops 200000000 | bytes 4000000 | tf_op jit(solution)/shard_map/pallas_call | solution.py:492
  88.4 0.9 constant_dynamic-slice_fusion
  89.3 0.6 collective-permute-start
  89.9 5.1 %collective-permute-done = f32[8,32,128]{2,1,0:T(8,128)S(1)} collective-permute-done((f32[8,32,128]{2,1,0:T(8,128)S(1)}, f32[8,32,128]{2,1,0:T(8,128)S(1)}, u32[]{:S(2)}, u32[]{:S(2)}) %collective-permute-start) | collective-permute-done | bytes 131104 | tf_op jit(solution)/shard_map/ppermute | solution.py:520
  95.0 1.6 %dynamic-slice_add_fusion = f32[8,32,128]{2,1,0:T(8,128)} fusion(f32[8,32,128]{2,1,0:T(8,128)S(1)} %collective-permute-done, f32[8,64,128]{2,1,0:T(8,128)} %get-tuple-element.5, s32[]{:T(128)S(6)} %select_n.44), kind=kLoop, calls=%fused_computation | loop fusion | flops 32768 | bytes 393220 | tf_op jit(solution)/shard_map/add | solution.py:520
Async XLA Ops:
  7.2 48.1 %all-gather.2.cloned.1.call-start = ((), (), s32[]{:S(2)}) async-start(), calls=%async_computation | async-start | bytes 2228224 | tf_op jit(solution)/shard_map/all_gather | solution.py:485
  89.3 5.7 %collective-permute-start = (f32[8,32,128]{2,1,0:T(8,128)S(1)}, f32[8,32,128]{2,1,0:T(8,128)S(1)}, u32[]{:S(2)}, u32[]{:S(2)}) collective-permute-start(f32[8,32,128]{2,1,0:T(8,128)S(1)} %constant_dynamic-slice_fusion), channel_id=1, source_target_pairs={{0,1},{1,0},{2,3},{3,2},{4,5},{5,4},{6,7},{7,6},{8,9},{9,8},{10,11... | collective-permute-start | bytes 393224 | tf_op jit(solution)/shard_map/ppermute | solution.py:520
Sparse Core Ops, SparseCore 0:
  11.2 44.0 all-gather.1

commit v3 on v2

--- a/solution.py
+++ b/solution.py
@@ -122,6 +122,39 @@
 
 def twice(row):
     return jnp.concatenate([row[i // 2 : i // 2 + 1] for i in range(2 * row.shape[0])])
+
+
+def station_table(station):
+    cell_x, cell_y, cell_z = station >> 14, station >> 7 & 127, station & 127
+    register = ((cell_x & 7) * SIDE + (cell_z & 7)) * SIDE + (cell_y & 7)
+    line = register * SIDE + (cell_x >> 3) * 2 + (cell_y >> 6)
+    return line, (cell_y >> 3 & 7) * GROUP + (cell_z >> 3)
+
+
+def spread_planes(station, amounts, put):
+    electrodes = station.shape[1]
+    line, spot = station_table(station)
+    at_spot = iota((LANES, electrodes), 0) == spot
+    table = jnp.concatenate(pieces_of(jnp.where(at_spot, amounts, 0.0), 2))
+    plane_lines = iota((SIDE * SIDE * SIDE, electrodes), 0)
+
+    def plane(x, carry):
+        chosen = plane_lines + x * (SIDE * SIDE * SIDE) == line
+        chosen = jnp.where(chosen, 1.0, 0.0).astype(jnp.bfloat16)
+        both = lax.dot_general(
+            chosen, table, (((1,), (1,)), ((), ())), preferred_element_type=jnp.float32
+        )
+        put(x, both[:, :LANES] + both[:, LANES:])
+        return carry
+
+    lax.fori_loop(0, SIDE, plane, 0)
+
+
+def source_kernel(stations_ref, currents_ref, source_ref):
+    def put(x, value):
+        source_ref[pl.ds(x * SIDE * SIDE * SIDE, SIDE * SIDE * SIDE), :] = value
+
+    spread_planes(stations_ref[...], currents_ref[...], put)
 
 
 class Edged:
@@ -303,11 +336,20 @@
 
 
 def replicated_kernel(
+    count,
     device_ref,
     cells_ref,
-    blocks_ref,
+    *refs,
+):
+    solve_kernel(refs[:count], device_ref, cells_ref, *refs[count:])
+
+
+def solve_kernel(
+    part_refs,
+    device_ref,
+    cells_ref,
+    source_ref,
     stations_ref,
-    currents_ref,
     receivers_ref,
     observed_ref,
     potentials_ref,
@@ -324,12 +366,16 @@
     forward = Edged(forward_ref, SIDE)
     wide = SIDE * SIDE * SIDE
 
+    device = device_ref[0]
     def collect(x):
-        for z in range(SIDE):
-            rows = []
-            for y in range(SIDE):
-                rows.append(blocks_ref[pl.ds((x * SIDE + z) * SIDE + y, SIDE, stride=wide), :][None])
-            fine.cond.put(x, z, jnp.concatenate(rows), exact=True)
+        for k, part in enumerate(part_refs):
+            for z in range(SIDE):
+                start = fine.cond.start(x, z) + (device ^ k)
+                fine.cond.ref[pl.ds(start, SIDE, stride=SIDE), :] = part[
+                    pl.ds((x * SIDE + z) * SIDE, SIDE), :
+                ]
+        for z in (0, SIDE - 1):
+            fine.cond.put(x, z, fine.cond[x, z], exact=True)
 
     fine.planes(collect)
     fine.cond.close(exact=True)
@@ -394,33 +440,15 @@
         cycle(index + 1, below.second)
         level.ascend(lambda x, z: below.second[x // 2, z // 2], out, exact)
 
-    station = stations_ref[...]
-    cell_x, cell_y, cell_z = station >> 14, station >> 7 & 127, station & 127
-    register = ((cell_x & 7) * SIDE + (cell_z & 7)) * SIDE + (cell_y & 7)
-    line = register * SIDE + (cell_x >> 3) * 2 + (cell_y >> 6)
-    spot = (cell_y >> 3 & 7) * GROUP + (cell_z >> 3)
-    at_spot = iota((LANES, electrodes), 0) == spot
-    plane_lines = iota((SIDE * SIDE * SIDE, electrodes), 0)
-
-    def spread(amounts):
-        table = jnp.concatenate(pieces_of(jnp.where(at_spot, amounts, 0.0), 2))
-
-        def plane(x):
-            chosen = plane_lines + x * (SIDE * SIDE * SIDE) == line
-            chosen = jnp.where(chosen, 1.0, 0.0).astype(jnp.bfloat16)
-            both = lax.dot_general(
-                chosen, table, (((1,), (1,)), ((), ())), preferred_element_type=f32
-            )
-            value = (both[:, :LANES] + both[:, LANES:]).reshape(SIDE, SIDE, SIDE, LANES)
-            for z in range(SIDE):
-                row = fine.weight[x, z] * value[z]
-                fine.base[x, z] = row
-                fine.first.put(x, z, row)
-
-        fine.planes(plane)
-        fine.first.close()
-
-    spread(currents_ref[...])
+    def begin(x, rows):
+        value = rows.reshape(SIDE, SIDE, SIDE, LANES)
+        for z in range(SIDE):
+            row = fine.weight[x, z] * value[z]
+            fine.base[x, z] = row
+            fine.first.put(x, z, row)
+
+    fine.planes(lambda x: begin(x, source_ref[pl.ds(x * wide, wide), :]))
+    fine.first.close()
     cycle(0, forward, exact=True)
 
     def read(electrode, carry):
@@ -428,6 +456,8 @@
         return carry
 
     lax.fori_loop(0, electrodes, read, 0, unroll=8)
+    _, spot = station_table(stations_ref[...])
+    at_spot = iota((LANES, electrodes), 0) == spot
     readings = jnp.sum(jnp.where(at_spot, gathered[...].T, 0.0), axis=0, keepdims=True)
     receivers = receivers_ref[...]
     numbers = iota((receivers.shape[0], electrodes), 1)
@@ -440,10 +470,10 @@
         return product(jnp.broadcast_to(row, (16, row.shape[1])), pairs, 3, dims)[0:1]
 
     misfit = exact(readings, ((1,), (1,))) - observed_ref[...]
-    spread(exact(misfit, ((1,), (0,))))
+    spread_planes(stations_ref[...], exact(misfit, ((1,), (0,))), begin)
+    fine.first.close()
     cycle(0, fine.second, exact=True)
 
-    device = device_ref[0]
     order = lane_order()
     adjoint = fine.second
 
@@ -480,9 +510,22 @@
         in_specs=[vmem],
         out_specs=vmem,
     )(conductivity)
-    part = total // count_s
-    mine = lax.dynamic_slice_in_dim(mine, shot * part, part, axis=0)
-    blocks = lax.all_gather(mine, ("gx", "gy", "shot"), axis=0, tiled=True)
+    count_x, count_y = lax.axis_size("gx"), lax.axis_size("gy")
+    parts = []
+    for k in range(count_x):
+        pairs = [(i, i ^ k) for i in range(count_x)]
+        parts.append(lax.ppermute(mine, "gx", pairs) if k else mine)
+    swap = [(0, 1), (1, 0)]
+    parts = [part for own in parts for part in (own, lax.ppermute(own, "gy", swap))]
+    station_row = stations.reshape(1, electrodes)
+    source = pl.pallas_call(
+        source_kernel,
+        out_shape=jax.ShapeDtypeStruct((total * SIDE, LANES), f32),
+        in_specs=[vmem, vmem],
+        out_specs=vmem,
+        compiler_params=params,
+        cost_estimate=pl.CostEstimate(flops=600_000_000, bytes_accessed=4_000_000, transcendentals=0),
+    )(station_row, currents)
     device = (lax.axis_index("gx") * lax.axis_size("gy") + lax.axis_index("gy")).astype(jnp.int32)
     cell_x, cell_y, cell_z = stations >> 14, stations >> 7 & 127, stations & 127
     wide = SIDE + 2
@@ -490,12 +533,12 @@
     cells = cells * SIDE + cell_x // 8 * 2 + cell_y // 64
     levels = [shape for index in range(LEVELS - 1) for shape in Level.scratch(index)]
     potentials, gradient = pl.pallas_call(
-        replicated_kernel,
+        functools.partial(replicated_kernel, len(parts)),
         out_shape=(
             jax.ShapeDtypeStruct((rows, cols, LANES), f32),
             jax.ShapeDtypeStruct((rows, cols, LANES), f32),
         ),
-        in_specs=[smem, smem, vmem, vmem, vmem, vmem, vmem],
+        in_specs=[smem, smem] + [vmem] * (len(parts) + 4),
         out_specs=(vmem, vmem),
         scratch_shapes=[
             pltpu.VMEM((wide**3 * SIDE, LANES), f32),
@@ -507,9 +550,9 @@
     )(
         device.reshape(1),
         cells,
-        blocks,
-        stations.reshape(1, electrodes),
-        currents,
+        *parts,
+        source,
+        station_row,
         receivers,
         observed,
     )

time: 104 us -> 75.6 us (0.73)
  the two profiles are of different devices: /device:TPU:0 before, /device:TPU:12 now
where the time goes in v3:
time: 75.6 us; the launch traced here: 75.3 us
  Pallas kernels  38.3 us (51%)
  waiting for transfers between devices  25.7 us (34%)
  starting transfers between devices  5.05 us (7%)
  local copies, waits for them, and re-layouts  3.39 us (4%)
  other arithmetic  2.16 us (3%)
    pallas_call x1, Pallas kernels, replicated(): pl.pallas_call(functools.partial(replicated_kernel, len(parts)), out_shap...  31.8 us
    ppermute x3, waiting for transfers between devices, replicated(): parts.append(lax.ppermute(mine, 'gx', pairs) if k else mine)  21.3 us
    ppermute x1, waiting for transfers between devices, replicated(): lax.ppermute(theirs, 'shot', [(i, (i + k) % count_s) for i in range(count...  4.37 us
    pallas_call x1, Pallas kernels, replicated(): pl.pallas_call(source_kernel, out_shape=jax.ShapeDtypeStruct((total * SID...  4.23 us
    ppermute x3, starting transfers between devices, replicated(): parts.append(lax.ppermute(mine, 'gx', pairs) if k else mine)  3.49 us
    unnamed x17, local copies, waits for them, and re-layouts  2.48 us
    pallas_call x1, Pallas kernels, replicated(): pl.pallas_call(to_blocks_kernel, out_shape=jax.ShapeDtypeStruct((total, L...  2.25 us
    add x1, other arithmetic, replicated(): summed + lax.ppermute(theirs, 'shot', [(i, (i + k) % count_s) for i in ra...  1.58 us
  transfers between devices with their start and end apart: 8, of which 4 were waited for; matrix products, arithmetic and copies ran while one was open for 3% of the time, Pallas kernels for 6%

profile of v3, /device:TPU:12, one launch (start us, length us, event | category | flops | bytes accessed | tf_op | source)
XLA Modules:
  0.0 75.3 jit_solution(11049878870702731428)
XLA Ops:
  0.6 0.0 copy-start.7
  0.6 2.3 %shard_map.68.refs_0_ = f32[512,128]{1,0:T(8,128)} custom-call(f32[8,64,128]{2,1,0:T(8,128)} %natural_ref.1), custom_call_target="tpu_custom_call" | custom-call | tf_op jit(solution)/shard_map/pallas_call | solution.py:507
  2.9 0.4 collective-permute-start.1
  3.3 2.6 %collective-permute-start.3 = (f32[512,128]{1,0:T(8,128)}, f32[512,128]{1,0:T(8,128)S(1)}, u32[]{:S(2)}, u32[]{:S(2)}) collective-permute-start(f32[512,128]{1,0:T(8,128)} %shard_map.68.refs_0_), channel_id=1, source_target_pairs={{0,8},{4,12},{8,0},{12,4},{1,9},{5,13},{9,1},{13,5},{2,10},{6,14},... | collective-permute-start | bytes 786440 | tf_op jit(solution)/shard_map/ppermute | solution.py:517
  5.9 0.5 collective-permute-start.5
  6.4 0.0 collective-permute-start
  6.4 1.5 %copy.7.refs_10_ = s32[512,2]{1,0:T(8,128)} copy(s32[512,2]{0,1:T(2,128)} %param.8) | data formatting | bytes 8192 | tf_op args[3]
  7.9 6.1 %collective-permute-done.1.refs_2_ = f32[512,128]{1,0:T(8,128)S(1)} collective-permute-done((f32[512,128]{1,0:T(8,128)}, f32[512,128]{1,0:T(8,128)S(1)}, u32[]{:S(2)}, u32[]{:S(2)}) %collective-permute-start.1) | collective-permute-done | bytes 262176 | tf_op jit(solution)/shard_map/ppermute | solution.py:517
  14.1 0.0 collective-permute-start.2
  14.1 10.2 %collective-permute-done.3.refs_4_ = f32[512,128]{1,0:T(8,128)S(1)} collective-permute-done((f32[512,128]{1,0:T(8,128)}, f32[512,128]{1,0:T(8,128)S(1)}, u32[]{:S(2)}, u32[]{:S(2)}) %collective-permute-start.3) | collective-permute-done | bytes 262176 | tf_op jit(solution)/shard_map/ppermute | solution.py:517
  24.2 0.0 collective-permute-start.4
  24.2 5.0 %collective-permute-done.5.refs_6_ = f32[512,128]{1,0:T(8,128)S(1)} collective-permute-done((f32[512,128]{1,0:T(8,128)}, f32[512,128]{1,0:T(8,128)S(1)}, u32[]{:S(2)}, u32[]{:S(2)}) %collective-permute-start.5) | collective-permute-done | bytes 262176 | tf_op jit(solution)/shard_map/ppermute | solution.py:517
  29.3 0.0 collective-permute-start.6
  29.3 4.2 %shard_map.69.refs_8_ = f32[4096,128]{1,0:T(8,128)} custom-call(s32[1,256]{1,0:T(1,128)} %bitcast.3, f32[1,256]{1,0:T(1,128)} %currents_ref.1), custom_call_target="tpu_custom_call" | custom-call | flops 600000000 | bytes 4000000 | tf_op jit(solution)/shard_map/pallas_call | solution.py:521
  33.5 0.0 copy-done.7
  33.5 0.6 add_add_fusion.cells_ref
  34.1 0.0 collective-permute-done.refs_1_
  34.1 0.0 collective-permute-done.2.refs_3_
  34.1 0.0 copy-start.4
  34.1 0.0 collective-permute-done.4.refs_5_
  34.1 0.0 copy-start.5
  34.1 0.0 collective-permute-done.6.refs_7_
  34.1 0.0 copy-start.6
  34.2 0.6 copy-done.3
  34.8 0.1 copy-done.4
  34.9 0.1 copy-done.5
  35.0 0.1 copy-done.6
  35.1 31.8 %shard_map.70 = (f32[8,64,128]{2,1,0:T(8,128)}, f32[8,64,128]{2,1,0:T(8,128)}) custom-call(s32[1]{0:T(128)} %bitcast.device_ref, s32[256]{0:T(256)} %add_add_fusion.cells_ref, f32[512,128]{1,0:T(8,128)} %shard_map.68.refs_0_, f32[512,128]{1,0:T(8,128)} %copy-done.3, f32[512,128]{1,0:T(8,128)} %copy-done, f32[512,128]{1,0:T(8,128)} %copy-done.4, ...), custom_call_target="tpu_custom_call" | custom-call | flops 200000000 | bytes 4000000 | tf_op jit(solution)/shard_map/pallas_call | solution.py:535
  66.9 0.9 %constant_dynamic-slice_fusion = f32[8,32,128]{2,1,0:T(8,128)S(1)} fusion(f32[8,64,128]{2,1,0:T(8,128)} %get-tuple-element.5, s32[]{:T(128)S(6)} %select_n.42), kind=kLoop, calls=%fused_computation.21 | loop fusion | bytes 262148 | tf_op jit(solution)/shard_map/dynamic_slice | solution.py:562
  67.8 1.6 %collective-permute-start.7 = (f32[8,32,128]{2,1,0:T(8,128)S(1)}, f32[8,32,128]{2,1,0:T(8,128)S(1)}, u32[]{:S(2)}, u32[]{:S(2)}) collective-permute-start(f32[8,32,128]{2,1,0:T(8,128)S(1)} %constant_dynamic-slice_fusion), channel_id=1, source_target_pairs={{0,1},{1,0},{2,3},{3,2},{4,5},{5,4},{6,7},{7,6},{8,9},{9,8},{10,11... | collective-permute-start | bytes 393224 | tf_op jit(solution)/shard_map/ppermute | solution.py:563
  69.4 4.4 %collective-permute-done.7 = f32[8,32,128]{2,1,0:T(8,128)S(1)} collective-permute-done((f32[8,32,128]{2,1,0:T(8,128)S(1)}, f32[8,32,128]{2,1,0:T(8,128)S(1)}, u32[]{:S(2)}, u32[]{:S(2)}) %collective-permute-start.7) | collective-permute-done | bytes 131104 | tf_op jit(solution)/shard_map/ppermute | solution.py:563
  73.8 1.6 %dynamic-slice_add_fusion = f32[8,32,128]{2,1,0:T(8,128)} fusion(f32[8,32,128]{2,1,0:T(8,128)S(1)} %collective-permute-done.7, f32[8,64,128]{2,1,0:T(8,128)} %get-tuple-element.5, s32[]{:T(128)S(6)} %select_n.40), kind=kLoop, calls=%fused_computation | loop fusion | flops 32768 | bytes 393220 | tf_op jit(solution)/shard_map/add | solution.py:563
  (7 shorter events, 0.0 us)
Async XLA Ops:
  0.6 32.9 %copy-start.7 = (s32[256]{0:T(256)S(1)}, s32[256]{0:T(256)}, u32[]{:S(2)}) copy-start(s32[256]{0:T(256)} %param.6) | copy-start | bytes 3076
  2.9 11.2 %collective-permute-start.1 = (f32[512,128]{1,0:T(8,128)}, f32[512,128]{1,0:T(8,128)S(1)}, u32[]{:S(2)}, u32[]{:S(2)}) collective-permute-start(f32[512,128]{1,0:T(8,128)} %shard_map.68.refs_0_), channel_id=1, source_target_pairs={{0,4},{4,0},{8,12},{12,8},{1,5},{5,1},{9,13},{13,9},{2,6},{6,2},{1... | collective-permute-start | bytes 786440 | tf_op jit(solution)/shard_map/ppermute | solution.py:517
  3.3 20.9 %collective-permute-start.3 = (f32[512,128]{1,0:T(8,128)}, f32[512,128]{1,0:T(8,128)S(1)}, u32[]{:S(2)}, u32[]{:S(2)}) collective-permute-start(f32[512,128]{1,0:T(8,128)} %shard_map.68.refs_0_), channel_id=1, source_target_pairs={{0,8},{4,12},{8,0},{12,4},{1,9},{5,13},{9,1},{13,5},{2,10},{6,14},... | collective-permute-start | bytes 786440 | tf_op jit(solution)/shard_map/ppermute | solution.py:517
  5.9 23.3 %collective-permute-start.5 = (f32[512,128]{1,0:T(8,128)}, f32[512,128]{1,0:T(8,128)S(1)}, u32[]{:S(2)}, u32[]{:S(2)}) collective-permute-start(f32[512,128]{1,0:T(8,128)} %shard_map.68.refs_0_), channel_id=1, source_target_pairs={{0,12},{4,8},{8,4},{12,0},{1,13},{5,9},{9,5},{13,1},{2,14},{6,10},... | collective-permute-start | bytes 786440 | tf_op jit(solution)/shard_map/ppermute | solution.py:517
  6.4 27.7 %collective-permute-start = (f32[512,128]{1,0:T(8,128)}, f32[512,128]{1,0:T(8,128)S(1)}, u32[]{:S(2)}, u32[]{:S(2)}) collective-permute-start(f32[512,128]{1,0:T(8,128)} %shard_map.68.refs_0_), channel_id=1, source_target_pairs={{0,2},{2,0},{1,3},{3,1},{4,6},{6,4},{5,7},{7,5},{8,10},{10,8},{9,1... | collective-permute-start | bytes 786440 | tf_op jit(solution)/shard_map/ppermute | solution.py:519
  14.1 20.1 %copy-start = (f32[512,128]{1,0:T(8,128)}, f32[512,128]{1,0:T(8,128)S(1)}, u32[]{:S(2)}) copy-start(f32[512,128]{1,0:T(8,128)S(1)} %collective-permute-done.1.refs_2_) | copy-start | bytes 786436
  14.1 20.0 %collective-permute-start.2 = (f32[512,128]{1,0:T(8,128)S(1)}, f32[512,128]{1,0:T(8,128)S(1)}, u32[]{:S(2)}, u32[]{:S(2)}) collective-permute-start(f32[512,128]{1,0:T(8,128)S(1)} %collective-permute-done.1.refs_2_), channel_id=1, source_target_pairs={{0,2},{2,0},{1,3},{3,1},{4,6},{6,4},{5,7},{7,5},{8,10},{10,8},{9,1... | collective-permute-start | bytes 786440 | tf_op jit(solution)/shard_map/ppermute | solution.py:519
  24.2 9.9 %copy-start.1 = (f32[512,128]{1,0:T(8,128)}, f32[512,128]{1,0:T(8,128)S(1)}, u32[]{:S(2)}) copy-start(f32[512,128]{1,0:T(8,128)S(1)} %collective-permute-done.3.refs_4_) | copy-start | bytes 786436
  24.2 9.9 %collective-permute-start.4 = (f32[512,128]{1,0:T(8,128)S(1)}, f32[512,128]{1,0:T(8,128)S(1)}, u32[]{:S(2)}, u32[]{:S(2)}) collective-permute-start(f32[512,128]{1,0:T(8,128)S(1)} %collective-permute-done.3.refs_4_), channel_id=1, source_target_pairs={{0,2},{2,0},{1,3},{3,1},{4,6},{6,4},{5,7},{7,5},{8,10},{10,8},{9,1... | collective-permute-start | bytes 786440 | tf_op jit(solution)/shard_map/ppermute | solution.py:519
  29.2 4.9 %copy-start.2 = (f32[512,128]{1,0:T(8,128)}, f32[512,128]{1,0:T(8,128)S(1)}, u32[]{:S(2)}) copy-start(f32[512,128]{1,0:T(8,128)S(1)} %collective-permute-done.5.refs_6_) | copy-start | bytes 786436
  29.3 4.9 %collective-permute-start.6 = (f32[512,128]{1,0:T(8,128)S(1)}, f32[512,128]{1,0:T(8,128)S(1)}, u32[]{:S(2)}, u32[]{:S(2)}) collective-permute-start(f32[512,128]{1,0:T(8,128)S(1)} %collective-permute-done.5.refs_6_), channel_id=1, source_target_pairs={{0,2},{2,0},{1,3},{3,1},{4,6},{6,4},{5,7},{7,5},{8,10},{10,8},{9,1... | collective-permute-start | bytes 786440 | tf_op jit(solution)/shard_map/ppermute | solution.py:519
  34.1 0.7 copy-start.3
  34.1 0.8 %copy-start.4 = (f32[512,128]{1,0:T(8,128)}, f32[512,128]{1,0:T(8,128)S(1)}, u32[]{:S(2)}) copy-start(f32[512,128]{1,0:T(8,128)S(1)} %collective-permute-done.2.refs_3_) | copy-start | bytes 786436
  34.1 0.9 %copy-start.5 = (f32[512,128]{1,0:T(8,128)}, f32[512,128]{1,0:T(8,128)S(1)}, u32[]{:S(2)}) copy-start(f32[512,128]{1,0:T(8,128)S(1)} %collective-permute-done.4.refs_5_) | copy-start | bytes 786436
  34.1 1.0 %copy-start.6 = (f32[512,128]{1,0:T(8,128)}, f32[512,128]{1,0:T(8,128)S(1)}, u32[]{:S(2)}) copy-start(f32[512,128]{1,0:T(8,128)S(1)} %collective-permute-done.6.refs_7_) | copy-start | bytes 786436
  67.8 5.9 %collective-permute-start.7 = (f32[8,32,128]{2,1,0:T(8,128)S(1)}, f32[8,32,128]{2,1,0:T(8,128)S(1)}, u32[]{:S(2)}, u32[]{:S(2)}) collective-permute-start(f32[8,32,128]{2,1,0:T(8,128)S(1)} %constant_dynamic-slice_fusion), channel_id=1, source_target_pairs={{0,1},{1,0},{2,3},{3,2},{4,5},{5,4},{6,7},{7,6},{8,9},{9,8},{10,11... | collective-permute-start | bytes 393224 | tf_op jit(solution)/shard_map/ppermute | solution.py:563

commit v4 on v3

--- a/solution.py
+++ b/solution.py
@@ -16,7 +16,7 @@
 SIDE = 8
 LANES = 128
 GROUP = 16
-VMEM_BYTES = 56 * 2**20
+VMEM_BYTES = 48 * 2**20
 
 
 def pieces_of(value, count):
@@ -39,6 +39,12 @@
 
 def iota(shape, dim):
     return lax.broadcasted_iota(jnp.int32, shape, dim)
+
+
+def station_table(station):
+    cell_x, cell_y, cell_z = station >> 14, station >> 7 & 127, station & 127
+    row = (cell_x >> 3) * 2 + (cell_y >> 6)
+    return cell_x, cell_y, cell_z, row, (cell_y >> 3 & 7) * GROUP + (cell_z >> 3)
 
 
 def lane_order():
@@ -61,13 +67,17 @@
     return tiles
 
 
-def to_blocks_kernel(natural_ref, blocks_ref):
+def to_blocks_kernel(natural_ref, stations_ref, blocks_ref, cells_ref):
     order = lane_order()
     for x in range(SIDE):
         tiles = product(natural_ref[x], order, 3)
         tiles = [tiles[SIDE * k : SIDE * (k + 1)] for k in range(SIDE)]
         for z, tile in enumerate(exchange_groups(tiles)):
             blocks_ref[pl.ds((x * SIDE + z) * SIDE, SIDE), :] = tile
+    cell_x, cell_y, cell_z, row, _ = station_table(stations_ref[...])
+    wide = SIDE + 2
+    register = (((cell_x & 7) + 1) * wide + (cell_z & 7) + 1) * wide + (cell_y & 7) + 1
+    cells_ref[...] = register * SIDE + row
 
 
 def from_blocks(tiles, order):
@@ -122,39 +132,6 @@
 
 def twice(row):
     return jnp.concatenate([row[i // 2 : i // 2 + 1] for i in range(2 * row.shape[0])])
-
-
-def station_table(station):
-    cell_x, cell_y, cell_z = station >> 14, station >> 7 & 127, station & 127
-    register = ((cell_x & 7) * SIDE + (cell_z & 7)) * SIDE + (cell_y & 7)
-    line = register * SIDE + (cell_x >> 3) * 2 + (cell_y >> 6)
-    return line, (cell_y >> 3 & 7) * GROUP + (cell_z >> 3)
-
-
-def spread_planes(station, amounts, put):
-    electrodes = station.shape[1]
-    line, spot = station_table(station)
-    at_spot = iota((LANES, electrodes), 0) == spot
-    table = jnp.concatenate(pieces_of(jnp.where(at_spot, amounts, 0.0), 2))
-    plane_lines = iota((SIDE * SIDE * SIDE, electrodes), 0)
-
-    def plane(x, carry):
-        chosen = plane_lines + x * (SIDE * SIDE * SIDE) == line
-        chosen = jnp.where(chosen, 1.0, 0.0).astype(jnp.bfloat16)
-        both = lax.dot_general(
-            chosen, table, (((1,), (1,)), ((), ())), preferred_element_type=jnp.float32
-        )
-        put(x, both[:, :LANES] + both[:, LANES:])
-        return carry
-
-    lax.fori_loop(0, SIDE, plane, 0)
-
-
-def source_kernel(stations_ref, currents_ref, source_ref):
-    def put(x, value):
-        source_ref[pl.ds(x * SIDE * SIDE * SIDE, SIDE * SIDE * SIDE), :] = value
-
-    spread_planes(stations_ref[...], currents_ref[...], put)
 
 
 class Edged:
@@ -189,6 +166,11 @@
             before = inside_down(block_down(value[n - 1 :], 1), 1)
             self.ref[pl.ds(self.start(x, z, -1), SIDE), :] = before[0]
 
+    def close_z(self, x):
+        n = self.side
+        self[x, n] = block_up(self[x, 0], 2)
+        self[x, -1] = block_down(self[x, n - 1], 2)
+
     def close(self, exact=False):
         n = self.side
         for z in range(n):
@@ -213,34 +195,38 @@
         self.ref[pl.ds((x * self.side + z) * rows, rows), :] = value.reshape(-1, LANES)
 
 
+def planes_of(count, body):
+    if count < SIDE:
+        for x in range(count):
+            body(x)
+        return
+
+    def one(x, carry):
+        body(x)
+        return carry
+
+    lax.fori_loop(0, count, one, 0)
+
+
 class Level:
     def __init__(self, refs, index):
         self.side = side = SIDE >> index
         self.scale = 0.25**index
-        self.cond, self.first, self.second = [Edged(ref, side) for ref in refs[:3]]
-        self.links = [Plain(ref, side) for ref in refs[3:9]]
-        self.weight, self.back, self.base, self.half = [Plain(ref, side) for ref in refs[9:13]]
+        edged = [Edged(ref, side) for ref in refs[:5]]
+        self.cond, self.first, self.second, self.base, self.back = edged
+        self.links = [Plain(ref, side) for ref in refs[5:11]]
+        self.half = Plain(refs[11], side // 2)
+        self.weight = Plain(refs[12], side) if index else None
 
     @staticmethod
     def scratch(index):
         side = SIDE >> index
-        edged = pltpu.VMEM(((side + 2) ** 3 * SIDE, LANES), jnp.float32)
-        plain = pltpu.VMEM((side**3 * SIDE, LANES), jnp.float32)
-        return [edged] * 3 + [plain] * 10
-
-    def planes(self, body):
-        if self.side == SIDE:
-
-            def one(x, carry):
-                body(x)
-                return carry
-
-            lax.fori_loop(0, self.side, one, 0)
-        else:
-            for x in range(self.side):
-                body(x)
-
-    def shifted(self, field, x, z, here, exact=False):
+        edged = (side + 2) ** 3
+        sizes = [edged] * 5 + [side**3] * 6 + [side**3 // 4] + [side**3] * (index > 0)
+        return [pltpu.VMEM((size * SIDE, LANES), jnp.float32) for size in sizes]
+
+    def shifted(self, field, x, z, here, exact=False, along=None):
+        ahead, behind = along or (field[x, z + 1], field[x, z - 1])
         after = block_up(here[:1], 1)
         before = block_down(here[-1:], 1)
         if exact:
@@ -250,8 +236,8 @@
             field[x - 1, z],
             jnp.concatenate([here[1:], after]),
             jnp.concatenate([before, here[:-1]]),
-            field[x, z + 1],
-            field[x, z - 1],
+            ahead,
+            behind,
         ]
 
     def prepare(self):
@@ -266,7 +252,8 @@
                     total = total + other
                 total = 3.0 * here + 0.5 * total
                 inverse = DAMPING / total
-                self.weight[x, z] = inverse * (1.0 / self.scale)
+                if self.weight is not None:
+                    self.weight[x, z] = inverse * (1.0 / self.scale)
                 self.back[x, z] = total * (self.scale / DAMPING)
                 inverse = 0.5 * inverse
                 for index, other in enumerate(others):
@@ -281,58 +268,81 @@
                         link = inside_down(link, 2)
                     self.links[index][x, z] = link
 
-        self.planes(plane)
+        planes_of(n, plane)
         for z in range(n):
             self.links[0][n - 1, z] = inside_up(self.links[0][n - 1, z], 0)
             self.links[1][0, z] = inside_down(self.links[1][0, z], 0)
 
-    def total(self, field, x, z):
-        here = field[x, z]
-        result = self.base[x, z]
-        for link, other in zip(self.links, self.shifted(field, x, z, here)):
-            result = result + link[x, z] * other
-        return here, result
+    def rows(self, field, x):
+        behind, here = field[x, -1], field[x, 0]
+        for z in range(self.side):
+            ahead = field[x, z + 1]
+            result = self.base[x, z]
+            others = self.shifted(field, x, z, here, along=(ahead, behind))
+            for link, other in zip(self.links, others):
+                result = result + link[x, z] * other
+            yield z, here, result
+            behind, here = here, ahead
 
     def sweep(self, field, out, exact=False):
         def plane(x):
-            for z in range(self.side):
-                here, result = self.total(field, x, z)
+            for z, here, result in self.rows(field, x):
                 out.put(x, z, (1.0 - DAMPING) * here + result, exact)
 
-        self.planes(plane)
+        planes_of(self.side, plane)
         out.close(exact)
 
-    def halve(self, rows, coarse):
+    def halve(self, plane_rows, coarse):
         n = self.side
 
         def plane(x):
-            for z in range(n // 2):
-                self.half[x, z] = jnp.concatenate([pair_rows(rows(x, 2 * z) + rows(x, 2 * z + 1))] * 2)
-
-        self.planes(plane)
+            held = None
+            for z, row in enumerate(plane_rows(x)):
+                if z % 2 == 0:
+                    held = row
+                else:
+                    self.half[x, z // 2] = pair_rows(held + row)
+
+        planes_of(n, plane)
         for x in range(n // 2):
             for z in range(n // 2):
-                pair = self.half[2 * x, z][: n // 2] + self.half[2 * x + 1, z][: n // 2]
+                pair = self.half[2 * x, z] + self.half[2 * x + 1, z]
                 coarse(x, z, 0.125 * pair)
 
     def descend(self, coarse):
-        self.sweep(self.first, self.second)
-
-        def residual(x, z):
-            here, result = self.total(self.second, x, z)
-            return (result - DAMPING * here) * self.back[x, z]
-
-        self.halve(residual, coarse)
+        self.sweep(self.base, self.second)
+
+        def residuals(x):
+            for z, here, result in self.rows(self.second, x):
+                self.first[x, z] = (1.0 - DAMPING) * here + result
+                yield (result - DAMPING * here) * self.back[x, z]
+
+        self.halve(residuals, coarse)
 
     def ascend(self, correction, out, exact=False):
         def plane(x):
+            upper = (x + 1) // 2
             for z in range(self.side):
-                self.second.put(x, z, self.second[x, z] + twice(correction(x, z)))
-
-        self.planes(plane)
+                above = (z + 1) // 2
+                row = correction(x // 2, z // 2)
+                here = twice(row)
+                after, before = block_up(row[:1], 1), block_down(row[-1:], 1)
+                others = [
+                    twice(correction(upper, z // 2)),
+                    twice(correction(upper - 1, z // 2)),
+                    jnp.concatenate([here[1:], after]),
+                    jnp.concatenate([before, here[:-1]]),
+                    twice(correction(x // 2, above)),
+                    twice(correction(x // 2, above - 1)),
+                ]
+                result = self.first[x, z] + (1.0 - DAMPING) * here
+                for link, other in zip(self.links, others):
+                    result = result + link[x, z] * other
+                self.second.put(x, z, result)
+
+        planes_of(self.side, plane)
         self.second.close()
-        self.sweep(self.second, self.first)
-        self.sweep(self.first, out, exact)
+        self.sweep(self.second, out, exact)
 
 
 def replicated_kernel(
@@ -348,22 +358,26 @@
     part_refs,
     device_ref,
     cells_ref,
-    source_ref,
     stations_ref,
+    currents_ref,
     receivers_ref,
     observed_ref,
     potentials_ref,
-    gradient_ref,
-    forward_ref,
+    mine_ref,
+    theirs_ref,
     gathered,
+    weights,
     *level_refs,
 ):
     f32 = jnp.float32
     electrodes = stations_ref.shape[1]
-    per_level = len(Level.scratch(0))
-    levels = [Level(level_refs[per_level * k : per_level * (k + 1)], k) for k in range(LEVELS - 1)]
+    levels, used = [], 0
+    for index in range(LEVELS - 1):
+        count = len(Level.scratch(index))
+        levels.append(Level(level_refs[used : used + count], index))
+        used += count
     fine = levels[0]
-    forward = Edged(forward_ref, SIDE)
+    forward = fine.cond
     wide = SIDE * SIDE * SIDE
 
     device = device_ref[0]
@@ -377,7 +391,7 @@
         for z in (0, SIDE - 1):
             fine.cond.put(x, z, fine.cond[x, z], exact=True)
 
-    fine.planes(collect)
+    planes_of(SIDE, collect)
     fine.cond.close(exact=True)
 
     coarsest = []
@@ -390,7 +404,7 @@
             else:
                 below.cond.put(x, z, row, exact=True)
 
-        level.halve(lambda x, z, level=level: level.cond[x, z], coarse)
+        level.halve(lambda x, level=level: [level.cond[x, z] for z in range(level.side)], coarse)
         if below is not None:
             below.cond.close(exact=True)
 
@@ -426,38 +440,60 @@
             held = []
             level.descend(lambda x, z, row: held.append(row))
             solved = solve_last(held[0])
-            level.ascend(lambda x, z: solved, out, exact)
+
+            def correction(x, z):
+                if x != 0:
+                    return (block_up if x > 0 else block_down)(solved, 0)
+                if z != 0:
+                    return (block_up if z > 0 else block_down)(solved, 2)
+                return solved
+
+            level.ascend(correction, out, exact)
             return
         below = levels[index + 1]
-
-        def coarse(x, z, row):
-            row = below.weight[x, z] * row
-            below.base[x, z] = row
-            below.first.put(x, z, row)
-
-        level.descend(coarse)
-        below.first.close()
-        cycle(index + 1, below.second)
-        level.ascend(lambda x, z: below.second[x // 2, z // 2], out, exact)
-
-    def begin(x, rows):
-        value = rows.reshape(SIDE, SIDE, SIDE, LANES)
-        for z in range(SIDE):
-            row = fine.weight[x, z] * value[z]
-            fine.base[x, z] = row
-            fine.first.put(x, z, row)
-
-    fine.planes(lambda x: begin(x, source_ref[pl.ds(x * wide, wide), :]))
-    fine.first.close()
+        level.descend(lambda x, z, row: below.base.put(x, z, below.weight[x, z] * row))
+        below.base.close()
+        cycle(index + 1, below.first)
+        level.ascend(lambda x, z: below.first[x, z], out, exact)
+
+    _, cell_y, cell_z, row, spot = station_table(stations_ref[...])
+    at_spot = iota((LANES, electrodes), 0) == spot
+    line = stations_ref[...] & 0x1C387 | row << 20
+    same = jnp.broadcast_to(line, (electrodes, electrodes))
+    same = jnp.where(same == same.T, 1.0, 0.0).astype(jnp.bfloat16)
+
+    def each(body):
+        def one(electrode, carry):
+            body(pl.ds(electrode, 1), pl.ds(cells_ref[0, electrode], 1))
+            return carry
+
+        lax.fori_loop(0, electrodes, one, 0, unroll=8)
+
+    def weigh(electrode, cell):
+        weights[electrode, :] = fine.back.ref[cell, :]
+
+    each(weigh)
+    weights[...] = 1.0 / weights[...]
+    fine.base.ref[...] = jnp.zeros_like(fine.base.ref)
+
+    def spread(amounts):
+        shared = product(jnp.where(at_spot, amounts, 0.0), same, 3)
+        gathered[...] = shared.T * weights[...]
+
+        def put(electrode, cell):
+            fine.base.ref[cell, :] = gathered[electrode, :]
+
+        each(put)
+        planes_of(SIDE, fine.base.close_z)
+        fine.base.close()
+
+    spread(currents_ref[...])
     cycle(0, forward, exact=True)
 
-    def read(electrode, carry):
-        gathered[pl.ds(electrode, 1), :] = forward_ref[pl.ds(cells_ref[electrode], 1), :]
-        return carry
-
-    lax.fori_loop(0, electrodes, read, 0, unroll=8)
-    _, spot = station_table(stations_ref[...])
-    at_spot = iota((LANES, electrodes), 0) == spot
+    def read(electrode, cell):
+        gathered[electrode, :] = forward.ref[cell, :]
+
+    each(read)
     readings = jnp.sum(jnp.where(at_spot, gathered[...].T, 0.0), axis=0, keepdims=True)
     receivers = receivers_ref[...]
     numbers = iota((receivers.shape[0], electrodes), 1)
@@ -470,12 +506,13 @@
         return product(jnp.broadcast_to(row, (16, row.shape[1])), pairs, 3, dims)[0:1]
 
     misfit = exact(readings, ((1,), (1,))) - observed_ref[...]
-    spread_planes(stations_ref[...], exact(misfit, ((1,), (0,))), begin)
-    fine.first.close()
-    cycle(0, fine.second, exact=True)
+    spread(exact(misfit, ((1,), (0,))))
+    cycle(0, fine.first, exact=True)
 
     order = lane_order()
-    adjoint = fine.second
+    adjoint = fine.first
+    chunk = mine_ref.shape[1]
+    even = device_ref[1] == 0
 
     def own(field, x, z, y=0):
         return field.ref[pl.ds(field.start(x, z, y) + device, SIDE, stride=SIDE), :]
@@ -491,25 +528,29 @@
             tiles_u.append(here_u)
             tiles_g.append(-0.5 * total)
         potentials_ref[x] = from_blocks(tiles_u, order)
-        gradient_ref[x] = from_blocks(tiles_g, order)
+        natural = from_blocks(tiles_g, order)
+        low, high = natural[:chunk], natural[chunk:]
+        mine_ref[x] = jnp.where(even, low, high)
+        theirs_ref[x] = jnp.where(even, high, low)
 
 
 def replicated(conductivity, stations, currents, receivers, observed):
     rows, cols, depth = conductivity.shape
     f32 = jnp.float32
-    count_s = lax.axis_size("shot")
-    shot = lax.axis_index("shot")
     electrodes = stations.shape[0]
     total = rows * cols
     vmem = pl.BlockSpec(memory_space=pltpu.VMEM)
     smem = pl.BlockSpec(memory_space=pltpu.SMEM)
-    params = pltpu.CompilerParams(vmem_limit_bytes=VMEM_BYTES)
-    mine = pl.pallas_call(
+    station_row = stations.reshape(1, electrodes)
+    mine, cells = pl.pallas_call(
         to_blocks_kernel,
-        out_shape=jax.ShapeDtypeStruct((total, LANES), f32),
-        in_specs=[vmem],
-        out_specs=vmem,
-    )(conductivity)
+        out_shape=(
+            jax.ShapeDtypeStruct((total, LANES), f32),
+            jax.ShapeDtypeStruct((1, electrodes), jnp.int32),
+        ),
+        in_specs=[vmem, vmem],
+        out_specs=(vmem, vmem),
+    )(conductivity, station_row)
     count_x, count_y = lax.axis_size("gx"), lax.axis_size("gy")
     parts = []
     for k in range(count_x):
@@ -517,51 +558,28 @@
         parts.append(lax.ppermute(mine, "gx", pairs) if k else mine)
     swap = [(0, 1), (1, 0)]
     parts = [part for own in parts for part in (own, lax.ppermute(own, "gy", swap))]
-    station_row = stations.reshape(1, electrodes)
-    source = pl.pallas_call(
-        source_kernel,
-        out_shape=jax.ShapeDtypeStruct((total * SIDE, LANES), f32),
-        in_specs=[vmem, vmem],
-        out_specs=vmem,
-        compiler_params=params,
-        cost_estimate=pl.CostEstimate(flops=600_000_000, bytes_accessed=4_000_000, transcendentals=0),
-    )(station_row, currents)
-    device = (lax.axis_index("gx") * lax.axis_size("gy") + lax.axis_index("gy")).astype(jnp.int32)
-    cell_x, cell_y, cell_z = stations >> 14, stations >> 7 & 127, stations & 127
-    wide = SIDE + 2
-    cells = ((cell_x % 8 + 1) * wide + cell_z % 8 + 1) * wide + cell_y % 8 + 1
-    cells = cells * SIDE + cell_x // 8 * 2 + cell_y // 64
+    device = lax.axis_index("gx") * count_y + lax.axis_index("gy")
+    place = jnp.stack([device, lax.axis_index("shot")]).astype(jnp.int32)
+    chunk = cols // 2
     levels = [shape for index in range(LEVELS - 1) for shape in Level.scratch(index)]
-    potentials, gradient = pl.pallas_call(
+    potentials, own, theirs = pl.pallas_call(
         functools.partial(replicated_kernel, len(parts)),
         out_shape=(
             jax.ShapeDtypeStruct((rows, cols, LANES), f32),
-            jax.ShapeDtypeStruct((rows, cols, LANES), f32),
+            jax.ShapeDtypeStruct((rows, chunk, LANES), f32),
+            jax.ShapeDtypeStruct((rows, chunk, LANES), f32),
         ),
         in_specs=[smem, smem] + [vmem] * (len(parts) + 4),
-        out_specs=(vmem, vmem),
+        out_specs=(vmem, vmem, vmem),
         scratch_shapes=[
-            pltpu.VMEM((wide**3 * SIDE, LANES), f32),
+            pltpu.VMEM((electrodes, LANES), f32),
             pltpu.VMEM((electrodes, LANES), f32),
         ]
         + levels,
-        compiler_params=params,
+        compiler_params=pltpu.CompilerParams(vmem_limit_bytes=VMEM_BYTES),
         cost_estimate=pl.CostEstimate(flops=200_000_000, bytes_accessed=4_000_000, transcendentals=0),
-    )(
-        device.reshape(1),
-        cells,
-        *parts,
-        source,
-        station_row,
-        receivers,
-        observed,
-    )
-    chunk = cols // count_s
-    summed = lax.dynamic_slice_in_dim(gradient, shot * chunk, chunk, axis=1)
-    for k in range(1, count_s):
-        theirs = lax.dynamic_slice_in_dim(gradient, (shot + k) % count_s * chunk, chunk, axis=1)
-        summed = summed + lax.ppermute(theirs, "shot", [(i, (i + k) % count_s) for i in range(count_s)])
-    return potentials[None], summed
+    )(place, cells, *parts, station_row, currents, receivers, observed)
+    return potentials[None], own + lax.ppermute(theirs, "shot", swap)
 
 
 def extended(array, sides, width):
@@ -759,7 +777,8 @@
 def per_device(conductivity, stations, currents, receivers, observed):
     blocks = lax.axis_size("gx") * lax.axis_size("gy")
     fits = conductivity.shape == (SIDE, SIDE * SIDE, LANES) and blocks == SIDE
-    fits = fits and lax.axis_size("gy") == 2 and currents.shape[0] == 1
+    fits = fits and lax.axis_size("gy") == 2 and lax.axis_size("shot") == 2
+    fits = fits and currents.shape[0] == 1
     plan = replicated if fits else distributed
     return plan(conductivity, stations, currents, receivers, observed)
 

time: 75.6 us -> 66.5 us (0.88)
  the two profiles are of different devices: /device:TPU:12 before, /device:TPU:0 now
where the time goes in v4:
time: 66.5 us; the launch traced here: 66.4 us
  Pallas kernels  30 us (45%)
  waiting for transfers between devices  27 us (41%)
  starting transfers between devices  7.68 us (12%)
  other arithmetic  0.75 us (1%)
  between operations  0.71 us (1%)
    pallas_call x1, Pallas kernels, replicated(): pl.pallas_call(functools.partial(replicated_kernel, len(parts)), out_shap...  27.8 us
    ppermute x3, waiting for transfers between devices, replicated(): parts.append(lax.ppermute(mine, 'gx', pairs) if k else mine)  21.9 us
    ppermute x3, starting transfers between devices, replicated(): parts.append(lax.ppermute(mine, 'gx', pairs) if k else mine)  5.67 us
    ppermute x1, waiting for transfers between devices, replicated(): return (potentials[None], own + lax.ppermute(theirs, 'shot', swap))  4.05 us
    pallas_call x1, Pallas kernels, replicated(): pl.pallas_call(to_blocks_kernel, out_shape=(jax.ShapeDtypeStruct((total,...  2.24 us
    ppermute x1, starting transfers between devices, replicated(): return (potentials[None], own + lax.ppermute(theirs, 'shot', swap))  1.49 us
  transfers between devices with their start and end apart: 8, of which 5 were waited for; matrix products, arithmetic and copies ran while one was open for 0% of the time, Pallas kernels for 0%

profile of v4, /device:TPU:0, one launch (start us, length us, event | category | flops | bytes accessed | tf_op | source)
XLA Modules:
  0.0 66.4 jit_solution(10370637059369677133)
XLA Ops:
  0.6 0.0 copy-start.5
  0.6 2.2 %shard_map.68 = (f32[512,128]{1,0:T(8,128)}, s32[1,256]{1,0:T(1,128)}) custom-call(f32[8,64,128]{2,1,0:T(8,128)} %natural_ref.1, s32[1,256]{1,0:T(1,128)} %bitcast.4), custom_call_target="tpu_custom_call" | custom-call | tf_op jit(solution)/shard_map/pallas_call | solution.py:545
  2.9 0.0 copy-start
  2.9 5.0 %collective-permute-start.5 = (f32[512,128]{1,0:T(8,128)}, f32[512,128]{1,0:T(8,128)S(1)}, u32[]{:S(2)}, u32[]{:S(2)}) collective-permute-start(f32[512,128]{1,0:T(8,128)} %get-tuple-element.8.refs_0_), channel_id=1, source_target_pairs={{0,12},{4,8},{8,4},{12,0},{1,13},{5,9},{9,5},{13,1},{2,14},{6,10},... | collective-permute-start | bytes 786440 | tf_op jit(solution)/shard_map/ppermute | solution.py:558
  7.9 0.0 collective-permute-start.3
  7.9 0.6 collective-permute-start.1
  8.6 0.0 collective-permute-start
  8.6 6.9 %collective-permute-done.5.refs_6_ = f32[512,128]{1,0:T(8,128)S(1)} collective-permute-done((f32[512,128]{1,0:T(8,128)}, f32[512,128]{1,0:T(8,128)S(1)}, u32[]{:S(2)}, u32[]{:S(2)}) %collective-permute-start.5) | collective-permute-done | bytes 262176 | tf_op jit(solution)/shard_map/ppermute | solution.py:558
  15.5 0.0 collective-permute-start.6
  15.5 15.0 %collective-permute-done.3.refs_4_ = f32[512,128]{1,0:T(8,128)S(1)} collective-permute-done((f32[512,128]{1,0:T(8,128)}, f32[512,128]{1,0:T(8,128)S(1)}, u32[]{:S(2)}, u32[]{:S(2)}) %collective-permute-start.3) | collective-permute-done | bytes 262176 | tf_op jit(solution)/shard_map/ppermute | solution.py:558
  30.5 0.0 collective-permute-start.4
  30.5 0.0 collective-permute-done.1.refs_2_
  30.5 0.5 collective-permute-start.2
  31.0 0.0 copy-done.5
  31.0 0.1 copy.7.refs_10_
  31.1 0.0 copy-start.3
  31.1 0.0 copy-start.4
  31.2 0.0 copy-start.2
  31.2 0.1 pad_add_fusion.device_ref
  31.2 0.0 collective-permute-done.refs_1_
  31.2 0.0 collective-permute-done.6.refs_7_
  31.3 0.7 %collective-permute-done.4.refs_5_ = f32[512,128]{1,0:T(8,128)S(1)} collective-permute-done((f32[512,128]{1,0:T(8,128)S(1)}, f32[512,128]{1,0:T(8,128)S(1)}, u32[]{:S(2)}, u32[]{:S(2)}) %collective-permute-start.4) | collective-permute-done | bytes 262176 | tf_op jit(solution)/shard_map/ppermute | solution.py:560
  32.0 0.4 collective-permute-done.2.refs_3_
  32.4 0.0 copy-done
  32.4 0.0 copy-done.3
  32.4 0.0 copy-done.4
  32.4 0.0 copy-done.2
  32.4 0.0 copy-done.1
  32.4 27.8 %shard_map.69 = (f32[8,64,128]{2,1,0:T(8,128)}, f32[8,32,128]{2,1,0:T(8,128)S(1)}, f32[8,32,128]{2,1,0:T(8,128)S(1)}) custom-call(s32[2]{0:T(128)S(1)} %pad_add_fusion.device_ref, s32[1,256]{1,0:T(1,128)S(1)} %copy-done.4, f32[512,128]{1,0:T(8,128)S(1)} %copy-done, f32[512,128]{1,0:T(8,128)S(1)} %collective-permute-done.refs_1_, ...), custom_call_target="tpu_custom_call" | custom-call | flops 200000000 | bytes 4000000 | tf_op jit(solution)/shard_map/pallas_call | solution.py:565
  60.1 1.5 %collective-permute-start.7 = (f32[8,32,128]{2,1,0:T(8,128)S(1)}, f32[8,32,128]{2,1,0:T(8,128)S(1)}, u32[]{:S(2)}, u32[]{:S(2)}) collective-permute-start(f32[8,32,128]{2,1,0:T(8,128)S(1)} %get-tuple-element.11), channel_id=1, source_target_pairs={{0,1},{1,0},{2,3},{3,2},{4,5},{5,4},{6,7},{7,6},{8,9},{9,8},{10,11... | collective-permute-start | bytes 393224 | tf_op jit(solution)/shard_map/ppermute | solution.py:582
  61.6 4.0 %collective-permute-done.7 = f32[8,32,128]{2,1,0:T(8,128)S(1)} collective-permute-done((f32[8,32,128]{2,1,0:T(8,128)S(1)}, f32[8,32,128]{2,1,0:T(8,128)S(1)}, u32[]{:S(2)}, u32[]{:S(2)}) %collective-permute-start.7) | collective-permute-done | bytes 131104 | tf_op jit(solution)/shard_map/ppermute | solution.py:582
  65.7 0.7 %add.7 = f32[8,32,128]{2,1,0:T(8,128)} add(f32[8,32,128]{2,1,0:T(8,128)S(1)} %get-tuple-element.10, f32[8,32,128]{2,1,0:T(8,128)S(1)} %collective-permute-done.7) | non-fusion elementwise | flops 32768 | bytes 393216 | tf_op jit(solution)/shard_map/add | solution.py:582
  (1 shorter events, 0.0 us)
Async XLA Ops:
  0.6 30.3 %copy-start.5 = (s32[512,2]{0,1:T(2,128)S(1)}, s32[512,2]{0,1:T(2,128)}, u32[]{:S(2)}) copy-start(s32[512,2]{0,1:T(2,128)} %param.8) | copy-start | bytes 12292
  2.9 29.5 %copy-start = (f32[512,128]{1,0:T(8,128)S(1)}, f32[512,128]{1,0:T(8,128)}, u32[]{:S(2)}) copy-start(f32[512,128]{1,0:T(8,128)} %get-tuple-element.8.refs_0_) | copy-start | bytes 786436
  2.9 12.6 %collective-permute-start.5 = (f32[512,128]{1,0:T(8,128)}, f32[512,128]{1,0:T(8,128)S(1)}, u32[]{:S(2)}, u32[]{:S(2)}) collective-permute-start(f32[512,128]{1,0:T(8,128)} %get-tuple-element.8.refs_0_), channel_id=1, source_target_pairs={{0,12},{4,8},{8,4},{12,0},{1,13},{5,9},{9,5},{13,1},{2,14},{6,10},... | collective-permute-start | bytes 786440 | tf_op jit(solution)/shard_map/ppermute | solution.py:558
  7.9 22.5 %collective-permute-start.3 = (f32[512,128]{1,0:T(8,128)}, f32[512,128]{1,0:T(8,128)S(1)}, u32[]{:S(2)}, u32[]{:S(2)}) collective-permute-start(f32[512,128]{1,0:T(8,128)} %get-tuple-element.8.refs_0_), channel_id=1, source_target_pairs={{0,8},{4,12},{8,0},{12,4},{1,9},{5,13},{9,1},{13,5},{2,10},{6,14},... | collective-permute-start | bytes 786440 | tf_op jit(solution)/shard_map/ppermute | solution.py:558
  7.9 22.5 %collective-permute-start.1 = (f32[512,128]{1,0:T(8,128)}, f32[512,128]{1,0:T(8,128)S(1)}, u32[]{:S(2)}, u32[]{:S(2)}) collective-permute-start(f32[512,128]{1,0:T(8,128)} %get-tuple-element.8.refs_0_), channel_id=1, source_target_pairs={{0,4},{4,0},{8,12},{12,8},{1,5},{5,1},{9,13},{13,9},{2,6},{6,2},{1... | collective-permute-start | bytes 786440 | tf_op jit(solution)/shard_map/ppermute | solution.py:558
  8.6 22.7 %collective-permute-start = (f32[512,128]{1,0:T(8,128)}, f32[512,128]{1,0:T(8,128)S(1)}, u32[]{:S(2)}, u32[]{:S(2)}) collective-permute-start(f32[512,128]{1,0:T(8,128)} %get-tuple-element.8.refs_0_), channel_id=1, source_target_pairs={{0,2},{2,0},{1,3},{3,1},{4,6},{6,4},{5,7},{7,5},{8,10},{10,8},{9,1... | collective-permute-start | bytes 786440 | tf_op jit(solution)/shard_map/ppermute | solution.py:560
  15.5 15.8 %collective-permute-start.6 = (f32[512,128]{1,0:T(8,128)S(1)}, f32[512,128]{1,0:T(8,128)S(1)}, u32[]{:S(2)}, u32[]{:S(2)}) collective-permute-start(f32[512,128]{1,0:T(8,128)S(1)} %collective-permute-done.5.refs_6_), channel_id=1, source_target_pairs={{0,2},{2,0},{1,3},{3,1},{4,6},{6,4},{5,7},{7,5},{8,10},{10,8},{9,1... | collective-permute-start | bytes 786440 | tf_op jit(solution)/shard_map/ppermute | solution.py:560
  30.5 1.5 %collective-permute-start.4 = (f32[512,128]{1,0:T(8,128)S(1)}, f32[512,128]{1,0:T(8,128)S(1)}, u32[]{:S(2)}, u32[]{:S(2)}) collective-permute-start(f32[512,128]{1,0:T(8,128)S(1)} %collective-permute-done.3.refs_4_), channel_id=1, source_target_pairs={{0,2},{2,0},{1,3},{3,1},{4,6},{6,4},{5,7},{7,5},{8,10},{10,8},{9,1... | collective-permute-start | bytes 786440 | tf_op jit(solution)/shard_map/ppermute | solution.py:560
  30.5 1.9 %collective-permute-start.2 = (f32[512,128]{1,0:T(8,128)S(1)}, f32[512,128]{1,0:T(8,128)S(1)}, u32[]{:S(2)}, u32[]{:S(2)}) collective-permute-start(f32[512,128]{1,0:T(8,128)S(1)} %collective-permute-done.1.refs_2_), channel_id=1, source_target_pairs={{0,2},{2,0},{1,3},{3,1},{4,6},{6,4},{5,7},{7,5},{8,10},{10,8},{9,1... | collective-permute-start | bytes 786440 | tf_op jit(solution)/shard_map/ppermute | solution.py:560
  31.1 1.2 %copy-start.3 = (f32[1,256]{1,0:T(1,128)S(1)}, f32[1,256]{1,0:T(1,128)}, u32[]{:S(2)}) copy-start(f32[1,256]{1,0:T(1,128)} %refs_9_.1) | copy-start | bytes 3076
  31.1 1.2 %copy-start.4 = (s32[1,256]{1,0:T(1,128)S(1)}, s32[1,256]{1,0:T(1,128)}, u32[]{:S(2)}) copy-start(s32[1,256]{1,0:T(1,128)} %get-tuple-element.7.cells_ref) | copy-start | bytes 3076
  31.2 1.2 %copy-start.2 = (f32[1,512]{1,0:T(1,128)S(1)}, f32[1,512]{1,0:T(1,128)}, u32[]{:S(2)}) copy-start(f32[1,512]{1,0:T(1,128)} %refs_11_.1) | copy-start | bytes 6148
  31.2 1.1 %copy-start.1 = (s32[256]{0:T(256)S(1)}, s32[256]{0:T(256)}, u32[]{:S(2)}) copy-start(s32[256]{0:T(256)} %param.6) | copy-start | bytes 3076
  60.1 5.5 %collective-permute-start.7 = (f32[8,32,128]{2,1,0:T(8,128)S(1)}, f32[8,32,128]{2,1,0:T(8,128)S(1)}, u32[]{:S(2)}, u32[]{:S(2)}) collective-permute-start(f32[8,32,128]{2,1,0:T(8,128)S(1)} %get-tuple-element.11), channel_id=1, source_target_pairs={{0,1},{1,0},{2,3},{3,2},{4,5},{5,4},{6,7},{7,6},{8,9},{9,8},{10,11... | collective-permute-start | bytes 393224 | tf_op jit(solution)/shard_map/ppermute | solution.py:582

commit v5 on v4

--- a/solution.py
+++ b/solution.py
@@ -67,13 +67,16 @@
     return tiles
 
 
-def to_blocks_kernel(natural_ref, stations_ref, blocks_ref, cells_ref):
+def to_blocks_kernel(place_ref, natural_ref, stations_ref, blocks_ref, half_ref, cells_ref):
     order = lane_order()
     for x in range(SIDE):
         tiles = product(natural_ref[x], order, 3)
         tiles = [tiles[SIDE * k : SIDE * (k + 1)] for k in range(SIDE)]
         for z, tile in enumerate(exchange_groups(tiles)):
             blocks_ref[pl.ds((x * SIDE + z) * SIDE, SIDE), :] = tile
+    count = half_ref.shape[0]
+    low, high = blocks_ref[pl.ds(0, count), :], blocks_ref[pl.ds(count, count), :]
+    half_ref[...] = jnp.where(place_ref[1] == 0, low, high)
     cell_x, cell_y, cell_z, row, _ = station_table(stations_ref[...])
     wide = SIDE + 2
     register = (((cell_x & 7) + 1) * wide + (cell_z & 7) + 1) * wide + (cell_y & 7) + 1
@@ -346,16 +349,19 @@
 
 
 def replicated_kernel(
-    count,
+    whole,
+    halved,
     device_ref,
     cells_ref,
     *refs,
 ):
-    solve_kernel(refs[:count], device_ref, cells_ref, *refs[count:])
+    parts = refs[:whole], refs[whole : whole + halved]
+    solve_kernel(*parts, device_ref, cells_ref, *refs[whole + halved :])
 
 
 def solve_kernel(
     part_refs,
+    half_refs,
     device_ref,
     cells_ref,
     stations_ref,
@@ -381,17 +387,30 @@
     wide = SIDE * SIDE * SIDE
 
     device = device_ref[0]
+    shot = device_ref[1]
+
+    def place(part, row, x, index):
+        for z in range(SIDE):
+            fine.cond.ref[pl.ds(fine.cond.start(x, z) + index, SIDE, stride=SIDE), :] = part[
+                pl.ds((row * SIDE + z) * SIDE, SIDE), :
+            ]
+
     def collect(x):
         for k, part in enumerate(part_refs):
-            for z in range(SIDE):
-                start = fine.cond.start(x, z) + (device ^ k)
-                fine.cond.ref[pl.ds(start, SIDE, stride=SIDE), :] = part[
-                    pl.ds((x * SIDE + z) * SIDE, SIDE), :
-                ]
+            place(part, x, x, device ^ k)
+
+    def collect_half(x):
+        for k, part in enumerate(half_refs):
+            swapped, index = k // 2 % 2, len(part_refs) + k // 4 * 2 + k % 2
+            place(part, x, (shot ^ swapped) * (SIDE // 2) + x, device ^ index)
+
+    def edges(x):
         for z in (0, SIDE - 1):
             fine.cond.put(x, z, fine.cond[x, z], exact=True)
 
     planes_of(SIDE, collect)
+    planes_of(SIDE // 2, collect_half)
+    planes_of(SIDE, edges)
     fine.cond.close(exact=True)
 
     coarsest = []
@@ -512,7 +531,7 @@
     order = lane_order()
     adjoint = fine.first
     chunk = mine_ref.shape[1]
-    even = device_ref[1] == 0
+    even = shot == 0
 
     def own(field, x, z, y=0):
         return field.ref[pl.ds(field.start(x, z, y) + device, SIDE, stride=SIDE), :]
@@ -542,34 +561,42 @@
     vmem = pl.BlockSpec(memory_space=pltpu.VMEM)
     smem = pl.BlockSpec(memory_space=pltpu.SMEM)
     station_row = stations.reshape(1, electrodes)
-    mine, cells = pl.pallas_call(
+    device = lax.axis_index("gx") * lax.axis_size("gy") + lax.axis_index("gy")
+    place = jnp.stack([device, lax.axis_index("shot")]).astype(jnp.int32)
+    mine, half, cells = pl.pallas_call(
         to_blocks_kernel,
         out_shape=(
             jax.ShapeDtypeStruct((total, LANES), f32),
+            jax.ShapeDtypeStruct((total // 2, LANES), f32),
             jax.ShapeDtypeStruct((1, electrodes), jnp.int32),
         ),
-        in_specs=[vmem, vmem],
-        out_specs=(vmem, vmem),
-    )(conductivity, station_row)
-    count_x, count_y = lax.axis_size("gx"), lax.axis_size("gy")
-    parts = []
-    for k in range(count_x):
-        pairs = [(i, i ^ k) for i in range(count_x)]
-        parts.append(lax.ppermute(mine, "gx", pairs) if k else mine)
+        in_specs=[smem, vmem, vmem],
+        out_specs=(vmem, vmem, vmem),
+    )(place, conductivity, station_row)
     swap = [(0, 1), (1, 0)]
-    parts = [part for own in parts for part in (own, lax.ppermute(own, "gy", swap))]
-    device = lax.axis_index("gx") * count_y + lax.axis_index("gy")
-    place = jnp.stack([device, lax.axis_index("shot")]).astype(jnp.int32)
+
+    def partner(part, k):
+        count = lax.axis_size("gx")
+        return lax.ppermute(part, "gx", [(i, i ^ k) for i in range(count)])
+
+    def with_mate(part):
+        return [part, lax.ppermute(part, "gy", swap)]
+
+    far = [partner(half, k) for k in (2, 3)]
+    near = partner(mine, 1)
+    halved = [piece for own in far for piece in (own, lax.ppermute(own, "shot", swap))]
+    parts = [piece for own in (mine, near) for piece in with_mate(own)]
+    halved = [piece for own in halved for piece in with_mate(own)]
     chunk = cols // 2
     levels = [shape for index in range(LEVELS - 1) for shape in Level.scratch(index)]
     potentials, own, theirs = pl.pallas_call(
-        functools.partial(replicated_kernel, len(parts)),
+        functools.partial(replicated_kernel, len(parts), len(halved)),
         out_shape=(
             jax.ShapeDtypeStruct((rows, cols, LANES), f32),
             jax.ShapeDtypeStruct((rows, chunk, LANES), f32),
             jax.ShapeDtypeStruct((rows, chunk, LANES), f32),
         ),
-        in_specs=[smem, smem] + [vmem] * (len(parts) + 4),
+        in_specs=[smem, smem] + [vmem] * (len(parts) + len(halved) + 4),
         out_specs=(vmem, vmem, vmem),
         scratch_shapes=[
             pltpu.VMEM((electrodes, LANES), f32),
@@ -578,7 +605,7 @@
         + levels,
         compiler_params=pltpu.CompilerParams(vmem_limit_bytes=VMEM_BYTES),
         cost_estimate=pl.CostEstimate(flops=200_000_000, bytes_accessed=4_000_000, transcendentals=0),
-    )(place, cells, *parts, station_row, currents, receivers, observed)
+    )(place, cells, *parts, *halved, station_row, currents, receivers, observed)
     return potentials[None], own + lax.ppermute(theirs, "shot", swap)
 
 

time: 66.5 us -> 62.5 us (0.940)
  waiting for transfers between devices: 27 us -> 19.2 us
  starting transfers between devices: 7.68 us -> 10.9 us
    ppermute x7 -> x11, waiting for transfers between devices: 23 us -> 15.1 us  [the longest x3 10.1 us: partner(): return lax.ppermute(part, 'gx', [(i, i ^ k) for i in range(count)])]
    ppermute x7 -> x11, starting transfers between devices: 6.19 us -> 9.44 us  [the longest x3 5.61 us: partner(): return lax.ppermute(part, 'gx', [(i, i ^ k) for i in range(count)])]
  transfers between devices with their start and end apart: 8 -> 12, of which waited for: 5 -> 5; matrix products, arithmetic and copies ran while one was open for 0% -> 0% of each run, Pallas kernels for 0% -> 0%
where the time goes in v5:
time: 62.5 us; the launch traced here: 62.3 us
  Pallas kernels  30 us (48%)
  waiting for transfers between devices  19.2 us (31%)
  starting transfers between devices  10.9 us (17%)
  other arithmetic  1.27 us (2%)
  between operations  0.75 us (1%)
    pallas_call x1, Pallas kernels, replicated(): pl.pallas_call(functools.partial(replicated_kernel, len(parts), len(halve...  27.7 us
    ppermute x3, waiting for transfers between devices, partner(): return lax.ppermute(part, 'gx', [(i, i ^ k) for i in range(count)])  10.1 us
    ppermute x3, starting transfers between devices, partner(): return lax.ppermute(part, 'gx', [(i, i ^ k) for i in range(count)])  5.61 us
    ppermute x1, waiting for transfers between devices, replicated(): return (potentials[None], own + lax.ppermute(theirs, 'shot', swap))  4.05 us
    ppermute x2, waiting for transfers between devices, replicated(): lax.ppermute(own, 'shot', swap)  3.94 us
    ppermute x2, starting transfers between devices, replicated(): lax.ppermute(own, 'shot', swap)  2.8 us
    pallas_call x1, Pallas kernels, replicated(): pl.pallas_call(to_blocks_kernel, out_shape=(jax.ShapeDtypeStruct((total,...  2.29 us
    ppermute x1, starting transfers between devices, replicated(): return (potentials[None], own + lax.ppermute(theirs, 'shot', swap))  1.49 us
  transfers between devices with their start and end apart: 12, of which 5 were waited for; matrix products, arithmetic and copies ran while one was open for 0% of the time, Pallas kernels for 0%

profile of v5, /device:TPU:0, one launch (start us, length us, event | category | flops | bytes accessed | tf_op | source)
XLA Modules:
  0.0 62.3 jit_solution(17587927544212480553)
XLA Ops:
  0.6 0.6 pad_add_fusion.place_ref.device_ref
  1.2 2.3 %shard_map.68 = (f32[512,128]{1,0:T(8,128)}, f32[256,128]{1,0:T(8,128)}, s32[1,256]{1,0:T(1,128)}) custom-call(s32[2]{0:T(128)} %pad_add_fusion.place_ref.device_ref, f32[8,64,128]{2,1,0:T(8,128)} %natural_ref.1, s32[1,256]{1,0:T(1,128)} %bitcast.4), custom_call_target="tpu_custom_call" | custom-call | tf_op jit(solution)/shard_map/pallas_call | solution.py:566
  3.5 3.0 %collective-permute-start.1 = (f32[512,128]{1,0:T(8,128)}, f32[512,128]{1,0:T(8,128)S(1)}, u32[]{:S(2)}, u32[]{:S(2)}) collective-permute-start(f32[512,128]{1,0:T(8,128)} %get-tuple-element.9.refs_0_), channel_id=1, source_target_pairs={{0,4},{4,0},{8,12},{12,8},{1,5},{5,1},{9,13},{13,9},{2,6},{6,2},{1... | collective-permute-start | bytes 786440 | tf_op jit(solution)/shard_map/ppermute | solution.py:580
  6.6 2.5 %collective-permute-start.7 = (f32[256,128]{1,0:T(8,128)}, f32[256,128]{1,0:T(8,128)S(1)}, u32[]{:S(2)}, u32[]{:S(2)}) collective-permute-start(f32[256,128]{1,0:T(8,128)} %get-tuple-element.10), channel_id=1, source_target_pairs={{0,12},{4,8},{8,4},{12,0},{1,13},{5,9},{9,5},{13,1},{2,14},{6,10},... | collective-permute-start | bytes 393224 | tf_op jit(solution)/shard_map/ppermute | solution.py:580
  9.0 0.1 collective-permute-start.3
  9.1 10.1 %collective-permute-done.7.refs_8_ = f32[256,128]{1,0:T(8,128)S(1)} collective-permute-done((f32[256,128]{1,0:T(8,128)}, f32[256,128]{1,0:T(8,128)S(1)}, u32[]{:S(2)}, u32[]{:S(2)}) %collective-permute-start.7) | collective-permute-done | bytes 131104 | tf_op jit(solution)/shard_map/ppermute | solution.py:580
  19.2 1.5 %collective-permute-start.9 = (f32[256,128]{1,0:T(8,128)S(1)}, f32[256,128]{1,0:T(8,128)S(1)}, u32[]{:S(2)}, u32[]{:S(2)}) collective-permute-start(f32[256,128]{1,0:T(8,128)S(1)} %collective-permute-done.7.refs_8_), channel_id=1, source_target_pairs={{0,1},{1,0},{2,3},{3,2},{4,5},{5,4},{6,7},{7,6},{8,9},{9,8},{10,11... | collective-permute-start | bytes 393224 | tf_op jit(solution)/shard_map/ppermute | solution.py:587
  20.7 0.0 collective-permute-start
  20.7 0.5 collective-permute-start.8
  21.2 0.0 collective-permute-done.3.refs_4_
  21.2 1.3 %collective-permute-start.5 = (f32[256,128]{1,0:T(8,128)S(1)}, f32[256,128]{1,0:T(8,128)S(1)}, u32[]{:S(2)}, u32[]{:S(2)}) collective-permute-start(f32[256,128]{1,0:T(8,128)S(1)} %collective-permute-done.3.refs_4_), channel_id=1, source_target_pairs={{0,1},{1,0},{2,3},{3,2},{4,5},{5,4},{6,7},{7,6},{8,9},{9,8},{10,11... | collective-permute-start | bytes 393224 | tf_op jit(solution)/shard_map/ppermute | solution.py:587
  22.5 0.0 collective-permute-done.1.refs_2_
  22.5 0.0 collective-permute-start.2
  22.5 2.0 %collective-permute-done.9.refs_10_ = f32[256,128]{1,0:T(8,128)S(1)} collective-permute-done((f32[256,128]{1,0:T(8,128)S(1)}, f32[256,128]{1,0:T(8,128)S(1)}, u32[]{:S(2)}, u32[]{:S(2)}) %collective-permute-start.9) | collective-permute-done | bytes 131104 | tf_op jit(solution)/shard_map/ppermute | solution.py:587
  24.5 0.0 collective-permute-start.4
  24.5 0.0 collective-permute-done.8.refs_9_
  24.5 0.5 collective-permute-start.10
  25.1 1.9 %collective-permute-done.5.refs_6_ = f32[256,128]{1,0:T(8,128)S(1)} collective-permute-done((f32[256,128]{1,0:T(8,128)S(1)}, f32[256,128]{1,0:T(8,128)S(1)}, u32[]{:S(2)}, u32[]{:S(2)}) %collective-permute-start.5) | collective-permute-done | bytes 131104 | tf_op jit(solution)/shard_map/ppermute | solution.py:587
  27.0 0.0 collective-permute-start.6
  27.0 0.0 copy-start.4
  27.0 0.0 copy-start.5
  27.0 0.1 copy.7.refs_14_
  27.2 0.0 copy-start.1
  27.2 0.0 collective-permute-done.4.refs_5_
  27.2 0.0 collective-permute-done.refs_1_
  27.2 0.0 collective-permute-done.10.refs_11_
  27.2 1.1 %collective-permute-done.6.refs_7_ = f32[256,128]{1,0:T(8,128)S(1)} collective-permute-done((f32[256,128]{1,0:T(8,128)S(1)}, f32[256,128]{1,0:T(8,128)S(1)}, u32[]{:S(2)}, u32[]{:S(2)}) %collective-permute-start.6) | collective-permute-done | bytes 131104 | tf_op jit(solution)/shard_map/ppermute | solution.py:583
  28.3 0.0 collective-permute-done.2.refs_3_
  28.4 27.7 %shard_map.69 = (f32[8,64,128]{2,1,0:T(8,128)}, f32[8,32,128]{2,1,0:T(8,128)S(1)}, f32[8,32,128]{2,1,0:T(8,128)S(1)}) custom-call(s32[2]{0:T(128)S(1)} %copy-done.3, s32[1,256]{1,0:T(1,128)S(1)} %copy-done.5, f32[512,128]{1,0:T(8,128)S(1)} %copy-done, f32[512,128]{1,0:T(8,128)S(1)} %collective-permute-done.refs_1_, ...), custom_call_target="tpu_custom_call" | custom-call | flops 200000000 | bytes 4000000 | tf_op jit(solution)/shard_map/pallas_call | solution.py:592
  56.1 1.5 %collective-permute-start.11 = (f32[8,32,128]{2,1,0:T(8,128)S(1)}, f32[8,32,128]{2,1,0:T(8,128)S(1)}, u32[]{:S(2)}, u32[]{:S(2)}) collective-permute-start(f32[8,32,128]{2,1,0:T(8,128)S(1)} %get-tuple-element.13), channel_id=1, source_target_pairs={{0,1},{1,0},{2,3},{3,2},{4,5},{5,4},{6,7},{7,6},{8,9},{9,8},{10,11... | collective-permute-start | bytes 393224 | tf_op jit(solution)/shard_map/ppermute | solution.py:609
  57.6 4.1 %collective-permute-done.11 = f32[8,32,128]{2,1,0:T(8,128)S(1)} collective-permute-done((f32[8,32,128]{2,1,0:T(8,128)S(1)}, f32[8,32,128]{2,1,0:T(8,128)S(1)}, u32[]{:S(2)}, u32[]{:S(2)}) %collective-permute-start.11) | collective-permute-done | bytes 131104 | tf_op jit(solution)/shard_map/ppermute | solution.py:609
  61.7 0.7 %add.7 = f32[8,32,128]{2,1,0:T(8,128)} add(f32[8,32,128]{2,1,0:T(8,128)S(1)} %get-tuple-element.12, f32[8,32,128]{2,1,0:T(8,128)S(1)} %collective-permute-done.11) | non-fusion elementwise | flops 32768 | bytes 393216 | tf_op jit(solution)/shard_map/add | solution.py:609
  (11 shorter events, 0.0 us)
Async XLA Ops:
  1.2 25.8 %copy-start.6 = (s32[512,2]{0,1:T(2,128)S(1)}, s32[512,2]{0,1:T(2,128)}, u32[]{:S(2)}) copy-start(s32[512,2]{0,1:T(2,128)} %param.8) | copy-start | bytes 12292
  3.5 24.8 %copy-start = (f32[512,128]{1,0:T(8,128)S(1)}, f32[512,128]{1,0:T(8,128)}, u32[]{:S(2)}) copy-start(f32[512,128]{1,0:T(8,128)} %get-tuple-element.9.refs_0_) | copy-start | bytes 786436
  3.5 19.0 %collective-permute-start.1 = (f32[512,128]{1,0:T(8,128)}, f32[512,128]{1,0:T(8,128)S(1)}, u32[]{:S(2)}, u32[]{:S(2)}) collective-permute-start(f32[512,128]{1,0:T(8,128)} %get-tuple-element.9.refs_0_), channel_id=1, source_target_pairs={{0,4},{4,0},{8,12},{12,8},{1,5},{5,1},{9,13},{13,9},{2,6},{6,2},{1... | collective-permute-start | bytes 786440 | tf_op jit(solution)/shard_map/ppermute | solution.py:580
  6.6 12.7 %collective-permute-start.7 = (f32[256,128]{1,0:T(8,128)}, f32[256,128]{1,0:T(8,128)S(1)}, u32[]{:S(2)}, u32[]{:S(2)}) collective-permute-start(f32[256,128]{1,0:T(8,128)} %get-tuple-element.10), channel_id=1, source_target_pairs={{0,12},{4,8},{8,4},{12,0},{1,13},{5,9},{9,5},{13,1},{2,14},{6,10},... | collective-permute-start | bytes 393224 | tf_op jit(solution)/shard_map/ppermute | solution.py:580
  9.0 12.2 %collective-permute-start.3 = (f32[256,128]{1,0:T(8,128)}, f32[256,128]{1,0:T(8,128)S(1)}, u32[]{:S(2)}, u32[]{:S(2)}) collective-permute-start(f32[256,128]{1,0:T(8,128)} %get-tuple-element.10), channel_id=1, source_target_pairs={{0,8},{4,12},{8,0},{12,4},{1,9},{5,13},{9,1},{13,5},{2,10},{6,14},... | collective-permute-start | bytes 393224 | tf_op jit(solution)/shard_map/ppermute | solution.py:580
  19.2 5.3 %collective-permute-start.9 = (f32[256,128]{1,0:T(8,128)S(1)}, f32[256,128]{1,0:T(8,128)S(1)}, u32[]{:S(2)}, u32[]{:S(2)}) collective-permute-start(f32[256,128]{1,0:T(8,128)S(1)} %collective-permute-done.7.refs_8_), channel_id=1, source_target_pairs={{0,1},{1,0},{2,3},{3,2},{4,5},{5,4},{6,7},{7,6},{8,9},{9,8},{10,11... | collective-permute-start | bytes 393224 | tf_op jit(solution)/shard_map/ppermute | solution.py:587
  20.7 6.5 %collective-permute-start = (f32[512,128]{1,0:T(8,128)}, f32[512,128]{1,0:T(8,128)S(1)}, u32[]{:S(2)}, u32[]{:S(2)}) collective-permute-start(f32[512,128]{1,0:T(8,128)} %get-tuple-element.9.refs_0_), channel_id=1, source_target_pairs={{0,2},{2,0},{1,3},{3,1},{4,6},{6,4},{5,7},{7,5},{8,10},{10,8},{9,1... | collective-permute-start | bytes 786440 | tf_op jit(solution)/shard_map/ppermute | solution.py:583
  20.7 3.8 %collective-permute-start.8 = (f32[256,128]{1,0:T(8,128)S(1)}, f32[256,128]{1,0:T(8,128)S(1)}, u32[]{:S(2)}, u32[]{:S(2)}) collective-permute-start(f32[256,128]{1,0:T(8,128)S(1)} %collective-permute-done.7.refs_8_), channel_id=1, source_target_pairs={{0,2},{2,0},{1,3},{3,1},{4,6},{6,4},{5,7},{7,5},{8,10},{10,8},{9,1... | collective-permute-start | bytes 393224 | tf_op jit(solution)/shard_map/ppermute | solution.py:583
  21.2 5.8 %collective-permute-start.5 = (f32[256,128]{1,0:T(8,128)S(1)}, f32[256,128]{1,0:T(8,128)S(1)}, u32[]{:S(2)}, u32[]{:S(2)}) collective-permute-start(f32[256,128]{1,0:T(8,128)S(1)} %collective-permute-done.3.refs_4_), channel_id=1, source_target_pairs={{0,1},{1,0},{2,3},{3,2},{4,5},{5,4},{6,7},{7,6},{8,9},{9,8},{10,11... | collective-permute-start | bytes 393224 | tf_op jit(solution)/shard_map/ppermute | solution.py:587
  22.5 5.8 %collective-permute-start.2 = (f32[512,128]{1,0:T(8,128)S(1)}, f32[512,128]{1,0:T(8,128)S(1)}, u32[]{:S(2)}, u32[]{:S(2)}) collective-permute-start(f32[512,128]{1,0:T(8,128)S(1)} %collective-permute-done.1.refs_2_), channel_id=1, source_target_pairs={{0,2},{2,0},{1,3},{3,1},{4,6},{6,4},{5,7},{7,5},{8,10},{10,8},{9,1... | collective-permute-start | bytes 786440 | tf_op jit(solution)/shard_map/ppermute | solution.py:583
  24.5 2.7 %collective-permute-start.4 = (f32[256,128]{1,0:T(8,128)S(1)}, f32[256,128]{1,0:T(8,128)S(1)}, u32[]{:S(2)}, u32[]{:S(2)}) collective-permute-start(f32[256,128]{1,0:T(8,128)S(1)} %collective-permute-done.3.refs_4_), channel_id=1, source_target_pairs={{0,2},{2,0},{1,3},{3,1},{4,6},{6,4},{5,7},{7,5},{8,10},{10,8},{9,1... | collective-permute-start | bytes 393224 | tf_op jit(solution)/shard_map/ppermute | solution.py:583
  24.5 2.7 %collective-permute-start.10 = (f32[256,128]{1,0:T(8,128)S(1)}, f32[256,128]{1,0:T(8,128)S(1)}, u32[]{:S(2)}, u32[]{:S(2)}) collective-permute-start(f32[256,128]{1,0:T(8,128)S(1)} %collective-permute-done.9.refs_10_), channel_id=1, source_target_pairs={{0,2},{2,0},{1,3},{3,1},{4,6},{6,4},{5,7},{7,5},{8,10},{10,8},{9,1... | collective-permute-start | bytes 393224 | tf_op jit(solution)/shard_map/ppermute | solution.py:583
  27.0 1.3 %collective-permute-start.6 = (f32[256,128]{1,0:T(8,128)S(1)}, f32[256,128]{1,0:T(8,128)S(1)}, u32[]{:S(2)}, u32[]{:S(2)}) collective-permute-start(f32[256,128]{1,0:T(8,128)S(1)} %collective-permute-done.5.refs_6_), channel_id=1, source_target_pairs={{0,2},{2,0},{1,3},{3,1},{4,6},{6,4},{5,7},{7,5},{8,10},{10,8},{9,1... | collective-permute-start | bytes 393224 | tf_op jit(solution)/shard_map/ppermute | solution.py:583
  27.0 1.4 %copy-start.2 = (f32[1,512]{1,0:T(1,128)S(1)}, f32[1,512]{1,0:T(1,128)}, u32[]{:S(2)}) copy-start(f32[1,512]{1,0:T(1,128)} %refs_15_.1) | copy-start | bytes 6148
  27.0 1.4 %copy-start.4 = (f32[1,256]{1,0:T(1,128)S(1)}, f32[1,256]{1,0:T(1,128)}, u32[]{:S(2)}) copy-start(f32[1,256]{1,0:T(1,128)} %refs_13_.1) | copy-start | bytes 3076
  27.0 1.3 %copy-start.5 = (s32[1,256]{1,0:T(1,128)S(1)}, s32[1,256]{1,0:T(1,128)}, u32[]{:S(2)}) copy-start(s32[1,256]{1,0:T(1,128)} %get-tuple-element.8.cells_ref) | copy-start | bytes 3076
  27.2 1.2 %copy-start.1 = (s32[256]{0:T(256)S(1)}, s32[256]{0:T(256)}, u32[]{:S(2)}) copy-start(s32[256]{0:T(256)} %param.6) | copy-start | bytes 3076
  27.2 1.2 %copy-start.3 = (s32[2]{0:T(128)S(1)}, s32[2]{0:T(128)}, u32[]{:S(2)}) copy-start(s32[2]{0:T(128)} %pad_add_fusion.place_ref.device_ref) | copy-start | bytes 28
  56.1 5.5 %collective-permute-start.11 = (f32[8,32,128]{2,1,0:T(8,128)S(1)}, f32[8,32,128]{2,1,0:T(8,128)S(1)}, u32[]{:S(2)}, u32[]{:S(2)}) collective-permute-start(f32[8,32,128]{2,1,0:T(8,128)S(1)} %get-tuple-element.13), channel_id=1, source_target_pairs={{0,1},{1,0},{2,3},{3,2},{4,5},{5,4},{6,7},{7,6},{8,9},{9,8},{10,11... | collective-permute-start | bytes 393224 | tf_op jit(solution)/shard_map/ppermute | solution.py:609

commit v6 on v5

--- a/solution.py
+++ b/solution.py
@@ -67,7 +67,11 @@
     return tiles
 
 
-def to_blocks_kernel(place_ref, natural_ref, stations_ref, blocks_ref, half_ref, cells_ref):
+def own_place():
+    return lax.axis_index("gx") * 2 + lax.axis_index("gy"), lax.axis_index("shot")
+
+
+def to_blocks_kernel(natural_ref, stations_ref, blocks_ref, half_ref, cells_ref):
     order = lane_order()
     for x in range(SIDE):
         tiles = product(natural_ref[x], order, 3)
@@ -76,7 +80,7 @@
             blocks_ref[pl.ds((x * SIDE + z) * SIDE, SIDE), :] = tile
     count = half_ref.shape[0]
     low, high = blocks_ref[pl.ds(0, count), :], blocks_ref[pl.ds(count, count), :]
-    half_ref[...] = jnp.where(place_ref[1] == 0, low, high)
+    half_ref[...] = jnp.where(own_place()[1] == 0, low, high)
     cell_x, cell_y, cell_z, row, _ = station_table(stations_ref[...])
     wide = SIDE + 2
     register = (((cell_x & 7) + 1) * wide + (cell_z & 7) + 1) * wide + (cell_y & 7) + 1
@@ -135,6 +139,29 @@
 
 def twice(row):
     return jnp.concatenate([row[i // 2 : i // 2 + 1] for i in range(2 * row.shape[0])])
+
+
+def electrode_kernel(stations_ref, currents_ref, receivers_ref, rows_ref, same_ref, pairs_ref):
+    stations = stations_ref[...]
+    electrodes = stations.shape[1]
+    row, spot = station_table(stations)[3:]
+    line = stations & 0x1C387 | row << 20
+    same = jnp.broadcast_to(line, (electrodes, electrodes))
+    same = jnp.where(same == same.T, 1.0, 0.0).astype(jnp.bfloat16)
+    same_ref[...] = same
+    rows_ref[...] = shared_rows(currents_ref[...], spot, same)
+    receivers = receivers_ref[...]
+    numbers = iota((receivers.shape[0], electrodes), 1)
+    pairs = jnp.where(numbers == receivers[:, 0:1], 1.0, 0.0) - jnp.where(
+        numbers == receivers[:, 1:2], 1.0, 0.0
+    )
+    pairs_ref[...] = pairs.astype(jnp.bfloat16)
+
+
+def shared_rows(amounts, spot, same):
+    electrodes = amounts.shape[1]
+    at_spot = iota((LANES, electrodes), 0) == spot
+    return product(jnp.where(at_spot, amounts, 0.0), same, 3).T
 
 
 class Edged:
@@ -351,22 +378,21 @@
 def replicated_kernel(
     whole,
     halved,
-    device_ref,
     cells_ref,
     *refs,
 ):
     parts = refs[:whole], refs[whole : whole + halved]
-    solve_kernel(*parts, device_ref, cells_ref, *refs[whole + halved :])
+    solve_kernel(*parts, cells_ref, *refs[whole + halved :])
 
 
 def solve_kernel(
     part_refs,
     half_refs,
-    device_ref,
     cells_ref,
     stations_ref,
-    currents_ref,
-    receivers_ref,
+    rows_ref,
+    same_ref,
+    pairs_ref,
     observed_ref,
     potentials_ref,
     mine_ref,
@@ -386,8 +412,7 @@
     forward = fine.cond
     wide = SIDE * SIDE * SIDE
 
-    device = device_ref[0]
-    shot = device_ref[1]
+    device, shot = own_place()
 
     def place(part, row, x, index):
         for z in range(SIDE):
@@ -427,31 +452,63 @@
         if below is not None:
             below.cond.close(exact=True)
 
+    keep = iota((1, SIDE, LANES), 1) % 2 == 0
+    lane = iota((1, SIDE, LANES), 2)
+
+    def split(value):
+        return [jnp.where(keep, part, 0.0) for part in (value, pltpu.roll(value, SIDE - 1, 1))]
+
+    def around(value):
+        low, high = value
+        low_up, high_up = [pltpu.roll(part, LANES - GROUP, 2) for part in value]
+        low_down, high_down = [pltpu.roll(part, GROUP, 2) for part in value]
+        along = [[move(part, axis) for part in value] for axis in (0, 2) for move in (block_up, block_down)]
+        return along + [
+            [jnp.where(lane < LANES - GROUP, low_up, high_up), high_up],
+            [low_down, jnp.where(lane >= GROUP, high_down, low_down)],
+        ]
+
+    sub = iota((1, SIDE, LANES), 1)
+    inside_last = [
+        [sub < 6] * 2,
+        [sub >= 2] * 2,
+        [lane % GROUP < GROUP - 1] * 2,
+        [lane % GROUP > 0] * 2,
+        [keep, lane < LANES - GROUP],
+        [lane >= GROUP, keep],
+    ]
     last_scale = 0.25 ** (LEVELS - 1)
-    here = coarsest[0]
-    others = [inside(move(here, axis), axis) for axis in range(3) for inside, move in ((inside_up, block_up), (inside_down, block_down))]
-    total = others[0]
-    for other in others[1:]:
-        total = total + other
-    total = 3.0 * here + 0.5 * total
-    inverse = DAMPING / total
-    last_weight = inverse * (1.0 / last_scale)
-    last_links = []
-    for axis in range(3):
-        for inside, other in ((inside_up, others[2 * axis]), (inside_down, others[2 * axis + 1])):
-            last_links.append(inside(0.5 * inverse * (here + other), axis))
+    here = split(coarsest[0])
+    others = [
+        [jnp.where(inside & keep, part, 0.0) for inside, part in zip(pair, moved)]
+        for pair, moved in zip(inside_last, around(here))
+    ]
+    last_weight, last_links = [], []
+    for half, part in enumerate(here):
+        total = 3.0 * part
+        for other in others:
+            total = total + 0.5 * other[half]
+        inverse = jnp.where(keep, DAMPING / jnp.where(keep, total, 1.0), 0.0)
+        last_weight.append(inverse * (1.0 / last_scale))
+        last_links.append(
+            [
+                jnp.where(pair[half] & keep, 0.5 * inverse * (part + other[half]), 0.0)
+                for pair, other in zip(inside_last, others)
+            ]
+        )
 
     def solve_last(rhs):
-        base = last_weight * rhs
+        base = [weight * part for weight, part in zip(last_weight, split(rhs))]
         value = base
         for _ in range(COARSE_SWEEPS - 1):
-            parts = []
-            for axis in range(3):
-                parts.append(last_links[2 * axis] * block_up(value, axis))
-                parts.append(last_links[2 * axis + 1] * block_down(value, axis))
-            start = base + (1.0 - DAMPING) * value
-            value = ((start + parts[0]) + (parts[1] + parts[4])) + (parts[5] + (parts[2] + parts[3]))
-        return value
+            moved = around(value)
+            fresh = []
+            for half in range(2):
+                parts = [link * other[half] for link, other in zip(last_links[half], moved)]
+                start = base[half] + (1.0 - DAMPING) * value[half]
+                fresh.append(((start + parts[0]) + (parts[1] + parts[2])) + (parts[3] + (parts[4] + parts[5])))
+            value = fresh
+        return value[0] + pltpu.roll(value[1], 1, 1)
 
     def cycle(index, out, exact=False):
         level = levels[index]
@@ -475,11 +532,7 @@
         cycle(index + 1, below.first)
         level.ascend(lambda x, z: below.first[x, z], out, exact)
 
-    _, cell_y, cell_z, row, spot = station_table(stations_ref[...])
-    at_spot = iota((LANES, electrodes), 0) == spot
-    line = stations_ref[...] & 0x1C387 | row << 20
-    same = jnp.broadcast_to(line, (electrodes, electrodes))
-    same = jnp.where(same == same.T, 1.0, 0.0).astype(jnp.bfloat16)
+    spot = station_table(stations_ref[...])[4]
 
     def each(body):
         def one(electrode, carry):
@@ -495,9 +548,8 @@
     weights[...] = 1.0 / weights[...]
     fine.base.ref[...] = jnp.zeros_like(fine.base.ref)
 
-    def spread(amounts):
-        shared = product(jnp.where(at_spot, amounts, 0.0), same, 3)
-        gathered[...] = shared.T * weights[...]
+    def spread(rows):
+        gathered[...] = rows * weights[...]
 
         def put(electrode, cell):
             fine.base.ref[cell, :] = gathered[electrode, :]
@@ -506,26 +558,22 @@
         planes_of(SIDE, fine.base.close_z)
         fine.base.close()
 
-    spread(currents_ref[...])
+    spread(rows_ref[...])
     cycle(0, forward, exact=True)
 
     def read(electrode, cell):
         gathered[electrode, :] = forward.ref[cell, :]
 
     each(read)
+    at_spot = iota((LANES, electrodes), 0) == spot
     readings = jnp.sum(jnp.where(at_spot, gathered[...].T, 0.0), axis=0, keepdims=True)
-    receivers = receivers_ref[...]
-    numbers = iota((receivers.shape[0], electrodes), 1)
-    pairs = jnp.where(numbers == receivers[:, 0:1], 1.0, 0.0) - jnp.where(
-        numbers == receivers[:, 1:2], 1.0, 0.0
-    )
-    pairs = pairs.astype(jnp.bfloat16)
+    pairs = pairs_ref[...]
 
     def exact(row, dims):
         return product(jnp.broadcast_to(row, (16, row.shape[1])), pairs, 3, dims)[0:1]
 
     misfit = exact(readings, ((1,), (1,))) - observed_ref[...]
-    spread(exact(misfit, ((1,), (0,))))
+    spread(shared_rows(exact(misfit, ((1,), (0,))), spot, same_ref[...]))
     cycle(0, fine.first, exact=True)
 
     order = lane_order()
@@ -561,8 +609,6 @@
     vmem = pl.BlockSpec(memory_space=pltpu.VMEM)
     smem = pl.BlockSpec(memory_space=pltpu.SMEM)
     station_row = stations.reshape(1, electrodes)
-    device = lax.axis_index("gx") * lax.axis_size("gy") + lax.axis_index("gy")
-    place = jnp.stack([device, lax.axis_index("shot")]).astype(jnp.int32)
     mine, half, cells = pl.pallas_call(
         to_blocks_kernel,
         out_shape=(
@@ -570,9 +616,9 @@
             jax.ShapeDtypeStruct((total // 2, LANES), f32),
             jax.ShapeDtypeStruct((1, electrodes), jnp.int32),
         ),
-        in_specs=[smem, vmem, vmem],
+        in_specs=[vmem, vmem],
         out_specs=(vmem, vmem, vmem),
-    )(place, conductivity, station_row)
+    )(conductivity, station_row)
     swap = [(0, 1), (1, 0)]
 
     def partner(part, k):
@@ -582,8 +628,21 @@
     def with_mate(part):
         return [part, lax.ppermute(part, "gy", swap)]
 
-    far = [partner(half, k) for k in (2, 3)]
+    far = partner(half, 2)
     near = partner(mine, 1)
+    rows_of, same, pairs = pl.pallas_call(
+        electrode_kernel,
+        out_shape=(
+            jax.ShapeDtypeStruct((electrodes, LANES), f32),
+            jax.ShapeDtypeStruct((electrodes, electrodes), jnp.bfloat16),
+            jax.ShapeDtypeStruct((receivers.shape[0], electrodes), jnp.bfloat16),
+        ),
+        in_specs=[vmem, vmem, vmem],
+        out_specs=(vmem, vmem, vmem),
+        cost_estimate=pl.CostEstimate(flops=100_000_000, bytes_accessed=1_000_000, transcendentals=0),
+    )(station_row, currents, receivers)
+    far, rows_of = lax.optimization_barrier((far, rows_of))
+    far = [far, partner(far, 1)]
     halved = [piece for own in far for piece in (own, lax.ppermute(own, "shot", swap))]
     parts = [piece for own in (mine, near) for piece in with_mate(own)]
     halved = [piece for own in halved for piece in with_mate(own)]
@@ -596,7 +655,7 @@
             jax.ShapeDtypeStruct((rows, chunk, LANES), f32),
             jax.ShapeDtypeStruct((rows, chunk, LANES), f32),
         ),
-        in_specs=[smem, smem] + [vmem] * (len(parts) + len(halved) + 4),
+        in_specs=[smem] + [vmem] * (len(parts) + len(halved) + 5),
         out_specs=(vmem, vmem, vmem),
         scratch_shapes=[
             pltpu.VMEM((electrodes, LANES), f32),
@@ -605,7 +664,7 @@
         + levels,
         compiler_params=pltpu.CompilerParams(vmem_limit_bytes=VMEM_BYTES),
         cost_estimate=pl.CostEstimate(flops=200_000_000, bytes_accessed=4_000_000, transcendentals=0),
-    )(place, cells, *parts, *halved, station_row, currents, receivers, observed)
+    )(cells, *parts, *halved, station_row, rows_of, same, pairs, observed)
     return potentials[None], own + lax.ppermute(theirs, "shot", swap)
 
 

time: 62.5 us -> 62.8 us (level)
  waiting for transfers between devices: 19.2 us -> 13.2 us
  local copies, waits for them, and re-layouts: 0.18 us -> 4.32 us
  Pallas kernels: 30 us -> 31.6 us
  starting transfers between devices: 10.9 us -> 12.1 us
    ppermute x3, waiting for transfers between devices: 10.1 us -> 5.07 us  [partner(): return lax.ppermute(part, 'gx', [(i, i ^ k) for i in range(count)])]
    unnamed x15 -> x17, local copies, waits for them, and re-layouts: 0.18 us -> 4.32 us
    pallas_call x0 -> x1, Pallas kernels: none -> 2.14 us  [replicated(): pl.pallas_call(electrode_kernel, out_shape=(jax.ShapeDtypeStruct((electro...]
    ppermute x2, waiting for transfers between devices: 3.94 us -> 2.83 us  [replicated(): lax.ppermute(own, 'shot', swap)]
    ppermute x3, starting transfers between devices: 5.61 us -> 6.38 us  [partner(): return lax.ppermute(part, 'gx', [(i, i ^ k) for i in range(count)])]
  transfers between devices with their start and end apart: 12 -> 12, of which waited for: 5 -> 5; matrix products, arithmetic and copies ran while one was open for 0% -> 1% of each run, Pallas kernels for 0% -> 3%
where the time goes in v6:
time: 62.8 us; the launch traced here: 62.6 us
  Pallas kernels  31.6 us (50%)
  waiting for transfers between devices  13.2 us (21%)
  starting transfers between devices  12.1 us (19%)
  local copies, waits for them, and re-layouts  4.32 us (7%)
  between operations  0.68 us (1%)
  other arithmetic  0.67 us (1%)
    pallas_call x1, Pallas kernels, replicated(): pl.pallas_call(functools.partial(replicated_kernel, len(parts), len(halve...  27.2 us
    ppermute x3, starting transfers between devices, partner(): return lax.ppermute(part, 'gx', [(i, i ^ k) for i in range(count)])  6.38 us
    ppermute x3, waiting for transfers between devices, partner(): return lax.ppermute(part, 'gx', [(i, i ^ k) for i in range(count)])  5.07 us
    unnamed x17, local copies, waits for them, and re-layouts  4.32 us
    ppermute x1, waiting for transfers between devices, replicated(): return (potentials[None], own + lax.ppermute(theirs, 'shot', swap))  4 us
    ppermute x2, starting transfers between devices, replicated(): lax.ppermute(own, 'shot', swap)  3.03 us
    ppermute x2, waiting for transfers between devices, replicated(): lax.ppermute(own, 'shot', swap)  2.83 us
    pallas_call x1, Pallas kernels, replicated(): pl.pallas_call(to_blocks_kernel, out_shape=(jax.ShapeDtypeStruct((total,...  2.27 us
  transfers between devices with their start and end apart: 12, of which 5 were waited for; matrix products, arithmetic and copies ran while one was open for 1% of the time, Pallas kernels for 3%

profile of v6, /device:TPU:0, one launch (start us, length us, event | category | flops | bytes accessed | tf_op | source)
XLA Modules:
  0.0 62.6 jit_solution(17836618249354456982)
XLA Ops:
  0.6 2.3 %shard_map.68 = (f32[512,128]{1,0:T(8,128)}, f32[256,128]{1,0:T(8,128)}, s32[1,256]{1,0:T(1,128)}) custom-call(f32[8,64,128]{2,1,0:T(8,128)} %natural_ref.1, s32[1,256]{1,0:T(1,128)} %bitcast.2), custom_call_target="tpu_custom_call" | custom-call | tf_op jit(solution)/shard_map/pallas_call | solution.py:612
  2.9 4.0 %collective-permute-start.3 = (f32[256,128]{1,0:T(8,128)}, f32[256,128]{1,0:T(8,128)S(1)}, u32[]{:S(2)}, u32[]{:S(2)}) collective-permute-start(f32[256,128]{1,0:T(8,128)} %get-tuple-element.15), channel_id=1, source_target_pairs={{0,8},{4,12},{8,0},{12,4},{1,9},{5,13},{9,1},{13,5},{2,10},{6,14},... | collective-permute-start | bytes 393224 | tf_op jit(solution)/shard_map/ppermute | solution.py:626
  7.0 1.6 %collective-permute-start.1 = (f32[512,128]{1,0:T(8,128)}, f32[512,128]{1,0:T(8,128)S(1)}, u32[]{:S(2)}, u32[]{:S(2)}) collective-permute-start(f32[512,128]{1,0:T(8,128)} %get-tuple-element.14.refs_0_), channel_id=1, source_target_pairs={{0,4},{4,0},{8,12},{12,8},{1,5},{5,1},{9,13},{13,9},{2,6},{6,2},{1... | collective-permute-start | bytes 786440 | tf_op jit(solution)/shard_map/ppermute | solution.py:626
  8.5 0.9 %copy.7.receivers_ref = s32[512,2]{1,0:T(8,128)} copy(s32[512,2]{0,1:T(2,128)S(1)} %copy-done.7) | data formatting | bytes 8192 | tf_op args[3]
  9.4 2.1 %shard_map.69 = (f32[256,128]{1,0:T(8,128)}, bf16[256,256]{1,0:T(8,128)(2,1)}, bf16[512,256]{1,0:T(8,128)(2,1)}) custom-call(s32[1,256]{1,0:T(1,128)} %bitcast.3, f32[1,256]{1,0:T(1,128)} %currents_ref.1, s32[512,2]{1,0:T(8,128)} %copy.7.receivers_ref), custom_call_target="tpu_custom_call" | custom-call | flops 100000000 | bytes 1000000 | tf_op jit(solution)/shard_map/pallas_call | solution.py:633
  11.5 2.0 %collective-permute-done.3.refs_4_ = f32[256,128]{1,0:T(8,128)S(1)} collective-permute-done((f32[256,128]{1,0:T(8,128)}, f32[256,128]{1,0:T(8,128)S(1)}, u32[]{:S(2)}, u32[]{:S(2)}) %collective-permute-start.3) | collective-permute-done | bytes 131104 | tf_op jit(solution)/shard_map/ppermute | solution.py:626
  13.6 0.8 %collective-permute-start.7 = (f32[256,128]{1,0:T(8,128)S(1)}, f32[256,128]{1,0:T(8,128)S(1)}, u32[]{:S(2)}, u32[]{:S(2)}) collective-permute-start(f32[256,128]{1,0:T(8,128)S(1)} %collective-permute-done.3.refs_4_), channel_id=1, source_target_pairs={{0,4},{4,0},{8,12},{12,8},{1,5},{5,1},{9,13},{13,9},{2,6},{6,2},{1... | collective-permute-start | bytes 393224 | tf_op jit(solution)/shard_map/ppermute | solution.py:626
  14.3 1.5 %collective-permute-start.5 = (f32[256,128]{1,0:T(8,128)S(1)}, f32[256,128]{1,0:T(8,128)S(1)}, u32[]{:S(2)}, u32[]{:S(2)}) collective-permute-start(f32[256,128]{1,0:T(8,128)S(1)} %collective-permute-done.3.refs_4_), channel_id=1, source_target_pairs={{0,1},{1,0},{2,3},{3,2},{4,5},{5,4},{6,7},{7,6},{8,9},{9,8},{10,11... | collective-permute-start | bytes 393224 | tf_op jit(solution)/shard_map/ppermute | solution.py:646
  15.8 0.0 collective-permute-start
  15.8 0.5 collective-permute-start.4
  16.3 3.0 %collective-permute-done.7.refs_8_ = f32[256,128]{1,0:T(8,128)S(1)} collective-permute-done((f32[256,128]{1,0:T(8,128)S(1)}, f32[256,128]{1,0:T(8,128)S(1)}, u32[]{:S(2)}, u32[]{:S(2)}) %collective-permute-start.7) | collective-permute-done | bytes 131104 | tf_op jit(solution)/shard_map/ppermute | solution.py:626
  19.4 1.5 %collective-permute-start.9 = (f32[256,128]{1,0:T(8,128)S(1)}, f32[256,128]{1,0:T(8,128)S(1)}, u32[]{:S(2)}, u32[]{:S(2)}) collective-permute-start(f32[256,128]{1,0:T(8,128)S(1)} %collective-permute-done.7.refs_8_), channel_id=1, source_target_pairs={{0,1},{1,0},{2,3},{3,2},{4,5},{5,4},{6,7},{7,6},{8,9},{9,8},{10,11... | collective-permute-start | bytes 393224 | tf_op jit(solution)/shard_map/ppermute | solution.py:646
  20.9 0.0 collective-permute-done.1.refs_2_
  20.9 0.0 collective-permute-start.2
  20.9 0.0 collective-permute-done.5.refs_6_
  20.9 0.5 collective-permute-start.8
  21.4 0.0 collective-permute-done.4.refs_5_
  21.4 0.1 collective-permute-start.6
  21.5 2.8 %collective-permute-done.9.refs_10_ = f32[256,128]{1,0:T(8,128)S(1)} collective-permute-done((f32[256,128]{1,0:T(8,128)S(1)}, f32[256,128]{1,0:T(8,128)S(1)}, u32[]{:S(2)}, u32[]{:S(2)}) %collective-permute-start.9) | collective-permute-done | bytes 131104 | tf_op jit(solution)/shard_map/ppermute | solution.py:646
  24.3 0.0 collective-permute-done.refs_1_
  24.4 0.0 collective-permute-done.8.refs_9_
  24.4 0.0 collective-permute-done.6.refs_7_
  24.4 1.3 %collective-permute-done.10.refs_11_ = f32[256,128]{1,0:T(8,128)S(1)} collective-permute-done((f32[256,128]{1,0:T(8,128)S(1)}, f32[256,128]{1,0:T(8,128)S(1)}, u32[]{:S(2)}, u32[]{:S(2)}) %collective-permute-start.10) | collective-permute-done | bytes 131104 | tf_op jit(solution)/shard_map/ppermute | solution.py:629
  25.7 0.7 %copy-done.5 = f32[1,512]{1,0:T(1,128)S(1)} copy-done((f32[1,512]{1,0:T(1,128)S(1)}, f32[1,512]{1,0:T(1,128)}, u32[]{:S(2)}) %copy-start.5) | copy-done | bytes 2072
  26.4 0.0 copy-done.4
  26.4 0.9 %copy-done.1 = bf16[512,256]{1,0:T(8,128)(2,1)S(1)} copy-done((bf16[512,256]{1,0:T(8,128)(2,1)S(1)}, bf16[512,256]{1,0:T(8,128)(2,1)}, u32[]{:S(2)}) %copy-start.1) | copy-done | bytes 262168
  27.3 0.9 %copy-done.2 = f32[256,128]{1,0:T(8,128)S(1)} copy-done((f32[256,128]{1,0:T(8,128)S(1)}, f32[256,128]{1,0:T(8,128)}, u32[]{:S(2)}) %copy-start.2) | copy-done | bytes 131096
  28.3 0.9 %copy-done.3 = bf16[256,256]{1,0:T(8,128)(2,1)S(1)} copy-done((bf16[256,256]{1,0:T(8,128)(2,1)S(1)}, bf16[256,256]{1,0:T(8,128)(2,1)}, u32[]{:S(2)}) %copy-start.3) | copy-done | bytes 131096
  29.2 27.2 %shard_map.70 = (f32[8,64,128]{2,1,0:T(8,128)}, f32[8,32,128]{2,1,0:T(8,128)S(1)}, f32[8,32,128]{2,1,0:T(8,128)S(1)}) custom-call(s32[1,256]{1,0:T(1,128)S(1)} %copy-done.6, f32[512,128]{1,0:T(8,128)S(1)} %copy-done, f32[512,128]{1,0:T(8,128)S(1)} %collective-permute-done.refs_1_, f32[512,128]{1,0:T(8,128)S(1)} %collective-permute-done.1.refs_2_, ...), custom_call_target="tpu_custom_call" | custom-call | flops 200000000 | bytes 4000000 | tf_op jit(solution)/shard_map/pallas_call | solution.py:651
  56.4 1.5 %collective-permute-start.11 = (f32[8,32,128]{2,1,0:T(8,128)S(1)}, f32[8,32,128]{2,1,0:T(8,128)S(1)}, u32[]{:S(2)}, u32[]{:S(2)}) collective-permute-start(f32[8,32,128]{2,1,0:T(8,128)S(1)} %get-tuple-element.23), channel_id=1, source_target_pairs={{0,1},{1,0},{2,3},{3,2},{4,5},{5,4},{6,7},{7,6},{8,9},{9,8},{10,11... | collective-permute-start | bytes 393224 | tf_op jit(solution)/shard_map/ppermute | solution.py:668
  57.9 4.0 %collective-permute-done.11 = f32[8,32,128]{2,1,0:T(8,128)S(1)} collective-permute-done((f32[8,32,128]{2,1,0:T(8,128)S(1)}, f32[8,32,128]{2,1,0:T(8,128)S(1)}, u32[]{:S(2)}, u32[]{:S(2)}) %collective-permute-start.11) | collective-permute-done | bytes 131104 | tf_op jit(solution)/shard_map/ppermute | solution.py:668
  61.9 0.7 %add.3 = f32[8,32,128]{2,1,0:T(8,128)} add(f32[8,32,128]{2,1,0:T(8,128)S(1)} %get-tuple-element.22, f32[8,32,128]{2,1,0:T(8,128)S(1)} %collective-permute-done.11) | non-fusion elementwise | flops 32768 | bytes 393216 | tf_op jit(solution)/shard_map/add | solution.py:668
  (13 shorter events, 0.0 us)
Async XLA Ops:
  0.6 7.9 %copy-start.7 = (s32[512,2]{0,1:T(2,128)S(1)}, s32[512,2]{0,1:T(2,128)}, u32[]{:S(2)}) copy-start(s32[512,2]{0,1:T(2,128)} %param.8) | copy-start | bytes 12292
  2.9 10.7 %collective-permute-start.3 = (f32[256,128]{1,0:T(8,128)}, f32[256,128]{1,0:T(8,128)S(1)}, u32[]{:S(2)}, u32[]{:S(2)}) collective-permute-start(f32[256,128]{1,0:T(8,128)} %get-tuple-element.15), channel_id=1, source_target_pairs={{0,8},{4,12},{8,0},{12,4},{1,9},{5,13},{9,1},{13,5},{2,10},{6,14},... | collective-permute-start | bytes 393224 | tf_op jit(solution)/shard_map/ppermute | solution.py:626
  6.9 8.9 %copy-start = (f32[512,128]{1,0:T(8,128)S(1)}, f32[512,128]{1,0:T(8,128)}, u32[]{:S(2)}) copy-start(f32[512,128]{1,0:T(8,128)} %get-tuple-element.14.refs_0_) | copy-start | bytes 786436
  7.0 14.0 %collective-permute-start.1 = (f32[512,128]{1,0:T(8,128)}, f32[512,128]{1,0:T(8,128)S(1)}, u32[]{:S(2)}, u32[]{:S(2)}) collective-permute-start(f32[512,128]{1,0:T(8,128)} %get-tuple-element.14.refs_0_), channel_id=1, source_target_pairs={{0,4},{4,0},{8,12},{12,8},{1,5},{5,1},{9,13},{13,9},{2,6},{6,2},{1... | collective-permute-start | bytes 786440 | tf_op jit(solution)/shard_map/ppermute | solution.py:626
  9.4 16.3 %copy-start.6 = (s32[1,256]{1,0:T(1,128)S(1)}, s32[1,256]{1,0:T(1,128)}, u32[]{:S(2)}) copy-start(s32[1,256]{1,0:T(1,128)} %get-tuple-element.13.cells_ref) | copy-start | bytes 3076
  13.6 5.8 %collective-permute-start.7 = (f32[256,128]{1,0:T(8,128)S(1)}, f32[256,128]{1,0:T(8,128)S(1)}, u32[]{:S(2)}, u32[]{:S(2)}) collective-permute-start(f32[256,128]{1,0:T(8,128)S(1)} %collective-permute-done.3.refs_4_), channel_id=1, source_target_pairs={{0,4},{4,0},{8,12},{12,8},{1,5},{5,1},{9,13},{13,9},{2,6},{6,2},{1... | collective-permute-start | bytes 393224 | tf_op jit(solution)/shard_map/ppermute | solution.py:626
  14.3 6.6 %collective-permute-start.5 = (f32[256,128]{1,0:T(8,128)S(1)}, f32[256,128]{1,0:T(8,128)S(1)}, u32[]{:S(2)}, u32[]{:S(2)}) collective-permute-start(f32[256,128]{1,0:T(8,128)S(1)} %collective-permute-done.3.refs_4_), channel_id=1, source_target_pairs={{0,1},{1,0},{2,3},{3,2},{4,5},{5,4},{6,7},{7,6},{8,9},{9,8},{10,11... | collective-permute-start | bytes 393224 | tf_op jit(solution)/shard_map/ppermute | solution.py:646
  15.8 8.5 %collective-permute-start = (f32[512,128]{1,0:T(8,128)S(1)}, f32[512,128]{1,0:T(8,128)S(1)}, u32[]{:S(2)}, u32[]{:S(2)}) collective-permute-start(f32[512,128]{1,0:T(8,128)S(1)} %copy-done), channel_id=1, source_target_pairs={{0,2},{2,0},{1,3},{3,1},{4,6},{6,4},{5,7},{7,5},{8,10},{10,8},{9,1... | collective-permute-start | bytes 786440 | tf_op jit(solution)/shard_map/ppermute | solution.py:629
  15.8 5.6 %collective-permute-start.4 = (f32[256,128]{1,0:T(8,128)S(1)}, f32[256,128]{1,0:T(8,128)S(1)}, u32[]{:S(2)}, u32[]{:S(2)}) collective-permute-start(f32[256,128]{1,0:T(8,128)S(1)} %collective-permute-done.3.refs_4_), channel_id=1, source_target_pairs={{0,2},{2,0},{1,3},{3,1},{4,6},{6,4},{5,7},{7,5},{8,10},{10,8},{9,1... | collective-permute-start | bytes 393224 | tf_op jit(solution)/shard_map/ppermute | solution.py:629
  19.4 5.0 %collective-permute-start.9 = (f32[256,128]{1,0:T(8,128)S(1)}, f32[256,128]{1,0:T(8,128)S(1)}, u32[]{:S(2)}, u32[]{:S(2)}) collective-permute-start(f32[256,128]{1,0:T(8,128)S(1)} %collective-permute-done.7.refs_8_), channel_id=1, source_target_pairs={{0,1},{1,0},{2,3},{3,2},{4,5},{5,4},{6,7},{7,6},{8,9},{9,8},{10,11... | collective-permute-start | bytes 393224 | tf_op jit(solution)/shard_map/ppermute | solution.py:646
  20.9 4.8 %collective-permute-start.2 = (f32[512,128]{1,0:T(8,128)S(1)}, f32[512,128]{1,0:T(8,128)S(1)}, u32[]{:S(2)}, u32[]{:S(2)}) collective-permute-start(f32[512,128]{1,0:T(8,128)S(1)} %collective-permute-done.1.refs_2_), channel_id=1, source_target_pairs={{0,2},{2,0},{1,3},{3,1},{4,6},{6,4},{5,7},{7,5},{8,10},{10,8},{9,1... | collective-permute-start | bytes 786440 | tf_op jit(solution)/shard_map/ppermute | solution.py:629
  20.9 3.4 %collective-permute-start.8 = (f32[256,128]{1,0:T(8,128)S(1)}, f32[256,128]{1,0:T(8,128)S(1)}, u32[]{:S(2)}, u32[]{:S(2)}) collective-permute-start(f32[256,128]{1,0:T(8,128)S(1)} %collective-permute-done.7.refs_8_), channel_id=1, source_target_pairs={{0,2},{2,0},{1,3},{3,1},{4,6},{6,4},{5,7},{7,5},{8,10},{10,8},{9,1... | collective-permute-start | bytes 393224 | tf_op jit(solution)/shard_map/ppermute | solution.py:629
  21.4 2.9 %collective-permute-start.6 = (f32[256,128]{1,0:T(8,128)S(1)}, f32[256,128]{1,0:T(8,128)S(1)}, u32[]{:S(2)}, u32[]{:S(2)}) collective-permute-start(f32[256,128]{1,0:T(8,128)S(1)} %collective-permute-done.5.refs_6_), channel_id=1, source_target_pairs={{0,2},{2,0},{1,3},{3,1},{4,6},{6,4},{5,7},{7,5},{8,10},{10,8},{9,1... | collective-permute-start | bytes 393224 | tf_op jit(solution)/shard_map/ppermute | solution.py:629
  24.3 1.3 %collective-permute-start.10 = (f32[256,128]{1,0:T(8,128)S(1)}, f32[256,128]{1,0:T(8,128)S(1)}, u32[]{:S(2)}, u32[]{:S(2)}) collective-permute-start(f32[256,128]{1,0:T(8,128)S(1)} %collective-permute-done.9.refs_10_), channel_id=1, source_target_pairs={{0,2},{2,0},{1,3},{3,1},{4,6},{6,4},{5,7},{7,5},{8,10},{10,8},{9,1... | collective-permute-start | bytes 393224 | tf_op jit(solution)/shard_map/ppermute | solution.py:629
  25.7 0.7 %copy-start.5 = (f32[1,512]{1,0:T(1,128)S(1)}, f32[1,512]{1,0:T(1,128)}, u32[]{:S(2)}) copy-start(f32[1,512]{1,0:T(1,128)} %refs_16_.1) | copy-start | bytes 6148
  25.7 0.7 %copy-start.4 = (s32[256]{0:T(256)S(1)}, s32[256]{0:T(256)}, u32[]{:S(2)}) copy-start(s32[256]{0:T(256)} %param.6) | copy-start | bytes 3076
  26.4 0.9 %copy-start.1 = (bf16[512,256]{1,0:T(8,128)(2,1)S(1)}, bf16[512,256]{1,0:T(8,128)(2,1)}, u32[]{:S(2)}) copy-start(bf16[512,256]{1,0:T(8,128)(2,1)} %get-tuple-element.20.refs_15_) | copy-start | bytes 786436
  27.3 0.9 %copy-start.2 = (f32[256,128]{1,0:T(8,128)S(1)}, f32[256,128]{1,0:T(8,128)}, u32[]{:S(2)}) copy-start(f32[256,128]{1,0:T(8,128)} %get-tuple-element.18.refs_13_) | copy-start | bytes 393220
  28.2 0.9 %copy-start.3 = (bf16[256,256]{1,0:T(8,128)(2,1)S(1)}, bf16[256,256]{1,0:T(8,128)(2,1)}, u32[]{:S(2)}) copy-start(bf16[256,256]{1,0:T(8,128)(2,1)} %get-tuple-element.19.refs_14_) | copy-start | bytes 393220
  56.4 5.5 %collective-permute-start.11 = (f32[8,32,128]{2,1,0:T(8,128)S(1)}, f32[8,32,128]{2,1,0:T(8,128)S(1)}, u32[]{:S(2)}, u32[]{:S(2)}) collective-permute-start(f32[8,32,128]{2,1,0:T(8,128)S(1)} %get-tuple-element.23), channel_id=1, source_target_pairs={{0,1},{1,0},{2,3},{3,2},{4,5},{5,4},{6,7},{7,6},{8,9},{9,8},{10,11... | collective-permute-start | bytes 393224 | tf_op jit(solution)/shard_map/ppermute | solution.py:668

commit v7 on v6

--- a/solution.py
+++ b/solution.py
@@ -17,6 +17,7 @@
 LANES = 128
 GROUP = 16
 VMEM_BYTES = 48 * 2**20
+SMALL_BYTES = 6 * 2**20
 
 
 def pieces_of(value, count):
@@ -235,7 +236,7 @@
         body(x)
         return carry
 
-    lax.fori_loop(0, count, one, 0)
+    lax.fori_loop(0, count, one, 0, unroll=2)
 
 
 class Level:
@@ -375,6 +376,45 @@
         self.sweep(self.second, out, exact)
 
 
+class HeldLevel(Level):
+    def sums(self, field, base):
+        result = {}
+        for (x, z), here in field.items():
+            others = [
+                field[1, z] if x == 0 else block_up(field[0, z], 0),
+                field[0, z] if x == 1 else block_down(field[1, z], 0),
+                jnp.concatenate([here[1:], block_up(here[:1], 1)]),
+                jnp.concatenate([block_down(here[-1:], 1), here[:-1]]),
+                field[x, 1] if z == 0 else block_up(field[x, 0], 2),
+                field[x, 0] if z == 1 else block_down(field[x, 1], 2),
+            ]
+            total = base[x, z]
+            for link, other in zip(self.links, others):
+                total = total + link[x, z] * other
+            result[x, z] = total
+        return result
+
+    def swept(self, field, base):
+        sums = self.sums(field, base)
+        return {at: (1.0 - DAMPING) * field[at] + sums[at] for at in field}
+
+    def cycle(self, base, solve, out):
+        field = self.swept(base, base)
+        sums = self.sums(field, base)
+        total = None
+        for at in field:
+            residual = (sums[at] - DAMPING * field[at]) * self.back[at]
+            total = residual if total is None else total + residual
+        solved = solve(0.125 * (total[:1] + total[1:]))
+        row = twice(solved)
+        copied = {at: row for at in field}
+        change = {at: sums[at] + (1.0 - DAMPING) * (field[at] + row) for at in field}
+        field = self.sums(copied, change)
+        for (x, z), value in self.swept(field, base).items():
+            out.put(x, z, value)
+        out.close()
+
+
 def replicated_kernel(
     whole,
     halved,
@@ -399,6 +439,7 @@
     theirs_ref,
     gathered,
     weights,
+    owned,
     *level_refs,
 ):
     f32 = jnp.float32
@@ -406,7 +447,8 @@
     levels, used = [], 0
     for index in range(LEVELS - 1):
         count = len(Level.scratch(index))
-        levels.append(Level(level_refs[used : used + count], index))
+        kind = HeldLevel if index == LEVELS - 2 else Level
+        levels.append(kind(level_refs[used : used + count], index))
         used += count
     fine = levels[0]
     forward = fine.cond
@@ -512,24 +554,19 @@
 
     def cycle(index, out, exact=False):
         level = levels[index]
-        if index == LEVELS - 2:
-            held = []
-            level.descend(lambda x, z, row: held.append(row))
-            solved = solve_last(held[0])
-
-            def correction(x, z):
-                if x != 0:
-                    return (block_up if x > 0 else block_down)(solved, 0)
-                if z != 0:
-                    return (block_up if z > 0 else block_down)(solved, 2)
-                return solved
-
-            level.ascend(correction, out, exact)
-            return
         below = levels[index + 1]
-        level.descend(lambda x, z, row: below.base.put(x, z, below.weight[x, z] * row))
-        below.base.close()
-        cycle(index + 1, below.first)
+        if index == LEVELS - 3:
+            base = {}
+
+            def take(x, z, row):
+                base[x, z] = below.weight[x, z] * row
+
+            level.descend(take)
+            below.cycle(base, solve_last, below.first)
+        else:
+            level.descend(lambda x, z, row: below.base.put(x, z, below.weight[x, z] * row))
+            below.base.close()
+            cycle(index + 1, below.first)
         level.ascend(lambda x, z: below.first[x, z], out, exact)
 
     spot = station_table(stations_ref[...])[4]
@@ -539,7 +576,7 @@
             body(pl.ds(electrode, 1), pl.ds(cells_ref[0, electrode], 1))
             return carry
 
-        lax.fori_loop(0, electrodes, one, 0, unroll=8)
+        lax.fori_loop(0, electrodes, one, 0, unroll=32)
 
     def weigh(electrode, cell):
         weights[electrode, :] = fine.back.ref[cell, :]
@@ -584,14 +621,24 @@
     def own(field, x, z, y=0):
         return field.ref[pl.ds(field.start(x, z, y) + device, SIDE, stride=SIDE), :]
 
+    wide = SIDE + 2
+    for index, field in enumerate((forward, adjoint)):
+        for x in range(-1, SIDE + 1):
+            for z in range(-1, SIDE + 1):
+                if 0 <= x < SIDE or 0 <= z < SIDE:
+                    owned[index, (x + 1) * wide + z + 1] = own(field, x, z)
+
     for x in range(SIDE):
         tiles_u, tiles_g = [], []
         for z in range(SIDE):
-            here_u, here_w = own(forward, x, z), own(adjoint, x, z)
+            at = (x + 1) * wide + z + 1
+            here_u, here_w = owned[0, at], owned[1, at]
             total = None
-            for at in ((x + 1, z), (x - 1, z), (x, z, 1), (x, z, -1), (x, z + 1), (x, z - 1)):
-                term = (here_u - own(forward, *at)) * (here_w - own(adjoint, *at))
+            for step in (wide, -wide, 1, -1):
+                term = (here_u - owned[0, at + step]) * (here_w - owned[1, at + step])
                 total = term if total is None else total + term
+            for y in (1, -1):
+                total = total + (here_u - own(forward, x, z, y)) * (here_w - own(adjoint, x, z, y))
             tiles_u.append(here_u)
             tiles_g.append(-0.5 * total)
         potentials_ref[x] = from_blocks(tiles_u, order)
@@ -618,6 +665,7 @@
         ),
         in_specs=[vmem, vmem],
         out_specs=(vmem, vmem, vmem),
+        compiler_params=pltpu.CompilerParams(vmem_limit_bytes=SMALL_BYTES),
     )(conductivity, station_row)
     swap = [(0, 1), (1, 0)]
 
@@ -639,6 +687,7 @@
         ),
         in_specs=[vmem, vmem, vmem],
         out_specs=(vmem, vmem, vmem),
+        compiler_params=pltpu.CompilerParams(vmem_limit_bytes=SMALL_BYTES),
         cost_estimate=pl.CostEstimate(flops=100_000_000, bytes_accessed=1_000_000, transcendentals=0),
     )(station_row, currents, receivers)
     far, rows_of = lax.optimization_barrier((far, rows_of))
@@ -660,6 +709,7 @@
         scratch_shapes=[
             pltpu.VMEM((electrodes, LANES), f32),
             pltpu.VMEM((electrodes, LANES), f32),
+            pltpu.VMEM((2, (SIDE + 2) ** 2, SIDE, LANES), f32),
         ]
         + levels,
         compiler_params=pltpu.CompilerParams(vmem_limit_bytes=VMEM_BYTES),

time: 62.8 us -> 57 us (0.908)
  Pallas kernels: 31.6 us -> 25.4 us
  waiting for transfers between devices: 13.2 us -> 15.6 us
  local copies, waits for them, and re-layouts: 4.32 us -> 2.46 us
    pallas_call x1, Pallas kernels: 27.2 us -> 24.4 us  [replicated(): pl.pallas_call(functools.partial(replicated_kernel, len(parts), len(halve...]
    ppermute x3, waiting for transfers between devices: 5.07 us -> 7.39 us  [partner(): return lax.ppermute(part, 'gx', [(i, i ^ k) for i in range(count)])]
    unnamed x17 -> x11, local copies, waits for them, and re-layouts: 4.32 us -> 2.46 us
    pallas_call x1, Pallas kernels: 2.14 us -> 0.43 us  [replicated(): pl.pallas_call(electrode_kernel, out_shape=(jax.ShapeDtypeStruct((electro...]
    pallas_call x1, Pallas kernels: 2.27 us -> 0.58 us  [replicated(): pl.pallas_call(to_blocks_kernel, out_shape=(jax.ShapeDtypeStruct((total,...]
  transfers between devices with their start and end apart: 12 -> 12, of which waited for: 5 -> 5; matrix products, arithmetic and copies ran while one was open for 1% -> 0% of each run, Pallas kernels for 3% -> 1%
where the time goes in v7:
time: 57 us; the launch traced here: 56.8 us
  Pallas kernels  25.4 us (45%)
  waiting for transfers between devices  15.6 us (27%)
  starting transfers between devices  12 us (21%)
  local copies, waits for them, and re-layouts  2.46 us (4%)
  between operations  0.69 us (1%)
  other arithmetic  0.67 us (1%)
    pallas_call x1, Pallas kernels, replicated(): pl.pallas_call(functools.partial(replicated_kernel, len(parts), len(halve...  24.4 us
    ppermute x3, waiting for transfers between devices, partner(): return lax.ppermute(part, 'gx', [(i, i ^ k) for i in range(count)])  7.39 us
    ppermute x3, starting transfers between devices, partner(): return lax.ppermute(part, 'gx', [(i, i ^ k) for i in range(count)])  6.34 us
    ppermute x1, waiting for transfers between devices, replicated(): return (potentials[None], own + lax.ppermute(theirs, 'shot', swap))  4.02 us
    ppermute x2, starting transfers between devices, replicated(): lax.ppermute(own, 'shot', swap)  3.03 us
    ppermute x2, waiting for transfers between devices, replicated(): lax.ppermute(own, 'shot', swap)  2.84 us
    unnamed x11, local copies, waits for them, and re-layouts  2.46 us
    ppermute x1, starting transfers between devices, replicated(): return (potentials[None], own + lax.ppermute(theirs, 'shot', swap))  1.53 us
  transfers between devices with their start and end apart: 12, of which 5 were waited for; matrix products, arithmetic and copies ran while one was open for 0% of the time, Pallas kernels for 1%

profile of v7, /device:TPU:0, one launch (start us, length us, event | category | flops | bytes accessed | tf_op | source)
XLA Modules:
  0.0 56.8 jit_solution(5401341706019175220)
XLA Ops:
  0.6 0.7 %copy-done.1 = s32[256]{0:T(256)S(1)} copy-done((s32[256]{0:T(256)S(1)}, s32[256]{0:T(256)}, u32[]{:S(2)}) %copy-start.1) | copy-done | bytes 1048
  1.3 0.9 %copy-done = f32[8,64,128]{2,1,0:T(8,128)S(1)} copy-done((f32[8,64,128]{2,1,0:T(8,128)S(1)}, f32[8,64,128]{2,1,0:T(8,128)}, u32[]{:S(2)}) %copy-start) | copy-done | bytes 262168
  2.3 0.6 %shard_map.68 = (f32[512,128]{1,0:T(8,128)S(1)}, f32[256,128]{1,0:T(8,128)S(1)}, s32[1,256]{1,0:T(1,128)S(1)}) custom-call(f32[8,64,128]{2,1,0:T(8,128)S(1)} %copy-done, s32[1,256]{1,0:T(1,128)S(1)} %bitcast.2), custom_call_target="tpu_custom_call" | custom-call | tf_op jit(solution)/shard_map/pallas_call | solution.py:659
  2.8 4.1 %collective-permute-start.3 = (f32[256,128]{1,0:T(8,128)S(1)}, f32[256,128]{1,0:T(8,128)S(1)}, u32[]{:S(2)}, u32[]{:S(2)}) collective-permute-start(f32[256,128]{1,0:T(8,128)S(1)} %get-tuple-element.15), channel_id=1, source_target_pairs={{0,8},{4,12},{8,0},{12,4},{1,9},{5,13},{9,1},{13,5},{2,10},{6,14},... | collective-permute-start | bytes 393224 | tf_op jit(solution)/shard_map/ppermute | solution.py:674
  7.0 1.6 %collective-permute-start.1 = (f32[512,128]{1,0:T(8,128)S(1)}, f32[512,128]{1,0:T(8,128)S(1)}, u32[]{:S(2)}, u32[]{:S(2)}) collective-permute-start(f32[512,128]{1,0:T(8,128)S(1)} %get-tuple-element.14.refs_0_), channel_id=1, source_target_pairs={{0,4},{4,0},{8,12},{12,8},{1,5},{5,1},{9,13},{13,9},{2,6},{6,2},{1... | collective-permute-start | bytes 786440 | tf_op jit(solution)/shard_map/ppermute | solution.py:674
  8.5 0.1 copy.7.receivers_ref
  8.7 0.4 shard_map.69
  9.1 4.2 %collective-permute-done.3.refs_4_ = f32[256,128]{1,0:T(8,128)S(1)} collective-permute-done((f32[256,128]{1,0:T(8,128)S(1)}, f32[256,128]{1,0:T(8,128)S(1)}, u32[]{:S(2)}, u32[]{:S(2)}) %collective-permute-start.3) | collective-permute-done | bytes 131104 | tf_op jit(solution)/shard_map/ppermute | solution.py:674
  13.4 0.7 %collective-permute-start.7 = (f32[256,128]{1,0:T(8,128)S(1)}, f32[256,128]{1,0:T(8,128)S(1)}, u32[]{:S(2)}, u32[]{:S(2)}) collective-permute-start(f32[256,128]{1,0:T(8,128)S(1)} %collective-permute-done.3.refs_4_), channel_id=1, source_target_pairs={{0,4},{4,0},{8,12},{12,8},{1,5},{5,1},{9,13},{13,9},{2,6},{6,2},{1... | collective-permute-start | bytes 393224 | tf_op jit(solution)/shard_map/ppermute | solution.py:674
  14.0 1.5 %collective-permute-start.5 = (f32[256,128]{1,0:T(8,128)S(1)}, f32[256,128]{1,0:T(8,128)S(1)}, u32[]{:S(2)}, u32[]{:S(2)}) collective-permute-start(f32[256,128]{1,0:T(8,128)S(1)} %collective-permute-done.3.refs_4_), channel_id=1, source_target_pairs={{0,1},{1,0},{2,3},{3,2},{4,5},{5,4},{6,7},{7,6},{8,9},{9,8},{10,11... | collective-permute-start | bytes 393224 | tf_op jit(solution)/shard_map/ppermute | solution.py:695
  15.5 0.0 collective-permute-start
  15.5 0.5 collective-permute-start.4
  16.0 3.1 %collective-permute-done.7.refs_8_ = f32[256,128]{1,0:T(8,128)S(1)} collective-permute-done((f32[256,128]{1,0:T(8,128)S(1)}, f32[256,128]{1,0:T(8,128)S(1)}, u32[]{:S(2)}, u32[]{:S(2)}) %collective-permute-start.7) | collective-permute-done | bytes 131104 | tf_op jit(solution)/shard_map/ppermute | solution.py:674
  19.2 1.5 %collective-permute-start.9 = (f32[256,128]{1,0:T(8,128)S(1)}, f32[256,128]{1,0:T(8,128)S(1)}, u32[]{:S(2)}, u32[]{:S(2)}) collective-permute-start(f32[256,128]{1,0:T(8,128)S(1)} %collective-permute-done.7.refs_8_), channel_id=1, source_target_pairs={{0,1},{1,0},{2,3},{3,2},{4,5},{5,4},{6,7},{7,6},{8,9},{9,8},{10,11... | collective-permute-start | bytes 393224 | tf_op jit(solution)/shard_map/ppermute | solution.py:695
  20.7 0.0 collective-permute-done.1.refs_2_
  20.7 0.0 collective-permute-start.2
  20.7 0.0 collective-permute-done.5.refs_6_
  20.7 0.5 collective-permute-start.8
  21.2 0.0 collective-permute-done.4.refs_5_
  21.2 0.1 collective-permute-start.6
  21.3 2.8 %collective-permute-done.9.refs_10_ = f32[256,128]{1,0:T(8,128)S(1)} collective-permute-done((f32[256,128]{1,0:T(8,128)S(1)}, f32[256,128]{1,0:T(8,128)S(1)}, u32[]{:S(2)}, u32[]{:S(2)}) %collective-permute-start.9) | collective-permute-done | bytes 131104 | tf_op jit(solution)/shard_map/ppermute | solution.py:695
  24.1 0.0 collective-permute-start.10
  24.1 0.0 collective-permute-done.refs_1_
  24.1 0.0 collective-permute-done.8.refs_9_
  24.2 0.0 collective-permute-done.6.refs_7_
  24.2 1.3 %collective-permute-done.10.refs_11_ = f32[256,128]{1,0:T(8,128)S(1)} collective-permute-done((f32[256,128]{1,0:T(8,128)S(1)}, f32[256,128]{1,0:T(8,128)S(1)}, u32[]{:S(2)}, u32[]{:S(2)}) %collective-permute-start.10) | collective-permute-done | bytes 131104 | tf_op jit(solution)/shard_map/ppermute | solution.py:677
  25.5 0.0 collective-permute-done.2.refs_3_
  25.5 0.7 %copy-done.2 = f32[1,512]{1,0:T(1,128)S(1)} copy-done((f32[1,512]{1,0:T(1,128)S(1)}, f32[1,512]{1,0:T(1,128)}, u32[]{:S(2)}) %copy-start.2) | copy-done | bytes 2072
  26.2 24.4 %shard_map.70 = (f32[8,64,128]{2,1,0:T(8,128)}, f32[8,32,128]{2,1,0:T(8,128)S(1)}, f32[8,32,128]{2,1,0:T(8,128)S(1)}) custom-call(s32[1,256]{1,0:T(1,128)S(1)} %get-tuple-element.13.cells_ref, f32[512,128]{1,0:T(8,128)S(1)} %get-tuple-element.14.refs_0_, f32[512,128]{1,0:T(8,128)S(1)} %collective-permute-done.refs_1_, ...), custom_call_target="tpu_custom_call" | custom-call | flops 200000000 | bytes 4000000 | tf_op jit(solution)/shard_map/pallas_call | solution.py:700
  50.6 1.5 %collective-permute-start.11 = (f32[8,32,128]{2,1,0:T(8,128)S(1)}, f32[8,32,128]{2,1,0:T(8,128)S(1)}, u32[]{:S(2)}, u32[]{:S(2)}) collective-permute-start(f32[8,32,128]{2,1,0:T(8,128)S(1)} %get-tuple-element.23), channel_id=1, source_target_pairs={{0,1},{1,0},{2,3},{3,2},{4,5},{5,4},{6,7},{7,6},{8,9},{9,8},{10,11... | collective-permute-start | bytes 393224 | tf_op jit(solution)/shard_map/ppermute | solution.py:718
  52.2 4.0 %collective-permute-done.11 = f32[8,32,128]{2,1,0:T(8,128)S(1)} collective-permute-done((f32[8,32,128]{2,1,0:T(8,128)S(1)}, f32[8,32,128]{2,1,0:T(8,128)S(1)}, u32[]{:S(2)}, u32[]{:S(2)}) %collective-permute-start.11) | collective-permute-done | bytes 131104 | tf_op jit(solution)/shard_map/ppermute | solution.py:718
  56.2 0.7 %add.3 = f32[8,32,128]{2,1,0:T(8,128)} add(f32[8,32,128]{2,1,0:T(8,128)S(1)} %get-tuple-element.22, f32[8,32,128]{2,1,0:T(8,128)S(1)} %collective-permute-done.11) | non-fusion elementwise | flops 32768 | bytes 393216 | tf_op jit(solution)/shard_map/add | solution.py:718
  (7 shorter events, 0.0 us)
Async XLA Ops:
  0.6 0.7 %copy-start.1 = (s32[256]{0:T(256)S(1)}, s32[256]{0:T(256)}, u32[]{:S(2)}) copy-start(s32[256]{0:T(256)} %param.6) | copy-start | bytes 3076
  1.3 0.9 %copy-start = (f32[8,64,128]{2,1,0:T(8,128)S(1)}, f32[8,64,128]{2,1,0:T(8,128)}, u32[]{:S(2)}) copy-start(f32[8,64,128]{2,1,0:T(8,128)} %natural_ref.1) | copy-start | bytes 786436
  2.3 6.3 %copy-start.4 = (s32[512,2]{0,1:T(2,128)S(1)}, s32[512,2]{0,1:T(2,128)}, u32[]{:S(2)}) copy-start(s32[512,2]{0,1:T(2,128)} %param.8) | copy-start | bytes 12292
  2.8 10.5 %collective-permute-start.3 = (f32[256,128]{1,0:T(8,128)S(1)}, f32[256,128]{1,0:T(8,128)S(1)}, u32[]{:S(2)}, u32[]{:S(2)}) collective-permute-start(f32[256,128]{1,0:T(8,128)S(1)} %get-tuple-element.15), channel_id=1, source_target_pairs={{0,8},{4,12},{8,0},{12,4},{1,9},{5,13},{9,1},{13,5},{2,10},{6,14},... | collective-permute-start | bytes 393224 | tf_op jit(solution)/shard_map/ppermute | solution.py:674
  7.0 1.7 %copy-start.3 = (f32[1,256]{1,0:T(1,128)S(1)}, f32[1,256]{1,0:T(1,128)}, u32[]{:S(2)}) copy-start(f32[1,256]{1,0:T(1,128)} %currents_ref.1) | copy-start | bytes 3076
  7.0 13.8 %collective-permute-start.1 = (f32[512,128]{1,0:T(8,128)S(1)}, f32[512,128]{1,0:T(8,128)S(1)}, u32[]{:S(2)}, u32[]{:S(2)}) collective-permute-start(f32[512,128]{1,0:T(8,128)S(1)} %get-tuple-element.14.refs_0_), channel_id=1, source_target_pairs={{0,4},{4,0},{8,12},{12,8},{1,5},{5,1},{9,13},{13,9},{2,6},{6,2},{1... | collective-permute-start | bytes 786440 | tf_op jit(solution)/shard_map/ppermute | solution.py:674
  13.4 5.8 %collective-permute-start.7 = (f32[256,128]{1,0:T(8,128)S(1)}, f32[256,128]{1,0:T(8,128)S(1)}, u32[]{:S(2)}, u32[]{:S(2)}) collective-permute-start(f32[256,128]{1,0:T(8,128)S(1)} %collective-permute-done.3.refs_4_), channel_id=1, source_target_pairs={{0,4},{4,0},{8,12},{12,8},{1,5},{5,1},{9,13},{13,9},{2,6},{6,2},{1... | collective-permute-start | bytes 393224 | tf_op jit(solution)/shard_map/ppermute | solution.py:674
  14.0 6.7 %collective-permute-start.5 = (f32[256,128]{1,0:T(8,128)S(1)}, f32[256,128]{1,0:T(8,128)S(1)}, u32[]{:S(2)}, u32[]{:S(2)}) collective-permute-start(f32[256,128]{1,0:T(8,128)S(1)} %collective-permute-done.3.refs_4_), channel_id=1, source_target_pairs={{0,1},{1,0},{2,3},{3,2},{4,5},{5,4},{6,7},{7,6},{8,9},{9,8},{10,11... | collective-permute-start | bytes 393224 | tf_op jit(solution)/shard_map/ppermute | solution.py:695
  15.5 8.6 %collective-permute-start = (f32[512,128]{1,0:T(8,128)S(1)}, f32[512,128]{1,0:T(8,128)S(1)}, u32[]{:S(2)}, u32[]{:S(2)}) collective-permute-start(f32[512,128]{1,0:T(8,128)S(1)} %get-tuple-element.14.refs_0_), channel_id=1, source_target_pairs={{0,2},{2,0},{1,3},{3,1},{4,6},{6,4},{5,7},{7,5},{8,10},{10,8},{9,1... | collective-permute-start | bytes 786440 | tf_op jit(solution)/shard_map/ppermute | solution.py:677
  15.5 5.7 %collective-permute-start.4 = (f32[256,128]{1,0:T(8,128)S(1)}, f32[256,128]{1,0:T(8,128)S(1)}, u32[]{:S(2)}, u32[]{:S(2)}) collective-permute-start(f32[256,128]{1,0:T(8,128)S(1)} %collective-permute-done.3.refs_4_), channel_id=1, source_target_pairs={{0,2},{2,0},{1,3},{3,1},{4,6},{6,4},{5,7},{7,5},{8,10},{10,8},{9,1... | collective-permute-start | bytes 393224 | tf_op jit(solution)/shard_map/ppermute | solution.py:677
  19.2 5.0 %collective-permute-start.9 = (f32[256,128]{1,0:T(8,128)S(1)}, f32[256,128]{1,0:T(8,128)S(1)}, u32[]{:S(2)}, u32[]{:S(2)}) collective-permute-start(f32[256,128]{1,0:T(8,128)S(1)} %collective-permute-done.7.refs_8_), channel_id=1, source_target_pairs={{0,1},{1,0},{2,3},{3,2},{4,5},{5,4},{6,7},{7,6},{8,9},{9,8},{10,11... | collective-permute-start | bytes 393224 | tf_op jit(solution)/shard_map/ppermute | solution.py:695
  20.7 4.8 %collective-permute-start.2 = (f32[512,128]{1,0:T(8,128)S(1)}, f32[512,128]{1,0:T(8,128)S(1)}, u32[]{:S(2)}, u32[]{:S(2)}) collective-permute-start(f32[512,128]{1,0:T(8,128)S(1)} %collective-permute-done.1.refs_2_), channel_id=1, source_target_pairs={{0,2},{2,0},{1,3},{3,1},{4,6},{6,4},{5,7},{7,5},{8,10},{10,8},{9,1... | collective-permute-start | bytes 786440 | tf_op jit(solution)/shard_map/ppermute | solution.py:677
  20.7 3.4 %collective-permute-start.8 = (f32[256,128]{1,0:T(8,128)S(1)}, f32[256,128]{1,0:T(8,128)S(1)}, u32[]{:S(2)}, u32[]{:S(2)}) collective-permute-start(f32[256,128]{1,0:T(8,128)S(1)} %collective-permute-done.7.refs_8_), channel_id=1, source_target_pairs={{0,2},{2,0},{1,3},{3,1},{4,6},{6,4},{5,7},{7,5},{8,10},{10,8},{9,1... | collective-permute-start | bytes 393224 | tf_op jit(solution)/shard_map/ppermute | solution.py:677
  21.2 2.9 %collective-permute-start.6 = (f32[256,128]{1,0:T(8,128)S(1)}, f32[256,128]{1,0:T(8,128)S(1)}, u32[]{:S(2)}, u32[]{:S(2)}) collective-permute-start(f32[256,128]{1,0:T(8,128)S(1)} %collective-permute-done.5.refs_6_), channel_id=1, source_target_pairs={{0,2},{2,0},{1,3},{3,1},{4,6},{6,4},{5,7},{7,5},{8,10},{10,8},{9,1... | collective-permute-start | bytes 393224 | tf_op jit(solution)/shard_map/ppermute | solution.py:677
  24.1 1.3 %collective-permute-start.10 = (f32[256,128]{1,0:T(8,128)S(1)}, f32[256,128]{1,0:T(8,128)S(1)}, u32[]{:S(2)}, u32[]{:S(2)}) collective-permute-start(f32[256,128]{1,0:T(8,128)S(1)} %collective-permute-done.9.refs_10_), channel_id=1, source_target_pairs={{0,2},{2,0},{1,3},{3,1},{4,6},{6,4},{5,7},{7,5},{8,10},{10,8},{9,1... | collective-permute-start | bytes 393224 | tf_op jit(solution)/shard_map/ppermute | solution.py:677
  25.5 0.7 %copy-start.2 = (f32[1,512]{1,0:T(1,128)S(1)}, f32[1,512]{1,0:T(1,128)}, u32[]{:S(2)}) copy-start(f32[1,512]{1,0:T(1,128)} %refs_16_.1) | copy-start | bytes 6148
  50.6 5.5 %collective-permute-start.11 = (f32[8,32,128]{2,1,0:T(8,128)S(1)}, f32[8,32,128]{2,1,0:T(8,128)S(1)}, u32[]{:S(2)}, u32[]{:S(2)}) collective-permute-start(f32[8,32,128]{2,1,0:T(8,128)S(1)} %get-tuple-element.23), channel_id=1, source_target_pairs={{0,1},{1,0},{2,3},{3,2},{4,5},{5,4},{6,7},{7,6},{8,9},{9,8},{10,11... | collective-permute-start | bytes 393224 | tf_op jit(solution)/shard_map/ppermute | solution.py:718

commit v8 on v7

--- a/solution.py
+++ b/solution.py
@@ -72,7 +72,7 @@
     return lax.axis_index("gx") * 2 + lax.axis_index("gy"), lax.axis_index("shot")
 
 
-def to_blocks_kernel(natural_ref, stations_ref, blocks_ref, half_ref, cells_ref):
+def to_blocks_kernel(natural_ref, blocks_ref, half_ref):
     order = lane_order()
     for x in range(SIDE):
         tiles = product(natural_ref[x], order, 3)
@@ -82,10 +82,6 @@
     count = half_ref.shape[0]
     low, high = blocks_ref[pl.ds(0, count), :], blocks_ref[pl.ds(count, count), :]
     half_ref[...] = jnp.where(own_place()[1] == 0, low, high)
-    cell_x, cell_y, cell_z, row, _ = station_table(stations_ref[...])
-    wide = SIDE + 2
-    register = (((cell_x & 7) + 1) * wide + (cell_z & 7) + 1) * wide + (cell_y & 7) + 1
-    cells_ref[...] = register * SIDE + row
 
 
 def from_blocks(tiles, order):
@@ -142,10 +138,26 @@
     return jnp.concatenate([row[i // 2 : i // 2 + 1] for i in range(2 * row.shape[0])])
 
 
-def electrode_kernel(stations_ref, currents_ref, receivers_ref, rows_ref, same_ref, pairs_ref):
+def electrode_kernel(
+    stations_ref,
+    currents_ref,
+    receivers_ref,
+    observed_ref,
+    cells_ref,
+    spot_ref,
+    rows_ref,
+    same_ref,
+    pairs_ref,
+    held_ref,
+):
     stations = stations_ref[...]
     electrodes = stations.shape[1]
-    row, spot = station_table(stations)[3:]
+    cell_x, cell_y, cell_z, row, spot = station_table(stations)
+    wide = SIDE + 2
+    register = (((cell_x & 7) + 1) * wide + (cell_z & 7) + 1) * wide + (cell_y & 7) + 1
+    cells_ref[...] = register * SIDE + row
+    spot_ref[...] = spot
+    held_ref[...] = observed_ref[...]
     line = stations & 0x1C387 | row << 20
     same = jnp.broadcast_to(line, (electrodes, electrodes))
     same = jnp.where(same == same.T, 1.0, 0.0).astype(jnp.bfloat16)
@@ -197,10 +209,11 @@
             before = inside_down(block_down(value[n - 1 :], 1), 1)
             self.ref[pl.ds(self.start(x, z, -1), SIDE), :] = before[0]
 
-    def close_z(self, x):
+    def close_z(self, x, exact=False):
         n = self.side
-        self[x, n] = block_up(self[x, 0], 2)
-        self[x, -1] = block_down(self[x, n - 1], 2)
+        after, before = block_up(self[x, 0], 2), block_down(self[x, n - 1], 2)
+        self[x, n] = inside_up(after, 2) if exact else after
+        self[x, -1] = inside_down(before, 2) if exact else before
 
     def close(self, exact=False):
         n = self.side
@@ -211,32 +224,36 @@
             self[-1, z] = inside_down(before, 0) if exact else before
 
 
-class Plain:
-    def __init__(self, ref, side):
-        self.ref, self.side = ref, side
+class Rows:
+    def __init__(self, ref, side, first_x=0, first_z=0):
+        self.ref, self.side, self.first_x, self.first_z = ref, side, first_x, first_z
+
+    def place(self, at):
+        count = self.side - self.first_z
+        rows = self.side * SIDE
+        return pl.ds(((at[0] - self.first_x) * count + at[1] - self.first_z) * rows, rows)
 
     def __getitem__(self, at):
-        x, z = at
-        rows = self.side * SIDE
-        return self.ref[pl.ds((x * self.side + z) * rows, rows), :].reshape(self.side, SIDE, LANES)
+        return self.ref[self.place(at), :].reshape(self.side, SIDE, LANES)
 
     def __setitem__(self, at, value):
-        x, z = at
-        rows = self.side * SIDE
-        self.ref[pl.ds((x * self.side + z) * rows, rows), :] = value.reshape(-1, LANES)
-
-
-def planes_of(count, body):
-    if count < SIDE:
-        for x in range(count):
-            body(x)
-        return
-
+        self.ref[self.place(at), :] = value.reshape(-1, LANES)
+
+
+def rolled(count, body):
     def one(x, carry):
         body(x)
         return carry
 
-    lax.fori_loop(0, count, one, 0, unroll=2)
+    lax.fori_loop(0, count, one, 0)
+
+
+def next_in_y(row):
+    return jnp.concatenate([row[1:], block_up(row[:1], 1)])
+
+
+def last_in_y(row):
+    return jnp.concatenate([block_down(row[-1:], 1), row[:-1]])
 
 
 class Level:
@@ -244,154 +261,202 @@
         self.side = side = SIDE >> index
         self.scale = 0.25**index
         edged = [Edged(ref, side) for ref in refs[:5]]
-        self.cond, self.first, self.second, self.base, self.back = edged
-        self.links = [Plain(ref, side) for ref in refs[5:11]]
-        self.half = Plain(refs[11], side // 2)
-        self.weight = Plain(refs[12], side) if index else None
+        self.cond, self.first, self.second, self.base, self.weight = edged
+        self.link_x = Rows(refs[5], side, first_x=-1)
+        self.link_y = Rows(refs[6], side)
+        self.link_z = Rows(refs[7], side, first_z=-1)
+        self.back = Rows(refs[8], side)
 
     @staticmethod
     def scratch(index):
         side = SIDE >> index
-        edged = (side + 2) ** 3
-        sizes = [edged] * 5 + [side**3] * 6 + [side**3 // 4] + [side**3] * (index > 0)
+        sizes = [(side + 2) ** 3] * 5
+        sizes += [side**2 * (side + 1), side**3, side**2 * (side + 1), side**3]
         return [pltpu.VMEM((size * SIDE, LANES), jnp.float32) for size in sizes]
 
-    def shifted(self, field, x, z, here, exact=False, along=None):
-        ahead, behind = along or (field[x, z + 1], field[x, z - 1])
-        after = block_up(here[:1], 1)
-        before = block_down(here[-1:], 1)
-        if exact:
-            after, before = inside_up(after, 1), inside_down(before, 1)
-        return [
-            field[x + 1, z],
-            field[x - 1, z],
-            jnp.concatenate([here[1:], after]),
-            jnp.concatenate([before, here[:-1]]),
-            ahead,
-            behind,
-        ]
+    def pairs(self, body):
+        if self.side == SIDE:
+            rolled(self.side // 2, lambda i: body(2 * i))
+        else:
+            for i in range(self.side // 2):
+                body(2 * i)
 
     def prepare(self):
         n = self.side
+        cond = self.cond
 
         def plane(x):
             for z in range(n):
-                here = self.cond[x, z]
-                others = self.shifted(self.cond, x, z, here, exact=True)
-                total = others[0]
-                for other in others[1:]:
-                    total = total + other
+                here, ahead, next_x = cond[x, z], cond[x, z + 1], cond[x + 1, z]
+                after = inside_up(block_up(here[:1], 1), 1)
+                before = inside_down(block_down(here[-1:], 1), 1)
+                next_y = jnp.concatenate([here[1:], after])
+                last_y = jnp.concatenate([before, here[:-1]])
+                total = (next_x + cond[x - 1, z]) + (ahead + cond[x, z - 1]) + (next_y + last_y)
                 total = 3.0 * here + 0.5 * total
-                inverse = DAMPING / total
-                if self.weight is not None:
-                    self.weight[x, z] = inverse * (1.0 / self.scale)
+                self.weight[x, z] = DAMPING / total
                 self.back[x, z] = total * (self.scale / DAMPING)
-                inverse = 0.5 * inverse
-                for index, other in enumerate(others):
-                    link = inverse * (here + other)
-                    if index == 2:
-                        link = jnp.concatenate([link[:-1], inside_up(link[-1:], 1)])
-                    if index == 3:
-                        link = jnp.concatenate([inside_down(link[:1], 1), link[1:]])
-                    if index == 4 and z == n - 1:
-                        link = inside_up(link, 2)
-                    if index == 5 and z == 0:
-                        link = inside_down(link, 2)
-                    self.links[index][x, z] = link
-
-        planes_of(n, plane)
+                self.link_x[x, z] = 0.5 * (here + next_x)
+                link = 0.5 * (here + next_y)
+                self.link_y[x, z] = jnp.concatenate([link[:-1], inside_up(link[-1:], 1)])
+                link = 0.5 * (here + ahead)
+                if z == n - 1:
+                    link = inside_up(link, 2)
+                    self.link_z[x, -1] = block_down(link, 2)
+                self.link_z[x, z] = link
+
+        if n == SIDE:
+            rolled(n, plane)
+        else:
+            for x in range(n):
+                plane(x)
         for z in range(n):
-            self.links[0][n - 1, z] = inside_up(self.links[0][n - 1, z], 0)
-            self.links[1][0, z] = inside_down(self.links[1][0, z], 0)
+            link = inside_up(self.link_x[n - 1, z], 0)
+            self.link_x[n - 1, z] = link
+            self.link_x[-1, z] = block_down(link, 0)
+
+    def flows(self, x, z, here, ahead, outer, down):
+        result = []
+        inner = self.link_x[x, z]
+        sides = [
+            self.link_x[x - 1, z] * outer[0] + inner * here[1],
+            inner * here[0] + self.link_x[x + 1, z] * outer[1],
+        ]
+        for p in range(2):
+            link_y, link_z = self.link_y[x + p, z], self.link_z[x + p, z]
+            along = link_y * next_in_y(here[p]) + last_in_y(link_y * here[p])
+            total = sides[p] + (link_z * ahead[p] + down[p]) + along
+            down[p] = link_z * here[p]
+            result.append(self.weight[x + p, z] * total)
+        return result
 
     def rows(self, field, x):
-        behind, here = field[x, -1], field[x, 0]
+        here = [field[x, 0], field[x + 1, 0]]
+        down = [self.link_z[x + p, -1] * field[x + p, -1] for p in range(2)]
         for z in range(self.side):
-            ahead = field[x, z + 1]
-            result = self.base[x, z]
-            others = self.shifted(field, x, z, here, along=(ahead, behind))
-            for link, other in zip(self.links, others):
-                result = result + link[x, z] * other
-            yield z, here, result
-            behind, here = here, ahead
+            ahead = [field[x, z + 1], field[x + 1, z + 1]]
+            outer = [field[x - 1, z], field[x + 2, z]]
+            yield z, here, self.flows(x, z, here, ahead, outer, down)
+            here = ahead
 
     def sweep(self, field, out, exact=False):
-        def plane(x):
-            for z, here, result in self.rows(field, x):
-                out.put(x, z, (1.0 - DAMPING) * here + result, exact)
-
-        planes_of(self.side, plane)
+        def pair(x):
+            for z, here, sums in self.rows(field, x):
+                for p in range(2):
+                    if field is self.base:
+                        value = (2.0 - DAMPING) * here[p] + sums[p]
+                    else:
+                        value = (1.0 - DAMPING) * here[p] + (self.base[x + p, z] + sums[p])
+                    out.put(x + p, z, value, exact)
+
+        self.pairs(pair)
         out.close(exact)
 
-    def halve(self, plane_rows, coarse):
-        n = self.side
-
-        def plane(x):
+    def halve(self, rows, coarse):
+        def pair(x):
             held = None
-            for z, row in enumerate(plane_rows(x)):
+            for z, row in enumerate(rows(x)):
+                row = row[0] + row[1]
                 if z % 2 == 0:
                     held = row
                 else:
-                    self.half[x, z // 2] = pair_rows(held + row)
-
-        planes_of(n, plane)
-        for x in range(n // 2):
-            for z in range(n // 2):
-                pair = self.half[2 * x, z] + self.half[2 * x + 1, z]
-                coarse(x, z, 0.125 * pair)
+                    coarse(x // 2, z // 2, 0.125 * pair_rows(held + row))
+
+        self.pairs(pair)
 
     def descend(self, coarse):
         self.sweep(self.base, self.second)
 
         def residuals(x):
-            for z, here, result in self.rows(self.second, x):
-                self.first[x, z] = (1.0 - DAMPING) * here + result
-                yield (result - DAMPING * here) * self.back[x, z]
+            for z, here, sums in self.rows(self.second, x):
+                result = []
+                for p in range(2):
+                    total = self.base[x + p, z] + sums[p]
+                    self.first[x + p, z] = (1.0 - DAMPING) * here[p] + total
+                    result.append((total - DAMPING * here[p]) * self.back[x + p, z])
+                yield result
 
         self.halve(residuals, coarse)
 
     def ascend(self, correction, out, exact=False):
-        def plane(x):
-            upper = (x + 1) // 2
+        def pair(x):
+            i = x // 2
+            here = twice(correction(i, 0))
+            start = twice(correction(i, -1))
+            down = [self.link_z[x + p, -1] * start for p in range(2)]
             for z in range(self.side):
-                above = (z + 1) // 2
-                row = correction(x // 2, z // 2)
-                here = twice(row)
-                after, before = block_up(row[:1], 1), block_down(row[-1:], 1)
-                others = [
-                    twice(correction(upper, z // 2)),
-                    twice(correction(upper - 1, z // 2)),
-                    jnp.concatenate([here[1:], after]),
-                    jnp.concatenate([before, here[:-1]]),
-                    twice(correction(x // 2, above)),
-                    twice(correction(x // 2, above - 1)),
-                ]
-                result = self.first[x, z] + (1.0 - DAMPING) * here
-                for link, other in zip(self.links, others):
-                    result = result + link[x, z] * other
-                self.second.put(x, z, result)
-
-        planes_of(self.side, plane)
+                ahead = twice(correction(i, (z + 1) // 2))
+                outer = [twice(correction(i - 1, z // 2)), twice(correction(i + 1, z // 2))]
+                sums = self.flows(x, z, [here, here], [ahead, ahead], outer, down)
+                for p in range(2):
+                    value = self.first[x + p, z] + ((1.0 - DAMPING) * here + sums[p])
+                    self.second.put(x + p, z, value)
+                here = ahead
+
+        self.pairs(pair)
         self.second.close()
         self.sweep(self.second, out, exact)
 
 
-class HeldLevel(Level):
+class HeldLevel:
+    def __init__(self, refs, index):
+        self.side = 2
+        self.scale = 0.25**index
+        self.cond, self.first = Edged(refs[0], 2), Edged(refs[1], 2)
+        self.weight, self.back = Rows(refs[2], 2), Rows(refs[3], 2)
+        self.links = [Rows(ref, 2) for ref in refs[4:]]
+
+    @staticmethod
+    def scratch(index):
+        sizes = [4**3] * 2 + [2**3] * 8
+        return [pltpu.VMEM((size * SIDE, LANES), jnp.float32) for size in sizes]
+
+    def around(self, field, inside=False):
+        def moved(row, axis, up):
+            row = (block_up if up else block_down)(row, axis)
+            return (inside_up if up else inside_down)(row, axis) if inside else row
+
+        result = {}
+        for (x, z), here in field.items():
+            result[x, z] = [
+                field[1, z] if x == 0 else moved(field[0, z], 0, True),
+                field[0, z] if x == 1 else moved(field[1, z], 0, False),
+                jnp.concatenate([here[1:], moved(here[:1], 1, True)]),
+                jnp.concatenate([moved(here[-1:], 1, False), here[:-1]]),
+                field[x, 1] if z == 0 else moved(field[x, 0], 2, True),
+                field[x, 0] if z == 1 else moved(field[x, 1], 2, False),
+            ]
+        return result
+
+    def prepare(self):
+        field = {(x, z): self.cond[x, z] for x in range(2) for z in range(2)}
+        for at, others in self.around(field, inside=True).items():
+            here = field[at]
+            total = others[0]
+            for other in others[1:]:
+                total = total + other
+            total = 3.0 * here + 0.5 * total
+            inverse = DAMPING / total
+            self.weight[at] = inverse
+            self.back[at] = total * (self.scale / DAMPING)
+            for index, other in enumerate(others):
+                link = 0.5 * inverse * (here + other)
+                self.links[index][at] = jnp.where(other > 0.0, link, 0.0)
+
+    def halve(self, rows, coarse):
+        total = None
+        for row in rows(0):
+            row = row[0] + row[1]
+            total = row if total is None else total + row
+        coarse(0, 0, 0.125 * (total[:1] + total[1:]))
+
     def sums(self, field, base):
         result = {}
-        for (x, z), here in field.items():
-            others = [
-                field[1, z] if x == 0 else block_up(field[0, z], 0),
-                field[0, z] if x == 1 else block_down(field[1, z], 0),
-                jnp.concatenate([here[1:], block_up(here[:1], 1)]),
-                jnp.concatenate([block_down(here[-1:], 1), here[:-1]]),
-                field[x, 1] if z == 0 else block_up(field[x, 0], 2),
-                field[x, 0] if z == 1 else block_down(field[x, 1], 2),
-            ]
-            total = base[x, z]
+        for at, others in self.around(field).items():
+            total = base[at]
             for link, other in zip(self.links, others):
-                total = total + link[x, z] * other
-            result[x, z] = total
+                total = total + link[at] * other
+            result[at] = total
         return result
 
     def swept(self, field, base):
@@ -429,7 +494,7 @@
     part_refs,
     half_refs,
     cells_ref,
-    stations_ref,
+    spot_ref,
     rows_ref,
     same_ref,
     pairs_ref,
@@ -443,11 +508,11 @@
     *level_refs,
 ):
     f32 = jnp.float32
-    electrodes = stations_ref.shape[1]
+    electrodes = spot_ref.shape[1]
     levels, used = [], 0
     for index in range(LEVELS - 1):
-        count = len(Level.scratch(index))
         kind = HeldLevel if index == LEVELS - 2 else Level
+        count = len(kind.scratch(index))
         levels.append(kind(level_refs[used : used + count], index))
         used += count
     fine = levels[0]
@@ -472,12 +537,12 @@
             place(part, x, (shot ^ swapped) * (SIDE // 2) + x, device ^ index)
 
     def edges(x):
-        for z in (0, SIDE - 1):
-            fine.cond.put(x, z, fine.cond[x, z], exact=True)
-
-    planes_of(SIDE, collect)
-    planes_of(SIDE // 2, collect_half)
-    planes_of(SIDE, edges)
+        fine.cond.close_z(x, exact=True)
+
+    rolled(SIDE, collect)
+    for x in range(SIDE // 2):
+        collect_half(x)
+    rolled(SIDE, edges)
     fine.cond.close(exact=True)
 
     coarsest = []
@@ -490,7 +555,12 @@
             else:
                 below.cond.put(x, z, row, exact=True)
 
-        level.halve(lambda x, level=level: [level.cond[x, z] for z in range(level.side)], coarse)
+        level.halve(
+            lambda x, level=level: [
+                (level.cond[x, z], level.cond[x + 1, z]) for z in range(level.side)
+            ],
+            coarse,
+        )
         if below is not None:
             below.cond.close(exact=True)
 
@@ -559,17 +629,21 @@
             base = {}
 
             def take(x, z, row):
-                base[x, z] = below.weight[x, z] * row
+                base[x, z] = below.weight[x, z] * (row * (1.0 / below.scale))
 
             level.descend(take)
             below.cycle(base, solve_last, below.first)
         else:
-            level.descend(lambda x, z, row: below.base.put(x, z, below.weight[x, z] * row))
+            level.descend(
+                lambda x, z, row: below.base.put(
+                    x, z, below.weight[x, z] * (row * (1.0 / below.scale))
+                )
+            )
             below.base.close()
             cycle(index + 1, below.first)
         level.ascend(lambda x, z: below.first[x, z], out, exact)
 
-    spot = station_table(stations_ref[...])[4]
+    spot = spot_ref[...]
 
     def each(body):
         def one(electrode, carry):
@@ -579,10 +653,9 @@
         lax.fori_loop(0, electrodes, one, 0, unroll=32)
 
     def weigh(electrode, cell):
-        weights[electrode, :] = fine.back.ref[cell, :]
+        weights[electrode, :] = fine.weight.ref[cell, :]
 
     each(weigh)
-    weights[...] = 1.0 / weights[...]
     fine.base.ref[...] = jnp.zeros_like(fine.base.ref)
 
     def spread(rows):
@@ -592,7 +665,7 @@
             fine.base.ref[cell, :] = gathered[electrode, :]
 
         each(put)
-        planes_of(SIDE, fine.base.close_z)
+        rolled(SIDE, fine.base.close_z)
         fine.base.close()
 
     spread(rows_ref[...])
@@ -656,17 +729,16 @@
     vmem = pl.BlockSpec(memory_space=pltpu.VMEM)
     smem = pl.BlockSpec(memory_space=pltpu.SMEM)
     station_row = stations.reshape(1, electrodes)
-    mine, half, cells = pl.pallas_call(
+    mine, half = pl.pallas_call(
         to_blocks_kernel,
         out_shape=(
             jax.ShapeDtypeStruct((total, LANES), f32),
             jax.ShapeDtypeStruct((total // 2, LANES), f32),
-            jax.ShapeDtypeStruct((1, electrodes), jnp.int32),
         ),
-        in_specs=[vmem, vmem],
-        out_specs=(vmem, vmem, vmem),
+        in_specs=[vmem],
+        out_specs=(vmem, vmem),
         compiler_params=pltpu.CompilerParams(vmem_limit_bytes=SMALL_BYTES),
-    )(conductivity, station_row)
+    )(conductivity)
     swap = [(0, 1), (1, 0)]
 
     def partner(part, k):
@@ -678,25 +750,30 @@
 
     far = partner(half, 2)
     near = partner(mine, 1)
-    rows_of, same, pairs = pl.pallas_call(
+    line = jax.ShapeDtypeStruct((1, electrodes), jnp.int32)
+    cells, spot, rows_of, same, pairs, held = pl.pallas_call(
         electrode_kernel,
         out_shape=(
+            line,
+            line,
             jax.ShapeDtypeStruct((electrodes, LANES), f32),
             jax.ShapeDtypeStruct((electrodes, electrodes), jnp.bfloat16),
             jax.ShapeDtypeStruct((receivers.shape[0], electrodes), jnp.bfloat16),
+            jax.ShapeDtypeStruct(observed.shape, f32),
         ),
-        in_specs=[vmem, vmem, vmem],
-        out_specs=(vmem, vmem, vmem),
+        in_specs=[vmem] * 4,
+        out_specs=(vmem,) * 6,
         compiler_params=pltpu.CompilerParams(vmem_limit_bytes=SMALL_BYTES),
         cost_estimate=pl.CostEstimate(flops=100_000_000, bytes_accessed=1_000_000, transcendentals=0),
-    )(station_row, currents, receivers)
+    )(station_row, currents, receivers, observed)
     far, rows_of = lax.optimization_barrier((far, rows_of))
     far = [far, partner(far, 1)]
     halved = [piece for own in far for piece in (own, lax.ppermute(own, "shot", swap))]
     parts = [piece for own in (mine, near) for piece in with_mate(own)]
     halved = [piece for own in halved for piece in with_mate(own)]
     chunk = cols // 2
-    levels = [shape for index in range(LEVELS - 1) for shape in Level.scratch(index)]
+    levels = [shape for index in range(LEVELS - 2) for shape in Level.scratch(index)]
+    levels += HeldLevel.scratch(LEVELS - 2)
     potentials, own, theirs = pl.pallas_call(
         functools.partial(replicated_kernel, len(parts), len(halved)),
         out_shape=(
@@ -714,7 +791,7 @@
         + levels,
         compiler_params=pltpu.CompilerParams(vmem_limit_bytes=VMEM_BYTES),
         cost_estimate=pl.CostEstimate(flops=200_000_000, bytes_accessed=4_000_000, transcendentals=0),
-    )(cells, *parts, *halved, station_row, rows_of, same, pairs, observed)
+    )(cells, *parts, *halved, spot, rows_of, same, pairs, held)
     return potentials[None], own + lax.ppermute(theirs, "shot", swap)
 
 

time: 57 us -> 55.5 us (0.974)
  local copies, waits for them, and re-layouts: 2.46 us -> 1.76 us
  waiting for transfers between devices: 15.6 us -> 14.9 us
    unnamed x11, local copies, waits for them, and re-layouts: 2.46 us -> 1.76 us
    ppermute x3, waiting for transfers between devices: 7.39 us -> 6.72 us  [partner(): return lax.ppermute(part, 'gx', [(i, i ^ k) for i in range(count)])]
where the time goes in v8:
time: 55.5 us; the launch traced here: 55.3 us
  Pallas kernels  25.3 us (46%)
  waiting for transfers between devices  14.9 us (27%)
  starting transfers between devices  12 us (22%)
  local copies, waits for them, and re-layouts  1.76 us (3%)
  between operations  0.7 us (1%)
  other arithmetic  0.67 us (1%)
    pallas_call x1, Pallas kernels, replicated(): pl.pallas_call(functools.partial(replicated_kernel, len(parts), len(halve...  24.3 us
    ppermute x3, waiting for transfers between devices, partner(): return lax.ppermute(part, 'gx', [(i, i ^ k) for i in range(count)])  6.72 us
    ppermute x3, starting transfers between devices, partner(): return lax.ppermute(part, 'gx', [(i, i ^ k) for i in range(count)])  6.34 us
    ppermute x1, waiting for transfers between devices, replicated(): return (potentials[None], own + lax.ppermute(theirs, 'shot', swap))  4.01 us
    ppermute x2, starting transfers between devices, replicated(): lax.ppermute(own, 'shot', swap)  3.03 us
    ppermute x2, waiting for transfers between devices, replicated(): lax.ppermute(own, 'shot', swap)  2.84 us
    unnamed x11, local copies, waits for them, and re-layouts  1.76 us
    ppermute x1, starting transfers between devices, replicated(): return (potentials[None], own + lax.ppermute(theirs, 'shot', swap))  1.54 us
  transfers between devices with their start and end apart: 12, of which 5 were waited for; matrix products, arithmetic and copies ran while one was open for 0% of the time, Pallas kernels for 1%

profile of v8, /device:TPU:0, one launch (start us, length us, event | category | flops | bytes accessed | tf_op | source)
XLA Modules:
  0.0 55.3 jit_solution(718173517119770610)
XLA Ops:
  0.6 0.9 %copy-done = f32[8,64,128]{2,1,0:T(8,128)S(1)} copy-done((f32[8,64,128]{2,1,0:T(8,128)S(1)}, f32[8,64,128]{2,1,0:T(8,128)}, u32[]{:S(2)}) %copy-start) | copy-done | bytes 262168
  1.6 0.6 %shard_map.69 = (f32[512,128]{1,0:T(8,128)S(1)}, f32[256,128]{1,0:T(8,128)S(1)}) custom-call(f32[8,64,128]{2,1,0:T(8,128)S(1)} %copy-done), custom_call_target="tpu_custom_call" | custom-call | tf_op jit(solution)/shard_map/pallas_call | solution.py:732
  2.2 4.1 %collective-permute-start.3 = (f32[256,128]{1,0:T(8,128)S(1)}, f32[256,128]{1,0:T(8,128)S(1)}, u32[]{:S(2)}, u32[]{:S(2)}) collective-permute-start(f32[256,128]{1,0:T(8,128)S(1)} %get-tuple-element.17), channel_id=1, source_target_pairs={{0,8},{4,12},{8,0},{12,4},{1,9},{5,13},{9,1},{13,5},{2,10},{6,14},... | collective-permute-start | bytes 393224 | tf_op jit(solution)/shard_map/ppermute | solution.py:746
  6.3 1.6 %collective-permute-start.1 = (f32[512,128]{1,0:T(8,128)S(1)}, f32[512,128]{1,0:T(8,128)S(1)}, u32[]{:S(2)}, u32[]{:S(2)}) collective-permute-start(f32[512,128]{1,0:T(8,128)S(1)} %get-tuple-element.16.refs_0_), channel_id=1, source_target_pairs={{0,4},{4,0},{8,12},{12,8},{1,5},{5,1},{9,13},{13,9},{2,6},{6,2},{1... | collective-permute-start | bytes 786440 | tf_op jit(solution)/shard_map/ppermute | solution.py:746
  7.9 0.1 copy.7.receivers_ref
  8.0 0.0 copy-start.2
  8.0 0.5 copy-done.3
  8.5 0.2 copy-done.2
  8.7 0.4 shard_map.68
  9.1 3.6 %collective-permute-done.3.refs_4_ = f32[256,128]{1,0:T(8,128)S(1)} collective-permute-done((f32[256,128]{1,0:T(8,128)S(1)}, f32[256,128]{1,0:T(8,128)S(1)}, u32[]{:S(2)}, u32[]{:S(2)}) %collective-permute-start.3) | collective-permute-done | bytes 131104 | tf_op jit(solution)/shard_map/ppermute | solution.py:746
  12.7 0.7 %collective-permute-start.7 = (f32[256,128]{1,0:T(8,128)S(1)}, f32[256,128]{1,0:T(8,128)S(1)}, u32[]{:S(2)}, u32[]{:S(2)}) collective-permute-start(f32[256,128]{1,0:T(8,128)S(1)} %collective-permute-done.3.refs_4_), channel_id=1, source_target_pairs={{0,4},{4,0},{8,12},{12,8},{1,5},{5,1},{9,13},{13,9},{2,6},{6,2},{1... | collective-permute-start | bytes 393224 | tf_op jit(solution)/shard_map/ppermute | solution.py:746
  13.3 1.5 %collective-permute-start.5 = (f32[256,128]{1,0:T(8,128)S(1)}, f32[256,128]{1,0:T(8,128)S(1)}, u32[]{:S(2)}, u32[]{:S(2)}) collective-permute-start(f32[256,128]{1,0:T(8,128)S(1)} %collective-permute-done.3.refs_4_), channel_id=1, source_target_pairs={{0,1},{1,0},{2,3},{3,2},{4,5},{5,4},{6,7},{7,6},{8,9},{9,8},{10,11... | collective-permute-start | bytes 393224 | tf_op jit(solution)/shard_map/ppermute | solution.py:771
  14.8 0.0 collective-permute-start
  14.8 0.5 collective-permute-start.4
  15.3 3.1 %collective-permute-done.7.refs_8_ = f32[256,128]{1,0:T(8,128)S(1)} collective-permute-done((f32[256,128]{1,0:T(8,128)S(1)}, f32[256,128]{1,0:T(8,128)S(1)}, u32[]{:S(2)}, u32[]{:S(2)}) %collective-permute-start.7) | collective-permute-done | bytes 131104 | tf_op jit(solution)/shard_map/ppermute | solution.py:746
  18.5 1.5 %collective-permute-start.9 = (f32[256,128]{1,0:T(8,128)S(1)}, f32[256,128]{1,0:T(8,128)S(1)}, u32[]{:S(2)}, u32[]{:S(2)}) collective-permute-start(f32[256,128]{1,0:T(8,128)S(1)} %collective-permute-done.7.refs_8_), channel_id=1, source_target_pairs={{0,1},{1,0},{2,3},{3,2},{4,5},{5,4},{6,7},{7,6},{8,9},{9,8},{10,11... | collective-permute-start | bytes 393224 | tf_op jit(solution)/shard_map/ppermute | solution.py:771
  20.0 0.0 collective-permute-done.1.refs_2_
  20.0 0.0 collective-permute-start.2
  20.0 0.0 collective-permute-done.5.refs_6_
  20.0 0.5 collective-permute-start.8
  20.6 0.0 collective-permute-done.4.refs_5_
  20.6 0.1 collective-permute-start.6
  20.6 2.8 %collective-permute-done.9.refs_10_ = f32[256,128]{1,0:T(8,128)S(1)} collective-permute-done((f32[256,128]{1,0:T(8,128)S(1)}, f32[256,128]{1,0:T(8,128)S(1)}, u32[]{:S(2)}, u32[]{:S(2)}) %collective-permute-start.9) | collective-permute-done | bytes 131104 | tf_op jit(solution)/shard_map/ppermute | solution.py:771
  23.5 0.0 collective-permute-start.10
  23.5 0.0 collective-permute-done.refs_1_
  23.5 0.0 collective-permute-done.8.refs_9_
  23.5 0.0 collective-permute-done.6.refs_7_
  23.5 1.3 %collective-permute-done.10.refs_11_ = f32[256,128]{1,0:T(8,128)S(1)} collective-permute-done((f32[256,128]{1,0:T(8,128)S(1)}, f32[256,128]{1,0:T(8,128)S(1)}, u32[]{:S(2)}, u32[]{:S(2)}) %collective-permute-start.10) | collective-permute-done | bytes 131104 | tf_op jit(solution)/shard_map/ppermute | solution.py:749
  24.8 24.3 %shard_map.70 = (f32[8,64,128]{2,1,0:T(8,128)}, f32[8,32,128]{2,1,0:T(8,128)S(1)}, f32[8,32,128]{2,1,0:T(8,128)S(1)}) custom-call(s32[1,256]{1,0:T(1,128)S(1)} %get-tuple-element.15.cells_ref, f32[512,128]{1,0:T(8,128)S(1)} %get-tuple-element.16.refs_0_, f32[512,128]{1,0:T(8,128)S(1)} %collective-permute-done.refs_1_, ...), custom_call_target="tpu_custom_call" | custom-call | flops 200000000 | bytes 4000000 | tf_op jit(solution)/shard_map/pallas_call | solution.py:777
  49.1 1.5 %collective-permute-start.11 = (f32[8,32,128]{2,1,0:T(8,128)S(1)}, f32[8,32,128]{2,1,0:T(8,128)S(1)}, u32[]{:S(2)}, u32[]{:S(2)}) collective-permute-start(f32[8,32,128]{2,1,0:T(8,128)S(1)} %get-tuple-element.27), channel_id=1, source_target_pairs={{0,1},{1,0},{2,3},{3,2},{4,5},{5,4},{6,7},{7,6},{8,9},{9,8},{10,11... | collective-permute-start | bytes 393224 | tf_op jit(solution)/shard_map/ppermute | solution.py:795
  50.6 4.0 %collective-permute-done.11 = f32[8,32,128]{2,1,0:T(8,128)S(1)} collective-permute-done((f32[8,32,128]{2,1,0:T(8,128)S(1)}, f32[8,32,128]{2,1,0:T(8,128)S(1)}, u32[]{:S(2)}, u32[]{:S(2)}) %collective-permute-start.11) | collective-permute-done | bytes 131104 | tf_op jit(solution)/shard_map/ppermute | solution.py:795
  54.7 0.7 %add.3 = f32[8,32,128]{2,1,0:T(8,128)} add(f32[8,32,128]{2,1,0:T(8,128)S(1)} %get-tuple-element.26, f32[8,32,128]{2,1,0:T(8,128)S(1)} %collective-permute-done.11) | non-fusion elementwise | flops 32768 | bytes 393216 | tf_op jit(solution)/shard_map/add | solution.py:795
  (7 shorter events, 0.0 us)
Async XLA Ops:
  0.6 1.0 %copy-start = (f32[8,64,128]{2,1,0:T(8,128)S(1)}, f32[8,64,128]{2,1,0:T(8,128)}, u32[]{:S(2)}) copy-start(f32[8,64,128]{2,1,0:T(8,128)} %natural_ref.1) | copy-start | bytes 786436
  1.6 6.3 %copy-start.4 = (s32[512,2]{0,1:T(2,128)S(1)}, s32[512,2]{0,1:T(2,128)}, u32[]{:S(2)}) copy-start(s32[512,2]{0,1:T(2,128)} %param.8) | copy-start | bytes 12292
  2.2 10.5 %collective-permute-start.3 = (f32[256,128]{1,0:T(8,128)S(1)}, f32[256,128]{1,0:T(8,128)S(1)}, u32[]{:S(2)}, u32[]{:S(2)}) collective-permute-start(f32[256,128]{1,0:T(8,128)S(1)} %get-tuple-element.17), channel_id=1, source_target_pairs={{0,8},{4,12},{8,0},{12,4},{1,9},{5,13},{9,1},{13,5},{2,10},{6,14},... | collective-permute-start | bytes 393224 | tf_op jit(solution)/shard_map/ppermute | solution.py:746
  6.3 1.7 %copy-start.1 = (f32[1,512]{1,0:T(1,128)S(1)}, f32[1,512]{1,0:T(1,128)}, u32[]{:S(2)}) copy-start(f32[1,512]{1,0:T(1,128)} %observed_ref.1) | copy-start | bytes 6148
  6.3 13.8 %collective-permute-start.1 = (f32[512,128]{1,0:T(8,128)S(1)}, f32[512,128]{1,0:T(8,128)S(1)}, u32[]{:S(2)}, u32[]{:S(2)}) collective-permute-start(f32[512,128]{1,0:T(8,128)S(1)} %get-tuple-element.16.refs_0_), channel_id=1, source_target_pairs={{0,4},{4,0},{8,12},{12,8},{1,5},{5,1},{9,13},{13,9},{2,6},{6,2},{1... | collective-permute-start | bytes 786440 | tf_op jit(solution)/shard_map/ppermute | solution.py:746
  7.9 0.7 %copy-start.3 = (f32[1,256]{1,0:T(1,128)S(1)}, f32[1,256]{1,0:T(1,128)}, u32[]{:S(2)}) copy-start(f32[1,256]{1,0:T(1,128)} %currents_ref.1) | copy-start | bytes 3076
  8.0 0.7 %copy-start.2 = (s32[256]{0:T(256)S(1)}, s32[256]{0:T(256)}, u32[]{:S(2)}) copy-start(s32[256]{0:T(256)} %param.6) | copy-start | bytes 3076
  12.7 5.8 %collective-permute-start.7 = (f32[256,128]{1,0:T(8,128)S(1)}, f32[256,128]{1,0:T(8,128)S(1)}, u32[]{:S(2)}, u32[]{:S(2)}) collective-permute-start(f32[256,128]{1,0:T(8,128)S(1)} %collective-permute-done.3.refs_4_), channel_id=1, source_target_pairs={{0,4},{4,0},{8,12},{12,8},{1,5},{5,1},{9,13},{13,9},{2,6},{6,2},{1... | collective-permute-start | bytes 393224 | tf_op jit(solution)/shard_map/ppermute | solution.py:746
  13.3 6.7 %collective-permute-start.5 = (f32[256,128]{1,0:T(8,128)S(1)}, f32[256,128]{1,0:T(8,128)S(1)}, u32[]{:S(2)}, u32[]{:S(2)}) collective-permute-start(f32[256,128]{1,0:T(8,128)S(1)} %collective-permute-done.3.refs_4_), channel_id=1, source_target_pairs={{0,1},{1,0},{2,3},{3,2},{4,5},{5,4},{6,7},{7,6},{8,9},{9,8},{10,11... | collective-permute-start | bytes 393224 | tf_op jit(solution)/shard_map/ppermute | solution.py:771
  14.8 8.6 %collective-permute-start = (f32[512,128]{1,0:T(8,128)S(1)}, f32[512,128]{1,0:T(8,128)S(1)}, u32[]{:S(2)}, u32[]{:S(2)}) collective-permute-start(f32[512,128]{1,0:T(8,128)S(1)} %get-tuple-element.16.refs_0_), channel_id=1, source_target_pairs={{0,2},{2,0},{1,3},{3,1},{4,6},{6,4},{5,7},{7,5},{8,10},{10,8},{9,1... | collective-permute-start | bytes 786440 | tf_op jit(solution)/shard_map/ppermute | solution.py:749
  14.8 5.7 %collective-permute-start.4 = (f32[256,128]{1,0:T(8,128)S(1)}, f32[256,128]{1,0:T(8,128)S(1)}, u32[]{:S(2)}, u32[]{:S(2)}) collective-permute-start(f32[256,128]{1,0:T(8,128)S(1)} %collective-permute-done.3.refs_4_), channel_id=1, source_target_pairs={{0,2},{2,0},{1,3},{3,1},{4,6},{6,4},{5,7},{7,5},{8,10},{10,8},{9,1... | collective-permute-start | bytes 393224 | tf_op jit(solution)/shard_map/ppermute | solution.py:749
  18.5 5.0 %collective-permute-start.9 = (f32[256,128]{1,0:T(8,128)S(1)}, f32[256,128]{1,0:T(8,128)S(1)}, u32[]{:S(2)}, u32[]{:S(2)}) collective-permute-start(f32[256,128]{1,0:T(8,128)S(1)} %collective-permute-done.7.refs_8_), channel_id=1, source_target_pairs={{0,1},{1,0},{2,3},{3,2},{4,5},{5,4},{6,7},{7,6},{8,9},{9,8},{10,11... | collective-permute-start | bytes 393224 | tf_op jit(solution)/shard_map/ppermute | solution.py:771
  20.0 4.8 %collective-permute-start.2 = (f32[512,128]{1,0:T(8,128)S(1)}, f32[512,128]{1,0:T(8,128)S(1)}, u32[]{:S(2)}, u32[]{:S(2)}) collective-permute-start(f32[512,128]{1,0:T(8,128)S(1)} %collective-permute-done.1.refs_2_), channel_id=1, source_target_pairs={{0,2},{2,0},{1,3},{3,1},{4,6},{6,4},{5,7},{7,5},{8,10},{10,8},{9,1... | collective-permute-start | bytes 786440 | tf_op jit(solution)/shard_map/ppermute | solution.py:749
  20.0 3.4 %collective-permute-start.8 = (f32[256,128]{1,0:T(8,128)S(1)}, f32[256,128]{1,0:T(8,128)S(1)}, u32[]{:S(2)}, u32[]{:S(2)}) collective-permute-start(f32[256,128]{1,0:T(8,128)S(1)} %collective-permute-done.7.refs_8_), channel_id=1, source_target_pairs={{0,2},{2,0},{1,3},{3,1},{4,6},{6,4},{5,7},{7,5},{8,10},{10,8},{9,1... | collective-permute-start | bytes 393224 | tf_op jit(solution)/shard_map/ppermute | solution.py:749
  20.6 2.9 %collective-permute-start.6 = (f32[256,128]{1,0:T(8,128)S(1)}, f32[256,128]{1,0:T(8,128)S(1)}, u32[]{:S(2)}, u32[]{:S(2)}) collective-permute-start(f32[256,128]{1,0:T(8,128)S(1)} %collective-permute-done.5.refs_6_), channel_id=1, source_target_pairs={{0,2},{2,0},{1,3},{3,1},{4,6},{6,4},{5,7},{7,5},{8,10},{10,8},{9,1... | collective-permute-start | bytes 393224 | tf_op jit(solution)/shard_map/ppermute | solution.py:749
  23.5 1.3 %collective-permute-start.10 = (f32[256,128]{1,0:T(8,128)S(1)}, f32[256,128]{1,0:T(8,128)S(1)}, u32[]{:S(2)}, u32[]{:S(2)}) collective-permute-start(f32[256,128]{1,0:T(8,128)S(1)} %collective-permute-done.9.refs_10_), channel_id=1, source_target_pairs={{0,2},{2,0},{1,3},{3,1},{4,6},{6,4},{5,7},{7,5},{8,10},{10,8},{9,1... | collective-permute-start | bytes 393224 | tf_op jit(solution)/shard_map/ppermute | solution.py:749
  49.1 5.5 %collective-permute-start.11 = (f32[8,32,128]{2,1,0:T(8,128)S(1)}, f32[8,32,128]{2,1,0:T(8,128)S(1)}, u32[]{:S(2)}, u32[]{:S(2)}) collective-permute-start(f32[8,32,128]{2,1,0:T(8,128)S(1)} %get-tuple-element.27), channel_id=1, source_target_pairs={{0,1},{1,0},{2,3},{3,2},{4,5},{5,4},{6,7},{7,6},{8,9},{9,8},{10,11... | collective-permute-start | bytes 393224 | tf_op jit(solution)/shard_map/ppermute | solution.py:795

commit v9 on v8

--- a/solution.py
+++ b/solution.py
@@ -295,6 +295,8 @@
                 total = (next_x + cond[x - 1, z]) + (ahead + cond[x, z - 1]) + (next_y + last_y)
                 total = 3.0 * here + 0.5 * total
                 self.weight[x, z] = DAMPING / total
+                if n == SIDE:
+                    self.base[x, z] = jnp.zeros_like(here)
                 self.back[x, z] = total * (self.scale / DAMPING)
                 self.link_x[x, z] = 0.5 * (here + next_x)
                 link = 0.5 * (here + next_y)
@@ -371,9 +373,9 @@
             for z, here, sums in self.rows(self.second, x):
                 result = []
                 for p in range(2):
-                    total = self.base[x + p, z] + sums[p]
-                    self.first[x + p, z] = (1.0 - DAMPING) * here[p] + total
-                    result.append((total - DAMPING * here[p]) * self.back[x + p, z])
+                    swept = (1.0 - DAMPING) * here[p] + (self.base[x + p, z] + sums[p])
+                    self.first[x + p, z] = swept
+                    result.append((swept - here[p]) * self.back[x + p, z])
                 yield result
 
         self.halve(residuals, coarse)
@@ -503,8 +505,10 @@
     mine_ref,
     theirs_ref,
     gathered,
-    weights,
     owned,
+    beside,
+    sent,
+    sem,
     *level_refs,
 ):
     f32 = jnp.float32
@@ -644,6 +648,10 @@
         level.ascend(lambda x, z: below.first[x, z], out, exact)
 
     spot = spot_ref[...]
+    at_spot = iota((LANES, electrodes), 0) == spot
+    order = lane_order()
+    wide = SIDE + 2
+    sending = pltpu.make_async_copy(sent, potentials_ref, sem)
 
     def each(body):
         def one(electrode, carry):
@@ -652,57 +660,50 @@
 
         lax.fori_loop(0, electrodes, one, 0, unroll=32)
 
-    def weigh(electrode, cell):
-        weights[electrode, :] = fine.weight.ref[cell, :]
-
-    each(weigh)
-    fine.base.ref[...] = jnp.zeros_like(fine.base.ref)
-
-    def spread(rows):
-        gathered[...] = rows * weights[...]
-
-        def put(electrode, cell):
-            fine.base.ref[cell, :] = gathered[electrode, :]
-
+    def put(electrode, cell):
+        fine.base.ref[cell, :] = gathered[electrode, :] * fine.weight.ref[cell, :]
+
+    def read(electrode, cell):
+        gathered[electrode, :] = forward.ref[cell, :]
+
+    def exact(row, dims):
+        return product(jnp.broadcast_to(row, (16, row.shape[1])), pairs_ref[...], 3, dims)[0:1]
+
+    def own(x, z, y=0):
+        return forward.ref[pl.ds(forward.start(x, z, y) + device, SIDE, stride=SIDE), :]
+
+    def solve(index):
         each(put)
         rolled(SIDE, fine.base.close_z)
         fine.base.close()
-
-    spread(rows_ref[...])
-    cycle(0, forward, exact=True)
-
-    def read(electrode, cell):
-        gathered[electrode, :] = forward.ref[cell, :]
-
-    each(read)
-    at_spot = iota((LANES, electrodes), 0) == spot
-    readings = jnp.sum(jnp.where(at_spot, gathered[...].T, 0.0), axis=0, keepdims=True)
-    pairs = pairs_ref[...]
-
-    def exact(row, dims):
-        return product(jnp.broadcast_to(row, (16, row.shape[1])), pairs, 3, dims)[0:1]
-
-    misfit = exact(readings, ((1,), (1,))) - observed_ref[...]
-    spread(shared_rows(exact(misfit, ((1,), (0,))), spot, same_ref[...]))
-    cycle(0, fine.first, exact=True)
-
-    order = lane_order()
-    adjoint = fine.first
-    chunk = mine_ref.shape[1]
-    even = shot == 0
-
-    def own(field, x, z, y=0):
-        return field.ref[pl.ds(field.start(x, z, y) + device, SIDE, stride=SIDE), :]
-
-    wide = SIDE + 2
-    for index, field in enumerate((forward, adjoint)):
+        cycle(0, forward, exact=True)
         for x in range(-1, SIDE + 1):
             for z in range(-1, SIDE + 1):
                 if 0 <= x < SIDE or 0 <= z < SIDE:
-                    owned[index, (x + 1) * wide + z + 1] = own(field, x, z)
-
+                    owned[index, (x + 1) * wide + z + 1] = own(x, z)
+                if 0 <= x < SIDE and 0 <= z < SIDE:
+                    for side, y in enumerate((1, -1)):
+                        beside[index, side, x * SIDE + z] = own(x, z, y)
+
+        @pl.when(index == 0)
+        def _():
+            for x in range(SIDE):
+                tiles = [owned[0, (x + 1) * wide + z + 1] for z in range(SIDE)]
+                sent[x] = from_blocks(tiles, order)
+            sending.start()
+            each(read)
+            readings = jnp.where(at_spot, gathered[...].T, 0.0)
+            readings = jnp.sum(readings, axis=0, keepdims=True)
+            misfit = exact(readings, ((1,), (1,))) - observed_ref[...]
+            gathered[...] = shared_rows(exact(misfit, ((1,), (0,))), spot, same_ref[...])
+
+    gathered[...] = rows_ref[...]
+    rolled(2, solve)
+
+    chunk = mine_ref.shape[1]
+    even = shot == 0
     for x in range(SIDE):
-        tiles_u, tiles_g = [], []
+        tiles = []
         for z in range(SIDE):
             at = (x + 1) * wide + z + 1
             here_u, here_w = owned[0, at], owned[1, at]
@@ -710,15 +711,15 @@
             for step in (wide, -wide, 1, -1):
                 term = (here_u - owned[0, at + step]) * (here_w - owned[1, at + step])
                 total = term if total is None else total + term
-            for y in (1, -1):
-                total = total + (here_u - own(forward, x, z, y)) * (here_w - own(adjoint, x, z, y))
-            tiles_u.append(here_u)
-            tiles_g.append(-0.5 * total)
-        potentials_ref[x] = from_blocks(tiles_u, order)
-        natural = from_blocks(tiles_g, order)
+            for side in range(2):
+                other_u, other_w = beside[0, side, x * SIDE + z], beside[1, side, x * SIDE + z]
+                total = total + (here_u - other_u) * (here_w - other_w)
+            tiles.append(-0.5 * total)
+        natural = from_blocks(tiles, order)
         low, high = natural[:chunk], natural[chunk:]
         mine_ref[x] = jnp.where(even, low, high)
         theirs_ref[x] = jnp.where(even, high, low)
+    sending.wait()
 
 
 def replicated(conductivity, stations, currents, receivers, observed):
@@ -782,11 +783,13 @@
             jax.ShapeDtypeStruct((rows, chunk, LANES), f32),
         ),
         in_specs=[smem] + [vmem] * (len(parts) + len(halved) + 5),
-        out_specs=(vmem, vmem, vmem),
+        out_specs=(pl.BlockSpec(memory_space=pl.ANY), vmem, vmem),
         scratch_shapes=[
             pltpu.VMEM((electrodes, LANES), f32),
-            pltpu.VMEM((electrodes, LANES), f32),
             pltpu.VMEM((2, (SIDE + 2) ** 2, SIDE, LANES), f32),
+            pltpu.VMEM((2, 2, SIDE**2, SIDE, LANES), f32),
+            pltpu.VMEM((rows, cols, LANES), f32),
+            pltpu.SemaphoreType.DMA,
         ]
         + levels,
         compiler_params=pltpu.CompilerParams(vmem_limit_bytes=VMEM_BYTES),

time: 55.5 us -> 55.1 us (level)
  no operation moved by 1% of the time
where the time goes in v9:
time: 55.1 us; the launch traced here: 55 us
  Pallas kernels  24.8 us (45%)
  waiting for transfers between devices  14.9 us (27%)
  starting transfers between devices  12.1 us (22%)
  local copies, waits for them, and re-layouts  1.76 us (3%)
  between operations  0.71 us (1%)
  other arithmetic  0.67 us (1%)
    pallas_call x1, Pallas kernels, replicated(): pl.pallas_call(functools.partial(replicated_kernel, len(parts), len(halve...  23.8 us
    ppermute x3, waiting for transfers between devices, partner(): return lax.ppermute(part, 'gx', [(i, i ^ k) for i in range(count)])  6.72 us
    ppermute x3, starting transfers between devices, partner(): return lax.ppermute(part, 'gx', [(i, i ^ k) for i in range(count)])  6.34 us
    ppermute x1, waiting for transfers between devices, replicated(): return (potentials[None], own + lax.ppermute(theirs, 'shot', swap))  4.01 us
    ppermute x2, starting transfers between devices, replicated(): lax.ppermute(own, 'shot', swap)  3.03 us
    ppermute x2, waiting for transfers between devices, replicated(): lax.ppermute(own, 'shot', swap)  2.84 us
    unnamed x11, local copies, waits for them, and re-layouts  1.76 us
    ppermute x1, starting transfers between devices, replicated(): return (potentials[None], own + lax.ppermute(theirs, 'shot', swap))  1.6 us
  transfers between devices with their start and end apart: 12, of which 5 were waited for; matrix products, arithmetic and copies ran while one was open for 0% of the time, Pallas kernels for 1%

profile of v9, /device:TPU:0, one launch (start us, length us, event | category | flops | bytes accessed | tf_op | source)
XLA Modules:
  0.0 55.0 jit_solution(11607436295600368519)
XLA Ops:
  0.6 0.9 %copy-done = f32[8,64,128]{2,1,0:T(8,128)S(1)} copy-done((f32[8,64,128]{2,1,0:T(8,128)S(1)}, f32[8,64,128]{2,1,0:T(8,128)}, u32[]{:S(2)}) %copy-start) | copy-done | bytes 262168
  1.6 0.6 %shard_map.69 = (f32[512,128]{1,0:T(8,128)S(1)}, f32[256,128]{1,0:T(8,128)S(1)}) custom-call(f32[8,64,128]{2,1,0:T(8,128)S(1)} %copy-done), custom_call_target="tpu_custom_call" | custom-call | tf_op jit(solution)/shard_map/pallas_call | solution.py:733
  2.2 4.1 %collective-permute-start.3 = (f32[256,128]{1,0:T(8,128)S(1)}, f32[256,128]{1,0:T(8,128)S(1)}, u32[]{:S(2)}, u32[]{:S(2)}) collective-permute-start(f32[256,128]{1,0:T(8,128)S(1)} %get-tuple-element.17), channel_id=1, source_target_pairs={{0,8},{4,12},{8,0},{12,4},{1,9},{5,13},{9,1},{13,5},{2,10},{6,14},... | collective-permute-start | bytes 393224 | tf_op jit(solution)/shard_map/ppermute | solution.py:747
  6.3 1.6 %collective-permute-start.1 = (f32[512,128]{1,0:T(8,128)S(1)}, f32[512,128]{1,0:T(8,128)S(1)}, u32[]{:S(2)}, u32[]{:S(2)}) collective-permute-start(f32[512,128]{1,0:T(8,128)S(1)} %get-tuple-element.16.refs_0_), channel_id=1, source_target_pairs={{0,4},{4,0},{8,12},{12,8},{1,5},{5,1},{9,13},{13,9},{2,6},{6,2},{1... | collective-permute-start | bytes 786440 | tf_op jit(solution)/shard_map/ppermute | solution.py:747
  7.9 0.1 copy.7.receivers_ref
  8.0 0.0 copy-start.2
  8.0 0.5 copy-done.3
  8.5 0.2 copy-done.2
  8.7 0.4 shard_map.68
  9.1 3.6 %collective-permute-done.3.refs_4_ = f32[256,128]{1,0:T(8,128)S(1)} collective-permute-done((f32[256,128]{1,0:T(8,128)S(1)}, f32[256,128]{1,0:T(8,128)S(1)}, u32[]{:S(2)}, u32[]{:S(2)}) %collective-permute-start.3) | collective-permute-done | bytes 131104 | tf_op jit(solution)/shard_map/ppermute | solution.py:747
  12.7 0.7 %collective-permute-start.7 = (f32[256,128]{1,0:T(8,128)S(1)}, f32[256,128]{1,0:T(8,128)S(1)}, u32[]{:S(2)}, u32[]{:S(2)}) collective-permute-start(f32[256,128]{1,0:T(8,128)S(1)} %collective-permute-done.3.refs_4_), channel_id=1, source_target_pairs={{0,4},{4,0},{8,12},{12,8},{1,5},{5,1},{9,13},{13,9},{2,6},{6,2},{1... | collective-permute-start | bytes 393224 | tf_op jit(solution)/shard_map/ppermute | solution.py:747
  13.3 1.5 %collective-permute-start.5 = (f32[256,128]{1,0:T(8,128)S(1)}, f32[256,128]{1,0:T(8,128)S(1)}, u32[]{:S(2)}, u32[]{:S(2)}) collective-permute-start(f32[256,128]{1,0:T(8,128)S(1)} %collective-permute-done.3.refs_4_), channel_id=1, source_target_pairs={{0,1},{1,0},{2,3},{3,2},{4,5},{5,4},{6,7},{7,6},{8,9},{9,8},{10,11... | collective-permute-start | bytes 393224 | tf_op jit(solution)/shard_map/ppermute | solution.py:772
  14.8 0.0 collective-permute-start
  14.8 0.5 collective-permute-start.4
  15.3 3.1 %collective-permute-done.7.refs_8_ = f32[256,128]{1,0:T(8,128)S(1)} collective-permute-done((f32[256,128]{1,0:T(8,128)S(1)}, f32[256,128]{1,0:T(8,128)S(1)}, u32[]{:S(2)}, u32[]{:S(2)}) %collective-permute-start.7) | collective-permute-done | bytes 131104 | tf_op jit(solution)/shard_map/ppermute | solution.py:747
  18.5 1.5 %collective-permute-start.9 = (f32[256,128]{1,0:T(8,128)S(1)}, f32[256,128]{1,0:T(8,128)S(1)}, u32[]{:S(2)}, u32[]{:S(2)}) collective-permute-start(f32[256,128]{1,0:T(8,128)S(1)} %collective-permute-done.7.refs_8_), channel_id=1, source_target_pairs={{0,1},{1,0},{2,3},{3,2},{4,5},{5,4},{6,7},{7,6},{8,9},{9,8},{10,11... | collective-permute-start | bytes 393224 | tf_op jit(solution)/shard_map/ppermute | solution.py:772
  20.0 0.0 collective-permute-done.1.refs_2_
  20.0 0.0 collective-permute-start.2
  20.0 0.0 collective-permute-done.5.refs_6_
  20.0 0.5 collective-permute-start.8
  20.6 0.0 collective-permute-done.4.refs_5_
  20.6 0.1 collective-permute-start.6
  20.6 2.8 %collective-permute-done.9.refs_10_ = f32[256,128]{1,0:T(8,128)S(1)} collective-permute-done((f32[256,128]{1,0:T(8,128)S(1)}, f32[256,128]{1,0:T(8,128)S(1)}, u32[]{:S(2)}, u32[]{:S(2)}) %collective-permute-start.9) | collective-permute-done | bytes 131104 | tf_op jit(solution)/shard_map/ppermute | solution.py:772
  23.5 0.0 collective-permute-start.10
  23.5 0.0 collective-permute-done.refs_1_
  23.5 0.0 collective-permute-done.6.refs_7_
  23.5 1.3 %collective-permute-done.10.refs_11_ = f32[256,128]{1,0:T(8,128)S(1)} collective-permute-done((f32[256,128]{1,0:T(8,128)S(1)}, f32[256,128]{1,0:T(8,128)S(1)}, u32[]{:S(2)}, u32[]{:S(2)}) %collective-permute-start.10) | collective-permute-done | bytes 131104 | tf_op jit(solution)/shard_map/ppermute | solution.py:750
  24.8 0.0 collective-permute-done.2.refs_3_
  24.8 23.8 %shard_map.70 = (f32[8,64,128]{2,1,0:T(8,128)}, f32[8,32,128]{2,1,0:T(8,128)S(1)}, f32[8,32,128]{2,1,0:T(8,128)S(1)}) custom-call(s32[1,256]{1,0:T(1,128)S(1)} %get-tuple-element.15.cells_ref, f32[512,128]{1,0:T(8,128)S(1)} %get-tuple-element.16.refs_0_, f32[512,128]{1,0:T(8,128)S(1)} %collective-permute-done.refs_1_, ...), custom_call_target="tpu_custom_call" | custom-call | flops 200000000 | bytes 4000000 | tf_op jit(solution)/shard_map/pallas_call | solution.py:778
  48.7 1.6 %collective-permute-start.11 = (f32[8,32,128]{2,1,0:T(8,128)S(1)}, f32[8,32,128]{2,1,0:T(8,128)S(1)}, u32[]{:S(2)}, u32[]{:S(2)}) collective-permute-start(f32[8,32,128]{2,1,0:T(8,128)S(1)} %get-tuple-element.27), channel_id=1, source_target_pairs={{0,1},{1,0},{2,3},{3,2},{4,5},{5,4},{6,7},{7,6},{8,9},{9,8},{10,11... | collective-permute-start | bytes 393224 | tf_op jit(solution)/shard_map/ppermute | solution.py:798
  50.3 4.0 %collective-permute-done.11 = f32[8,32,128]{2,1,0:T(8,128)S(1)} collective-permute-done((f32[8,32,128]{2,1,0:T(8,128)S(1)}, f32[8,32,128]{2,1,0:T(8,128)S(1)}, u32[]{:S(2)}, u32[]{:S(2)}) %collective-permute-start.11) | collective-permute-done | bytes 131104 | tf_op jit(solution)/shard_map/ppermute | solution.py:798
  54.3 0.7 %add.3 = f32[8,32,128]{2,1,0:T(8,128)} add(f32[8,32,128]{2,1,0:T(8,128)S(1)} %get-tuple-element.26, f32[8,32,128]{2,1,0:T(8,128)S(1)} %collective-permute-done.11) | non-fusion elementwise | flops 32768 | bytes 393216 | tf_op jit(solution)/shard_map/add | solution.py:798
  (7 shorter events, 0.0 us)
Async XLA Ops:
  0.6 1.0 %copy-start = (f32[8,64,128]{2,1,0:T(8,128)S(1)}, f32[8,64,128]{2,1,0:T(8,128)}, u32[]{:S(2)}) copy-start(f32[8,64,128]{2,1,0:T(8,128)} %natural_ref.1) | copy-start | bytes 786436
  1.6 6.3 %copy-start.4 = (s32[512,2]{0,1:T(2,128)S(1)}, s32[512,2]{0,1:T(2,128)}, u32[]{:S(2)}) copy-start(s32[512,2]{0,1:T(2,128)} %param.8) | copy-start | bytes 12292
  2.2 10.5 %collective-permute-start.3 = (f32[256,128]{1,0:T(8,128)S(1)}, f32[256,128]{1,0:T(8,128)S(1)}, u32[]{:S(2)}, u32[]{:S(2)}) collective-permute-start(f32[256,128]{1,0:T(8,128)S(1)} %get-tuple-element.17), channel_id=1, source_target_pairs={{0,8},{4,12},{8,0},{12,4},{1,9},{5,13},{9,1},{13,5},{2,10},{6,14},... | collective-permute-start | bytes 393224 | tf_op jit(solution)/shard_map/ppermute | solution.py:747
  6.3 1.7 %copy-start.1 = (f32[1,512]{1,0:T(1,128)S(1)}, f32[1,512]{1,0:T(1,128)}, u32[]{:S(2)}) copy-start(f32[1,512]{1,0:T(1,128)} %observed_ref.1) | copy-start | bytes 6148
  6.3 13.8 %collective-permute-start.1 = (f32[512,128]{1,0:T(8,128)S(1)}, f32[512,128]{1,0:T(8,128)S(1)}, u32[]{:S(2)}, u32[]{:S(2)}) collective-permute-start(f32[512,128]{1,0:T(8,128)S(1)} %get-tuple-element.16.refs_0_), channel_id=1, source_target_pairs={{0,4},{4,0},{8,12},{12,8},{1,5},{5,1},{9,13},{13,9},{2,6},{6,2},{1... | collective-permute-start | bytes 786440 | tf_op jit(solution)/shard_map/ppermute | solution.py:747
  7.9 0.7 %copy-start.3 = (f32[1,256]{1,0:T(1,128)S(1)}, f32[1,256]{1,0:T(1,128)}, u32[]{:S(2)}) copy-start(f32[1,256]{1,0:T(1,128)} %currents_ref.1) | copy-start | bytes 3076
  8.0 0.7 %copy-start.2 = (s32[256]{0:T(256)S(1)}, s32[256]{0:T(256)}, u32[]{:S(2)}) copy-start(s32[256]{0:T(256)} %param.6) | copy-start | bytes 3076
  12.7 5.8 %collective-permute-start.7 = (f32[256,128]{1,0:T(8,128)S(1)}, f32[256,128]{1,0:T(8,128)S(1)}, u32[]{:S(2)}, u32[]{:S(2)}) collective-permute-start(f32[256,128]{1,0:T(8,128)S(1)} %collective-permute-done.3.refs_4_), channel_id=1, source_target_pairs={{0,4},{4,0},{8,12},{12,8},{1,5},{5,1},{9,13},{13,9},{2,6},{6,2},{1... | collective-permute-start | bytes 393224 | tf_op jit(solution)/shard_map/ppermute | solution.py:747
  13.3 6.7 %collective-permute-start.5 = (f32[256,128]{1,0:T(8,128)S(1)}, f32[256,128]{1,0:T(8,128)S(1)}, u32[]{:S(2)}, u32[]{:S(2)}) collective-permute-start(f32[256,128]{1,0:T(8,128)S(1)} %collective-permute-done.3.refs_4_), channel_id=1, source_target_pairs={{0,1},{1,0},{2,3},{3,2},{4,5},{5,4},{6,7},{7,6},{8,9},{9,8},{10,11... | collective-permute-start | bytes 393224 | tf_op jit(solution)/shard_map/ppermute | solution.py:772
  14.8 8.6 %collective-permute-start = (f32[512,128]{1,0:T(8,128)S(1)}, f32[512,128]{1,0:T(8,128)S(1)}, u32[]{:S(2)}, u32[]{:S(2)}) collective-permute-start(f32[512,128]{1,0:T(8,128)S(1)} %get-tuple-element.16.refs_0_), channel_id=1, source_target_pairs={{0,2},{2,0},{1,3},{3,1},{4,6},{6,4},{5,7},{7,5},{8,10},{10,8},{9,1... | collective-permute-start | bytes 786440 | tf_op jit(solution)/shard_map/ppermute | solution.py:750
  14.8 5.7 %collective-permute-start.4 = (f32[256,128]{1,0:T(8,128)S(1)}, f32[256,128]{1,0:T(8,128)S(1)}, u32[]{:S(2)}, u32[]{:S(2)}) collective-permute-start(f32[256,128]{1,0:T(8,128)S(1)} %collective-permute-done.3.refs_4_), channel_id=1, source_target_pairs={{0,2},{2,0},{1,3},{3,1},{4,6},{6,4},{5,7},{7,5},{8,10},{10,8},{9,1... | collective-permute-start | bytes 393224 | tf_op jit(solution)/shard_map/ppermute | solution.py:750
  18.5 5.0 %collective-permute-start.9 = (f32[256,128]{1,0:T(8,128)S(1)}, f32[256,128]{1,0:T(8,128)S(1)}, u32[]{:S(2)}, u32[]{:S(2)}) collective-permute-start(f32[256,128]{1,0:T(8,128)S(1)} %collective-permute-done.7.refs_8_), channel_id=1, source_target_pairs={{0,1},{1,0},{2,3},{3,2},{4,5},{5,4},{6,7},{7,6},{8,9},{9,8},{10,11... | collective-permute-start | bytes 393224 | tf_op jit(solution)/shard_map/ppermute | solution.py:772
  20.0 4.8 %collective-permute-start.2 = (f32[512,128]{1,0:T(8,128)S(1)}, f32[512,128]{1,0:T(8,128)S(1)}, u32[]{:S(2)}, u32[]{:S(2)}) collective-permute-start(f32[512,128]{1,0:T(8,128)S(1)} %collective-permute-done.1.refs_2_), channel_id=1, source_target_pairs={{0,2},{2,0},{1,3},{3,1},{4,6},{6,4},{5,7},{7,5},{8,10},{10,8},{9,1... | collective-permute-start | bytes 786440 | tf_op jit(solution)/shard_map/ppermute | solution.py:750
  20.0 3.4 %collective-permute-start.8 = (f32[256,128]{1,0:T(8,128)S(1)}, f32[256,128]{1,0:T(8,128)S(1)}, u32[]{:S(2)}, u32[]{:S(2)}) collective-permute-start(f32[256,128]{1,0:T(8,128)S(1)} %collective-permute-done.7.refs_8_), channel_id=1, source_target_pairs={{0,2},{2,0},{1,3},{3,1},{4,6},{6,4},{5,7},{7,5},{8,10},{10,8},{9,1... | collective-permute-start | bytes 393224 | tf_op jit(solution)/shard_map/ppermute | solution.py:750
  20.6 2.9 %collective-permute-start.6 = (f32[256,128]{1,0:T(8,128)S(1)}, f32[256,128]{1,0:T(8,128)S(1)}, u32[]{:S(2)}, u32[]{:S(2)}) collective-permute-start(f32[256,128]{1,0:T(8,128)S(1)} %collective-permute-done.5.refs_6_), channel_id=1, source_target_pairs={{0,2},{2,0},{1,3},{3,1},{4,6},{6,4},{5,7},{7,5},{8,10},{10,8},{9,1... | collective-permute-start | bytes 393224 | tf_op jit(solution)/shard_map/ppermute | solution.py:750
  23.5 1.3 %collective-permute-start.10 = (f32[256,128]{1,0:T(8,128)S(1)}, f32[256,128]{1,0:T(8,128)S(1)}, u32[]{:S(2)}, u32[]{:S(2)}) collective-permute-start(f32[256,128]{1,0:T(8,128)S(1)} %collective-permute-done.9.refs_10_), channel_id=1, source_target_pairs={{0,2},{2,0},{1,3},{3,1},{4,6},{6,4},{5,7},{7,5},{8,10},{10,8},{9,1... | collective-permute-start | bytes 393224 | tf_op jit(solution)/shard_map/ppermute | solution.py:750
  48.7 5.6 %collective-permute-start.11 = (f32[8,32,128]{2,1,0:T(8,128)S(1)}, f32[8,32,128]{2,1,0:T(8,128)S(1)}, u32[]{:S(2)}, u32[]{:S(2)}) collective-permute-start(f32[8,32,128]{2,1,0:T(8,128)S(1)} %get-tuple-element.27), channel_id=1, source_target_pairs={{0,1},{1,0},{2,3},{3,2},{4,5},{5,4},{6,7},{7,6},{8,9},{9,8},{10,11... | collective-permute-start | bytes 393224 | tf_op jit(solution)/shard_map/ppermute | solution.py:798

commit v10 on v9

--- a/solution.py
+++ b/solution.py
@@ -203,6 +203,12 @@
         if z == n - 1:
             edge = block_down(value, 2)
             self[x, -1] = inside_down(edge, 2) if exact else edge
+        if x == 0:
+            edge = block_up(value, 0)
+            self[n, z] = inside_up(edge, 0) if exact else edge
+        if x == n - 1:
+            edge = block_down(value, 0)
+            self[-1, z] = inside_down(edge, 0) if exact else edge
         if exact:
             after = inside_up(block_up(value[:1], 1), 1)
             self.ref[pl.ds(self.start(x, z, n), SIDE), :] = after[0]
@@ -275,11 +281,8 @@
         return [pltpu.VMEM((size * SIDE, LANES), jnp.float32) for size in sizes]
 
     def pairs(self, body):
-        if self.side == SIDE:
-            rolled(self.side // 2, lambda i: body(2 * i))
-        else:
-            for i in range(self.side // 2):
-                body(2 * i)
+        for i in range(self.side // 2):
+            body(2 * i)
 
     def prepare(self):
         n = self.side
@@ -352,7 +355,6 @@
                     out.put(x + p, z, value, exact)
 
         self.pairs(pair)
-        out.close(exact)
 
     def halve(self, rows, coarse):
         def pair(x):
@@ -396,7 +398,6 @@
                 here = ahead
 
         self.pairs(pair)
-        self.second.close()
         self.sweep(self.second, out, exact)
 
 
@@ -479,7 +480,6 @@
         field = self.sums(copied, change)
         for (x, z), value in self.swept(field, base).items():
             out.put(x, z, value)
-        out.close()
 
 
 def replicated_kernel(
@@ -565,8 +565,6 @@
             ],
             coarse,
         )
-        if below is not None:
-            below.cond.close(exact=True)
 
     keep = iota((1, SIDE, LANES), 1) % 2 == 0
     lane = iota((1, SIDE, LANES), 2)
@@ -643,7 +641,6 @@
                     x, z, below.weight[x, z] * (row * (1.0 / below.scale))
                 )
             )
-            below.base.close()
             cycle(index + 1, below.first)
         level.ascend(lambda x, z: below.first[x, z], out, exact)
 

time: 55.1 us -> 54.9 us (level)
  no operation moved by 1% of the time
where the time goes in v10:
time: 54.9 us; the launch traced here: 54.7 us
  Pallas kernels  24.6 us (45%)
  waiting for transfers between devices  14.9 us (27%)
  starting transfers between devices  12.1 us (22%)
  local copies, waits for them, and re-layouts  1.76 us (3%)
  between operations  0.71 us (1%)
  other arithmetic  0.67 us (1%)
    pallas_call x1, Pallas kernels, replicated(): pl.pallas_call(functools.partial(replicated_kernel, len(parts), len(halve...  23.6 us
    ppermute x3, waiting for transfers between devices, partner(): return lax.ppermute(part, 'gx', [(i, i ^ k) for i in range(count)])  6.72 us
    ppermute x3, starting transfers between devices, partner(): return lax.ppermute(part, 'gx', [(i, i ^ k) for i in range(count)])  6.34 us
    ppermute x1, waiting for transfers between devices, replicated(): return (potentials[None], own + lax.ppermute(theirs, 'shot', swap))  4.01 us
    ppermute x2, starting transfers between devices, replicated(): lax.ppermute(own, 'shot', swap)  3.03 us
    ppermute x2, waiting for transfers between devices, replicated(): lax.ppermute(own, 'shot', swap)  2.84 us
    unnamed x11, local copies, waits for them, and re-layouts  1.76 us
    ppermute x1, starting transfers between devices, replicated(): return (potentials[None], own + lax.ppermute(theirs, 'shot', swap))  1.6 us
  transfers between devices with their start and end apart: 12, of which 5 were waited for; matrix products, arithmetic and copies ran while one was open for 0% of the time, Pallas kernels for 1%

profile of v10, /device:TPU:0, one launch (start us, length us, event | category | flops | bytes accessed | tf_op | source)
XLA Modules:
  0.0 54.7 jit_solution(8131186335100478790)
XLA Ops:
  0.6 0.9 %copy-done = f32[8,64,128]{2,1,0:T(8,128)S(1)} copy-done((f32[8,64,128]{2,1,0:T(8,128)S(1)}, f32[8,64,128]{2,1,0:T(8,128)}, u32[]{:S(2)}) %copy-start) | copy-done | bytes 262168
  1.6 0.6 %shard_map.69 = (f32[512,128]{1,0:T(8,128)S(1)}, f32[256,128]{1,0:T(8,128)S(1)}) custom-call(f32[8,64,128]{2,1,0:T(8,128)S(1)} %copy-done), custom_call_target="tpu_custom_call" | custom-call | tf_op jit(solution)/shard_map/pallas_call | solution.py:730
  2.2 4.1 %collective-permute-start.3 = (f32[256,128]{1,0:T(8,128)S(1)}, f32[256,128]{1,0:T(8,128)S(1)}, u32[]{:S(2)}, u32[]{:S(2)}) collective-permute-start(f32[256,128]{1,0:T(8,128)S(1)} %get-tuple-element.17), channel_id=1, source_target_pairs={{0,8},{4,12},{8,0},{12,4},{1,9},{5,13},{9,1},{13,5},{2,10},{6,14},... | collective-permute-start | bytes 393224 | tf_op jit(solution)/shard_map/ppermute | solution.py:744
  6.3 1.6 %collective-permute-start.1 = (f32[512,128]{1,0:T(8,128)S(1)}, f32[512,128]{1,0:T(8,128)S(1)}, u32[]{:S(2)}, u32[]{:S(2)}) collective-permute-start(f32[512,128]{1,0:T(8,128)S(1)} %get-tuple-element.16.refs_0_), channel_id=1, source_target_pairs={{0,4},{4,0},{8,12},{12,8},{1,5},{5,1},{9,13},{13,9},{2,6},{6,2},{1... | collective-permute-start | bytes 786440 | tf_op jit(solution)/shard_map/ppermute | solution.py:744
  7.9 0.1 copy.7.receivers_ref
  8.0 0.0 copy-start.2
  8.0 0.5 copy-done.3
  8.5 0.2 copy-done.2
  8.7 0.4 shard_map.68
  9.1 3.6 %collective-permute-done.3.refs_4_ = f32[256,128]{1,0:T(8,128)S(1)} collective-permute-done((f32[256,128]{1,0:T(8,128)S(1)}, f32[256,128]{1,0:T(8,128)S(1)}, u32[]{:S(2)}, u32[]{:S(2)}) %collective-permute-start.3) | collective-permute-done | bytes 131104 | tf_op jit(solution)/shard_map/ppermute | solution.py:744
  12.7 0.7 %collective-permute-start.7 = (f32[256,128]{1,0:T(8,128)S(1)}, f32[256,128]{1,0:T(8,128)S(1)}, u32[]{:S(2)}, u32[]{:S(2)}) collective-permute-start(f32[256,128]{1,0:T(8,128)S(1)} %collective-permute-done.3.refs_4_), channel_id=1, source_target_pairs={{0,4},{4,0},{8,12},{12,8},{1,5},{5,1},{9,13},{13,9},{2,6},{6,2},{1... | collective-permute-start | bytes 393224 | tf_op jit(solution)/shard_map/ppermute | solution.py:744
  13.3 1.5 %collective-permute-start.5 = (f32[256,128]{1,0:T(8,128)S(1)}, f32[256,128]{1,0:T(8,128)S(1)}, u32[]{:S(2)}, u32[]{:S(2)}) collective-permute-start(f32[256,128]{1,0:T(8,128)S(1)} %collective-permute-done.3.refs_4_), channel_id=1, source_target_pairs={{0,1},{1,0},{2,3},{3,2},{4,5},{5,4},{6,7},{7,6},{8,9},{9,8},{10,11... | collective-permute-start | bytes 393224 | tf_op jit(solution)/shard_map/ppermute | solution.py:769
  14.8 0.0 collective-permute-start
  14.8 0.5 collective-permute-start.4
  15.3 3.1 %collective-permute-done.7.refs_8_ = f32[256,128]{1,0:T(8,128)S(1)} collective-permute-done((f32[256,128]{1,0:T(8,128)S(1)}, f32[256,128]{1,0:T(8,128)S(1)}, u32[]{:S(2)}, u32[]{:S(2)}) %collective-permute-start.7) | collective-permute-done | bytes 131104 | tf_op jit(solution)/shard_map/ppermute | solution.py:744
  18.5 1.5 %collective-permute-start.9 = (f32[256,128]{1,0:T(8,128)S(1)}, f32[256,128]{1,0:T(8,128)S(1)}, u32[]{:S(2)}, u32[]{:S(2)}) collective-permute-start(f32[256,128]{1,0:T(8,128)S(1)} %collective-permute-done.7.refs_8_), channel_id=1, source_target_pairs={{0,1},{1,0},{2,3},{3,2},{4,5},{5,4},{6,7},{7,6},{8,9},{9,8},{10,11... | collective-permute-start | bytes 393224 | tf_op jit(solution)/shard_map/ppermute | solution.py:769
  20.0 0.0 collective-permute-done.1.refs_2_
  20.0 0.0 collective-permute-start.2
  20.0 0.0 collective-permute-done.5.refs_6_
  20.0 0.5 collective-permute-start.8
  20.6 0.0 collective-permute-done.4.refs_5_
  20.6 0.1 collective-permute-start.6
  20.6 2.8 %collective-permute-done.9.refs_10_ = f32[256,128]{1,0:T(8,128)S(1)} collective-permute-done((f32[256,128]{1,0:T(8,128)S(1)}, f32[256,128]{1,0:T(8,128)S(1)}, u32[]{:S(2)}, u32[]{:S(2)}) %collective-permute-start.9) | collective-permute-done | bytes 131104 | tf_op jit(solution)/shard_map/ppermute | solution.py:769
  23.5 0.0 collective-permute-start.10
  23.5 0.0 collective-permute-done.refs_1_
  23.5 0.0 collective-permute-done.8.refs_9_
  23.5 1.3 %collective-permute-done.10.refs_11_ = f32[256,128]{1,0:T(8,128)S(1)} collective-permute-done((f32[256,128]{1,0:T(8,128)S(1)}, f32[256,128]{1,0:T(8,128)S(1)}, u32[]{:S(2)}, u32[]{:S(2)}) %collective-permute-start.10) | collective-permute-done | bytes 131104 | tf_op jit(solution)/shard_map/ppermute | solution.py:747
  24.8 0.0 collective-permute-done.2.refs_3_
  24.8 23.6 %shard_map.70 = (f32[8,64,128]{2,1,0:T(8,128)}, f32[8,32,128]{2,1,0:T(8,128)S(1)}, f32[8,32,128]{2,1,0:T(8,128)S(1)}) custom-call(s32[1,256]{1,0:T(1,128)S(1)} %get-tuple-element.15.cells_ref, f32[512,128]{1,0:T(8,128)S(1)} %get-tuple-element.16.refs_0_, f32[512,128]{1,0:T(8,128)S(1)} %collective-permute-done.refs_1_, ...), custom_call_target="tpu_custom_call" | custom-call | flops 200000000 | bytes 4000000 | tf_op jit(solution)/shard_map/pallas_call | solution.py:775
  48.4 1.6 %collective-permute-start.11 = (f32[8,32,128]{2,1,0:T(8,128)S(1)}, f32[8,32,128]{2,1,0:T(8,128)S(1)}, u32[]{:S(2)}, u32[]{:S(2)}) collective-permute-start(f32[8,32,128]{2,1,0:T(8,128)S(1)} %get-tuple-element.27), channel_id=1, source_target_pairs={{0,1},{1,0},{2,3},{3,2},{4,5},{5,4},{6,7},{7,6},{8,9},{9,8},{10,11... | collective-permute-start | bytes 393224 | tf_op jit(solution)/shard_map/ppermute | solution.py:795
  50.0 4.0 %collective-permute-done.11 = f32[8,32,128]{2,1,0:T(8,128)S(1)} collective-permute-done((f32[8,32,128]{2,1,0:T(8,128)S(1)}, f32[8,32,128]{2,1,0:T(8,128)S(1)}, u32[]{:S(2)}, u32[]{:S(2)}) %collective-permute-start.11) | collective-permute-done | bytes 131104 | tf_op jit(solution)/shard_map/ppermute | solution.py:795
  54.0 0.7 %add.3 = f32[8,32,128]{2,1,0:T(8,128)} add(f32[8,32,128]{2,1,0:T(8,128)S(1)} %get-tuple-element.26, f32[8,32,128]{2,1,0:T(8,128)S(1)} %collective-permute-done.11) | non-fusion elementwise | flops 32768 | bytes 393216 | tf_op jit(solution)/shard_map/add | solution.py:795
  (7 shorter events, 0.0 us)
Async XLA Ops:
  0.6 1.0 %copy-start = (f32[8,64,128]{2,1,0:T(8,128)S(1)}, f32[8,64,128]{2,1,0:T(8,128)}, u32[]{:S(2)}) copy-start(f32[8,64,128]{2,1,0:T(8,128)} %natural_ref.1) | copy-start | bytes 786436
  1.6 6.3 %copy-start.4 = (s32[512,2]{0,1:T(2,128)S(1)}, s32[512,2]{0,1:T(2,128)}, u32[]{:S(2)}) copy-start(s32[512,2]{0,1:T(2,128)} %param.8) | copy-start | bytes 12292
  2.2 10.5 %collective-permute-start.3 = (f32[256,128]{1,0:T(8,128)S(1)}, f32[256,128]{1,0:T(8,128)S(1)}, u32[]{:S(2)}, u32[]{:S(2)}) collective-permute-start(f32[256,128]{1,0:T(8,128)S(1)} %get-tuple-element.17), channel_id=1, source_target_pairs={{0,8},{4,12},{8,0},{12,4},{1,9},{5,13},{9,1},{13,5},{2,10},{6,14},... | collective-permute-start | bytes 393224 | tf_op jit(solution)/shard_map/ppermute | solution.py:744
  6.3 1.7 %copy-start.1 = (f32[1,512]{1,0:T(1,128)S(1)}, f32[1,512]{1,0:T(1,128)}, u32[]{:S(2)}) copy-start(f32[1,512]{1,0:T(1,128)} %observed_ref.1) | copy-start | bytes 6148
  6.3 13.8 %collective-permute-start.1 = (f32[512,128]{1,0:T(8,128)S(1)}, f32[512,128]{1,0:T(8,128)S(1)}, u32[]{:S(2)}, u32[]{:S(2)}) collective-permute-start(f32[512,128]{1,0:T(8,128)S(1)} %get-tuple-element.16.refs_0_), channel_id=1, source_target_pairs={{0,4},{4,0},{8,12},{12,8},{1,5},{5,1},{9,13},{13,9},{2,6},{6,2},{1... | collective-permute-start | bytes 786440 | tf_op jit(solution)/shard_map/ppermute | solution.py:744
  7.9 0.7 %copy-start.3 = (f32[1,256]{1,0:T(1,128)S(1)}, f32[1,256]{1,0:T(1,128)}, u32[]{:S(2)}) copy-start(f32[1,256]{1,0:T(1,128)} %currents_ref.1) | copy-start | bytes 3076
  8.0 0.7 %copy-start.2 = (s32[256]{0:T(256)S(1)}, s32[256]{0:T(256)}, u32[]{:S(2)}) copy-start(s32[256]{0:T(256)} %param.6) | copy-start | bytes 3076
  12.7 5.8 %collective-permute-start.7 = (f32[256,128]{1,0:T(8,128)S(1)}, f32[256,128]{1,0:T(8,128)S(1)}, u32[]{:S(2)}, u32[]{:S(2)}) collective-permute-start(f32[256,128]{1,0:T(8,128)S(1)} %collective-permute-done.3.refs_4_), channel_id=1, source_target_pairs={{0,4},{4,0},{8,12},{12,8},{1,5},{5,1},{9,13},{13,9},{2,6},{6,2},{1... | collective-permute-start | bytes 393224 | tf_op jit(solution)/shard_map/ppermute | solution.py:744
  13.3 6.7 %collective-permute-start.5 = (f32[256,128]{1,0:T(8,128)S(1)}, f32[256,128]{1,0:T(8,128)S(1)}, u32[]{:S(2)}, u32[]{:S(2)}) collective-permute-start(f32[256,128]{1,0:T(8,128)S(1)} %collective-permute-done.3.refs_4_), channel_id=1, source_target_pairs={{0,1},{1,0},{2,3},{3,2},{4,5},{5,4},{6,7},{7,6},{8,9},{9,8},{10,11... | collective-permute-start | bytes 393224 | tf_op jit(solution)/shard_map/ppermute | solution.py:769
  14.8 8.6 %collective-permute-start = (f32[512,128]{1,0:T(8,128)S(1)}, f32[512,128]{1,0:T(8,128)S(1)}, u32[]{:S(2)}, u32[]{:S(2)}) collective-permute-start(f32[512,128]{1,0:T(8,128)S(1)} %get-tuple-element.16.refs_0_), channel_id=1, source_target_pairs={{0,2},{2,0},{1,3},{3,1},{4,6},{6,4},{5,7},{7,5},{8,10},{10,8},{9,1... | collective-permute-start | bytes 786440 | tf_op jit(solution)/shard_map/ppermute | solution.py:747
  14.8 5.7 %collective-permute-start.4 = (f32[256,128]{1,0:T(8,128)S(1)}, f32[256,128]{1,0:T(8,128)S(1)}, u32[]{:S(2)}, u32[]{:S(2)}) collective-permute-start(f32[256,128]{1,0:T(8,128)S(1)} %collective-permute-done.3.refs_4_), channel_id=1, source_target_pairs={{0,2},{2,0},{1,3},{3,1},{4,6},{6,4},{5,7},{7,5},{8,10},{10,8},{9,1... | collective-permute-start | bytes 393224 | tf_op jit(solution)/shard_map/ppermute | solution.py:747
  18.5 5.0 %collective-permute-start.9 = (f32[256,128]{1,0:T(8,128)S(1)}, f32[256,128]{1,0:T(8,128)S(1)}, u32[]{:S(2)}, u32[]{:S(2)}) collective-permute-start(f32[256,128]{1,0:T(8,128)S(1)} %collective-permute-done.7.refs_8_), channel_id=1, source_target_pairs={{0,1},{1,0},{2,3},{3,2},{4,5},{5,4},{6,7},{7,6},{8,9},{9,8},{10,11... | collective-permute-start | bytes 393224 | tf_op jit(solution)/shard_map/ppermute | solution.py:769
  20.0 4.8 %collective-permute-start.2 = (f32[512,128]{1,0:T(8,128)S(1)}, f32[512,128]{1,0:T(8,128)S(1)}, u32[]{:S(2)}, u32[]{:S(2)}) collective-permute-start(f32[512,128]{1,0:T(8,128)S(1)} %collective-permute-done.1.refs_2_), channel_id=1, source_target_pairs={{0,2},{2,0},{1,3},{3,1},{4,6},{6,4},{5,7},{7,5},{8,10},{10,8},{9,1... | collective-permute-start | bytes 786440 | tf_op jit(solution)/shard_map/ppermute | solution.py:747
  20.0 3.4 %collective-permute-start.8 = (f32[256,128]{1,0:T(8,128)S(1)}, f32[256,128]{1,0:T(8,128)S(1)}, u32[]{:S(2)}, u32[]{:S(2)}) collective-permute-start(f32[256,128]{1,0:T(8,128)S(1)} %collective-permute-done.7.refs_8_), channel_id=1, source_target_pairs={{0,2},{2,0},{1,3},{3,1},{4,6},{6,4},{5,7},{7,5},{8,10},{10,8},{9,1... | collective-permute-start | bytes 393224 | tf_op jit(solution)/shard_map/ppermute | solution.py:747
  20.6 2.9 %collective-permute-start.6 = (f32[256,128]{1,0:T(8,128)S(1)}, f32[256,128]{1,0:T(8,128)S(1)}, u32[]{:S(2)}, u32[]{:S(2)}) collective-permute-start(f32[256,128]{1,0:T(8,128)S(1)} %collective-permute-done.5.refs_6_), channel_id=1, source_target_pairs={{0,2},{2,0},{1,3},{3,1},{4,6},{6,4},{5,7},{7,5},{8,10},{10,8},{9,1... | collective-permute-start | bytes 393224 | tf_op jit(solution)/shard_map/ppermute | solution.py:747
  23.5 1.3 %collective-permute-start.10 = (f32[256,128]{1,0:T(8,128)S(1)}, f32[256,128]{1,0:T(8,128)S(1)}, u32[]{:S(2)}, u32[]{:S(2)}) collective-permute-start(f32[256,128]{1,0:T(8,128)S(1)} %collective-permute-done.9.refs_10_), channel_id=1, source_target_pairs={{0,2},{2,0},{1,3},{3,1},{4,6},{6,4},{5,7},{7,5},{8,10},{10,8},{9,1... | collective-permute-start | bytes 393224 | tf_op jit(solution)/shard_map/ppermute | solution.py:747
  48.4 5.6 %collective-permute-start.11 = (f32[8,32,128]{2,1,0:T(8,128)S(1)}, f32[8,32,128]{2,1,0:T(8,128)S(1)}, u32[]{:S(2)}, u32[]{:S(2)}) collective-permute-start(f32[8,32,128]{2,1,0:T(8,128)S(1)} %get-tuple-element.27), channel_id=1, source_target_pairs={{0,1},{1,0},{2,3},{3,2},{4,5},{5,4},{6,7},{7,6},{8,9},{9,8},{10,11... | collective-permute-start | bytes 393224 | tf_op jit(solution)/shard_map/ppermute | solution.py:795

commit v11 on v10

--- a/solution.py
+++ b/solution.py
@@ -72,10 +72,16 @@
     return lax.axis_index("gx") * 2 + lax.axis_index("gy"), lax.axis_index("shot")
 
 
-def to_blocks_kernel(natural_ref, blocks_ref, half_ref):
+def to_blocks_kernel(natural_ref, blocks_ref, half_ref, planes, sems):
+    copies = [
+        pltpu.make_async_copy(natural_ref.at[x], planes.at[x], sems.at[x]) for x in range(SIDE)
+    ]
+    for copy in copies:
+        copy.start()
     order = lane_order()
     for x in range(SIDE):
-        tiles = product(natural_ref[x], order, 3)
+        copies[x].wait()
+        tiles = product(planes[x], order, 3)
         tiles = [tiles[SIDE * k : SIDE * (k + 1)] for k in range(SIDE)]
         for z, tile in enumerate(exchange_groups(tiles)):
             blocks_ref[pl.ds((x * SIDE + z) * SIDE, SIDE), :] = tile
@@ -296,15 +302,15 @@
                 next_y = jnp.concatenate([here[1:], after])
                 last_y = jnp.concatenate([before, here[:-1]])
                 total = (next_x + cond[x - 1, z]) + (ahead + cond[x, z - 1]) + (next_y + last_y)
-                total = 3.0 * here + 0.5 * total
+                total = 6.0 * here + total
                 self.weight[x, z] = DAMPING / total
                 if n == SIDE:
                     self.base[x, z] = jnp.zeros_like(here)
-                self.back[x, z] = total * (self.scale / DAMPING)
-                self.link_x[x, z] = 0.5 * (here + next_x)
-                link = 0.5 * (here + next_y)
+                self.back[x, z] = total * (0.5 * self.scale / DAMPING)
+                self.link_x[x, z] = here + next_x
+                link = here + next_y
                 self.link_y[x, z] = jnp.concatenate([link[:-1], inside_up(link[-1:], 1)])
-                link = 0.5 * (here + ahead)
+                link = here + ahead
                 if z == n - 1:
                     link = inside_up(link, 2)
                     self.link_z[x, -1] = block_down(link, 2)
@@ -638,7 +644,7 @@
         else:
             level.descend(
                 lambda x, z, row: below.base.put(
-                    x, z, below.weight[x, z] * (row * (1.0 / below.scale))
+                    x, z, below.weight[x, z] * (row * (2.0 / below.scale))
                 )
             )
             cycle(index + 1, below.first)
@@ -658,7 +664,7 @@
         lax.fori_loop(0, electrodes, one, 0, unroll=32)
 
     def put(electrode, cell):
-        fine.base.ref[cell, :] = gathered[electrode, :] * fine.weight.ref[cell, :]
+        fine.base.ref[cell, :] = (2.0 * gathered[electrode, :]) * fine.weight.ref[cell, :]
 
     def read(electrode, cell):
         gathered[electrode, :] = forward.ref[cell, :]
@@ -666,21 +672,37 @@
     def exact(row, dims):
         return product(jnp.broadcast_to(row, (16, row.shape[1])), pairs_ref[...], 3, dims)[0:1]
 
-    def own(x, z, y=0):
-        return forward.ref[pl.ds(forward.start(x, z, y) + device, SIDE, stride=SIDE), :]
+    sub, lane = iota((SIDE, LANES), 0), iota((SIDE, LANES), 1)
+
+    def margin(x, z, y):
+        return forward.ref[pl.ds(forward.start(x, z, y) + device, 1), :]
+
+    def extract(index):
+        for x in range(-1, SIDE + 1):
+            for z in range(SIDE):
+                at = (x + 1) * wide + z + 1
+                start = forward.start(x, z) + device
+                row = forward.ref[pl.ds(start, SIDE, stride=SIDE), :]
+                owned[index, at] = row
+                if 0 <= x < SIDE:
+                    after, before = margin(x, z, SIDE), margin(x, z, -1)
+                    place = x * SIDE + z
+                    turned = pltpu.roll(row, SIDE - 1, 0)
+                    beside[index, 0, place] = jnp.where(sub == SIDE - 1, after, turned)
+                    beside[index, 1, place] = jnp.where(sub == 0, before, pltpu.roll(row, 1, 0))
+                    if z == 0:
+                        edge = pltpu.roll(row, LANES - 1, 1)
+                        owned[index, at + SIDE] = jnp.where(lane % GROUP < GROUP - 1, edge, 0.0)
+                    if z == SIDE - 1:
+                        edge = pltpu.roll(row, 1, 1)
+                        owned[index, at - SIDE] = jnp.where(lane % GROUP > 0, edge, 0.0)
 
     def solve(index):
         each(put)
         rolled(SIDE, fine.base.close_z)
         fine.base.close()
         cycle(0, forward, exact=True)
-        for x in range(-1, SIDE + 1):
-            for z in range(-1, SIDE + 1):
-                if 0 <= x < SIDE or 0 <= z < SIDE:
-                    owned[index, (x + 1) * wide + z + 1] = own(x, z)
-                if 0 <= x < SIDE and 0 <= z < SIDE:
-                    for side, y in enumerate((1, -1)):
-                        beside[index, side, x * SIDE + z] = own(x, z, y)
+        extract(index)
 
         @pl.when(index == 0)
         def _():
@@ -733,8 +755,12 @@
             jax.ShapeDtypeStruct((total, LANES), f32),
             jax.ShapeDtypeStruct((total // 2, LANES), f32),
         ),
-        in_specs=[vmem],
+        in_specs=[pl.BlockSpec(memory_space=pl.ANY)],
         out_specs=(vmem, vmem),
+        scratch_shapes=[
+            pltpu.VMEM((rows, cols, LANES), f32),
+            pltpu.SemaphoreType.DMA((rows,)),
+        ],
         compiler_params=pltpu.CompilerParams(vmem_limit_bytes=SMALL_BYTES),
     )(conductivity)
     swap = [(0, 1), (1, 0)]

time: 54.9 us -> 57.3 us (1.044)
  Pallas kernels: 24.6 us -> 27 us
    pallas_call x1, Pallas kernels: 0.58 us -> 3.47 us  [replicated(): pl.pallas_call(to_blocks_kernel, out_shape=(jax.ShapeDtypeStruct((total,...]
where the time goes in v11:
time: 57.3 us; the launch traced here: 57.1 us
  Pallas kernels  27 us (47%)
  waiting for transfers between devices  14.9 us (26%)
  starting transfers between devices  12.1 us (21%)
  local copies, waits for them, and re-layouts  1.76 us (3%)
  between operations  0.71 us (1%)
  other arithmetic  0.67 us (1%)
    pallas_call x1, Pallas kernels, replicated(): pl.pallas_call(functools.partial(replicated_kernel, len(parts), len(halve...  23.1 us
    ppermute x3, waiting for transfers between devices, partner(): return lax.ppermute(part, 'gx', [(i, i ^ k) for i in range(count)])  6.72 us
    ppermute x3, starting transfers between devices, partner(): return lax.ppermute(part, 'gx', [(i, i ^ k) for i in range(count)])  6.34 us
    ppermute x1, waiting for transfers between devices, replicated(): return (potentials[None], own + lax.ppermute(theirs, 'shot', swap))  4.01 us
    pallas_call x1, Pallas kernels, replicated(): pl.pallas_call(to_blocks_kernel, out_shape=(jax.ShapeDtypeStruct((total,...  3.47 us
    ppermute x2, starting transfers between devices, replicated(): lax.ppermute(own, 'shot', swap)  3.03 us
    ppermute x2, waiting for transfers between devices, replicated(): lax.ppermute(own, 'shot', swap)  2.84 us
    unnamed x11, local copies, waits for them, and re-layouts  1.76 us
  transfers between devices with their start and end apart: 12, of which 5 were waited for; matrix products, arithmetic and copies ran while one was open for 0% of the time, Pallas kernels for 1%

profile of v11, /device:TPU:0, one launch (start us, length us, event | category | flops | bytes accessed | tf_op | source)
XLA Modules:
  0.0 57.1 jit_solution(17092003651821497750)
XLA Ops:
  0.6 0.9 %copy-done = f32[8,64,128]{2,1,0:T(8,128)S(1)} copy-done((f32[8,64,128]{2,1,0:T(8,128)S(1)}, f32[8,64,128]{2,1,0:T(8,128)}, u32[]{:S(2)}) %copy-start) | copy-done | bytes 262168
  1.6 3.5 %shard_map.69 = (f32[512,128]{1,0:T(8,128)S(1)}, f32[256,128]{1,0:T(8,128)S(1)}) custom-call(f32[8,64,128]{2,1,0:T(8,128)S(1)} %copy-done), custom_call_target="tpu_custom_call" | custom-call | tf_op jit(solution)/shard_map/pallas_call | solution.py:752
  5.1 4.1 %collective-permute-start.3 = (f32[256,128]{1,0:T(8,128)S(1)}, f32[256,128]{1,0:T(8,128)S(1)}, u32[]{:S(2)}, u32[]{:S(2)}) collective-permute-start(f32[256,128]{1,0:T(8,128)S(1)} %get-tuple-element.17), channel_id=1, source_target_pairs={{0,8},{4,12},{8,0},{12,4},{1,9},{5,13},{9,1},{13,5},{2,10},{6,14},... | collective-permute-start | bytes 393224 | tf_op jit(solution)/shard_map/ppermute | solution.py:770
  9.2 1.6 %collective-permute-start.1 = (f32[512,128]{1,0:T(8,128)S(1)}, f32[512,128]{1,0:T(8,128)S(1)}, u32[]{:S(2)}, u32[]{:S(2)}) collective-permute-start(f32[512,128]{1,0:T(8,128)S(1)} %get-tuple-element.16.refs_0_), channel_id=1, source_target_pairs={{0,4},{4,0},{8,12},{12,8},{1,5},{5,1},{9,13},{13,9},{2,6},{6,2},{1... | collective-permute-start | bytes 786440 | tf_op jit(solution)/shard_map/ppermute | solution.py:770
  10.7 0.1 copy.7.receivers_ref
  10.9 0.0 copy-start.2
  10.9 0.5 copy-done.3
  11.4 0.2 copy-done.2
  11.6 0.4 shard_map.68
  12.0 3.6 %collective-permute-done.3.refs_4_ = f32[256,128]{1,0:T(8,128)S(1)} collective-permute-done((f32[256,128]{1,0:T(8,128)S(1)}, f32[256,128]{1,0:T(8,128)S(1)}, u32[]{:S(2)}, u32[]{:S(2)}) %collective-permute-start.3) | collective-permute-done | bytes 131104 | tf_op jit(solution)/shard_map/ppermute | solution.py:770
  15.6 0.7 %collective-permute-start.7 = (f32[256,128]{1,0:T(8,128)S(1)}, f32[256,128]{1,0:T(8,128)S(1)}, u32[]{:S(2)}, u32[]{:S(2)}) collective-permute-start(f32[256,128]{1,0:T(8,128)S(1)} %collective-permute-done.3.refs_4_), channel_id=1, source_target_pairs={{0,4},{4,0},{8,12},{12,8},{1,5},{5,1},{9,13},{13,9},{2,6},{6,2},{1... | collective-permute-start | bytes 393224 | tf_op jit(solution)/shard_map/ppermute | solution.py:770
  16.2 1.5 %collective-permute-start.5 = (f32[256,128]{1,0:T(8,128)S(1)}, f32[256,128]{1,0:T(8,128)S(1)}, u32[]{:S(2)}, u32[]{:S(2)}) collective-permute-start(f32[256,128]{1,0:T(8,128)S(1)} %collective-permute-done.3.refs_4_), channel_id=1, source_target_pairs={{0,1},{1,0},{2,3},{3,2},{4,5},{5,4},{6,7},{7,6},{8,9},{9,8},{10,11... | collective-permute-start | bytes 393224 | tf_op jit(solution)/shard_map/ppermute | solution.py:795
  17.7 0.0 collective-permute-start
  17.7 0.5 collective-permute-start.4
  18.2 3.1 %collective-permute-done.7.refs_8_ = f32[256,128]{1,0:T(8,128)S(1)} collective-permute-done((f32[256,128]{1,0:T(8,128)S(1)}, f32[256,128]{1,0:T(8,128)S(1)}, u32[]{:S(2)}, u32[]{:S(2)}) %collective-permute-start.7) | collective-permute-done | bytes 131104 | tf_op jit(solution)/shard_map/ppermute | solution.py:770
  21.4 1.5 %collective-permute-start.9 = (f32[256,128]{1,0:T(8,128)S(1)}, f32[256,128]{1,0:T(8,128)S(1)}, u32[]{:S(2)}, u32[]{:S(2)}) collective-permute-start(f32[256,128]{1,0:T(8,128)S(1)} %collective-permute-done.7.refs_8_), channel_id=1, source_target_pairs={{0,1},{1,0},{2,3},{3,2},{4,5},{5,4},{6,7},{7,6},{8,9},{9,8},{10,11... | collective-permute-start | bytes 393224 | tf_op jit(solution)/shard_map/ppermute | solution.py:795
  22.9 0.0 collective-permute-done.1.refs_2_
  22.9 0.0 collective-permute-start.2
  22.9 0.0 collective-permute-done.5.refs_6_
  22.9 0.5 collective-permute-start.8
  23.4 0.0 collective-permute-done.4.refs_5_
  23.5 0.1 collective-permute-start.6
  23.5 2.8 %collective-permute-done.9.refs_10_ = f32[256,128]{1,0:T(8,128)S(1)} collective-permute-done((f32[256,128]{1,0:T(8,128)S(1)}, f32[256,128]{1,0:T(8,128)S(1)}, u32[]{:S(2)}, u32[]{:S(2)}) %collective-permute-start.9) | collective-permute-done | bytes 131104 | tf_op jit(solution)/shard_map/ppermute | solution.py:795
  26.4 0.0 collective-permute-start.10
  26.4 0.0 collective-permute-done.refs_1_
  26.4 0.0 collective-permute-done.8.refs_9_
  26.4 1.3 %collective-permute-done.10.refs_11_ = f32[256,128]{1,0:T(8,128)S(1)} collective-permute-done((f32[256,128]{1,0:T(8,128)S(1)}, f32[256,128]{1,0:T(8,128)S(1)}, u32[]{:S(2)}, u32[]{:S(2)}) %collective-permute-start.10) | collective-permute-done | bytes 131104 | tf_op jit(solution)/shard_map/ppermute | solution.py:773
  27.7 0.0 collective-permute-done.2.refs_3_
  27.7 23.1 %shard_map.70 = (f32[8,64,128]{2,1,0:T(8,128)}, f32[8,32,128]{2,1,0:T(8,128)S(1)}, f32[8,32,128]{2,1,0:T(8,128)S(1)}) custom-call(s32[1,256]{1,0:T(1,128)S(1)} %get-tuple-element.15.cells_ref, f32[512,128]{1,0:T(8,128)S(1)} %get-tuple-element.16.refs_0_, f32[512,128]{1,0:T(8,128)S(1)} %collective-permute-done.refs_1_, ...), custom_call_target="tpu_custom_call" | custom-call | flops 200000000 | bytes 4000000 | tf_op jit(solution)/shard_map/pallas_call | solution.py:801
  50.8 1.6 %collective-permute-start.11 = (f32[8,32,128]{2,1,0:T(8,128)S(1)}, f32[8,32,128]{2,1,0:T(8,128)S(1)}, u32[]{:S(2)}, u32[]{:S(2)}) collective-permute-start(f32[8,32,128]{2,1,0:T(8,128)S(1)} %get-tuple-element.27), channel_id=1, source_target_pairs={{0,1},{1,0},{2,3},{3,2},{4,5},{5,4},{6,7},{7,6},{8,9},{9,8},{10,11... | collective-permute-start | bytes 393224 | tf_op jit(solution)/shard_map/ppermute | solution.py:821
  52.4 4.0 %collective-permute-done.11 = f32[8,32,128]{2,1,0:T(8,128)S(1)} collective-permute-done((f32[8,32,128]{2,1,0:T(8,128)S(1)}, f32[8,32,128]{2,1,0:T(8,128)S(1)}, u32[]{:S(2)}, u32[]{:S(2)}) %collective-permute-start.11) | collective-permute-done | bytes 131104 | tf_op jit(solution)/shard_map/ppermute | solution.py:821
  56.5 0.7 %add.3 = f32[8,32,128]{2,1,0:T(8,128)} add(f32[8,32,128]{2,1,0:T(8,128)S(1)} %get-tuple-element.26, f32[8,32,128]{2,1,0:T(8,128)S(1)} %collective-permute-done.11) | non-fusion elementwise | flops 32768 | bytes 393216 | tf_op jit(solution)/shard_map/add | solution.py:821
  (7 shorter events, 0.0 us)
Async XLA Ops:
  0.6 1.0 %copy-start = (f32[8,64,128]{2,1,0:T(8,128)S(1)}, f32[8,64,128]{2,1,0:T(8,128)}, u32[]{:S(2)}) copy-start(f32[8,64,128]{2,1,0:T(8,128)} %natural_ref.1) | copy-start | bytes 786436
  1.6 9.2 %copy-start.4 = (s32[512,2]{0,1:T(2,128)S(1)}, s32[512,2]{0,1:T(2,128)}, u32[]{:S(2)}) copy-start(s32[512,2]{0,1:T(2,128)} %param.8) | copy-start | bytes 12292
  5.1 10.5 %collective-permute-start.3 = (f32[256,128]{1,0:T(8,128)S(1)}, f32[256,128]{1,0:T(8,128)S(1)}, u32[]{:S(2)}, u32[]{:S(2)}) collective-permute-start(f32[256,128]{1,0:T(8,128)S(1)} %get-tuple-element.17), channel_id=1, source_target_pairs={{0,8},{4,12},{8,0},{12,4},{1,9},{5,13},{9,1},{13,5},{2,10},{6,14},... | collective-permute-start | bytes 393224 | tf_op jit(solution)/shard_map/ppermute | solution.py:770
  9.2 1.7 %copy-start.1 = (f32[1,512]{1,0:T(1,128)S(1)}, f32[1,512]{1,0:T(1,128)}, u32[]{:S(2)}) copy-start(f32[1,512]{1,0:T(1,128)} %observed_ref.1) | copy-start | bytes 6148
  9.2 13.8 %collective-permute-start.1 = (f32[512,128]{1,0:T(8,128)S(1)}, f32[512,128]{1,0:T(8,128)S(1)}, u32[]{:S(2)}, u32[]{:S(2)}) collective-permute-start(f32[512,128]{1,0:T(8,128)S(1)} %get-tuple-element.16.refs_0_), channel_id=1, source_target_pairs={{0,4},{4,0},{8,12},{12,8},{1,5},{5,1},{9,13},{13,9},{2,6},{6,2},{1... | collective-permute-start | bytes 786440 | tf_op jit(solution)/shard_map/ppermute | solution.py:770
  10.7 0.7 %copy-start.3 = (f32[1,256]{1,0:T(1,128)S(1)}, f32[1,256]{1,0:T(1,128)}, u32[]{:S(2)}) copy-start(f32[1,256]{1,0:T(1,128)} %currents_ref.1) | copy-start | bytes 3076
  10.9 0.7 %copy-start.2 = (s32[256]{0:T(256)S(1)}, s32[256]{0:T(256)}, u32[]{:S(2)}) copy-start(s32[256]{0:T(256)} %param.6) | copy-start | bytes 3076
  15.6 5.8 %collective-permute-start.7 = (f32[256,128]{1,0:T(8,128)S(1)}, f32[256,128]{1,0:T(8,128)S(1)}, u32[]{:S(2)}, u32[]{:S(2)}) collective-permute-start(f32[256,128]{1,0:T(8,128)S(1)} %collective-permute-done.3.refs_4_), channel_id=1, source_target_pairs={{0,4},{4,0},{8,12},{12,8},{1,5},{5,1},{9,13},{13,9},{2,6},{6,2},{1... | collective-permute-start | bytes 393224 | tf_op jit(solution)/shard_map/ppermute | solution.py:770
  16.2 6.7 %collective-permute-start.5 = (f32[256,128]{1,0:T(8,128)S(1)}, f32[256,128]{1,0:T(8,128)S(1)}, u32[]{:S(2)}, u32[]{:S(2)}) collective-permute-start(f32[256,128]{1,0:T(8,128)S(1)} %collective-permute-done.3.refs_4_), channel_id=1, source_target_pairs={{0,1},{1,0},{2,3},{3,2},{4,5},{5,4},{6,7},{7,6},{8,9},{9,8},{10,11... | collective-permute-start | bytes 393224 | tf_op jit(solution)/shard_map/ppermute | solution.py:795
  17.7 8.6 %collective-permute-start = (f32[512,128]{1,0:T(8,128)S(1)}, f32[512,128]{1,0:T(8,128)S(1)}, u32[]{:S(2)}, u32[]{:S(2)}) collective-permute-start(f32[512,128]{1,0:T(8,128)S(1)} %get-tuple-element.16.refs_0_), channel_id=1, source_target_pairs={{0,2},{2,0},{1,3},{3,1},{4,6},{6,4},{5,7},{7,5},{8,10},{10,8},{9,1... | collective-permute-start | bytes 786440 | tf_op jit(solution)/shard_map/ppermute | solution.py:773
  17.7 5.7 %collective-permute-start.4 = (f32[256,128]{1,0:T(8,128)S(1)}, f32[256,128]{1,0:T(8,128)S(1)}, u32[]{:S(2)}, u32[]{:S(2)}) collective-permute-start(f32[256,128]{1,0:T(8,128)S(1)} %collective-permute-done.3.refs_4_), channel_id=1, source_target_pairs={{0,2},{2,0},{1,3},{3,1},{4,6},{6,4},{5,7},{7,5},{8,10},{10,8},{9,1... | collective-permute-start | bytes 393224 | tf_op jit(solution)/shard_map/ppermute | solution.py:773
  21.4 5.0 %collective-permute-start.9 = (f32[256,128]{1,0:T(8,128)S(1)}, f32[256,128]{1,0:T(8,128)S(1)}, u32[]{:S(2)}, u32[]{:S(2)}) collective-permute-start(f32[256,128]{1,0:T(8,128)S(1)} %collective-permute-done.7.refs_8_), channel_id=1, source_target_pairs={{0,1},{1,0},{2,3},{3,2},{4,5},{5,4},{6,7},{7,6},{8,9},{9,8},{10,11... | collective-permute-start | bytes 393224 | tf_op jit(solution)/shard_map/ppermute | solution.py:795
  22.9 4.8 %collective-permute-start.2 = (f32[512,128]{1,0:T(8,128)S(1)}, f32[512,128]{1,0:T(8,128)S(1)}, u32[]{:S(2)}, u32[]{:S(2)}) collective-permute-start(f32[512,128]{1,0:T(8,128)S(1)} %collective-permute-done.1.refs_2_), channel_id=1, source_target_pairs={{0,2},{2,0},{1,3},{3,1},{4,6},{6,4},{5,7},{7,5},{8,10},{10,8},{9,1... | collective-permute-start | bytes 786440 | tf_op jit(solution)/shard_map/ppermute | solution.py:773
  22.9 3.4 %collective-permute-start.8 = (f32[256,128]{1,0:T(8,128)S(1)}, f32[256,128]{1,0:T(8,128)S(1)}, u32[]{:S(2)}, u32[]{:S(2)}) collective-permute-start(f32[256,128]{1,0:T(8,128)S(1)} %collective-permute-done.7.refs_8_), channel_id=1, source_target_pairs={{0,2},{2,0},{1,3},{3,1},{4,6},{6,4},{5,7},{7,5},{8,10},{10,8},{9,1... | collective-permute-start | bytes 393224 | tf_op jit(solution)/shard_map/ppermute | solution.py:773
  23.5 2.9 %collective-permute-start.6 = (f32[256,128]{1,0:T(8,128)S(1)}, f32[256,128]{1,0:T(8,128)S(1)}, u32[]{:S(2)}, u32[]{:S(2)}) collective-permute-start(f32[256,128]{1,0:T(8,128)S(1)} %collective-permute-done.5.refs_6_), channel_id=1, source_target_pairs={{0,2},{2,0},{1,3},{3,1},{4,6},{6,4},{5,7},{7,5},{8,10},{10,8},{9,1... | collective-permute-start | bytes 393224 | tf_op jit(solution)/shard_map/ppermute | solution.py:773
  26.4 1.3 %collective-permute-start.10 = (f32[256,128]{1,0:T(8,128)S(1)}, f32[256,128]{1,0:T(8,128)S(1)}, u32[]{:S(2)}, u32[]{:S(2)}) collective-permute-start(f32[256,128]{1,0:T(8,128)S(1)} %collective-permute-done.9.refs_10_), channel_id=1, source_target_pairs={{0,2},{2,0},{1,3},{3,1},{4,6},{6,4},{5,7},{7,5},{8,10},{10,8},{9,1... | collective-permute-start | bytes 393224 | tf_op jit(solution)/shard_map/ppermute | solution.py:773
  50.8 5.6 %collective-permute-start.11 = (f32[8,32,128]{2,1,0:T(8,128)S(1)}, f32[8,32,128]{2,1,0:T(8,128)S(1)}, u32[]{:S(2)}, u32[]{:S(2)}) collective-permute-start(f32[8,32,128]{2,1,0:T(8,128)S(1)} %get-tuple-element.27), channel_id=1, source_target_pairs={{0,1},{1,0},{2,3},{3,2},{4,5},{5,4},{6,7},{7,6},{8,9},{9,8},{10,11... | collective-permute-start | bytes 393224 | tf_op jit(solution)/shard_map/ppermute | solution.py:821

commit v12 on v11

--- a/solution.py
+++ b/solution.py
@@ -72,16 +72,10 @@
     return lax.axis_index("gx") * 2 + lax.axis_index("gy"), lax.axis_index("shot")
 
 
-def to_blocks_kernel(natural_ref, blocks_ref, half_ref, planes, sems):
-    copies = [
-        pltpu.make_async_copy(natural_ref.at[x], planes.at[x], sems.at[x]) for x in range(SIDE)
-    ]
-    for copy in copies:
-        copy.start()
+def to_blocks_kernel(natural_ref, blocks_ref, half_ref):
     order = lane_order()
     for x in range(SIDE):
-        copies[x].wait()
-        tiles = product(planes[x], order, 3)
+        tiles = product(natural_ref[x], order, 3)
         tiles = [tiles[SIDE * k : SIDE * (k + 1)] for k in range(SIDE)]
         for z, tile in enumerate(exchange_groups(tiles)):
             blocks_ref[pl.ds((x * SIDE + z) * SIDE, SIDE), :] = tile
@@ -95,53 +89,44 @@
     return product(natural, order, 3, ((1,), (1,)))
 
 
-def block_up(field, axis):
+def block_up(register, axis):
     if axis == 0:
-        return pltpu.roll(field, 6, 1)
+        return pltpu.roll(register, 6, 0)
     if axis == 2:
-        return pltpu.roll(field, LANES - 1, 2)
-    turned = pltpu.roll(field, LANES - GROUP, 2)
-    return jnp.where(iota(field.shape, 2) < LANES - GROUP, turned, pltpu.roll(turned, 7, 1))
-
-
-def block_down(field, axis):
+        return pltpu.roll(register, LANES - 1, 1)
+    turned = pltpu.roll(register, LANES - GROUP, 1)
+    return jnp.where(iota(register.shape, 1) < LANES - GROUP, turned, pltpu.roll(turned, 7, 0))
+
+
+def block_down(register, axis):
     if axis == 0:
-        return pltpu.roll(field, 2, 1)
+        return pltpu.roll(register, 2, 0)
     if axis == 2:
-        return pltpu.roll(field, 1, 2)
-    turned = pltpu.roll(field, GROUP, 2)
-    return jnp.where(iota(field.shape, 2) >= GROUP, turned, pltpu.roll(turned, 1, 1))
-
-
-def inside_up(field, axis):
-    sub, lane = iota(field.shape, 1), iota(field.shape, 2)
+        return pltpu.roll(register, 1, 1)
+    turned = pltpu.roll(register, GROUP, 1)
+    return jnp.where(iota(register.shape, 1) >= GROUP, turned, pltpu.roll(turned, 1, 0))
+
+
+def inside_up(register, axis):
+    sub, lane = iota(register.shape, 0), iota(register.shape, 1)
     if axis == 0:
         keep = sub < 6
     elif axis == 1:
         keep = (lane < LANES - GROUP) | (sub % 2 == 0)
     else:
         keep = lane % GROUP < GROUP - 1
-    return jnp.where(keep, field, 0.0)
-
-
-def inside_down(field, axis):
-    sub, lane = iota(field.shape, 1), iota(field.shape, 2)
+    return jnp.where(keep, register, 0.0)
+
+
+def inside_down(register, axis):
+    sub, lane = iota(register.shape, 0), iota(register.shape, 1)
     if axis == 0:
         keep = sub >= 2
     elif axis == 1:
         keep = (lane >= GROUP) | (sub % 2 == 1)
     else:
         keep = lane % GROUP > 0
-    return jnp.where(keep, field, 0.0)
-
-
-def pair_rows(row):
-    count = row.shape[0] // 2
-    return jnp.concatenate([row[2 * i : 2 * i + 1] + row[2 * i + 1 : 2 * i + 2] for i in range(count)])
-
-
-def twice(row):
-    return jnp.concatenate([row[i // 2 : i // 2 + 1] for i in range(2 * row.shape[0])])
+    return jnp.where(keep, register, 0.0)
 
 
 def electrode_kernel(
@@ -192,64 +177,68 @@
         return (((x + 1) * wide + z + 1) * wide + y + 1) * SIDE
 
     def __getitem__(self, at):
-        x, z = at
-        rows = self.ref[pl.ds(self.start(x, z), self.side * SIDE), :]
-        return rows.reshape(self.side, SIDE, LANES)
+        return self.ref[pl.ds(self.start(*at), SIDE), :]
 
     def __setitem__(self, at, value):
-        x, z = at
-        self.ref[pl.ds(self.start(x, z), self.side * SIDE), :] = value.reshape(-1, LANES)
-
-    def put(self, x, z, value, exact=False):
-        self[x, z] = value
+        self.ref[pl.ds(self.start(*at), SIDE), :] = value
+
+    def put(self, x, z, y, value, exact=False):
+        self[x, z, y] = value
         n = self.side
-        if z == 0:
-            edge = block_up(value, 2)
-            self[x, n] = inside_up(edge, 2) if exact else edge
-        if z == n - 1:
-            edge = block_down(value, 2)
-            self[x, -1] = inside_down(edge, 2) if exact else edge
-        if x == 0:
-            edge = block_up(value, 0)
-            self[n, z] = inside_up(edge, 0) if exact else edge
-        if x == n - 1:
-            edge = block_down(value, 0)
-            self[-1, z] = inside_down(edge, 0) if exact else edge
-        if exact:
-            after = inside_up(block_up(value[:1], 1), 1)
-            self.ref[pl.ds(self.start(x, z, n), SIDE), :] = after[0]
-            before = inside_down(block_down(value[n - 1 :], 1), 1)
-            self.ref[pl.ds(self.start(x, z, -1), SIDE), :] = before[0]
+        for axis, place in enumerate((x, y, z)):
+            if axis == 1 and not exact:
+                continue
+            if place == 0:
+                edge = block_up(value, axis)
+                self.set_margin(x, z, y, axis, n, inside_up(edge, axis) if exact else edge)
+            if place == n - 1:
+                edge = block_down(value, axis)
+                self.set_margin(x, z, y, axis, -1, inside_down(edge, axis) if exact else edge)
+
+    def set_margin(self, x, z, y, axis, place, value):
+        at = [x, y, z]
+        at[axis] = place
+        self[at[0], at[2], at[1]] = value
 
     def close_z(self, x, exact=False):
         n = self.side
-        after, before = block_up(self[x, 0], 2), block_down(self[x, n - 1], 2)
-        self[x, n] = inside_up(after, 2) if exact else after
-        self[x, -1] = inside_down(before, 2) if exact else before
+        for y in range(n):
+            after, before = block_up(self[x, 0, y], 2), block_down(self[x, n - 1, y], 2)
+            self[x, n, y] = inside_up(after, 2) if exact else after
+            self[x, -1, y] = inside_down(before, 2) if exact else before
 
     def close(self, exact=False):
         n = self.side
         for z in range(n):
-            after = block_up(self[0, z], 0)
-            self[n, z] = inside_up(after, 0) if exact else after
-            before = block_down(self[n - 1, z], 0)
-            self[-1, z] = inside_down(before, 0) if exact else before
+            for y in range(n):
+                after, before = block_up(self[0, z, y], 0), block_down(self[n - 1, z, y], 0)
+                self[n, z, y] = inside_up(after, 0) if exact else after
+                self[-1, z, y] = inside_down(before, 0) if exact else before
 
 
 class Rows:
     def __init__(self, ref, side, first_x=0, first_z=0):
         self.ref, self.side, self.first_x, self.first_z = ref, side, first_x, first_z
 
-    def place(self, at):
+    def place(self, x, z, y):
         count = self.side - self.first_z
-        rows = self.side * SIDE
-        return pl.ds(((at[0] - self.first_x) * count + at[1] - self.first_z) * rows, rows)
+        row = ((x - self.first_x) * count + z - self.first_z) * self.side + y
+        return pl.ds(row * SIDE, SIDE)
 
     def __getitem__(self, at):
-        return self.ref[self.place(at), :].reshape(self.side, SIDE, LANES)
+        return self.ref[self.place(*at), :]
 
     def __setitem__(self, at, value):
-        self.ref[self.place(at), :] = value.reshape(-1, LANES)
+        self.ref[self.place(*at), :] = value
+
+
+class Copied:
+    def __init__(self, coarse):
+        self.coarse = coarse
+
+    def __getitem__(self, at):
+        x, z, y = at
+        return self.coarse[x // 2, z // 2, y // 2]
 
 
 def rolled(count, body):
@@ -258,14 +247,6 @@
         return carry
 
     lax.fori_loop(0, count, one, 0)
-
-
-def next_in_y(row):
-    return jnp.concatenate([row[1:], block_up(row[:1], 1)])
-
-
-def last_in_y(row):
-    return jnp.concatenate([block_down(row[-1:], 1), row[:-1]])
 
 
 class Level:
@@ -286,35 +267,33 @@
         sizes += [side**2 * (side + 1), side**3, side**2 * (side + 1), side**3]
         return [pltpu.VMEM((size * SIDE, LANES), jnp.float32) for size in sizes]
 
-    def pairs(self, body):
-        for i in range(self.side // 2):
-            body(2 * i)
-
     def prepare(self):
         n = self.side
         cond = self.cond
 
         def plane(x):
             for z in range(n):
-                here, ahead, next_x = cond[x, z], cond[x, z + 1], cond[x + 1, z]
-                after = inside_up(block_up(here[:1], 1), 1)
-                before = inside_down(block_down(here[-1:], 1), 1)
-                next_y = jnp.concatenate([here[1:], after])
-                last_y = jnp.concatenate([before, here[:-1]])
-                total = (next_x + cond[x - 1, z]) + (ahead + cond[x, z - 1]) + (next_y + last_y)
-                total = 6.0 * here + total
-                self.weight[x, z] = DAMPING / total
-                if n == SIDE:
-                    self.base[x, z] = jnp.zeros_like(here)
-                self.back[x, z] = total * (0.5 * self.scale / DAMPING)
-                self.link_x[x, z] = here + next_x
-                link = here + next_y
-                self.link_y[x, z] = jnp.concatenate([link[:-1], inside_up(link[-1:], 1)])
-                link = here + ahead
-                if z == n - 1:
-                    link = inside_up(link, 2)
-                    self.link_z[x, -1] = block_down(link, 2)
-                self.link_z[x, z] = link
+                row = [cond[x, z, y] for y in range(n)]
+                after = inside_up(block_up(row[0], 1), 1)
+                before = inside_down(block_down(row[-1], 1), 1)
+                for y, here in enumerate(row):
+                    ahead, next_x = cond[x, z + 1, y], cond[x + 1, z, y]
+                    next_y = row[y + 1] if y < n - 1 else after
+                    last_y = row[y - 1] if y > 0 else before
+                    total = (next_x + cond[x - 1, z, y]) + (ahead + cond[x, z - 1, y])
+                    total = 6.0 * here + (total + (next_y + last_y))
+                    self.weight[x, z, y] = DAMPING / total
+                    if n == SIDE:
+                        self.base[x, z, y] = jnp.zeros_like(here)
+                    self.back[x, z, y] = total * (0.5 * self.scale / DAMPING)
+                    self.link_x[x, z, y] = here + next_x
+                    link = here + next_y
+                    self.link_y[x, z, y] = link if y < n - 1 else inside_up(link, 1)
+                    link = here + ahead
+                    if z == n - 1:
+                        link = inside_up(link, 2)
+                        self.link_z[x, -1, y] = block_down(link, 2)
+                    self.link_z[x, z, y] = link
 
         if n == SIDE:
             rolled(n, plane)
@@ -322,89 +301,72 @@
             for x in range(n):
                 plane(x)
         for z in range(n):
-            link = inside_up(self.link_x[n - 1, z], 0)
-            self.link_x[n - 1, z] = link
-            self.link_x[-1, z] = block_down(link, 0)
-
-    def flows(self, x, z, here, ahead, outer, down):
-        result = []
-        inner = self.link_x[x, z]
-        sides = [
-            self.link_x[x - 1, z] * outer[0] + inner * here[1],
-            inner * here[0] + self.link_x[x + 1, z] * outer[1],
-        ]
-        for p in range(2):
-            link_y, link_z = self.link_y[x + p, z], self.link_z[x + p, z]
-            along = link_y * next_in_y(here[p]) + last_in_y(link_y * here[p])
-            total = sides[p] + (link_z * ahead[p] + down[p]) + along
-            down[p] = link_z * here[p]
-            result.append(self.weight[x + p, z] * total)
-        return result
-
-    def rows(self, field, x):
-        here = [field[x, 0], field[x + 1, 0]]
-        down = [self.link_z[x + p, -1] * field[x + p, -1] for p in range(2)]
-        for z in range(self.side):
-            ahead = [field[x, z + 1], field[x + 1, z + 1]]
-            outer = [field[x - 1, z], field[x + 2, z]]
-            yield z, here, self.flows(x, z, here, ahead, outer, down)
+            for y in range(n):
+                link = inside_up(self.link_x[n - 1, z, y], 0)
+                self.link_x[n - 1, z, y] = link
+                self.link_x[-1, z, y] = block_down(link, 0)
+
+    def visit(self, field, x, body):
+        n = self.side
+        both = (0, 1)
+        link_x, link_y, link_z = self.link_x, self.link_y, self.link_z
+        here = [[field[x + p, 0, y] for y in range(n)] for p in both]
+        down = [[link_z[x + p, -1, y] * field[x + p, -1, y] for y in range(n)] for p in both]
+        for z in range(n):
+            ahead = [[], []]
+            last = [block_down(link_y[x + p, z, n - 1] * here[p][n - 1], 1) for p in both]
+            for y in range(n):
+                inner = link_x[x, z, y]
+                sides = [
+                    link_x[x - 1, z, y] * field[x - 1, z, y] + inner * here[1][y],
+                    inner * here[0][y] + link_x[x + 1, z, y] * field[x + 2, z, y],
+                ]
+                for p in both:
+                    across, along = link_y[x + p, z, y], link_z[x + p, z, y]
+                    ahead[p].append(field[x + p, z + 1, y])
+                    next_y = here[p][y + 1] if y < n - 1 else block_up(here[p][0], 1)
+                    total = sides[p] + (along * ahead[p][y] + down[p][y])
+                    total = total + (across * next_y + last[p])
+                    last[p] = across * here[p][y]
+                    down[p][y] = along * here[p][y]
+                    body(x + p, z, y, here[p][y], self.weight[x + p, z, y] * total)
             here = ahead
 
     def sweep(self, field, out, exact=False):
-        def pair(x):
-            for z, here, sums in self.rows(field, x):
-                for p in range(2):
-                    if field is self.base:
-                        value = (2.0 - DAMPING) * here[p] + sums[p]
-                    else:
-                        value = (1.0 - DAMPING) * here[p] + (self.base[x + p, z] + sums[p])
-                    out.put(x + p, z, value, exact)
-
-        self.pairs(pair)
-
-    def halve(self, rows, coarse):
-        def pair(x):
-            held = None
-            for z, row in enumerate(rows(x)):
-                row = row[0] + row[1]
-                if z % 2 == 0:
-                    held = row
-                else:
-                    coarse(x // 2, z // 2, 0.125 * pair_rows(held + row))
-
-        self.pairs(pair)
+        def body(x, z, y, here, total):
+            if field is self.base:
+                value = (2.0 - DAMPING) * here + total
+            else:
+                value = (1.0 - DAMPING) * here + (self.base[x, z, y] + total)
+            out.put(x, z, y, value, exact)
+
+        for x in range(0, self.side, 2):
+            self.visit(field, x, body)
 
     def descend(self, coarse):
         self.sweep(self.base, self.second)
-
-        def residuals(x):
-            for z, here, sums in self.rows(self.second, x):
-                result = []
-                for p in range(2):
-                    swept = (1.0 - DAMPING) * here[p] + (self.base[x + p, z] + sums[p])
-                    self.first[x + p, z] = swept
-                    result.append((swept - here[p]) * self.back[x + p, z])
-                yield result
-
-        self.halve(residuals, coarse)
-
-    def ascend(self, correction, out, exact=False):
-        def pair(x):
-            i = x // 2
-            here = twice(correction(i, 0))
-            start = twice(correction(i, -1))
-            down = [self.link_z[x + p, -1] * start for p in range(2)]
-            for z in range(self.side):
-                ahead = twice(correction(i, (z + 1) // 2))
-                outer = [twice(correction(i - 1, z // 2)), twice(correction(i + 1, z // 2))]
-                sums = self.flows(x, z, [here, here], [ahead, ahead], outer, down)
-                for p in range(2):
-                    value = self.first[x + p, z] + ((1.0 - DAMPING) * here + sums[p])
-                    self.second.put(x + p, z, value)
-                here = ahead
-
-        self.pairs(pair)
-        self.sweep(self.second, out, exact)
+        held = {}
+
+        def body(x, z, y, here, total):
+            swept = (1.0 - DAMPING) * here + (self.base[x, z, y] + total)
+            self.first[x, z, y] = swept
+            residual = (swept - here) * self.back[x, z, y]
+            at = x // 2, z // 2, y // 2
+            held[at] = held[at] + residual if at in held else residual
+            if x % 2 and z % 2 and y % 2:
+                coarse(*at, 0.125 * held.pop(at))
+
+        for x in range(0, self.side, 2):
+            self.visit(self.second, x, body)
+
+    def ascend(self, correction, out):
+        def body(x, z, y, here, total):
+            value = self.first[x, z, y] + ((1.0 - DAMPING) * here + total)
+            self.second.put(x, z, y, value)
+
+        for x in range(0, self.side, 2):
+            self.visit(Copied(correction), x, body)
+        self.sweep(self.second, out, exact=self.side == SIDE)
 
 
 class HeldLevel:
@@ -421,51 +383,43 @@
         return [pltpu.VMEM((size * SIDE, LANES), jnp.float32) for size in sizes]
 
     def around(self, field, inside=False):
-        def moved(row, axis, up):
-            row = (block_up if up else block_down)(row, axis)
-            return (inside_up if up else inside_down)(row, axis) if inside else row
-
         result = {}
-        for (x, z), here in field.items():
-            result[x, z] = [
-                field[1, z] if x == 0 else moved(field[0, z], 0, True),
-                field[0, z] if x == 1 else moved(field[1, z], 0, False),
-                jnp.concatenate([here[1:], moved(here[:1], 1, True)]),
-                jnp.concatenate([moved(here[-1:], 1, False), here[:-1]]),
-                field[x, 1] if z == 0 else moved(field[x, 0], 2, True),
-                field[x, 0] if z == 1 else moved(field[x, 1], 2, False),
-            ]
+        for at, here in field.items():
+            others = []
+            for axis, dim in ((0, 0), (1, 2), (2, 1)):
+                other = list(at)
+                other[dim] = 1 - at[dim]
+                other = field[tuple(other)]
+                far_up, far_down = block_up(other, axis), block_down(other, axis)
+                if inside:
+                    far_up, far_down = inside_up(far_up, axis), inside_down(far_down, axis)
+                others += [other, far_down] if at[dim] == 0 else [far_up, other]
+            result[at] = others
         return result
 
     def prepare(self):
-        field = {(x, z): self.cond[x, z] for x in range(2) for z in range(2)}
+        field = {
+            (x, z, y): self.cond[x, z, y] for x in range(2) for z in range(2) for y in range(2)
+        }
         for at, others in self.around(field, inside=True).items():
             here = field[at]
             total = others[0]
             for other in others[1:]:
                 total = total + other
-            total = 3.0 * here + 0.5 * total
+            total = 6.0 * here + total
             inverse = DAMPING / total
             self.weight[at] = inverse
-            self.back[at] = total * (self.scale / DAMPING)
+            self.back[at] = total * (0.5 * self.scale / DAMPING)
             for index, other in enumerate(others):
-                link = 0.5 * inverse * (here + other)
+                link = inverse * (here + other)
                 self.links[index][at] = jnp.where(other > 0.0, link, 0.0)
-
-    def halve(self, rows, coarse):
-        total = None
-        for row in rows(0):
-            row = row[0] + row[1]
-            total = row if total is None else total + row
-        coarse(0, 0, 0.125 * (total[:1] + total[1:]))
 
     def sums(self, field, base):
         result = {}
         for at, others in self.around(field).items():
-            total = base[at]
-            for link, other in zip(self.links, others):
-                total = total + link[at] * other
-            result[at] = total
+            terms = [link[at] * other for link, other in zip(self.links, others)]
+            total = (terms[0] + terms[1]) + (terms[4] + terms[5])
+            result[at] = (base[at] + total) + (terms[2] + terms[3])
         return result
 
     def swept(self, field, base):
@@ -479,13 +433,12 @@
         for at in field:
             residual = (sums[at] - DAMPING * field[at]) * self.back[at]
             total = residual if total is None else total + residual
-        solved = solve(0.125 * (total[:1] + total[1:]))
-        row = twice(solved)
-        copied = {at: row for at in field}
-        change = {at: sums[at] + (1.0 - DAMPING) * (field[at] + row) for at in field}
+        solved = solve(0.125 * total)
+        copied = {at: solved for at in field}
+        change = {at: sums[at] + (1.0 - DAMPING) * (field[at] + solved) for at in field}
         field = self.sums(copied, change)
-        for (x, z), value in self.swept(field, base).items():
-            out.put(x, z, value)
+        for (x, z, y), value in self.swept(field, base).items():
+            out.put(x, z, y, value, exact=True)
 
 
 def replicated_kernel(
@@ -555,40 +508,37 @@
     rolled(SIDE, edges)
     fine.cond.close(exact=True)
 
-    coarsest = []
+    coarsest = None
     for level, below in zip(levels, levels[1:] + [None]):
         level.prepare()
-
-        def coarse(x, z, row, below=below):
+        for at in [(x, z, y) for x in range(level.side // 2) for z in range(level.side // 2) for y in range(level.side // 2)]:
+            total = None
+            for step in range(8):
+                part = level.cond[
+                    2 * at[0] + step // 4, 2 * at[1] + step // 2 % 2, 2 * at[2] + step % 2
+                ]
+                total = part if total is None else total + part
             if below is None:
-                coarsest.append(row)
+                coarsest = 0.125 * total
             else:
-                below.cond.put(x, z, row, exact=True)
-
-        level.halve(
-            lambda x, level=level: [
-                (level.cond[x, z], level.cond[x + 1, z]) for z in range(level.side)
-            ],
-            coarse,
-        )
-
-    keep = iota((1, SIDE, LANES), 1) % 2 == 0
-    lane = iota((1, SIDE, LANES), 2)
+                below.cond.put(*at, 0.125 * total, exact=True)
+
+    sub, lane = iota((SIDE, LANES), 0), iota((SIDE, LANES), 1)
+    keep = sub % 2 == 0
 
     def split(value):
-        return [jnp.where(keep, part, 0.0) for part in (value, pltpu.roll(value, SIDE - 1, 1))]
+        return [jnp.where(keep, part, 0.0) for part in (value, pltpu.roll(value, SIDE - 1, 0))]
 
     def around(value):
         low, high = value
-        low_up, high_up = [pltpu.roll(part, LANES - GROUP, 2) for part in value]
-        low_down, high_down = [pltpu.roll(part, GROUP, 2) for part in value]
+        low_up, high_up = [pltpu.roll(part, LANES - GROUP, 1) for part in value]
+        low_down, high_down = [pltpu.roll(part, GROUP, 1) for part in value]
         along = [[move(part, axis) for part in value] for axis in (0, 2) for move in (block_up, block_down)]
         return along + [
             [jnp.where(lane < LANES - GROUP, low_up, high_up), high_up],
             [low_down, jnp.where(lane >= GROUP, high_down, low_down)],
         ]
 
-    sub = iota((1, SIDE, LANES), 1)
     inside_last = [
         [sub < 6] * 2,
         [sub >= 2] * 2,
@@ -598,21 +548,21 @@
         [lane >= GROUP, keep],
     ]
     last_scale = 0.25 ** (LEVELS - 1)
-    here = split(coarsest[0])
+    here = split(coarsest)
     others = [
         [jnp.where(inside & keep, part, 0.0) for inside, part in zip(pair, moved)]
         for pair, moved in zip(inside_last, around(here))
     ]
     last_weight, last_links = [], []
     for half, part in enumerate(here):
-        total = 3.0 * part
+        total = 6.0 * part
         for other in others:
-            total = total + 0.5 * other[half]
+            total = total + other[half]
         inverse = jnp.where(keep, DAMPING / jnp.where(keep, total, 1.0), 0.0)
-        last_weight.append(inverse * (1.0 / last_scale))
+        last_weight.append(inverse * (2.0 / last_scale))
         last_links.append(
             [
-                jnp.where(pair[half] & keep, 0.5 * inverse * (part + other[half]), 0.0)
+                jnp.where(pair[half] & keep, inverse * (part + other[half]), 0.0)
                 for pair, other in zip(inside_last, others)
             ]
         )
@@ -628,27 +578,28 @@
                 start = base[half] + (1.0 - DAMPING) * value[half]
                 fresh.append(((start + parts[0]) + (parts[1] + parts[2])) + (parts[3] + (parts[4] + parts[5])))
             value = fresh
-        return value[0] + pltpu.roll(value[1], 1, 1)
-
-    def cycle(index, out, exact=False):
-        level = levels[index]
-        below = levels[index + 1]
+        return value[0] + pltpu.roll(value[1], 1, 0)
+
+    def cycle(index, out):
+        level, below = levels[index], levels[index + 1]
+
+        def weighed(x, z, y, value):
+            return below.weight[x, z, y] * (value * (2.0 / below.scale))
+
         if index == LEVELS - 3:
             base = {}
 
-            def take(x, z, row):
-                base[x, z] = below.weight[x, z] * (row * (1.0 / below.scale))
+            def take(x, z, y, value):
+                base[x, z, y] = weighed(x, z, y, value)
 
             level.descend(take)
             below.cycle(base, solve_last, below.first)
         else:
             level.descend(
-                lambda x, z, row: below.base.put(
-                    x, z, below.weight[x, z] * (row * (2.0 / below.scale))
-                )
+                lambda x, z, y, value: below.base.put(x, z, y, weighed(x, z, y, value))
             )
             cycle(index + 1, below.first)
-        level.ascend(lambda x, z: below.first[x, z], out, exact)
+        level.ascend(below.first, out)
 
     spot = spot_ref[...]
     at_spot = iota((LANES, electrodes), 0) == spot
@@ -671,8 +622,6 @@
 
     def exact(row, dims):
         return product(jnp.broadcast_to(row, (16, row.shape[1])), pairs_ref[...], 3, dims)[0:1]
-
-    sub, lane = iota((SIDE, LANES), 0), iota((SIDE, LANES), 1)
 
     def margin(x, z, y):
         return forward.ref[pl.ds(forward.start(x, z, y) + device, 1), :]
@@ -701,7 +650,7 @@
         each(put)
         rolled(SIDE, fine.base.close_z)
         fine.base.close()
-        cycle(0, forward, exact=True)
+        cycle(0, forward)
         extract(index)
 
         @pl.when(index == 0)
@@ -755,12 +704,8 @@
             jax.ShapeDtypeStruct((total, LANES), f32),
             jax.ShapeDtypeStruct((total // 2, LANES), f32),
         ),
-        in_specs=[pl.BlockSpec(memory_space=pl.ANY)],
+        in_specs=[vmem],
         out_specs=(vmem, vmem),
-        scratch_shapes=[
-            pltpu.VMEM((rows, cols, LANES), f32),
-            pltpu.SemaphoreType.DMA((rows,)),
-        ],
         compiler_params=pltpu.CompilerParams(vmem_limit_bytes=SMALL_BYTES),
     )(conductivity)
     swap = [(0, 1), (1, 0)]

time: 57.3 us -> 54.8 us (0.956)
  Pallas kernels: 27 us -> 24.5 us
    pallas_call x1, Pallas kernels: 3.47 us -> 0.58 us  [replicated(): pl.pallas_call(to_blocks_kernel, out_shape=(jax.ShapeDtypeStruct((total,...]
where the time goes in v12:
time: 54.8 us; the launch traced here: 54.6 us
  Pallas kernels  24.5 us (45%)
  waiting for transfers between devices  14.9 us (27%)
  starting transfers between devices  12.1 us (22%)
  local copies, waits for them, and re-layouts  1.76 us (3%)
  between operations  0.71 us (1%)
  other arithmetic  0.67 us (1%)
    pallas_call x1, Pallas kernels, replicated(): pl.pallas_call(functools.partial(replicated_kernel, len(parts), len(halve...  23.5 us
    ppermute x3, waiting for transfers between devices, partner(): return lax.ppermute(part, 'gx', [(i, i ^ k) for i in range(count)])  6.72 us
    ppermute x3, starting transfers between devices, partner(): return lax.ppermute(part, 'gx', [(i, i ^ k) for i in range(count)])  6.34 us
    ppermute x1, waiting for transfers between devices, replicated(): return (potentials[None], own + lax.ppermute(theirs, 'shot', swap))  4.01 us
    ppermute x2, starting transfers between devices, replicated(): lax.ppermute(own, 'shot', swap)  3.03 us
    ppermute x2, waiting for transfers between devices, replicated(): lax.ppermute(own, 'shot', swap)  2.84 us
    unnamed x11, local copies, waits for them, and re-layouts  1.76 us
    ppermute x1, starting transfers between devices, replicated(): return (potentials[None], own + lax.ppermute(theirs, 'shot', swap))  1.6 us
  transfers between devices with their start and end apart: 12, of which 5 were waited for; matrix products, arithmetic and copies ran while one was open for 0% of the time, Pallas kernels for 1%

profile of v12, /device:TPU:0, one launch (start us, length us, event | category | flops | bytes accessed | tf_op | source)
XLA Modules:
  0.0 54.6 jit_solution(11980772933096097124)
XLA Ops:
  0.6 0.9 %copy-done = f32[8,64,128]{2,1,0:T(8,128)S(1)} copy-done((f32[8,64,128]{2,1,0:T(8,128)S(1)}, f32[8,64,128]{2,1,0:T(8,128)}, u32[]{:S(2)}) %copy-start) | copy-done | bytes 262168
  1.6 0.6 %shard_map.69 = (f32[512,128]{1,0:T(8,128)S(1)}, f32[256,128]{1,0:T(8,128)S(1)}) custom-call(f32[8,64,128]{2,1,0:T(8,128)S(1)} %copy-done), custom_call_target="tpu_custom_call" | custom-call | tf_op jit(solution)/shard_map/pallas_call | solution.py:701
  2.2 4.1 %collective-permute-start.3 = (f32[256,128]{1,0:T(8,128)S(1)}, f32[256,128]{1,0:T(8,128)S(1)}, u32[]{:S(2)}, u32[]{:S(2)}) collective-permute-start(f32[256,128]{1,0:T(8,128)S(1)} %get-tuple-element.17), channel_id=1, source_target_pairs={{0,8},{4,12},{8,0},{12,4},{1,9},{5,13},{9,1},{13,5},{2,10},{6,14},... | collective-permute-start | bytes 393224 | tf_op jit(solution)/shard_map/ppermute | solution.py:715
  6.3 1.6 %collective-permute-start.1 = (f32[512,128]{1,0:T(8,128)S(1)}, f32[512,128]{1,0:T(8,128)S(1)}, u32[]{:S(2)}, u32[]{:S(2)}) collective-permute-start(f32[512,128]{1,0:T(8,128)S(1)} %get-tuple-element.16.refs_0_), channel_id=1, source_target_pairs={{0,4},{4,0},{8,12},{12,8},{1,5},{5,1},{9,13},{13,9},{2,6},{6,2},{1... | collective-permute-start | bytes 786440 | tf_op jit(solution)/shard_map/ppermute | solution.py:715
  7.9 0.1 copy.7.receivers_ref
  8.0 0.0 copy-start.2
  8.0 0.5 copy-done.3
  8.5 0.2 copy-done.2
  8.7 0.4 shard_map.68
  9.1 3.6 %collective-permute-done.3.refs_4_ = f32[256,128]{1,0:T(8,128)S(1)} collective-permute-done((f32[256,128]{1,0:T(8,128)S(1)}, f32[256,128]{1,0:T(8,128)S(1)}, u32[]{:S(2)}, u32[]{:S(2)}) %collective-permute-start.3) | collective-permute-done | bytes 131104 | tf_op jit(solution)/shard_map/ppermute | solution.py:715
  12.7 0.7 %collective-permute-start.7 = (f32[256,128]{1,0:T(8,128)S(1)}, f32[256,128]{1,0:T(8,128)S(1)}, u32[]{:S(2)}, u32[]{:S(2)}) collective-permute-start(f32[256,128]{1,0:T(8,128)S(1)} %collective-permute-done.3.refs_4_), channel_id=1, source_target_pairs={{0,4},{4,0},{8,12},{12,8},{1,5},{5,1},{9,13},{13,9},{2,6},{6,2},{1... | collective-permute-start | bytes 393224 | tf_op jit(solution)/shard_map/ppermute | solution.py:715
  13.3 1.5 %collective-permute-start.5 = (f32[256,128]{1,0:T(8,128)S(1)}, f32[256,128]{1,0:T(8,128)S(1)}, u32[]{:S(2)}, u32[]{:S(2)}) collective-permute-start(f32[256,128]{1,0:T(8,128)S(1)} %collective-permute-done.3.refs_4_), channel_id=1, source_target_pairs={{0,1},{1,0},{2,3},{3,2},{4,5},{5,4},{6,7},{7,6},{8,9},{9,8},{10,11... | collective-permute-start | bytes 393224 | tf_op jit(solution)/shard_map/ppermute | solution.py:740
  14.8 0.0 collective-permute-start
  14.8 0.5 collective-permute-start.4
  15.3 3.1 %collective-permute-done.7.refs_8_ = f32[256,128]{1,0:T(8,128)S(1)} collective-permute-done((f32[256,128]{1,0:T(8,128)S(1)}, f32[256,128]{1,0:T(8,128)S(1)}, u32[]{:S(2)}, u32[]{:S(2)}) %collective-permute-start.7) | collective-permute-done | bytes 131104 | tf_op jit(solution)/shard_map/ppermute | solution.py:715
  18.5 1.5 %collective-permute-start.9 = (f32[256,128]{1,0:T(8,128)S(1)}, f32[256,128]{1,0:T(8,128)S(1)}, u32[]{:S(2)}, u32[]{:S(2)}) collective-permute-start(f32[256,128]{1,0:T(8,128)S(1)} %collective-permute-done.7.refs_8_), channel_id=1, source_target_pairs={{0,1},{1,0},{2,3},{3,2},{4,5},{5,4},{6,7},{7,6},{8,9},{9,8},{10,11... | collective-permute-start | bytes 393224 | tf_op jit(solution)/shard_map/ppermute | solution.py:740
  20.0 0.0 collective-permute-done.1.refs_2_
  20.0 0.0 collective-permute-start.2
  20.0 0.0 collective-permute-done.5.refs_6_
  20.0 0.5 collective-permute-start.8
  20.6 0.0 collective-permute-done.4.refs_5_
  20.6 0.1 collective-permute-start.6
  20.6 2.8 %collective-permute-done.9.refs_10_ = f32[256,128]{1,0:T(8,128)S(1)} collective-permute-done((f32[256,128]{1,0:T(8,128)S(1)}, f32[256,128]{1,0:T(8,128)S(1)}, u32[]{:S(2)}, u32[]{:S(2)}) %collective-permute-start.9) | collective-permute-done | bytes 131104 | tf_op jit(solution)/shard_map/ppermute | solution.py:740
  23.5 0.0 collective-permute-start.10
  23.5 0.0 collective-permute-done.refs_1_
  23.5 0.0 collective-permute-done.8.refs_9_
  23.5 1.3 %collective-permute-done.10.refs_11_ = f32[256,128]{1,0:T(8,128)S(1)} collective-permute-done((f32[256,128]{1,0:T(8,128)S(1)}, f32[256,128]{1,0:T(8,128)S(1)}, u32[]{:S(2)}, u32[]{:S(2)}) %collective-permute-start.10) | collective-permute-done | bytes 131104 | tf_op jit(solution)/shard_map/ppermute | solution.py:718
  24.8 0.0 collective-permute-done.2.refs_3_
  24.8 23.5 %shard_map.70 = (f32[8,64,128]{2,1,0:T(8,128)}, f32[8,32,128]{2,1,0:T(8,128)S(1)}, f32[8,32,128]{2,1,0:T(8,128)S(1)}) custom-call(s32[1,256]{1,0:T(1,128)S(1)} %get-tuple-element.15.cells_ref, f32[512,128]{1,0:T(8,128)S(1)} %get-tuple-element.16.refs_0_, f32[512,128]{1,0:T(8,128)S(1)} %collective-permute-done.refs_1_, ...), custom_call_target="tpu_custom_call" | custom-call | flops 200000000 | bytes 4000000 | tf_op jit(solution)/shard_map/pallas_call | solution.py:746
  48.3 1.6 %collective-permute-start.11 = (f32[8,32,128]{2,1,0:T(8,128)S(1)}, f32[8,32,128]{2,1,0:T(8,128)S(1)}, u32[]{:S(2)}, u32[]{:S(2)}) collective-permute-start(f32[8,32,128]{2,1,0:T(8,128)S(1)} %get-tuple-element.27), channel_id=1, source_target_pairs={{0,1},{1,0},{2,3},{3,2},{4,5},{5,4},{6,7},{7,6},{8,9},{9,8},{10,11... | collective-permute-start | bytes 393224 | tf_op jit(solution)/shard_map/ppermute | solution.py:766
  49.9 4.0 %collective-permute-done.11 = f32[8,32,128]{2,1,0:T(8,128)S(1)} collective-permute-done((f32[8,32,128]{2,1,0:T(8,128)S(1)}, f32[8,32,128]{2,1,0:T(8,128)S(1)}, u32[]{:S(2)}, u32[]{:S(2)}) %collective-permute-start.11) | collective-permute-done | bytes 131104 | tf_op jit(solution)/shard_map/ppermute | solution.py:766
  53.9 0.7 %add.3 = f32[8,32,128]{2,1,0:T(8,128)} add(f32[8,32,128]{2,1,0:T(8,128)S(1)} %get-tuple-element.26, f32[8,32,128]{2,1,0:T(8,128)S(1)} %collective-permute-done.11) | non-fusion elementwise | flops 32768 | bytes 393216 | tf_op jit(solution)/shard_map/add | solution.py:766
  (7 shorter events, 0.0 us)
Async XLA Ops:
  0.6 1.0 %copy-start = (f32[8,64,128]{2,1,0:T(8,128)S(1)}, f32[8,64,128]{2,1,0:T(8,128)}, u32[]{:S(2)}) copy-start(f32[8,64,128]{2,1,0:T(8,128)} %natural_ref.1) | copy-start | bytes 786436
  1.6 6.3 %copy-start.4 = (s32[512,2]{0,1:T(2,128)S(1)}, s32[512,2]{0,1:T(2,128)}, u32[]{:S(2)}) copy-start(s32[512,2]{0,1:T(2,128)} %param.8) | copy-start | bytes 12292
  2.2 10.5 %collective-permute-start.3 = (f32[256,128]{1,0:T(8,128)S(1)}, f32[256,128]{1,0:T(8,128)S(1)}, u32[]{:S(2)}, u32[]{:S(2)}) collective-permute-start(f32[256,128]{1,0:T(8,128)S(1)} %get-tuple-element.17), channel_id=1, source_target_pairs={{0,8},{4,12},{8,0},{12,4},{1,9},{5,13},{9,1},{13,5},{2,10},{6,14},... | collective-permute-start | bytes 393224 | tf_op jit(solution)/shard_map/ppermute | solution.py:715
  6.3 1.7 %copy-start.1 = (f32[1,512]{1,0:T(1,128)S(1)}, f32[1,512]{1,0:T(1,128)}, u32[]{:S(2)}) copy-start(f32[1,512]{1,0:T(1,128)} %observed_ref.1) | copy-start | bytes 6148
  6.3 13.8 %collective-permute-start.1 = (f32[512,128]{1,0:T(8,128)S(1)}, f32[512,128]{1,0:T(8,128)S(1)}, u32[]{:S(2)}, u32[]{:S(2)}) collective-permute-start(f32[512,128]{1,0:T(8,128)S(1)} %get-tuple-element.16.refs_0_), channel_id=1, source_target_pairs={{0,4},{4,0},{8,12},{12,8},{1,5},{5,1},{9,13},{13,9},{2,6},{6,2},{1... | collective-permute-start | bytes 786440 | tf_op jit(solution)/shard_map/ppermute | solution.py:715
  7.9 0.7 %copy-start.3 = (f32[1,256]{1,0:T(1,128)S(1)}, f32[1,256]{1,0:T(1,128)}, u32[]{:S(2)}) copy-start(f32[1,256]{1,0:T(1,128)} %currents_ref.1) | copy-start | bytes 3076
  8.0 0.7 %copy-start.2 = (s32[256]{0:T(256)S(1)}, s32[256]{0:T(256)}, u32[]{:S(2)}) copy-start(s32[256]{0:T(256)} %param.6) | copy-start | bytes 3076
  12.7 5.8 %collective-permute-start.7 = (f32[256,128]{1,0:T(8,128)S(1)}, f32[256,128]{1,0:T(8,128)S(1)}, u32[]{:S(2)}, u32[]{:S(2)}) collective-permute-start(f32[256,128]{1,0:T(8,128)S(1)} %collective-permute-done.3.refs_4_), channel_id=1, source_target_pairs={{0,4},{4,0},{8,12},{12,8},{1,5},{5,1},{9,13},{13,9},{2,6},{6,2},{1... | collective-permute-start | bytes 393224 | tf_op jit(solution)/shard_map/ppermute | solution.py:715
  13.3 6.7 %collective-permute-start.5 = (f32[256,128]{1,0:T(8,128)S(1)}, f32[256,128]{1,0:T(8,128)S(1)}, u32[]{:S(2)}, u32[]{:S(2)}) collective-permute-start(f32[256,128]{1,0:T(8,128)S(1)} %collective-permute-done.3.refs_4_), channel_id=1, source_target_pairs={{0,1},{1,0},{2,3},{3,2},{4,5},{5,4},{6,7},{7,6},{8,9},{9,8},{10,11... | collective-permute-start | bytes 393224 | tf_op jit(solution)/shard_map/ppermute | solution.py:740
  14.8 8.6 %collective-permute-start = (f32[512,128]{1,0:T(8,128)S(1)}, f32[512,128]{1,0:T(8,128)S(1)}, u32[]{:S(2)}, u32[]{:S(2)}) collective-permute-start(f32[512,128]{1,0:T(8,128)S(1)} %get-tuple-element.16.refs_0_), channel_id=1, source_target_pairs={{0,2},{2,0},{1,3},{3,1},{4,6},{6,4},{5,7},{7,5},{8,10},{10,8},{9,1... | collective-permute-start | bytes 786440 | tf_op jit(solution)/shard_map/ppermute | solution.py:718
  14.8 5.7 %collective-permute-start.4 = (f32[256,128]{1,0:T(8,128)S(1)}, f32[256,128]{1,0:T(8,128)S(1)}, u32[]{:S(2)}, u32[]{:S(2)}) collective-permute-start(f32[256,128]{1,0:T(8,128)S(1)} %collective-permute-done.3.refs_4_), channel_id=1, source_target_pairs={{0,2},{2,0},{1,3},{3,1},{4,6},{6,4},{5,7},{7,5},{8,10},{10,8},{9,1... | collective-permute-start | bytes 393224 | tf_op jit(solution)/shard_map/ppermute | solution.py:718
  18.5 5.0 %collective-permute-start.9 = (f32[256,128]{1,0:T(8,128)S(1)}, f32[256,128]{1,0:T(8,128)S(1)}, u32[]{:S(2)}, u32[]{:S(2)}) collective-permute-start(f32[256,128]{1,0:T(8,128)S(1)} %collective-permute-done.7.refs_8_), channel_id=1, source_target_pairs={{0,1},{1,0},{2,3},{3,2},{4,5},{5,4},{6,7},{7,6},{8,9},{9,8},{10,11... | collective-permute-start | bytes 393224 | tf_op jit(solution)/shard_map/ppermute | solution.py:740
  20.0 4.8 %collective-permute-start.2 = (f32[512,128]{1,0:T(8,128)S(1)}, f32[512,128]{1,0:T(8,128)S(1)}, u32[]{:S(2)}, u32[]{:S(2)}) collective-permute-start(f32[512,128]{1,0:T(8,128)S(1)} %collective-permute-done.1.refs_2_), channel_id=1, source_target_pairs={{0,2},{2,0},{1,3},{3,1},{4,6},{6,4},{5,7},{7,5},{8,10},{10,8},{9,1... | collective-permute-start | bytes 786440 | tf_op jit(solution)/shard_map/ppermute | solution.py:718
  20.0 3.4 %collective-permute-start.8 = (f32[256,128]{1,0:T(8,128)S(1)}, f32[256,128]{1,0:T(8,128)S(1)}, u32[]{:S(2)}, u32[]{:S(2)}) collective-permute-start(f32[256,128]{1,0:T(8,128)S(1)} %collective-permute-done.7.refs_8_), channel_id=1, source_target_pairs={{0,2},{2,0},{1,3},{3,1},{4,6},{6,4},{5,7},{7,5},{8,10},{10,8},{9,1... | collective-permute-start | bytes 393224 | tf_op jit(solution)/shard_map/ppermute | solution.py:718
  20.6 2.9 %collective-permute-start.6 = (f32[256,128]{1,0:T(8,128)S(1)}, f32[256,128]{1,0:T(8,128)S(1)}, u32[]{:S(2)}, u32[]{:S(2)}) collective-permute-start(f32[256,128]{1,0:T(8,128)S(1)} %collective-permute-done.5.refs_6_), channel_id=1, source_target_pairs={{0,2},{2,0},{1,3},{3,1},{4,6},{6,4},{5,7},{7,5},{8,10},{10,8},{9,1... | collective-permute-start | bytes 393224 | tf_op jit(solution)/shard_map/ppermute | solution.py:718
  23.5 1.3 %collective-permute-start.10 = (f32[256,128]{1,0:T(8,128)S(1)}, f32[256,128]{1,0:T(8,128)S(1)}, u32[]{:S(2)}, u32[]{:S(2)}) collective-permute-start(f32[256,128]{1,0:T(8,128)S(1)} %collective-permute-done.9.refs_10_), channel_id=1, source_target_pairs={{0,2},{2,0},{1,3},{3,1},{4,6},{6,4},{5,7},{7,5},{8,10},{10,8},{9,1... | collective-permute-start | bytes 393224 | tf_op jit(solution)/shard_map/ppermute | solution.py:718
  48.3 5.6 %collective-permute-start.11 = (f32[8,32,128]{2,1,0:T(8,128)S(1)}, f32[8,32,128]{2,1,0:T(8,128)S(1)}, u32[]{:S(2)}, u32[]{:S(2)}) collective-permute-start(f32[8,32,128]{2,1,0:T(8,128)S(1)} %get-tuple-element.27), channel_id=1, source_target_pairs={{0,1},{1,0},{2,3},{3,2},{4,5},{5,4},{6,7},{7,6},{8,9},{9,8},{10,11... | collective-permute-start | bytes 393224 | tf_op jit(solution)/shard_map/ppermute | solution.py:766

commit v13 on v11

--- a/solution.py
+++ b/solution.py
@@ -48,8 +48,10 @@
     return cell_x, cell_y, cell_z, row, (cell_y >> 3 & 7) * GROUP + (cell_z >> 3)
 
 
-def lane_order():
+def lane_order(back=False):
     row, col = iota((LANES, LANES), 0), iota((LANES, LANES), 1)
+    if back:
+        row, col = col, row
     chosen = row == col % GROUP * SIDE + col // GROUP
     return jnp.where(chosen, 1.0, 0.0).astype(jnp.bfloat16)
 
@@ -72,16 +74,10 @@
     return lax.axis_index("gx") * 2 + lax.axis_index("gy"), lax.axis_index("shot")
 
 
-def to_blocks_kernel(natural_ref, blocks_ref, half_ref, planes, sems):
-    copies = [
-        pltpu.make_async_copy(natural_ref.at[x], planes.at[x], sems.at[x]) for x in range(SIDE)
-    ]
-    for copy in copies:
-        copy.start()
+def to_blocks_kernel(natural_ref, blocks_ref, half_ref):
     order = lane_order()
     for x in range(SIDE):
-        copies[x].wait()
-        tiles = product(planes[x], order, 3)
+        tiles = product(natural_ref[x], order, 3)
         tiles = [tiles[SIDE * k : SIDE * (k + 1)] for k in range(SIDE)]
         for z, tile in enumerate(exchange_groups(tiles)):
             blocks_ref[pl.ds((x * SIDE + z) * SIDE, SIDE), :] = tile
@@ -92,7 +88,7 @@
 
 def from_blocks(tiles, order):
     natural = jnp.concatenate(exchange_groups(tiles), axis=0)
-    return product(natural, order, 3, ((1,), (1,)))
+    return product(natural, order, 3)
 
 
 def block_up(field, axis):
@@ -154,6 +150,7 @@
     rows_ref,
     same_ref,
     pairs_ref,
+    turned_ref,
     held_ref,
 ):
     stations = stations_ref[...]
@@ -175,6 +172,7 @@
         numbers == receivers[:, 1:2], 1.0, 0.0
     )
     pairs_ref[...] = pairs.astype(jnp.bfloat16)
+    turned_ref[...] = pairs.T.astype(jnp.bfloat16)
 
 
 def shared_rows(amounts, spot, same):
@@ -506,6 +504,7 @@
     rows_ref,
     same_ref,
     pairs_ref,
+    turned_ref,
     observed_ref,
     potentials_ref,
     mine_ref,
@@ -652,7 +651,7 @@
 
     spot = spot_ref[...]
     at_spot = iota((LANES, electrodes), 0) == spot
-    order = lane_order()
+    order = lane_order(back=True)
     wide = SIDE + 2
     sending = pltpu.make_async_copy(sent, potentials_ref, sem)
 
@@ -669,8 +668,8 @@
     def read(electrode, cell):
         gathered[electrode, :] = forward.ref[cell, :]
 
-    def exact(row, dims):
-        return product(jnp.broadcast_to(row, (16, row.shape[1])), pairs_ref[...], 3, dims)[0:1]
+    def exact(row, matrix_ref):
+        return product(jnp.broadcast_to(row, (16, row.shape[1])), matrix_ref[...], 3)[0:1]
 
     sub, lane = iota((SIDE, LANES), 0), iota((SIDE, LANES), 1)
 
@@ -713,8 +712,8 @@
             each(read)
             readings = jnp.where(at_spot, gathered[...].T, 0.0)
             readings = jnp.sum(readings, axis=0, keepdims=True)
-            misfit = exact(readings, ((1,), (1,))) - observed_ref[...]
-            gathered[...] = shared_rows(exact(misfit, ((1,), (0,))), spot, same_ref[...])
+            misfit = exact(readings, turned_ref) - observed_ref[...]
+            gathered[...] = shared_rows(exact(misfit, pairs_ref), spot, same_ref[...])
 
     gathered[...] = rows_ref[...]
     rolled(2, solve)
@@ -755,12 +754,8 @@
             jax.ShapeDtypeStruct((total, LANES), f32),
             jax.ShapeDtypeStruct((total // 2, LANES), f32),
         ),
-        in_specs=[pl.BlockSpec(memory_space=pl.ANY)],
+        in_specs=[vmem],
         out_specs=(vmem, vmem),
-        scratch_shapes=[
-            pltpu.VMEM((rows, cols, LANES), f32),
-            pltpu.SemaphoreType.DMA((rows,)),
-        ],
         compiler_params=pltpu.CompilerParams(vmem_limit_bytes=SMALL_BYTES),
     )(conductivity)
     swap = [(0, 1), (1, 0)]
@@ -775,7 +770,7 @@
     far = partner(half, 2)
     near = partner(mine, 1)
     line = jax.ShapeDtypeStruct((1, electrodes), jnp.int32)
-    cells, spot, rows_of, same, pairs, held = pl.pallas_call(
+    cells, spot, rows_of, same, pairs, turned, held = pl.pallas_call(
         electrode_kernel,
         out_shape=(
             line,
@@ -783,16 +778,17 @@
             jax.ShapeDtypeStruct((electrodes, LANES), f32),
             jax.ShapeDtypeStruct((electrodes, electrodes), jnp.bfloat16),
             jax.ShapeDtypeStruct((receivers.shape[0], electrodes), jnp.bfloat16),
+            jax.ShapeDtypeStruct((electrodes, receivers.shape[0]), jnp.bfloat16),
             jax.ShapeDtypeStruct(observed.shape, f32),
         ),
         in_specs=[vmem] * 4,
-        out_specs=(vmem,) * 6,
+        out_specs=(vmem,) * 7,
         compiler_params=pltpu.CompilerParams(vmem_limit_bytes=SMALL_BYTES),
         cost_estimate=pl.CostEstimate(flops=100_000_000, bytes_accessed=1_000_000, transcendentals=0),
     )(station_row, currents, receivers, observed)
     far, rows_of = lax.optimization_barrier((far, rows_of))
-    far = [far, partner(far, 1)]
-    halved = [piece for own in far for piece in (own, lax.ppermute(own, "shot", swap))]
+    far = [far, lax.ppermute(far, "shot", swap)]
+    halved = far + [partner(piece, 1) for piece in far]
     parts = [piece for own in (mine, near) for piece in with_mate(own)]
     halved = [piece for own in halved for piece in with_mate(own)]
     chunk = cols // 2
@@ -805,7 +801,7 @@
             jax.ShapeDtypeStruct((rows, chunk, LANES), f32),
             jax.ShapeDtypeStruct((rows, chunk, LANES), f32),
         ),
-        in_specs=[smem] + [vmem] * (len(parts) + len(halved) + 5),
+        in_specs=[smem] + [vmem] * (len(parts) + len(halved) + 6),
         out_specs=(pl.BlockSpec(memory_space=pl.ANY), vmem, vmem),
         scratch_shapes=[
             pltpu.VMEM((electrodes, LANES), f32),
@@ -817,7 +813,7 @@
         + levels,
         compiler_params=pltpu.CompilerParams(vmem_limit_bytes=VMEM_BYTES),
         cost_estimate=pl.CostEstimate(flops=200_000_000, bytes_accessed=4_000_000, transcendentals=0),
-    )(cells, *parts, *halved, spot, rows_of, same, pairs, held)
+    )(cells, *parts, *halved, spot, rows_of, same, pairs, turned, held)
     return potentials[None], own + lax.ppermute(theirs, "shot", swap)
 
 

time: 57.3 us -> 53 us (0.925)
  Pallas kernels: 27 us -> 23.6 us
  starting transfers between devices: 12.1 us -> 11.2 us
    pallas_call x1, Pallas kernels: 3.47 us -> 0.58 us  [replicated(): pl.pallas_call(to_blocks_kernel, out_shape=(jax.ShapeDtypeStruct((total,...]
    ppermute x2 -> x1, starting transfers between devices: 3.03 us -> 1.54 us  [replicated(): far = [far, lax.ppermute(far, 'shot', swap)]]
    ppermute x3 -> x4, waiting for transfers between devices: 6.72 us -> 7.91 us  [partner(): return lax.ppermute(part, 'gx', [(i, i ^ k) for i in range(count)])]
    ppermute x3 -> x4, starting transfers between devices: 6.34 us -> 7.4 us  [partner(): return lax.ppermute(part, 'gx', [(i, i ^ k) for i in range(count)])]
    ppermute x2 -> x1, waiting for transfers between devices: 2.84 us -> 1.77 us  [replicated(): far = [far, lax.ppermute(far, 'shot', swap)]]
  transfers between devices with their start and end apart: 12 -> 12, of which waited for: 5 -> 7; matrix products, arithmetic and copies ran while one was open for 0% -> 0% of each run, Pallas kernels for 1% -> 1%
where the time goes in v13:
time: 53 us; the launch traced here: 52.8 us
  Pallas kernels  23.6 us (45%)
  waiting for transfers between devices  14.8 us (28%)
  starting transfers between devices  11.2 us (21%)
  local copies, waits for them, and re-layouts  1.76 us (3%)
  between operations  0.72 us (1%)
  other arithmetic  0.67 us (1%)
    pallas_call x1, Pallas kernels, replicated(): pl.pallas_call(functools.partial(replicated_kernel, len(parts), len(halve...  22.6 us
    ppermute x4, waiting for transfers between devices, partner(): return lax.ppermute(part, 'gx', [(i, i ^ k) for i in range(count)])  7.91 us
    ppermute x4, starting transfers between devices, partner(): return lax.ppermute(part, 'gx', [(i, i ^ k) for i in range(count)])  7.4 us
    ppermute x1, waiting for transfers between devices, replicated(): return (potentials[None], own + lax.ppermute(theirs, 'shot', swap))  3.83 us
    ppermute x1, starting transfers between devices, replicated(): return (potentials[None], own + lax.ppermute(theirs, 'shot', swap))  1.78 us
    ppermute x1, waiting for transfers between devices, replicated(): far = [far, lax.ppermute(far, 'shot', swap)]  1.77 us
    unnamed x11, local copies, waits for them, and re-layouts  1.76 us
    ppermute x1, starting transfers between devices, replicated(): far = [far, lax.ppermute(far, 'shot', swap)]  1.54 us
  transfers between devices with their start and end apart: 12, of which 7 were waited for; matrix products, arithmetic and copies ran while one was open for 0% of the time, Pallas kernels for 1%

profile of v13, /device:TPU:0, one launch (start us, length us, event | category | flops | bytes accessed | tf_op | source)
XLA Modules:
  0.0 52.8 jit_solution(17978517682504204452)
XLA Ops:
  0.6 0.9 %copy-done = f32[8,64,128]{2,1,0:T(8,128)S(1)} copy-done((f32[8,64,128]{2,1,0:T(8,128)S(1)}, f32[8,64,128]{2,1,0:T(8,128)}, u32[]{:S(2)}) %copy-start) | copy-done | bytes 262168
  1.6 0.6 %shard_map.69 = (f32[512,128]{1,0:T(8,128)S(1)}, f32[256,128]{1,0:T(8,128)S(1)}) custom-call(f32[8,64,128]{2,1,0:T(8,128)S(1)} %copy-done), custom_call_target="tpu_custom_call" | custom-call | tf_op jit(solution)/shard_map/pallas_call | solution.py:751
  2.2 4.1 %collective-permute-start.3 = (f32[256,128]{1,0:T(8,128)S(1)}, f32[256,128]{1,0:T(8,128)S(1)}, u32[]{:S(2)}, u32[]{:S(2)}) collective-permute-start(f32[256,128]{1,0:T(8,128)S(1)} %get-tuple-element.18), channel_id=1, source_target_pairs={{0,8},{4,12},{8,0},{12,4},{1,9},{5,13},{9,1},{13,5},{2,10},{6,14},... | collective-permute-start | bytes 393224 | tf_op jit(solution)/shard_map/ppermute | solution.py:765
  6.3 1.6 %collective-permute-start.1 = (f32[512,128]{1,0:T(8,128)S(1)}, f32[512,128]{1,0:T(8,128)S(1)}, u32[]{:S(2)}, u32[]{:S(2)}) collective-permute-start(f32[512,128]{1,0:T(8,128)S(1)} %get-tuple-element.17.refs_0_), channel_id=1, source_target_pairs={{0,4},{4,0},{8,12},{12,8},{1,5},{5,1},{9,13},{13,9},{2,6},{6,2},{1... | collective-permute-start | bytes 786440 | tf_op jit(solution)/shard_map/ppermute | solution.py:765
  7.8 0.0 collective-permute-start
  7.9 0.1 copy.7.receivers_ref
  8.0 0.0 copy-start.2
  8.0 0.5 copy-done.3
  8.5 0.2 copy-done.2
  8.7 0.4 shard_map.68
  9.1 3.5 %collective-permute-done.3.refs_4_ = f32[256,128]{1,0:T(8,128)S(1)} collective-permute-done((f32[256,128]{1,0:T(8,128)S(1)}, f32[256,128]{1,0:T(8,128)S(1)}, u32[]{:S(2)}, u32[]{:S(2)}) %collective-permute-start.3) | collective-permute-done | bytes 131104 | tf_op jit(solution)/shard_map/ppermute | solution.py:765
  12.7 1.5 %collective-permute-start.5 = (f32[256,128]{1,0:T(8,128)S(1)}, f32[256,128]{1,0:T(8,128)S(1)}, u32[]{:S(2)}, u32[]{:S(2)}) collective-permute-start(f32[256,128]{1,0:T(8,128)S(1)} %collective-permute-done.3.refs_4_), channel_id=1, source_target_pairs={{0,1},{1,0},{2,3},{3,2},{4,5},{5,4},{6,7},{7,6},{8,9},{9,8},{10,11... | collective-permute-start | bytes 393224 | tf_op jit(solution)/shard_map/ppermute | solution.py:790
  14.2 0.6 %collective-permute-start.7 = (f32[256,128]{1,0:T(8,128)S(1)}, f32[256,128]{1,0:T(8,128)S(1)}, u32[]{:S(2)}, u32[]{:S(2)}) collective-permute-start(f32[256,128]{1,0:T(8,128)S(1)} %collective-permute-done.3.refs_4_), channel_id=1, source_target_pairs={{0,4},{4,0},{8,12},{12,8},{1,5},{5,1},{9,13},{13,9},{2,6},{6,2},{1... | collective-permute-start | bytes 393224 | tf_op jit(solution)/shard_map/ppermute | solution.py:765
  14.8 1.0 %collective-permute-done.1.refs_2_ = f32[512,128]{1,0:T(8,128)S(1)} collective-permute-done((f32[512,128]{1,0:T(8,128)S(1)}, f32[512,128]{1,0:T(8,128)S(1)}, u32[]{:S(2)}, u32[]{:S(2)}) %collective-permute-start.1) | collective-permute-done | bytes 262176 | tf_op jit(solution)/shard_map/ppermute | solution.py:765
  15.9 0.0 collective-permute-start.2
  15.9 1.8 %collective-permute-done.5.refs_6_ = f32[256,128]{1,0:T(8,128)S(1)} collective-permute-done((f32[256,128]{1,0:T(8,128)S(1)}, f32[256,128]{1,0:T(8,128)S(1)}, u32[]{:S(2)}, u32[]{:S(2)}) %collective-permute-start.5) | collective-permute-done | bytes 131104 | tf_op jit(solution)/shard_map/ppermute | solution.py:790
  17.7 1.1 %collective-permute-start.9 = (f32[256,128]{1,0:T(8,128)S(1)}, f32[256,128]{1,0:T(8,128)S(1)}, u32[]{:S(2)}, u32[]{:S(2)}) collective-permute-start(f32[256,128]{1,0:T(8,128)S(1)} %collective-permute-done.5.refs_6_), channel_id=1, source_target_pairs={{0,4},{4,0},{8,12},{12,8},{1,5},{5,1},{9,13},{13,9},{2,6},{6,2},{1... | collective-permute-start | bytes 393224 | tf_op jit(solution)/shard_map/ppermute | solution.py:765
  18.8 0.0 collective-permute-start.4
  18.8 0.6 %collective-permute-done.7.refs_8_ = f32[256,128]{1,0:T(8,128)S(1)} collective-permute-done((f32[256,128]{1,0:T(8,128)S(1)}, f32[256,128]{1,0:T(8,128)S(1)}, u32[]{:S(2)}, u32[]{:S(2)}) %collective-permute-start.7) | collective-permute-done | bytes 131104 | tf_op jit(solution)/shard_map/ppermute | solution.py:765
  19.4 0.0 collective-permute-start.8
  19.4 0.0 collective-permute-done.refs_1_
  19.4 0.5 collective-permute-start.6
  19.9 2.7 %collective-permute-done.9.refs_10_ = f32[256,128]{1,0:T(8,128)S(1)} collective-permute-done((f32[256,128]{1,0:T(8,128)S(1)}, f32[256,128]{1,0:T(8,128)S(1)}, u32[]{:S(2)}, u32[]{:S(2)}) %collective-permute-start.9) | collective-permute-done | bytes 131104 | tf_op jit(solution)/shard_map/ppermute | solution.py:765
  22.6 0.0 collective-permute-start.10
  22.6 0.0 collective-permute-done.4.refs_5_
  22.6 0.0 collective-permute-done.8.refs_9_
  22.6 0.0 collective-permute-done.2.refs_3_
  22.7 1.3 %collective-permute-done.10.refs_11_ = f32[256,128]{1,0:T(8,128)S(1)} collective-permute-done((f32[256,128]{1,0:T(8,128)S(1)}, f32[256,128]{1,0:T(8,128)S(1)}, u32[]{:S(2)}, u32[]{:S(2)}) %collective-permute-start.10) | collective-permute-done | bytes 131104 | tf_op jit(solution)/shard_map/ppermute | solution.py:768
  24.0 22.6 %shard_map.70 = (f32[8,64,128]{2,1,0:T(8,128)}, f32[8,32,128]{2,1,0:T(8,128)S(1)}, f32[8,32,128]{2,1,0:T(8,128)S(1)}) custom-call(s32[1,256]{1,0:T(1,128)S(1)} %get-tuple-element.16.cells_ref, f32[512,128]{1,0:T(8,128)S(1)} %get-tuple-element.17.refs_0_, f32[512,128]{1,0:T(8,128)S(1)} %collective-permute-done.refs_1_, ...), custom_call_target="tpu_custom_call" | custom-call | flops 200000000 | bytes 4000000 | tf_op jit(solution)/shard_map/pallas_call | solution.py:797
  46.6 1.8 %collective-permute-start.11 = (f32[8,32,128]{2,1,0:T(8,128)S(1)}, f32[8,32,128]{2,1,0:T(8,128)S(1)}, u32[]{:S(2)}, u32[]{:S(2)}) collective-permute-start(f32[8,32,128]{2,1,0:T(8,128)S(1)} %get-tuple-element.29), channel_id=1, source_target_pairs={{0,1},{1,0},{2,3},{3,2},{4,5},{5,4},{6,7},{7,6},{8,9},{9,8},{10,11... | collective-permute-start | bytes 393224 | tf_op jit(solution)/shard_map/ppermute | solution.py:817
  48.3 3.8 %collective-permute-done.11 = f32[8,32,128]{2,1,0:T(8,128)S(1)} collective-permute-done((f32[8,32,128]{2,1,0:T(8,128)S(1)}, f32[8,32,128]{2,1,0:T(8,128)S(1)}, u32[]{:S(2)}, u32[]{:S(2)}) %collective-permute-start.11) | collective-permute-done | bytes 131104 | tf_op jit(solution)/shard_map/ppermute | solution.py:817
  52.2 0.7 %add.3 = f32[8,32,128]{2,1,0:T(8,128)} add(f32[8,32,128]{2,1,0:T(8,128)S(1)} %get-tuple-element.28, f32[8,32,128]{2,1,0:T(8,128)S(1)} %collective-permute-done.11) | non-fusion elementwise | flops 32768 | bytes 393216 | tf_op jit(solution)/shard_map/add | solution.py:817
  (7 shorter events, 0.0 us)
Async XLA Ops:
  0.6 1.0 %copy-start = (f32[8,64,128]{2,1,0:T(8,128)S(1)}, f32[8,64,128]{2,1,0:T(8,128)}, u32[]{:S(2)}) copy-start(f32[8,64,128]{2,1,0:T(8,128)} %natural_ref.1) | copy-start | bytes 786436
  1.6 6.3 %copy-start.4 = (s32[512,2]{0,1:T(2,128)S(1)}, s32[512,2]{0,1:T(2,128)}, u32[]{:S(2)}) copy-start(s32[512,2]{0,1:T(2,128)} %param.8) | copy-start | bytes 12292
  2.2 10.5 %collective-permute-start.3 = (f32[256,128]{1,0:T(8,128)S(1)}, f32[256,128]{1,0:T(8,128)S(1)}, u32[]{:S(2)}, u32[]{:S(2)}) collective-permute-start(f32[256,128]{1,0:T(8,128)S(1)} %get-tuple-element.18), channel_id=1, source_target_pairs={{0,8},{4,12},{8,0},{12,4},{1,9},{5,13},{9,1},{13,5},{2,10},{6,14},... | collective-permute-start | bytes 393224 | tf_op jit(solution)/shard_map/ppermute | solution.py:765
  6.3 1.8 %copy-start.1 = (f32[1,512]{1,0:T(1,128)S(1)}, f32[1,512]{1,0:T(1,128)}, u32[]{:S(2)}) copy-start(f32[1,512]{1,0:T(1,128)} %observed_ref.1) | copy-start | bytes 6148
  6.3 9.6 %collective-permute-start.1 = (f32[512,128]{1,0:T(8,128)S(1)}, f32[512,128]{1,0:T(8,128)S(1)}, u32[]{:S(2)}, u32[]{:S(2)}) collective-permute-start(f32[512,128]{1,0:T(8,128)S(1)} %get-tuple-element.17.refs_0_), channel_id=1, source_target_pairs={{0,4},{4,0},{8,12},{12,8},{1,5},{5,1},{9,13},{13,9},{2,6},{6,2},{1... | collective-permute-start | bytes 786440 | tf_op jit(solution)/shard_map/ppermute | solution.py:765
  7.8 11.5 %collective-permute-start = (f32[512,128]{1,0:T(8,128)S(1)}, f32[512,128]{1,0:T(8,128)S(1)}, u32[]{:S(2)}, u32[]{:S(2)}) collective-permute-start(f32[512,128]{1,0:T(8,128)S(1)} %get-tuple-element.17.refs_0_), channel_id=1, source_target_pairs={{0,2},{2,0},{1,3},{3,1},{4,6},{6,4},{5,7},{7,5},{8,10},{10,8},{9,1... | collective-permute-start | bytes 786440 | tf_op jit(solution)/shard_map/ppermute | solution.py:768
  7.9 0.7 %copy-start.3 = (f32[1,256]{1,0:T(1,128)S(1)}, f32[1,256]{1,0:T(1,128)}, u32[]{:S(2)}) copy-start(f32[1,256]{1,0:T(1,128)} %currents_ref.1) | copy-start | bytes 3076
  8.0 0.7 %copy-start.2 = (s32[256]{0:T(256)S(1)}, s32[256]{0:T(256)}, u32[]{:S(2)}) copy-start(s32[256]{0:T(256)} %param.6) | copy-start | bytes 3076
  12.7 5.0 %collective-permute-start.5 = (f32[256,128]{1,0:T(8,128)S(1)}, f32[256,128]{1,0:T(8,128)S(1)}, u32[]{:S(2)}, u32[]{:S(2)}) collective-permute-start(f32[256,128]{1,0:T(8,128)S(1)} %collective-permute-done.3.refs_4_), channel_id=1, source_target_pairs={{0,1},{1,0},{2,3},{3,2},{4,5},{5,4},{6,7},{7,6},{8,9},{9,8},{10,11... | collective-permute-start | bytes 393224 | tf_op jit(solution)/shard_map/ppermute | solution.py:790
  14.2 5.1 %collective-permute-start.7 = (f32[256,128]{1,0:T(8,128)S(1)}, f32[256,128]{1,0:T(8,128)S(1)}, u32[]{:S(2)}, u32[]{:S(2)}) collective-permute-start(f32[256,128]{1,0:T(8,128)S(1)} %collective-permute-done.3.refs_4_), channel_id=1, source_target_pairs={{0,4},{4,0},{8,12},{12,8},{1,5},{5,1},{9,13},{13,9},{2,6},{6,2},{1... | collective-permute-start | bytes 393224 | tf_op jit(solution)/shard_map/ppermute | solution.py:765
  15.9 6.8 %collective-permute-start.2 = (f32[512,128]{1,0:T(8,128)S(1)}, f32[512,128]{1,0:T(8,128)S(1)}, u32[]{:S(2)}, u32[]{:S(2)}) collective-permute-start(f32[512,128]{1,0:T(8,128)S(1)} %collective-permute-done.1.refs_2_), channel_id=1, source_target_pairs={{0,2},{2,0},{1,3},{3,1},{4,6},{6,4},{5,7},{7,5},{8,10},{10,8},{9,1... | collective-permute-start | bytes 786440 | tf_op jit(solution)/shard_map/ppermute | solution.py:768
  17.7 5.0 %collective-permute-start.9 = (f32[256,128]{1,0:T(8,128)S(1)}, f32[256,128]{1,0:T(8,128)S(1)}, u32[]{:S(2)}, u32[]{:S(2)}) collective-permute-start(f32[256,128]{1,0:T(8,128)S(1)} %collective-permute-done.5.refs_6_), channel_id=1, source_target_pairs={{0,4},{4,0},{8,12},{12,8},{1,5},{5,1},{9,13},{13,9},{2,6},{6,2},{1... | collective-permute-start | bytes 393224 | tf_op jit(solution)/shard_map/ppermute | solution.py:765
  18.8 3.9 %collective-permute-start.4 = (f32[256,128]{1,0:T(8,128)S(1)}, f32[256,128]{1,0:T(8,128)S(1)}, u32[]{:S(2)}, u32[]{:S(2)}) collective-permute-start(f32[256,128]{1,0:T(8,128)S(1)} %collective-permute-done.3.refs_4_), channel_id=1, source_target_pairs={{0,2},{2,0},{1,3},{3,1},{4,6},{6,4},{5,7},{7,5},{8,10},{10,8},{9,1... | collective-permute-start | bytes 393224 | tf_op jit(solution)/shard_map/ppermute | solution.py:768
  19.4 3.3 %collective-permute-start.8 = (f32[256,128]{1,0:T(8,128)S(1)}, f32[256,128]{1,0:T(8,128)S(1)}, u32[]{:S(2)}, u32[]{:S(2)}) collective-permute-start(f32[256,128]{1,0:T(8,128)S(1)} %collective-permute-done.7.refs_8_), channel_id=1, source_target_pairs={{0,2},{2,0},{1,3},{3,1},{4,6},{6,4},{5,7},{7,5},{8,10},{10,8},{9,1... | collective-permute-start | bytes 393224 | tf_op jit(solution)/shard_map/ppermute | solution.py:768
  19.4 3.3 %collective-permute-start.6 = (f32[256,128]{1,0:T(8,128)S(1)}, f32[256,128]{1,0:T(8,128)S(1)}, u32[]{:S(2)}, u32[]{:S(2)}) collective-permute-start(f32[256,128]{1,0:T(8,128)S(1)} %collective-permute-done.5.refs_6_), channel_id=1, source_target_pairs={{0,2},{2,0},{1,3},{3,1},{4,6},{6,4},{5,7},{7,5},{8,10},{10,8},{9,1... | collective-permute-start | bytes 393224 | tf_op jit(solution)/shard_map/ppermute | solution.py:768
  22.6 1.3 %collective-permute-start.10 = (f32[256,128]{1,0:T(8,128)S(1)}, f32[256,128]{1,0:T(8,128)S(1)}, u32[]{:S(2)}, u32[]{:S(2)}) collective-permute-start(f32[256,128]{1,0:T(8,128)S(1)} %collective-permute-done.9.refs_10_), channel_id=1, source_target_pairs={{0,2},{2,0},{1,3},{3,1},{4,6},{6,4},{5,7},{7,5},{8,10},{10,8},{9,1... | collective-permute-start | bytes 393224 | tf_op jit(solution)/shard_map/ppermute | solution.py:768
  46.6 5.6 %collective-permute-start.11 = (f32[8,32,128]{2,1,0:T(8,128)S(1)}, f32[8,32,128]{2,1,0:T(8,128)S(1)}, u32[]{:S(2)}, u32[]{:S(2)}) collective-permute-start(f32[8,32,128]{2,1,0:T(8,128)S(1)} %get-tuple-element.29), channel_id=1, source_target_pairs={{0,1},{1,0},{2,3},{3,2},{4,5},{5,4},{6,7},{7,6},{8,9},{9,8},{10,11... | collective-permute-start | bytes 393224 | tf_op jit(solution)/shard_map/ppermute | solution.py:817

commit v14 on v13

--- a/solution.py
+++ b/solution.py
@@ -250,12 +250,12 @@
         self.ref[self.place(at), :] = value.reshape(-1, LANES)
 
 
-def rolled(count, body):
+def rolled(count, body, unroll=1):
     def one(x, carry):
         body(x)
         return carry
 
-    lax.fori_loop(0, count, one, 0)
+    lax.fori_loop(0, count, one, 0, unroll=unroll)
 
 
 def next_in_y(row):
@@ -315,7 +315,7 @@
                 self.link_z[x, z] = link
 
         if n == SIDE:
-            rolled(n, plane)
+            rolled(n, plane, unroll=2)
         else:
             for x in range(n):
                 plane(x)
@@ -548,10 +548,11 @@
     def edges(x):
         fine.cond.close_z(x, exact=True)
 
-    rolled(SIDE, collect)
+    rolled(SIDE, collect, unroll=4)
     for x in range(SIDE // 2):
         collect_half(x)
-    rolled(SIDE, edges)
+    for x in range(SIDE):
+        edges(x)
     fine.cond.close(exact=True)
 
     coarsest = []
@@ -660,7 +661,7 @@
             body(pl.ds(electrode, 1), pl.ds(cells_ref[0, electrode], 1))
             return carry
 
-        lax.fori_loop(0, electrodes, one, 0, unroll=32)
+        lax.fori_loop(0, electrodes, one, 0, unroll=64)
 
     def put(electrode, cell):
         fine.base.ref[cell, :] = (2.0 * gathered[electrode, :]) * fine.weight.ref[cell, :]
@@ -698,7 +699,8 @@
 
     def solve(index):
         each(put)
-        rolled(SIDE, fine.base.close_z)
+        for x in range(SIDE):
+            fine.base.close_z(x)
         fine.base.close()
         cycle(0, forward, exact=True)
         extract(index)

time: 53 us -> 51.3 us (0.968)
  Pallas kernels: 23.6 us -> 21.9 us
    pallas_call x1, Pallas kernels: 22.6 us -> 20.9 us  [replicated(): pl.pallas_call(functools.partial(replicated_kernel, len(parts), len(halve...]
where the time goes in v14:
time: 51.3 us; the launch traced here: 51.1 us
  Pallas kernels  21.9 us (43%)
  waiting for transfers between devices  14.8 us (29%)
  starting transfers between devices  11.2 us (22%)
  local copies, waits for them, and re-layouts  1.76 us (3%)
  between operations  0.72 us (1%)
  other arithmetic  0.67 us (1%)
    pallas_call x1, Pallas kernels, replicated(): pl.pallas_call(functools.partial(replicated_kernel, len(parts), len(halve...  20.9 us
    ppermute x4, waiting for transfers between devices, partner(): return lax.ppermute(part, 'gx', [(i, i ^ k) for i in range(count)])  7.91 us
    ppermute x4, starting transfers between devices, partner(): return lax.ppermute(part, 'gx', [(i, i ^ k) for i in range(count)])  7.4 us
    ppermute x1, waiting for transfers between devices, replicated(): return (potentials[None], own + lax.ppermute(theirs, 'shot', swap))  3.83 us
    ppermute x1, starting transfers between devices, replicated(): return (potentials[None], own + lax.ppermute(theirs, 'shot', swap))  1.78 us
    ppermute x1, waiting for transfers between devices, replicated(): far = [far, lax.ppermute(far, 'shot', swap)]  1.77 us
    unnamed x11, local copies, waits for them, and re-layouts  1.76 us
    ppermute x1, starting transfers between devices, replicated(): far = [far, lax.ppermute(far, 'shot', swap)]  1.54 us
  transfers between devices with their start and end apart: 12, of which 7 were waited for; matrix products, arithmetic and copies ran while one was open for 0% of the time, Pallas kernels for 1%

profile of v14, /device:TPU:0, one launch (start us, length us, event | category | flops | bytes accessed | tf_op | source)
XLA Modules:
  0.0 51.1 jit_solution(17901151697601106526)
XLA Ops:
  0.6 0.9 %copy-done = f32[8,64,128]{2,1,0:T(8,128)S(1)} copy-done((f32[8,64,128]{2,1,0:T(8,128)S(1)}, f32[8,64,128]{2,1,0:T(8,128)}, u32[]{:S(2)}) %copy-start) | copy-done | bytes 262168
  1.6 0.6 %shard_map.69 = (f32[512,128]{1,0:T(8,128)S(1)}, f32[256,128]{1,0:T(8,128)S(1)}) custom-call(f32[8,64,128]{2,1,0:T(8,128)S(1)} %copy-done), custom_call_target="tpu_custom_call" | custom-call | tf_op jit(solution)/shard_map/pallas_call | solution.py:753
  2.2 4.1 %collective-permute-start.3 = (f32[256,128]{1,0:T(8,128)S(1)}, f32[256,128]{1,0:T(8,128)S(1)}, u32[]{:S(2)}, u32[]{:S(2)}) collective-permute-start(f32[256,128]{1,0:T(8,128)S(1)} %get-tuple-element.18), channel_id=1, source_target_pairs={{0,8},{4,12},{8,0},{12,4},{1,9},{5,13},{9,1},{13,5},{2,10},{6,14},... | collective-permute-start | bytes 393224 | tf_op jit(solution)/shard_map/ppermute | solution.py:767
  6.3 1.6 %collective-permute-start.1 = (f32[512,128]{1,0:T(8,128)S(1)}, f32[512,128]{1,0:T(8,128)S(1)}, u32[]{:S(2)}, u32[]{:S(2)}) collective-permute-start(f32[512,128]{1,0:T(8,128)S(1)} %get-tuple-element.17.refs_0_), channel_id=1, source_target_pairs={{0,4},{4,0},{8,12},{12,8},{1,5},{5,1},{9,13},{13,9},{2,6},{6,2},{1... | collective-permute-start | bytes 786440 | tf_op jit(solution)/shard_map/ppermute | solution.py:767
  7.8 0.0 collective-permute-start
  7.9 0.1 copy.7.receivers_ref
  8.0 0.0 copy-start.2
  8.0 0.5 copy-done.3
  8.5 0.2 copy-done.2
  8.7 0.4 shard_map.68
  9.1 3.5 %collective-permute-done.3.refs_4_ = f32[256,128]{1,0:T(8,128)S(1)} collective-permute-done((f32[256,128]{1,0:T(8,128)S(1)}, f32[256,128]{1,0:T(8,128)S(1)}, u32[]{:S(2)}, u32[]{:S(2)}) %collective-permute-start.3) | collective-permute-done | bytes 131104 | tf_op jit(solution)/shard_map/ppermute | solution.py:767
  12.7 1.5 %collective-permute-start.5 = (f32[256,128]{1,0:T(8,128)S(1)}, f32[256,128]{1,0:T(8,128)S(1)}, u32[]{:S(2)}, u32[]{:S(2)}) collective-permute-start(f32[256,128]{1,0:T(8,128)S(1)} %collective-permute-done.3.refs_4_), channel_id=1, source_target_pairs={{0,1},{1,0},{2,3},{3,2},{4,5},{5,4},{6,7},{7,6},{8,9},{9,8},{10,11... | collective-permute-start | bytes 393224 | tf_op jit(solution)/shard_map/ppermute | solution.py:792
  14.2 0.6 %collective-permute-start.7 = (f32[256,128]{1,0:T(8,128)S(1)}, f32[256,128]{1,0:T(8,128)S(1)}, u32[]{:S(2)}, u32[]{:S(2)}) collective-permute-start(f32[256,128]{1,0:T(8,128)S(1)} %collective-permute-done.3.refs_4_), channel_id=1, source_target_pairs={{0,4},{4,0},{8,12},{12,8},{1,5},{5,1},{9,13},{13,9},{2,6},{6,2},{1... | collective-permute-start | bytes 393224 | tf_op jit(solution)/shard_map/ppermute | solution.py:767
  14.8 1.0 %collective-permute-done.1.refs_2_ = f32[512,128]{1,0:T(8,128)S(1)} collective-permute-done((f32[512,128]{1,0:T(8,128)S(1)}, f32[512,128]{1,0:T(8,128)S(1)}, u32[]{:S(2)}, u32[]{:S(2)}) %collective-permute-start.1) | collective-permute-done | bytes 262176 | tf_op jit(solution)/shard_map/ppermute | solution.py:767
  15.9 0.0 collective-permute-start.2
  15.9 1.8 %collective-permute-done.5.refs_6_ = f32[256,128]{1,0:T(8,128)S(1)} collective-permute-done((f32[256,128]{1,0:T(8,128)S(1)}, f32[256,128]{1,0:T(8,128)S(1)}, u32[]{:S(2)}, u32[]{:S(2)}) %collective-permute-start.5) | collective-permute-done | bytes 131104 | tf_op jit(solution)/shard_map/ppermute | solution.py:792
  17.7 1.1 %collective-permute-start.9 = (f32[256,128]{1,0:T(8,128)S(1)}, f32[256,128]{1,0:T(8,128)S(1)}, u32[]{:S(2)}, u32[]{:S(2)}) collective-permute-start(f32[256,128]{1,0:T(8,128)S(1)} %collective-permute-done.5.refs_6_), channel_id=1, source_target_pairs={{0,4},{4,0},{8,12},{12,8},{1,5},{5,1},{9,13},{13,9},{2,6},{6,2},{1... | collective-permute-start | bytes 393224 | tf_op jit(solution)/shard_map/ppermute | solution.py:767
  18.8 0.0 collective-permute-start.4
  18.8 0.6 %collective-permute-done.7.refs_8_ = f32[256,128]{1,0:T(8,128)S(1)} collective-permute-done((f32[256,128]{1,0:T(8,128)S(1)}, f32[256,128]{1,0:T(8,128)S(1)}, u32[]{:S(2)}, u32[]{:S(2)}) %collective-permute-start.7) | collective-permute-done | bytes 131104 | tf_op jit(solution)/shard_map/ppermute | solution.py:767
  19.4 0.0 collective-permute-start.8
  19.4 0.0 collective-permute-done.refs_1_
  19.4 0.5 collective-permute-start.6
  19.9 2.7 %collective-permute-done.9.refs_10_ = f32[256,128]{1,0:T(8,128)S(1)} collective-permute-done((f32[256,128]{1,0:T(8,128)S(1)}, f32[256,128]{1,0:T(8,128)S(1)}, u32[]{:S(2)}, u32[]{:S(2)}) %collective-permute-start.9) | collective-permute-done | bytes 131104 | tf_op jit(solution)/shard_map/ppermute | solution.py:767
  22.6 0.0 collective-permute-start.10
  22.6 0.0 collective-permute-done.4.refs_5_
  22.6 0.0 collective-permute-done.8.refs_9_
  22.6 0.0 collective-permute-done.6.refs_7_
  22.7 1.3 %collective-permute-done.10.refs_11_ = f32[256,128]{1,0:T(8,128)S(1)} collective-permute-done((f32[256,128]{1,0:T(8,128)S(1)}, f32[256,128]{1,0:T(8,128)S(1)}, u32[]{:S(2)}, u32[]{:S(2)}) %collective-permute-start.10) | collective-permute-done | bytes 131104 | tf_op jit(solution)/shard_map/ppermute | solution.py:770
  24.0 20.9 %shard_map.70 = (f32[8,64,128]{2,1,0:T(8,128)}, f32[8,32,128]{2,1,0:T(8,128)S(1)}, f32[8,32,128]{2,1,0:T(8,128)S(1)}) custom-call(s32[1,256]{1,0:T(1,128)S(1)} %get-tuple-element.16.cells_ref, f32[512,128]{1,0:T(8,128)S(1)} %get-tuple-element.17.refs_0_, f32[512,128]{1,0:T(8,128)S(1)} %collective-permute-done.refs_1_, ...), custom_call_target="tpu_custom_call" | custom-call | flops 200000000 | bytes 4000000 | tf_op jit(solution)/shard_map/pallas_call | solution.py:799
  44.8 1.8 %collective-permute-start.11 = (f32[8,32,128]{2,1,0:T(8,128)S(1)}, f32[8,32,128]{2,1,0:T(8,128)S(1)}, u32[]{:S(2)}, u32[]{:S(2)}) collective-permute-start(f32[8,32,128]{2,1,0:T(8,128)S(1)} %get-tuple-element.29), channel_id=1, source_target_pairs={{0,1},{1,0},{2,3},{3,2},{4,5},{5,4},{6,7},{7,6},{8,9},{9,8},{10,11... | collective-permute-start | bytes 393224 | tf_op jit(solution)/shard_map/ppermute | solution.py:819
  46.6 3.8 %collective-permute-done.11 = f32[8,32,128]{2,1,0:T(8,128)S(1)} collective-permute-done((f32[8,32,128]{2,1,0:T(8,128)S(1)}, f32[8,32,128]{2,1,0:T(8,128)S(1)}, u32[]{:S(2)}, u32[]{:S(2)}) %collective-permute-start.11) | collective-permute-done | bytes 131104 | tf_op jit(solution)/shard_map/ppermute | solution.py:819
  50.5 0.7 %add.3 = f32[8,32,128]{2,1,0:T(8,128)} add(f32[8,32,128]{2,1,0:T(8,128)S(1)} %get-tuple-element.28, f32[8,32,128]{2,1,0:T(8,128)S(1)} %collective-permute-done.11) | non-fusion elementwise | flops 32768 | bytes 393216 | tf_op jit(solution)/shard_map/add | solution.py:819
  (7 shorter events, 0.0 us)
Async XLA Ops:
  0.6 1.0 %copy-start = (f32[8,64,128]{2,1,0:T(8,128)S(1)}, f32[8,64,128]{2,1,0:T(8,128)}, u32[]{:S(2)}) copy-start(f32[8,64,128]{2,1,0:T(8,128)} %natural_ref.1) | copy-start | bytes 786436
  1.6 6.3 %copy-start.4 = (s32[512,2]{0,1:T(2,128)S(1)}, s32[512,2]{0,1:T(2,128)}, u32[]{:S(2)}) copy-start(s32[512,2]{0,1:T(2,128)} %param.8) | copy-start | bytes 12292
  2.2 10.5 %collective-permute-start.3 = (f32[256,128]{1,0:T(8,128)S(1)}, f32[256,128]{1,0:T(8,128)S(1)}, u32[]{:S(2)}, u32[]{:S(2)}) collective-permute-start(f32[256,128]{1,0:T(8,128)S(1)} %get-tuple-element.18), channel_id=1, source_target_pairs={{0,8},{4,12},{8,0},{12,4},{1,9},{5,13},{9,1},{13,5},{2,10},{6,14},... | collective-permute-start | bytes 393224 | tf_op jit(solution)/shard_map/ppermute | solution.py:767
  6.3 1.8 %copy-start.1 = (f32[1,512]{1,0:T(1,128)S(1)}, f32[1,512]{1,0:T(1,128)}, u32[]{:S(2)}) copy-start(f32[1,512]{1,0:T(1,128)} %observed_ref.1) | copy-start | bytes 6148
  6.3 9.6 %collective-permute-start.1 = (f32[512,128]{1,0:T(8,128)S(1)}, f32[512,128]{1,0:T(8,128)S(1)}, u32[]{:S(2)}, u32[]{:S(2)}) collective-permute-start(f32[512,128]{1,0:T(8,128)S(1)} %get-tuple-element.17.refs_0_), channel_id=1, source_target_pairs={{0,4},{4,0},{8,12},{12,8},{1,5},{5,1},{9,13},{13,9},{2,6},{6,2},{1... | collective-permute-start | bytes 786440 | tf_op jit(solution)/shard_map/ppermute | solution.py:767
  7.8 11.5 %collective-permute-start = (f32[512,128]{1,0:T(8,128)S(1)}, f32[512,128]{1,0:T(8,128)S(1)}, u32[]{:S(2)}, u32[]{:S(2)}) collective-permute-start(f32[512,128]{1,0:T(8,128)S(1)} %get-tuple-element.17.refs_0_), channel_id=1, source_target_pairs={{0,2},{2,0},{1,3},{3,1},{4,6},{6,4},{5,7},{7,5},{8,10},{10,8},{9,1... | collective-permute-start | bytes 786440 | tf_op jit(solution)/shard_map/ppermute | solution.py:770
  7.9 0.7 %copy-start.3 = (f32[1,256]{1,0:T(1,128)S(1)}, f32[1,256]{1,0:T(1,128)}, u32[]{:S(2)}) copy-start(f32[1,256]{1,0:T(1,128)} %currents_ref.1) | copy-start | bytes 3076
  8.0 0.7 %copy-start.2 = (s32[256]{0:T(256)S(1)}, s32[256]{0:T(256)}, u32[]{:S(2)}) copy-start(s32[256]{0:T(256)} %param.6) | copy-start | bytes 3076
  12.7 5.0 %collective-permute-start.5 = (f32[256,128]{1,0:T(8,128)S(1)}, f32[256,128]{1,0:T(8,128)S(1)}, u32[]{:S(2)}, u32[]{:S(2)}) collective-permute-start(f32[256,128]{1,0:T(8,128)S(1)} %collective-permute-done.3.refs_4_), channel_id=1, source_target_pairs={{0,1},{1,0},{2,3},{3,2},{4,5},{5,4},{6,7},{7,6},{8,9},{9,8},{10,11... | collective-permute-start | bytes 393224 | tf_op jit(solution)/shard_map/ppermute | solution.py:792
  14.2 5.1 %collective-permute-start.7 = (f32[256,128]{1,0:T(8,128)S(1)}, f32[256,128]{1,0:T(8,128)S(1)}, u32[]{:S(2)}, u32[]{:S(2)}) collective-permute-start(f32[256,128]{1,0:T(8,128)S(1)} %collective-permute-done.3.refs_4_), channel_id=1, source_target_pairs={{0,4},{4,0},{8,12},{12,8},{1,5},{5,1},{9,13},{13,9},{2,6},{6,2},{1... | collective-permute-start | bytes 393224 | tf_op jit(solution)/shard_map/ppermute | solution.py:767
  15.9 6.8 %collective-permute-start.2 = (f32[512,128]{1,0:T(8,128)S(1)}, f32[512,128]{1,0:T(8,128)S(1)}, u32[]{:S(2)}, u32[]{:S(2)}) collective-permute-start(f32[512,128]{1,0:T(8,128)S(1)} %collective-permute-done.1.refs_2_), channel_id=1, source_target_pairs={{0,2},{2,0},{1,3},{3,1},{4,6},{6,4},{5,7},{7,5},{8,10},{10,8},{9,1... | collective-permute-start | bytes 786440 | tf_op jit(solution)/shard_map/ppermute | solution.py:770
  17.7 5.0 %collective-permute-start.9 = (f32[256,128]{1,0:T(8,128)S(1)}, f32[256,128]{1,0:T(8,128)S(1)}, u32[]{:S(2)}, u32[]{:S(2)}) collective-permute-start(f32[256,128]{1,0:T(8,128)S(1)} %collective-permute-done.5.refs_6_), channel_id=1, source_target_pairs={{0,4},{4,0},{8,12},{12,8},{1,5},{5,1},{9,13},{13,9},{2,6},{6,2},{1... | collective-permute-start | bytes 393224 | tf_op jit(solution)/shard_map/ppermute | solution.py:767
  18.8 3.9 %collective-permute-start.4 = (f32[256,128]{1,0:T(8,128)S(1)}, f32[256,128]{1,0:T(8,128)S(1)}, u32[]{:S(2)}, u32[]{:S(2)}) collective-permute-start(f32[256,128]{1,0:T(8,128)S(1)} %collective-permute-done.3.refs_4_), channel_id=1, source_target_pairs={{0,2},{2,0},{1,3},{3,1},{4,6},{6,4},{5,7},{7,5},{8,10},{10,8},{9,1... | collective-permute-start | bytes 393224 | tf_op jit(solution)/shard_map/ppermute | solution.py:770
  19.4 3.3 %collective-permute-start.8 = (f32[256,128]{1,0:T(8,128)S(1)}, f32[256,128]{1,0:T(8,128)S(1)}, u32[]{:S(2)}, u32[]{:S(2)}) collective-permute-start(f32[256,128]{1,0:T(8,128)S(1)} %collective-permute-done.7.refs_8_), channel_id=1, source_target_pairs={{0,2},{2,0},{1,3},{3,1},{4,6},{6,4},{5,7},{7,5},{8,10},{10,8},{9,1... | collective-permute-start | bytes 393224 | tf_op jit(solution)/shard_map/ppermute | solution.py:770
  19.4 3.3 %collective-permute-start.6 = (f32[256,128]{1,0:T(8,128)S(1)}, f32[256,128]{1,0:T(8,128)S(1)}, u32[]{:S(2)}, u32[]{:S(2)}) collective-permute-start(f32[256,128]{1,0:T(8,128)S(1)} %collective-permute-done.5.refs_6_), channel_id=1, source_target_pairs={{0,2},{2,0},{1,3},{3,1},{4,6},{6,4},{5,7},{7,5},{8,10},{10,8},{9,1... | collective-permute-start | bytes 393224 | tf_op jit(solution)/shard_map/ppermute | solution.py:770
  22.6 1.3 %collective-permute-start.10 = (f32[256,128]{1,0:T(8,128)S(1)}, f32[256,128]{1,0:T(8,128)S(1)}, u32[]{:S(2)}, u32[]{:S(2)}) collective-permute-start(f32[256,128]{1,0:T(8,128)S(1)} %collective-permute-done.9.refs_10_), channel_id=1, source_target_pairs={{0,2},{2,0},{1,3},{3,1},{4,6},{6,4},{5,7},{7,5},{8,10},{10,8},{9,1... | collective-permute-start | bytes 393224 | tf_op jit(solution)/shard_map/ppermute | solution.py:770
  44.8 5.6 %collective-permute-start.11 = (f32[8,32,128]{2,1,0:T(8,128)S(1)}, f32[8,32,128]{2,1,0:T(8,128)S(1)}, u32[]{:S(2)}, u32[]{:S(2)}) collective-permute-start(f32[8,32,128]{2,1,0:T(8,128)S(1)} %get-tuple-element.29), channel_id=1, source_target_pairs={{0,1},{1,0},{2,3},{3,2},{4,5},{5,4},{6,7},{7,6},{8,9},{9,8},{10,11... | collective-permute-start | bytes 393224 | tf_op jit(solution)/shard_map/ppermute | solution.py:819

commit v15 on v14

--- a/solution.py
+++ b/solution.py
@@ -314,11 +314,8 @@
                     self.link_z[x, -1] = block_down(link, 2)
                 self.link_z[x, z] = link
 
-        if n == SIDE:
-            rolled(n, plane, unroll=2)
-        else:
-            for x in range(n):
-                plane(x)
+        for x in range(n):
+            plane(x)
         for z in range(n):
             link = inside_up(self.link_x[n - 1, z], 0)
             self.link_x[n - 1, z] = link
@@ -530,27 +527,29 @@
 
     device, shot = own_place()
 
-    def place(part, row, x, index):
-        for z in range(SIDE):
-            fine.cond.ref[pl.ds(fine.cond.start(x, z) + index, SIDE, stride=SIDE), :] = part[
-                pl.ds((row * SIDE + z) * SIDE, SIDE), :
-            ]
-
-    def collect(x):
-        for k, part in enumerate(part_refs):
-            place(part, x, x, device ^ k)
-
-    def collect_half(x):
-        for k, part in enumerate(half_refs):
-            swapped, index = k // 2 % 2, len(part_refs) + k // 4 * 2 + k % 2
-            place(part, x, (shot ^ swapped) * (SIDE // 2) + x, device ^ index)
+    def collect(sources, x):
+        held = [
+            [part[pl.ds((row * SIDE + z) * SIDE, SIDE), :] for z in range(SIDE)]
+            for part, row, _ in sources
+        ]
+        for rows, (_, _, index) in zip(held, sources):
+            for z, row in enumerate(rows):
+                start = fine.cond.start(x, z) + (device ^ index)
+                fine.cond.ref[pl.ds(start, SIDE, stride=SIDE), :] = row
+
+    for x in range(SIDE):
+        collect([(part, x, k) for k, part in enumerate(part_refs)], x)
+    for x in range(SIDE // 2):
+        for swapped in range(2):
+            sources = []
+            for k, part in enumerate(half_refs):
+                if k // 2 % 2 == swapped:
+                    sources.append((part, x, len(part_refs) + k // 4 * 2 + k % 2))
+            collect(sources, (shot ^ swapped) * (SIDE // 2) + x)
 
     def edges(x):
         fine.cond.close_z(x, exact=True)
 
-    rolled(SIDE, collect, unroll=4)
-    for x in range(SIDE // 2):
-        collect_half(x)
     for x in range(SIDE):
         edges(x)
     fine.cond.close(exact=True)
@@ -656,18 +655,30 @@
     wide = SIDE + 2
     sending = pltpu.make_async_copy(sent, potentials_ref, sem)
 
-    def each(body):
-        def one(electrode, carry):
-            body(pl.ds(electrode, 1), pl.ds(cells_ref[0, electrode], 1))
+    batch = 32
+
+    def each(load, store):
+        def one(group, carry):
+            first = group * batch
+            cells = [pl.ds(cells_ref[0, first + k], 1) for k in range(batch)]
+            rows = [load(pl.ds(first + k, 1), cell) for k, cell in enumerate(cells)]
+            for k, (cell, row) in enumerate(zip(cells, rows)):
+                store(pl.ds(first + k, 1), cell, row)
             return carry
 
-        lax.fori_loop(0, electrodes, one, 0, unroll=64)
-
-    def put(electrode, cell):
-        fine.base.ref[cell, :] = (2.0 * gathered[electrode, :]) * fine.weight.ref[cell, :]
+        lax.fori_loop(0, electrodes // batch, one, 0, unroll=2)
+
+    def source_row(electrode, cell):
+        return gathered[electrode, :] * fine.weight.ref[cell, :]
+
+    def put(electrode, cell, row):
+        fine.base.ref[cell, :] = row
 
     def read(electrode, cell):
-        gathered[electrode, :] = forward.ref[cell, :]
+        return forward.ref[cell, :]
+
+    def keep_row(electrode, cell, row):
+        gathered[electrode, :] = row
 
     def exact(row, matrix_ref):
         return product(jnp.broadcast_to(row, (16, row.shape[1])), matrix_ref[...], 3)[0:1]
@@ -679,26 +690,30 @@
 
     def extract(index):
         for x in range(-1, SIDE + 1):
-            for z in range(SIDE):
+            inner = 0 <= x < SIDE
+            starts = [forward.start(x, z) + device for z in range(SIDE)]
+            rows = [forward.ref[pl.ds(start, SIDE, stride=SIDE), :] for start in starts]
+            if inner:
+                after = [margin(x, z, SIDE) for z in range(SIDE)]
+                before = [margin(x, z, -1) for z in range(SIDE)]
+            for z, row in enumerate(rows):
                 at = (x + 1) * wide + z + 1
-                start = forward.start(x, z) + device
-                row = forward.ref[pl.ds(start, SIDE, stride=SIDE), :]
                 owned[index, at] = row
-                if 0 <= x < SIDE:
-                    after, before = margin(x, z, SIDE), margin(x, z, -1)
-                    place = x * SIDE + z
-                    turned = pltpu.roll(row, SIDE - 1, 0)
-                    beside[index, 0, place] = jnp.where(sub == SIDE - 1, after, turned)
-                    beside[index, 1, place] = jnp.where(sub == 0, before, pltpu.roll(row, 1, 0))
-                    if z == 0:
-                        edge = pltpu.roll(row, LANES - 1, 1)
-                        owned[index, at + SIDE] = jnp.where(lane % GROUP < GROUP - 1, edge, 0.0)
-                    if z == SIDE - 1:
-                        edge = pltpu.roll(row, 1, 1)
-                        owned[index, at - SIDE] = jnp.where(lane % GROUP > 0, edge, 0.0)
+                if not inner:
+                    continue
+                place = x * SIDE + z
+                turned = pltpu.roll(row, SIDE - 1, 0)
+                beside[index, 0, place] = jnp.where(sub == SIDE - 1, after[z], turned)
+                beside[index, 1, place] = jnp.where(sub == 0, before[z], pltpu.roll(row, 1, 0))
+                if z == 0:
+                    edge = pltpu.roll(row, LANES - 1, 1)
+                    owned[index, at + SIDE] = jnp.where(lane % GROUP < GROUP - 1, edge, 0.0)
+                if z == SIDE - 1:
+                    edge = pltpu.roll(row, 1, 1)
+                    owned[index, at - SIDE] = jnp.where(lane % GROUP > 0, edge, 0.0)
 
     def solve(index):
-        each(put)
+        each(source_row, put)
         for x in range(SIDE):
             fine.base.close_z(x)
         fine.base.close()
@@ -711,13 +726,13 @@
                 tiles = [owned[0, (x + 1) * wide + z + 1] for z in range(SIDE)]
                 sent[x] = from_blocks(tiles, order)
             sending.start()
-            each(read)
+            each(read, keep_row)
             readings = jnp.where(at_spot, gathered[...].T, 0.0)
             readings = jnp.sum(readings, axis=0, keepdims=True)
             misfit = exact(readings, turned_ref) - observed_ref[...]
-            gathered[...] = shared_rows(exact(misfit, pairs_ref), spot, same_ref[...])
-
-    gathered[...] = rows_ref[...]
+            gathered[...] = 2.0 * shared_rows(exact(misfit, pairs_ref), spot, same_ref[...])
+
+    gathered[...] = 2.0 * rows_ref[...]
     rolled(2, solve)
 
     chunk = mine_ref.shape[1]

time: 51.3 us -> 51.4 us (level)
  no operation moved by 1% of the time
where the time goes in v15:
time: 51.4 us; the launch traced here: 51.2 us
  Pallas kernels  22 us (43%)
  waiting for transfers between devices  14.8 us (29%)
  starting transfers between devices  11.2 us (22%)
  local copies, waits for them, and re-layouts  1.76 us (3%)
  between operations  0.72 us (1%)
  other arithmetic  0.67 us (1%)
    pallas_call x1, Pallas kernels, replicated(): pl.pallas_call(functools.partial(replicated_kernel, len(parts), len(halve...  20.9 us
    ppermute x4, waiting for transfers between devices, partner(): return lax.ppermute(part, 'gx', [(i, i ^ k) for i in range(count)])  7.91 us
    ppermute x4, starting transfers between devices, partner(): return lax.ppermute(part, 'gx', [(i, i ^ k) for i in range(count)])  7.4 us
    ppermute x1, waiting for transfers between devices, replicated(): return (potentials[None], own + lax.ppermute(theirs, 'shot', swap))  3.83 us
    ppermute x1, starting transfers between devices, replicated(): return (potentials[None], own + lax.ppermute(theirs, 'shot', swap))  1.78 us
    ppermute x1, waiting for transfers between devices, replicated(): far = [far, lax.ppermute(far, 'shot', swap)]  1.77 us
    unnamed x11, local copies, waits for them, and re-layouts  1.76 us
    ppermute x1, starting transfers between devices, replicated(): far = [far, lax.ppermute(far, 'shot', swap)]  1.54 us
  transfers between devices with their start and end apart: 12, of which 7 were waited for; matrix products, arithmetic and copies ran while one was open for 0% of the time, Pallas kernels for 1%

profile of v15, /device:TPU:0, one launch (start us, length us, event | category | flops | bytes accessed | tf_op | source)
XLA Modules:
  0.0 51.2 jit_solution(804703853935793741)
XLA Ops:
  0.6 0.9 %copy-done = f32[8,64,128]{2,1,0:T(8,128)S(1)} copy-done((f32[8,64,128]{2,1,0:T(8,128)S(1)}, f32[8,64,128]{2,1,0:T(8,128)}, u32[]{:S(2)}) %copy-start) | copy-done | bytes 262168
  1.6 0.6 %shard_map.69 = (f32[512,128]{1,0:T(8,128)S(1)}, f32[256,128]{1,0:T(8,128)S(1)}) custom-call(f32[8,64,128]{2,1,0:T(8,128)S(1)} %copy-done), custom_call_target="tpu_custom_call" | custom-call | tf_op jit(solution)/shard_map/pallas_call | solution.py:768
  2.2 4.1 %collective-permute-start.3 = (f32[256,128]{1,0:T(8,128)S(1)}, f32[256,128]{1,0:T(8,128)S(1)}, u32[]{:S(2)}, u32[]{:S(2)}) collective-permute-start(f32[256,128]{1,0:T(8,128)S(1)} %get-tuple-element.18), channel_id=1, source_target_pairs={{0,8},{4,12},{8,0},{12,4},{1,9},{5,13},{9,1},{13,5},{2,10},{6,14},... | collective-permute-start | bytes 393224 | tf_op jit(solution)/shard_map/ppermute | solution.py:782
  6.3 1.6 %collective-permute-start.1 = (f32[512,128]{1,0:T(8,128)S(1)}, f32[512,128]{1,0:T(8,128)S(1)}, u32[]{:S(2)}, u32[]{:S(2)}) collective-permute-start(f32[512,128]{1,0:T(8,128)S(1)} %get-tuple-element.17.refs_0_), channel_id=1, source_target_pairs={{0,4},{4,0},{8,12},{12,8},{1,5},{5,1},{9,13},{13,9},{2,6},{6,2},{1... | collective-permute-start | bytes 786440 | tf_op jit(solution)/shard_map/ppermute | solution.py:782
  7.8 0.0 collective-permute-start
  7.9 0.1 copy.7.receivers_ref
  8.0 0.0 copy-start.2
  8.0 0.5 copy-done.3
  8.5 0.2 copy-done.2
  8.7 0.4 shard_map.68
  9.1 3.5 %collective-permute-done.3.refs_4_ = f32[256,128]{1,0:T(8,128)S(1)} collective-permute-done((f32[256,128]{1,0:T(8,128)S(1)}, f32[256,128]{1,0:T(8,128)S(1)}, u32[]{:S(2)}, u32[]{:S(2)}) %collective-permute-start.3) | collective-permute-done | bytes 131104 | tf_op jit(solution)/shard_map/ppermute | solution.py:782
  12.7 1.5 %collective-permute-start.5 = (f32[256,128]{1,0:T(8,128)S(1)}, f32[256,128]{1,0:T(8,128)S(1)}, u32[]{:S(2)}, u32[]{:S(2)}) collective-permute-start(f32[256,128]{1,0:T(8,128)S(1)} %collective-permute-done.3.refs_4_), channel_id=1, source_target_pairs={{0,1},{1,0},{2,3},{3,2},{4,5},{5,4},{6,7},{7,6},{8,9},{9,8},{10,11... | collective-permute-start | bytes 393224 | tf_op jit(solution)/shard_map/ppermute | solution.py:807
  14.2 0.6 %collective-permute-start.7 = (f32[256,128]{1,0:T(8,128)S(1)}, f32[256,128]{1,0:T(8,128)S(1)}, u32[]{:S(2)}, u32[]{:S(2)}) collective-permute-start(f32[256,128]{1,0:T(8,128)S(1)} %collective-permute-done.3.refs_4_), channel_id=1, source_target_pairs={{0,4},{4,0},{8,12},{12,8},{1,5},{5,1},{9,13},{13,9},{2,6},{6,2},{1... | collective-permute-start | bytes 393224 | tf_op jit(solution)/shard_map/ppermute | solution.py:782
  14.8 1.0 %collective-permute-done.1.refs_2_ = f32[512,128]{1,0:T(8,128)S(1)} collective-permute-done((f32[512,128]{1,0:T(8,128)S(1)}, f32[512,128]{1,0:T(8,128)S(1)}, u32[]{:S(2)}, u32[]{:S(2)}) %collective-permute-start.1) | collective-permute-done | bytes 262176 | tf_op jit(solution)/shard_map/ppermute | solution.py:782
  15.9 0.0 collective-permute-start.2
  15.9 1.8 %collective-permute-done.5.refs_6_ = f32[256,128]{1,0:T(8,128)S(1)} collective-permute-done((f32[256,128]{1,0:T(8,128)S(1)}, f32[256,128]{1,0:T(8,128)S(1)}, u32[]{:S(2)}, u32[]{:S(2)}) %collective-permute-start.5) | collective-permute-done | bytes 131104 | tf_op jit(solution)/shard_map/ppermute | solution.py:807
  17.7 1.1 %collective-permute-start.9 = (f32[256,128]{1,0:T(8,128)S(1)}, f32[256,128]{1,0:T(8,128)S(1)}, u32[]{:S(2)}, u32[]{:S(2)}) collective-permute-start(f32[256,128]{1,0:T(8,128)S(1)} %collective-permute-done.5.refs_6_), channel_id=1, source_target_pairs={{0,4},{4,0},{8,12},{12,8},{1,5},{5,1},{9,13},{13,9},{2,6},{6,2},{1... | collective-permute-start | bytes 393224 | tf_op jit(solution)/shard_map/ppermute | solution.py:782
  18.8 0.0 collective-permute-start.4
  18.8 0.6 %collective-permute-done.7.refs_8_ = f32[256,128]{1,0:T(8,128)S(1)} collective-permute-done((f32[256,128]{1,0:T(8,128)S(1)}, f32[256,128]{1,0:T(8,128)S(1)}, u32[]{:S(2)}, u32[]{:S(2)}) %collective-permute-start.7) | collective-permute-done | bytes 131104 | tf_op jit(solution)/shard_map/ppermute | solution.py:782
  19.4 0.0 collective-permute-start.8
  19.4 0.0 collective-permute-done.refs_1_
  19.4 0.5 collective-permute-start.6
  19.9 2.7 %collective-permute-done.9.refs_10_ = f32[256,128]{1,0:T(8,128)S(1)} collective-permute-done((f32[256,128]{1,0:T(8,128)S(1)}, f32[256,128]{1,0:T(8,128)S(1)}, u32[]{:S(2)}, u32[]{:S(2)}) %collective-permute-start.9) | collective-permute-done | bytes 131104 | tf_op jit(solution)/shard_map/ppermute | solution.py:782
  22.6 0.0 collective-permute-start.10
  22.6 0.0 collective-permute-done.4.refs_5_
  22.6 0.0 collective-permute-done.8.refs_9_
  22.6 0.0 collective-permute-done.6.refs_7_
  22.7 1.3 %collective-permute-done.10.refs_11_ = f32[256,128]{1,0:T(8,128)S(1)} collective-permute-done((f32[256,128]{1,0:T(8,128)S(1)}, f32[256,128]{1,0:T(8,128)S(1)}, u32[]{:S(2)}, u32[]{:S(2)}) %collective-permute-start.10) | collective-permute-done | bytes 131104 | tf_op jit(solution)/shard_map/ppermute | solution.py:785
  24.0 20.9 %shard_map.70 = (f32[8,64,128]{2,1,0:T(8,128)}, f32[8,32,128]{2,1,0:T(8,128)S(1)}, f32[8,32,128]{2,1,0:T(8,128)S(1)}) custom-call(s32[1,256]{1,0:T(1,128)S(1)} %get-tuple-element.16.cells_ref, f32[512,128]{1,0:T(8,128)S(1)} %get-tuple-element.17.refs_0_, f32[512,128]{1,0:T(8,128)S(1)} %collective-permute-done.refs_1_, ...), custom_call_target="tpu_custom_call" | custom-call | flops 200000000 | bytes 4000000 | tf_op jit(solution)/shard_map/pallas_call | solution.py:814
  44.9 1.8 %collective-permute-start.11 = (f32[8,32,128]{2,1,0:T(8,128)S(1)}, f32[8,32,128]{2,1,0:T(8,128)S(1)}, u32[]{:S(2)}, u32[]{:S(2)}) collective-permute-start(f32[8,32,128]{2,1,0:T(8,128)S(1)} %get-tuple-element.29), channel_id=1, source_target_pairs={{0,1},{1,0},{2,3},{3,2},{4,5},{5,4},{6,7},{7,6},{8,9},{9,8},{10,11... | collective-permute-start | bytes 393224 | tf_op jit(solution)/shard_map/ppermute | solution.py:834
  46.7 3.8 %collective-permute-done.11 = f32[8,32,128]{2,1,0:T(8,128)S(1)} collective-permute-done((f32[8,32,128]{2,1,0:T(8,128)S(1)}, f32[8,32,128]{2,1,0:T(8,128)S(1)}, u32[]{:S(2)}, u32[]{:S(2)}) %collective-permute-start.11) | collective-permute-done | bytes 131104 | tf_op jit(solution)/shard_map/ppermute | solution.py:834
  50.5 0.7 %add.3 = f32[8,32,128]{2,1,0:T(8,128)} add(f32[8,32,128]{2,1,0:T(8,128)S(1)} %get-tuple-element.28, f32[8,32,128]{2,1,0:T(8,128)S(1)} %collective-permute-done.11) | non-fusion elementwise | flops 32768 | bytes 393216 | tf_op jit(solution)/shard_map/add | solution.py:834
  (7 shorter events, 0.0 us)
Async XLA Ops:
  0.6 1.0 %copy-start = (f32[8,64,128]{2,1,0:T(8,128)S(1)}, f32[8,64,128]{2,1,0:T(8,128)}, u32[]{:S(2)}) copy-start(f32[8,64,128]{2,1,0:T(8,128)} %natural_ref.1) | copy-start | bytes 786436
  1.6 6.3 %copy-start.4 = (s32[512,2]{0,1:T(2,128)S(1)}, s32[512,2]{0,1:T(2,128)}, u32[]{:S(2)}) copy-start(s32[512,2]{0,1:T(2,128)} %param.8) | copy-start | bytes 12292
  2.2 10.5 %collective-permute-start.3 = (f32[256,128]{1,0:T(8,128)S(1)}, f32[256,128]{1,0:T(8,128)S(1)}, u32[]{:S(2)}, u32[]{:S(2)}) collective-permute-start(f32[256,128]{1,0:T(8,128)S(1)} %get-tuple-element.18), channel_id=1, source_target_pairs={{0,8},{4,12},{8,0},{12,4},{1,9},{5,13},{9,1},{13,5},{2,10},{6,14},... | collective-permute-start | bytes 393224 | tf_op jit(solution)/shard_map/ppermute | solution.py:782
  6.3 1.8 %copy-start.1 = (f32[1,512]{1,0:T(1,128)S(1)}, f32[1,512]{1,0:T(1,128)}, u32[]{:S(2)}) copy-start(f32[1,512]{1,0:T(1,128)} %observed_ref.1) | copy-start | bytes 6148
  6.3 9.6 %collective-permute-start.1 = (f32[512,128]{1,0:T(8,128)S(1)}, f32[512,128]{1,0:T(8,128)S(1)}, u32[]{:S(2)}, u32[]{:S(2)}) collective-permute-start(f32[512,128]{1,0:T(8,128)S(1)} %get-tuple-element.17.refs_0_), channel_id=1, source_target_pairs={{0,4},{4,0},{8,12},{12,8},{1,5},{5,1},{9,13},{13,9},{2,6},{6,2},{1... | collective-permute-start | bytes 786440 | tf_op jit(solution)/shard_map/ppermute | solution.py:782
  7.8 11.5 %collective-permute-start = (f32[512,128]{1,0:T(8,128)S(1)}, f32[512,128]{1,0:T(8,128)S(1)}, u32[]{:S(2)}, u32[]{:S(2)}) collective-permute-start(f32[512,128]{1,0:T(8,128)S(1)} %get-tuple-element.17.refs_0_), channel_id=1, source_target_pairs={{0,2},{2,0},{1,3},{3,1},{4,6},{6,4},{5,7},{7,5},{8,10},{10,8},{9,1... | collective-permute-start | bytes 786440 | tf_op jit(solution)/shard_map/ppermute | solution.py:785
  7.9 0.7 %copy-start.3 = (f32[1,256]{1,0:T(1,128)S(1)}, f32[1,256]{1,0:T(1,128)}, u32[]{:S(2)}) copy-start(f32[1,256]{1,0:T(1,128)} %currents_ref.1) | copy-start | bytes 3076
  8.0 0.7 %copy-start.2 = (s32[256]{0:T(256)S(1)}, s32[256]{0:T(256)}, u32[]{:S(2)}) copy-start(s32[256]{0:T(256)} %param.6) | copy-start | bytes 3076
  12.7 5.0 %collective-permute-start.5 = (f32[256,128]{1,0:T(8,128)S(1)}, f32[256,128]{1,0:T(8,128)S(1)}, u32[]{:S(2)}, u32[]{:S(2)}) collective-permute-start(f32[256,128]{1,0:T(8,128)S(1)} %collective-permute-done.3.refs_4_), channel_id=1, source_target_pairs={{0,1},{1,0},{2,3},{3,2},{4,5},{5,4},{6,7},{7,6},{8,9},{9,8},{10,11... | collective-permute-start | bytes 393224 | tf_op jit(solution)/shard_map/ppermute | solution.py:807
  14.2 5.1 %collective-permute-start.7 = (f32[256,128]{1,0:T(8,128)S(1)}, f32[256,128]{1,0:T(8,128)S(1)}, u32[]{:S(2)}, u32[]{:S(2)}) collective-permute-start(f32[256,128]{1,0:T(8,128)S(1)} %collective-permute-done.3.refs_4_), channel_id=1, source_target_pairs={{0,4},{4,0},{8,12},{12,8},{1,5},{5,1},{9,13},{13,9},{2,6},{6,2},{1... | collective-permute-start | bytes 393224 | tf_op jit(solution)/shard_map/ppermute | solution.py:782
  15.9 6.8 %collective-permute-start.2 = (f32[512,128]{1,0:T(8,128)S(1)}, f32[512,128]{1,0:T(8,128)S(1)}, u32[]{:S(2)}, u32[]{:S(2)}) collective-permute-start(f32[512,128]{1,0:T(8,128)S(1)} %collective-permute-done.1.refs_2_), channel_id=1, source_target_pairs={{0,2},{2,0},{1,3},{3,1},{4,6},{6,4},{5,7},{7,5},{8,10},{10,8},{9,1... | collective-permute-start | bytes 786440 | tf_op jit(solution)/shard_map/ppermute | solution.py:785
  17.7 5.0 %collective-permute-start.9 = (f32[256,128]{1,0:T(8,128)S(1)}, f32[256,128]{1,0:T(8,128)S(1)}, u32[]{:S(2)}, u32[]{:S(2)}) collective-permute-start(f32[256,128]{1,0:T(8,128)S(1)} %collective-permute-done.5.refs_6_), channel_id=1, source_target_pairs={{0,4},{4,0},{8,12},{12,8},{1,5},{5,1},{9,13},{13,9},{2,6},{6,2},{1... | collective-permute-start | bytes 393224 | tf_op jit(solution)/shard_map/ppermute | solution.py:782
  18.8 3.9 %collective-permute-start.4 = (f32[256,128]{1,0:T(8,128)S(1)}, f32[256,128]{1,0:T(8,128)S(1)}, u32[]{:S(2)}, u32[]{:S(2)}) collective-permute-start(f32[256,128]{1,0:T(8,128)S(1)} %collective-permute-done.3.refs_4_), channel_id=1, source_target_pairs={{0,2},{2,0},{1,3},{3,1},{4,6},{6,4},{5,7},{7,5},{8,10},{10,8},{9,1... | collective-permute-start | bytes 393224 | tf_op jit(solution)/shard_map/ppermute | solution.py:785
  19.4 3.3 %collective-permute-start.8 = (f32[256,128]{1,0:T(8,128)S(1)}, f32[256,128]{1,0:T(8,128)S(1)}, u32[]{:S(2)}, u32[]{:S(2)}) collective-permute-start(f32[256,128]{1,0:T(8,128)S(1)} %collective-permute-done.7.refs_8_), channel_id=1, source_target_pairs={{0,2},{2,0},{1,3},{3,1},{4,6},{6,4},{5,7},{7,5},{8,10},{10,8},{9,1... | collective-permute-start | bytes 393224 | tf_op jit(solution)/shard_map/ppermute | solution.py:785
  19.4 3.3 %collective-permute-start.6 = (f32[256,128]{1,0:T(8,128)S(1)}, f32[256,128]{1,0:T(8,128)S(1)}, u32[]{:S(2)}, u32[]{:S(2)}) collective-permute-start(f32[256,128]{1,0:T(8,128)S(1)} %collective-permute-done.5.refs_6_), channel_id=1, source_target_pairs={{0,2},{2,0},{1,3},{3,1},{4,6},{6,4},{5,7},{7,5},{8,10},{10,8},{9,1... | collective-permute-start | bytes 393224 | tf_op jit(solution)/shard_map/ppermute | solution.py:785
  22.6 1.3 %collective-permute-start.10 = (f32[256,128]{1,0:T(8,128)S(1)}, f32[256,128]{1,0:T(8,128)S(1)}, u32[]{:S(2)}, u32[]{:S(2)}) collective-permute-start(f32[256,128]{1,0:T(8,128)S(1)} %collective-permute-done.9.refs_10_), channel_id=1, source_target_pairs={{0,2},{2,0},{1,3},{3,1},{4,6},{6,4},{5,7},{7,5},{8,10},{10,8},{9,1... | collective-permute-start | bytes 393224 | tf_op jit(solution)/shard_map/ppermute | solution.py:785
  44.9 5.6 %collective-permute-start.11 = (f32[8,32,128]{2,1,0:T(8,128)S(1)}, f32[8,32,128]{2,1,0:T(8,128)S(1)}, u32[]{:S(2)}, u32[]{:S(2)}) collective-permute-start(f32[8,32,128]{2,1,0:T(8,128)S(1)} %get-tuple-element.29), channel_id=1, source_target_pairs={{0,1},{1,0},{2,3},{3,2},{4,5},{5,4},{6,7},{7,6},{8,9},{9,8},{10,11... | collective-permute-start | bytes 393224 | tf_op jit(solution)/shard_map/ppermute | solution.py:834

commit v16 on v14

--- a/solution.py
+++ b/solution.py
@@ -89,6 +89,13 @@
 def from_blocks(tiles, order):
     natural = jnp.concatenate(exchange_groups(tiles), axis=0)
     return product(natural, order, 3)
+
+
+def potentials_kernel(rows_ref, potentials_ref):
+    order = lane_order(back=True)
+    for x in range(SIDE):
+        tiles = [rows_ref[pl.ds((x * SIDE + z) * SIDE, SIDE), :] for z in range(SIDE)]
+        potentials_ref[x] = from_blocks(tiles, order)
 
 
 def block_up(field, axis):
@@ -512,8 +519,6 @@
     gathered,
     owned,
     beside,
-    sent,
-    sem,
     *level_refs,
 ):
     f32 = jnp.float32
@@ -654,7 +659,6 @@
     at_spot = iota((LANES, electrodes), 0) == spot
     order = lane_order(back=True)
     wide = SIDE + 2
-    sending = pltpu.make_async_copy(sent, potentials_ref, sem)
 
     def each(body):
         def one(electrode, carry):
@@ -707,10 +711,6 @@
 
         @pl.when(index == 0)
         def _():
-            for x in range(SIDE):
-                tiles = [owned[0, (x + 1) * wide + z + 1] for z in range(SIDE)]
-                sent[x] = from_blocks(tiles, order)
-            sending.start()
             each(read)
             readings = jnp.where(at_spot, gathered[...].T, 0.0)
             readings = jnp.sum(readings, axis=0, keepdims=True)
@@ -727,6 +727,7 @@
         for z in range(SIDE):
             at = (x + 1) * wide + z + 1
             here_u, here_w = owned[0, at], owned[1, at]
+            potentials_ref[pl.ds((x * SIDE + z) * SIDE, SIDE), :] = here_u
             total = None
             for step in (wide, -wide, 1, -1):
                 term = (here_u - owned[0, at + step]) * (here_w - owned[1, at + step])
@@ -739,7 +740,6 @@
         low, high = natural[:chunk], natural[chunk:]
         mine_ref[x] = jnp.where(even, low, high)
         theirs_ref[x] = jnp.where(even, high, low)
-    sending.wait()
 
 
 def replicated(conductivity, stations, currents, receivers, observed):
@@ -789,34 +789,45 @@
         cost_estimate=pl.CostEstimate(flops=100_000_000, bytes_accessed=1_000_000, transcendentals=0),
     )(station_row, currents, receivers, observed)
     far, rows_of = lax.optimization_barrier((far, rows_of))
-    far = [far, lax.ppermute(far, "shot", swap)]
-    halved = far + [partner(piece, 1) for piece in far]
+    count_x = lax.axis_size("gx")
+    diagonal = [(2 * i + j, 2 * (i ^ 1) + 1 - j) for i in range(count_x) for j in range(2)]
+    crossed, relayed = lax.ppermute(far, "shot", swap), partner(far, 1)
+    slanted = lax.ppermute(far, ("gx", "shot"), diagonal)
     parts = [piece for own in (mine, near) for piece in with_mate(own)]
-    halved = [piece for own in halved for piece in with_mate(own)]
+    halved = [piece for own in (far, crossed, relayed) for piece in with_mate(own)]
+    slanted, halved[3] = lax.optimization_barrier((slanted, halved[3]))
+    halved += with_mate(slanted)
     chunk = cols // 2
     levels = [shape for index in range(LEVELS - 2) for shape in Level.scratch(index)]
     levels += HeldLevel.scratch(LEVELS - 2)
     potentials, own, theirs = pl.pallas_call(
         functools.partial(replicated_kernel, len(parts), len(halved)),
         out_shape=(
-            jax.ShapeDtypeStruct((rows, cols, LANES), f32),
+            jax.ShapeDtypeStruct((total, LANES), f32),
             jax.ShapeDtypeStruct((rows, chunk, LANES), f32),
             jax.ShapeDtypeStruct((rows, chunk, LANES), f32),
         ),
         in_specs=[smem] + [vmem] * (len(parts) + len(halved) + 6),
-        out_specs=(pl.BlockSpec(memory_space=pl.ANY), vmem, vmem),
+        out_specs=(vmem, vmem, vmem),
         scratch_shapes=[
             pltpu.VMEM((electrodes, LANES), f32),
             pltpu.VMEM((2, (SIDE + 2) ** 2, SIDE, LANES), f32),
             pltpu.VMEM((2, 2, SIDE**2, SIDE, LANES), f32),
-            pltpu.VMEM((rows, cols, LANES), f32),
-            pltpu.SemaphoreType.DMA,
         ]
         + levels,
         compiler_params=pltpu.CompilerParams(vmem_limit_bytes=VMEM_BYTES),
         cost_estimate=pl.CostEstimate(flops=200_000_000, bytes_accessed=4_000_000, transcendentals=0),
     )(cells, *parts, *halved, spot, rows_of, same, pairs, turned, held)
-    return potentials[None], own + lax.ppermute(theirs, "shot", swap)
+    arrived = lax.ppermute(theirs, "shot", swap)
+    potentials = pl.pallas_call(
+        potentials_kernel,
+        out_shape=jax.ShapeDtypeStruct((rows, cols, LANES), f32),
+        in_specs=[vmem],
+        out_specs=vmem,
+        compiler_params=pltpu.CompilerParams(vmem_limit_bytes=SMALL_BYTES),
+        cost_estimate=pl.CostEstimate(flops=50_000_000, bytes_accessed=500_000, transcendentals=0),
+    )(potentials)
+    return potentials[None], own + arrived
 
 
 def extended(array, sides, width):

time: 51.3 us -> 50.6 us (0.986)
  waiting for transfers between devices: 14.8 us -> 13.3 us
  Pallas kernels: 21.9 us -> 22.6 us
    ppermute x4 -> x3, waiting for transfers between devices: 7.91 us -> 5.85 us  [partner(): return lax.ppermute(part, 'gx', [(i, i ^ k) for i in range(count)])]
    pallas_call x0 -> x1, Pallas kernels: none -> 1.37 us  [replicated(): pl.pallas_call(potentials_kernel, out_shape=jax.ShapeDtypeStruct((rows, c...]
    ppermute x4 -> x3, starting transfers between devices: 7.4 us -> 6.29 us  [partner(): return lax.ppermute(part, 'gx', [(i, i ^ k) for i in range(count)])]
    ppermute x2 -> x3, waiting for transfers between devices: 5.61 us -> 6.45 us  [the longest x1 3.17 us: replicated(): arrived = lax.ppermute(theirs, 'shot', swap)]
    ppermute x2 -> x3, starting transfers between devices: 3.32 us -> 4.13 us  [the longest x1 1.54 us: replicated(): crossed, relayed = (lax.ppermute(far, 'shot', swap), partner(far, 1))]
    pallas_call x1, Pallas kernels: 20.9 us -> 20.2 us  [replicated(): pl.pallas_call(functools.partial(replicated_kernel, len(parts), len(halve...]
  transfers between devices with their start and end apart: 12 -> 12, of which waited for: 7 -> 7; matrix products, arithmetic and copies ran while one was open for 0% -> 0% of each run, Pallas kernels for 1% -> 4%
where the time goes in v16:
time: 50.6 us; the launch traced here: 50.5 us
  Pallas kernels  22.6 us (45%)
  waiting for transfers between devices  13.3 us (26%)
  starting transfers between devices  11.4 us (23%)
  local copies, waits for them, and re-layouts  1.76 us (3%)
  between operations  0.7 us (1%)
  other arithmetic  0.67 us (1%)
    pallas_call x1, Pallas kernels, replicated(): pl.pallas_call(functools.partial(replicated_kernel, len(parts), len(halve...  20.2 us
    ppermute x3, starting transfers between devices, partner(): return lax.ppermute(part, 'gx', [(i, i ^ k) for i in range(count)])  6.29 us
    ppermute x3, waiting for transfers between devices, partner(): return lax.ppermute(part, 'gx', [(i, i ^ k) for i in range(count)])  5.85 us
    ppermute x1, waiting for transfers between devices, replicated(): arrived = lax.ppermute(theirs, 'shot', swap)  3.17 us
    ppermute x1, waiting for transfers between devices, replicated(): slanted = lax.ppermute(far, ('gx', 'shot'), diagonal)  1.8 us
    unnamed x11, local copies, waits for them, and re-layouts  1.76 us
    ppermute x1, starting transfers between devices, replicated(): crossed, relayed = (lax.ppermute(far, 'shot', swap), partner(far, 1))  1.54 us
    ppermute x1, waiting for transfers between devices, replicated(): crossed, relayed = (lax.ppermute(far, 'shot', swap), partner(far, 1))  1.48 us
  transfers between devices with their start and end apart: 12, of which 7 were waited for; matrix products, arithmetic and copies ran while one was open for 0% of the time, Pallas kernels for 4%

profile of v16, /device:TPU:0, one launch (start us, length us, event | category | flops | bytes accessed | tf_op | source)
XLA Modules:
  0.0 50.5 jit_solution(78041846313035096)
XLA Ops:
  0.6 0.9 %copy-done = f32[8,64,128]{2,1,0:T(8,128)S(1)} copy-done((f32[8,64,128]{2,1,0:T(8,128)S(1)}, f32[8,64,128]{2,1,0:T(8,128)}, u32[]{:S(2)}) %copy-start) | copy-done | bytes 262168
  1.6 0.6 %shard_map.69 = (f32[512,128]{1,0:T(8,128)S(1)}, f32[256,128]{1,0:T(8,128)S(1)}) custom-call(f32[8,64,128]{2,1,0:T(8,128)S(1)} %copy-done), custom_call_target="tpu_custom_call" | custom-call | tf_op jit(solution)/shard_map/pallas_call | solution.py:753
  2.2 4.1 %collective-permute-start.3 = (f32[256,128]{1,0:T(8,128)S(1)}, f32[256,128]{1,0:T(8,128)S(1)}, u32[]{:S(2)}, u32[]{:S(2)}) collective-permute-start(f32[256,128]{1,0:T(8,128)S(1)} %get-tuple-element.20), channel_id=1, source_target_pairs={{0,8},{4,12},{8,0},{12,4},{1,9},{5,13},{9,1},{13,5},{2,10},{6,14},... | collective-permute-start | bytes 393224 | tf_op jit(solution)/shard_map/ppermute | solution.py:767
  6.3 1.6 %collective-permute-start.1 = (f32[512,128]{1,0:T(8,128)S(1)}, f32[512,128]{1,0:T(8,128)S(1)}, u32[]{:S(2)}, u32[]{:S(2)}) collective-permute-start(f32[512,128]{1,0:T(8,128)S(1)} %get-tuple-element.19.refs_0_), channel_id=1, source_target_pairs={{0,4},{4,0},{8,12},{12,8},{1,5},{5,1},{9,13},{13,9},{2,6},{6,2},{1... | collective-permute-start | bytes 786440 | tf_op jit(solution)/shard_map/ppermute | solution.py:767
  7.9 0.1 copy.7.receivers_ref
  8.0 0.0 copy-start.2
  8.0 0.5 copy-done.3
  8.5 0.2 copy-done.2
  8.7 0.4 shard_map.68
  9.1 3.5 %collective-permute-done.3.refs_4_ = f32[256,128]{1,0:T(8,128)S(1)} collective-permute-done((f32[256,128]{1,0:T(8,128)S(1)}, f32[256,128]{1,0:T(8,128)S(1)}, u32[]{:S(2)}, u32[]{:S(2)}) %collective-permute-start.3) | collective-permute-done | bytes 131104 | tf_op jit(solution)/shard_map/ppermute | solution.py:767
  12.7 1.5 %collective-permute-start.5 = (f32[256,128]{1,0:T(8,128)S(1)}, f32[256,128]{1,0:T(8,128)S(1)}, u32[]{:S(2)}, u32[]{:S(2)}) collective-permute-start(f32[256,128]{1,0:T(8,128)S(1)} %collective-permute-done.3.refs_4_), channel_id=1, source_target_pairs={{0,1},{1,0},{2,3},{3,2},{4,5},{5,4},{6,7},{7,6},{8,9},{9,8},{10,11... | collective-permute-start | bytes 393224 | tf_op jit(solution)/shard_map/ppermute | solution.py:794
  14.2 0.6 %collective-permute-start.8 = (f32[256,128]{1,0:T(8,128)S(1)}, f32[256,128]{1,0:T(8,128)S(1)}, u32[]{:S(2)}, u32[]{:S(2)}) collective-permute-start(f32[256,128]{1,0:T(8,128)S(1)} %collective-permute-done.3.refs_4_), channel_id=1, source_target_pairs={{0,4},{4,0},{8,12},{12,8},{1,5},{5,1},{9,13},{13,9},{2,6},{6,2},{1... | collective-permute-start | bytes 393224 | tf_op jit(solution)/shard_map/ppermute | solution.py:767
  14.8 0.0 collective-permute-start
  14.8 1.3 %collective-permute-start.6 = (f32[256,128]{1,0:T(8,128)S(1)}, f32[256,128]{1,0:T(8,128)S(1)}, u32[]{:S(2)}, u32[]{:S(2)}) collective-permute-start(f32[256,128]{1,0:T(8,128)S(1)} %collective-permute-done.3.refs_4_), channel_id=1, source_target_pairs={{0,5},{1,4},{4,1},{5,0},{8,13},{9,12},{12,9},{13,8},{2,7},{3,6},{6... | collective-permute-start | bytes 393224 | tf_op jit(solution)/shard_map/ppermute | solution.py:795
  16.2 1.5 %collective-permute-done.5.refs_6_ = f32[256,128]{1,0:T(8,128)S(1)} collective-permute-done((f32[256,128]{1,0:T(8,128)S(1)}, f32[256,128]{1,0:T(8,128)S(1)}, u32[]{:S(2)}, u32[]{:S(2)}) %collective-permute-start.5) | collective-permute-done | bytes 131104 | tf_op jit(solution)/shard_map/ppermute | solution.py:794
  17.7 0.0 collective-permute-start.7
  17.7 0.0 collective-permute-done.1.refs_2_
  17.7 0.5 %collective-permute-start.2 = (f32[512,128]{1,0:T(8,128)S(1)}, f32[512,128]{1,0:T(8,128)S(1)}, u32[]{:S(2)}, u32[]{:S(2)}) collective-permute-start(f32[512,128]{1,0:T(8,128)S(1)} %collective-permute-done.1.refs_2_), channel_id=1, source_target_pairs={{0,2},{2,0},{1,3},{3,1},{4,6},{6,4},{5,7},{7,5},{8,10},{10,8},{9,1... | collective-permute-start | bytes 786440 | tf_op jit(solution)/shard_map/ppermute | solution.py:770
  18.2 2.3 %collective-permute-done.8.refs_8_ = f32[256,128]{1,0:T(8,128)S(1)} collective-permute-done((f32[256,128]{1,0:T(8,128)S(1)}, f32[256,128]{1,0:T(8,128)S(1)}, u32[]{:S(2)}, u32[]{:S(2)}) %collective-permute-start.8) | collective-permute-done | bytes 131104 | tf_op jit(solution)/shard_map/ppermute | solution.py:767
  20.5 0.0 collective-permute-start.4
  20.5 1.8 %collective-permute-done.6.refs_10_ = f32[256,128]{1,0:T(8,128)S(1)} collective-permute-done((f32[256,128]{1,0:T(8,128)S(1)}, f32[256,128]{1,0:T(8,128)S(1)}, u32[]{:S(2)}, u32[]{:S(2)}) %collective-permute-start.6) | collective-permute-done | bytes 131104 | tf_op jit(solution)/shard_map/ppermute | solution.py:795
  22.3 0.0 collective-permute-start.9
  22.3 0.0 collective-permute-done.7.refs_7_
  22.3 0.5 %collective-permute-start.10 = (f32[256,128]{1,0:T(8,128)S(1)}, f32[256,128]{1,0:T(8,128)S(1)}, u32[]{:S(2)}, u32[]{:S(2)}) collective-permute-start(f32[256,128]{1,0:T(8,128)S(1)} %collective-permute-done.6.refs_10_), channel_id=1, source_target_pairs={{0,2},{2,0},{1,3},{3,1},{4,6},{6,4},{5,7},{7,5},{8,10},{10,8},{9,1... | collective-permute-start | bytes 393224 | tf_op jit(solution)/shard_map/ppermute | solution.py:770
  22.8 0.8 %collective-permute-done.9.refs_9_ = f32[256,128]{1,0:T(8,128)S(1)} collective-permute-done((f32[256,128]{1,0:T(8,128)S(1)}, f32[256,128]{1,0:T(8,128)S(1)}, u32[]{:S(2)}, u32[]{:S(2)}) %collective-permute-start.9) | collective-permute-done | bytes 131104 | tf_op jit(solution)/shard_map/ppermute | solution.py:770
  23.6 0.0 collective-permute-done.2.refs_3_
  23.6 0.2 collective-permute-done.10.refs_11_
  23.8 20.2 %shard_map.70 = (f32[512,128]{1,0:T(8,128)S(1)}, f32[8,32,128]{2,1,0:T(8,128)S(1)}, f32[8,32,128]{2,1,0:T(8,128)S(1)}) custom-call(s32[1,256]{1,0:T(1,128)S(1)} %get-tuple-element.18.cells_ref, f32[512,128]{1,0:T(8,128)S(1)} %get-tuple-element.19.refs_0_, f32[512,128]{1,0:T(8,128)S(1)} %collective-permute-done.refs_1_, ...), custom_call_target="tpu_custom_call" | custom-call | flops 200000000 | bytes 4000000 | tf_op jit(solution)/shard_map/pallas_call | solution.py:803
  44.0 1.3 %collective-permute-start.11 = (f32[8,32,128]{2,1,0:T(8,128)S(1)}, f32[8,32,128]{2,1,0:T(8,128)S(1)}, u32[]{:S(2)}, u32[]{:S(2)}) collective-permute-start(f32[8,32,128]{2,1,0:T(8,128)S(1)} %get-tuple-element.33), channel_id=1, source_target_pairs={{0,1},{1,0},{2,3},{3,2},{4,5},{5,4},{6,7},{7,6},{8,9},{9,8},{10,11... | collective-permute-start | bytes 393224 | tf_op jit(solution)/shard_map/ppermute | solution.py:821
  45.2 1.4 %shard_map.71 = f32[8,64,128]{2,1,0:T(8,128)} custom-call(f32[512,128]{1,0:T(8,128)S(1)} %get-tuple-element.31.rows_ref), custom_call_target="tpu_custom_call" | custom-call | flops 50000000 | bytes 500000 | tf_op jit(solution)/shard_map/pallas_call | solution.py:822
  46.6 3.2 %collective-permute-done.11 = f32[8,32,128]{2,1,0:T(8,128)S(1)} collective-permute-done((f32[8,32,128]{2,1,0:T(8,128)S(1)}, f32[8,32,128]{2,1,0:T(8,128)S(1)}, u32[]{:S(2)}, u32[]{:S(2)}) %collective-permute-start.11) | collective-permute-done | bytes 131104 | tf_op jit(solution)/shard_map/ppermute | solution.py:821
  49.8 0.7 %add.3 = f32[8,32,128]{2,1,0:T(8,128)} add(f32[8,32,128]{2,1,0:T(8,128)S(1)} %get-tuple-element.32, f32[8,32,128]{2,1,0:T(8,128)S(1)} %collective-permute-done.11) | non-fusion elementwise | flops 32768 | bytes 393216 | tf_op jit(solution)/shard_map/add | solution.py:830
  (8 shorter events, 0.0 us)
Async XLA Ops:
  0.6 1.0 %copy-start = (f32[8,64,128]{2,1,0:T(8,128)S(1)}, f32[8,64,128]{2,1,0:T(8,128)}, u32[]{:S(2)}) copy-start(f32[8,64,128]{2,1,0:T(8,128)} %natural_ref.1) | copy-start | bytes 786436
  1.6 6.3 %copy-start.4 = (s32[512,2]{0,1:T(2,128)S(1)}, s32[512,2]{0,1:T(2,128)}, u32[]{:S(2)}) copy-start(s32[512,2]{0,1:T(2,128)} %param.8) | copy-start | bytes 12292
  2.2 10.5 %collective-permute-start.3 = (f32[256,128]{1,0:T(8,128)S(1)}, f32[256,128]{1,0:T(8,128)S(1)}, u32[]{:S(2)}, u32[]{:S(2)}) collective-permute-start(f32[256,128]{1,0:T(8,128)S(1)} %get-tuple-element.20), channel_id=1, source_target_pairs={{0,8},{4,12},{8,0},{12,4},{1,9},{5,13},{9,1},{13,5},{2,10},{6,14},... | collective-permute-start | bytes 393224 | tf_op jit(solution)/shard_map/ppermute | solution.py:767
  6.3 1.7 %copy-start.1 = (f32[1,512]{1,0:T(1,128)S(1)}, f32[1,512]{1,0:T(1,128)}, u32[]{:S(2)}) copy-start(f32[1,512]{1,0:T(1,128)} %observed_ref.1) | copy-start | bytes 6148
  6.3 11.4 %collective-permute-start.1 = (f32[512,128]{1,0:T(8,128)S(1)}, f32[512,128]{1,0:T(8,128)S(1)}, u32[]{:S(2)}, u32[]{:S(2)}) collective-permute-start(f32[512,128]{1,0:T(8,128)S(1)} %get-tuple-element.19.refs_0_), channel_id=1, source_target_pairs={{0,4},{4,0},{8,12},{12,8},{1,5},{5,1},{9,13},{13,9},{2,6},{6,2},{1... | collective-permute-start | bytes 786440 | tf_op jit(solution)/shard_map/ppermute | solution.py:767
  7.9 0.7 %copy-start.3 = (f32[1,256]{1,0:T(1,128)S(1)}, f32[1,256]{1,0:T(1,128)}, u32[]{:S(2)}) copy-start(f32[1,256]{1,0:T(1,128)} %currents_ref.1) | copy-start | bytes 3076
  8.0 0.7 %copy-start.2 = (s32[256]{0:T(256)S(1)}, s32[256]{0:T(256)}, u32[]{:S(2)}) copy-start(s32[256]{0:T(256)} %param.6) | copy-start | bytes 3076
  12.7 5.0 %collective-permute-start.5 = (f32[256,128]{1,0:T(8,128)S(1)}, f32[256,128]{1,0:T(8,128)S(1)}, u32[]{:S(2)}, u32[]{:S(2)}) collective-permute-start(f32[256,128]{1,0:T(8,128)S(1)} %collective-permute-done.3.refs_4_), channel_id=1, source_target_pairs={{0,1},{1,0},{2,3},{3,2},{4,5},{5,4},{6,7},{7,6},{8,9},{9,8},{10,11... | collective-permute-start | bytes 393224 | tf_op jit(solution)/shard_map/ppermute | solution.py:794
  14.2 6.2 %collective-permute-start.8 = (f32[256,128]{1,0:T(8,128)S(1)}, f32[256,128]{1,0:T(8,128)S(1)}, u32[]{:S(2)}, u32[]{:S(2)}) collective-permute-start(f32[256,128]{1,0:T(8,128)S(1)} %collective-permute-done.3.refs_4_), channel_id=1, source_target_pairs={{0,4},{4,0},{8,12},{12,8},{1,5},{5,1},{9,13},{13,9},{2,6},{6,2},{1... | collective-permute-start | bytes 393224 | tf_op jit(solution)/shard_map/ppermute | solution.py:767
  14.8 8.0 %collective-permute-start = (f32[512,128]{1,0:T(8,128)S(1)}, f32[512,128]{1,0:T(8,128)S(1)}, u32[]{:S(2)}, u32[]{:S(2)}) collective-permute-start(f32[512,128]{1,0:T(8,128)S(1)} %get-tuple-element.19.refs_0_), channel_id=1, source_target_pairs={{0,2},{2,0},{1,3},{3,1},{4,6},{6,4},{5,7},{7,5},{8,10},{10,8},{9,1... | collective-permute-start | bytes 786440 | tf_op jit(solution)/shard_map/ppermute | solution.py:770
  14.8 7.4 %collective-permute-start.6 = (f32[256,128]{1,0:T(8,128)S(1)}, f32[256,128]{1,0:T(8,128)S(1)}, u32[]{:S(2)}, u32[]{:S(2)}) collective-permute-start(f32[256,128]{1,0:T(8,128)S(1)} %collective-permute-done.3.refs_4_), channel_id=1, source_target_pairs={{0,5},{1,4},{4,1},{5,0},{8,13},{9,12},{12,9},{13,8},{2,7},{3,6},{6... | collective-permute-start | bytes 393224 | tf_op jit(solution)/shard_map/ppermute | solution.py:795
  17.7 4.6 %collective-permute-start.7 = (f32[256,128]{1,0:T(8,128)S(1)}, f32[256,128]{1,0:T(8,128)S(1)}, u32[]{:S(2)}, u32[]{:S(2)}) collective-permute-start(f32[256,128]{1,0:T(8,128)S(1)} %collective-permute-done.5.refs_6_), channel_id=1, source_target_pairs={{0,2},{2,0},{1,3},{3,1},{4,6},{6,4},{5,7},{7,5},{8,10},{10,8},{9,1... | collective-permute-start | bytes 393224 | tf_op jit(solution)/shard_map/ppermute | solution.py:770
  17.7 6.0 %collective-permute-start.2 = (f32[512,128]{1,0:T(8,128)S(1)}, f32[512,128]{1,0:T(8,128)S(1)}, u32[]{:S(2)}, u32[]{:S(2)}) collective-permute-start(f32[512,128]{1,0:T(8,128)S(1)} %collective-permute-done.1.refs_2_), channel_id=1, source_target_pairs={{0,2},{2,0},{1,3},{3,1},{4,6},{6,4},{5,7},{7,5},{8,10},{10,8},{9,1... | collective-permute-start | bytes 786440 | tf_op jit(solution)/shard_map/ppermute | solution.py:770
  20.5 2.3 %collective-permute-start.4 = (f32[256,128]{1,0:T(8,128)S(1)}, f32[256,128]{1,0:T(8,128)S(1)}, u32[]{:S(2)}, u32[]{:S(2)}) collective-permute-start(f32[256,128]{1,0:T(8,128)S(1)} %collective-permute-done.3.refs_4_), channel_id=1, source_target_pairs={{0,2},{2,0},{1,3},{3,1},{4,6},{6,4},{5,7},{7,5},{8,10},{10,8},{9,1... | collective-permute-start | bytes 393224 | tf_op jit(solution)/shard_map/ppermute | solution.py:770
  22.3 1.3 %collective-permute-start.9 = (f32[256,128]{1,0:T(8,128)S(1)}, f32[256,128]{1,0:T(8,128)S(1)}, u32[]{:S(2)}, u32[]{:S(2)}) collective-permute-start(f32[256,128]{1,0:T(8,128)S(1)} %collective-permute-done.8.refs_8_), channel_id=1, source_target_pairs={{0,2},{2,0},{1,3},{3,1},{4,6},{6,4},{5,7},{7,5},{8,10},{10,8},{9,1... | collective-permute-start | bytes 393224 | tf_op jit(solution)/shard_map/ppermute | solution.py:770
  22.3 1.5 %collective-permute-start.10 = (f32[256,128]{1,0:T(8,128)S(1)}, f32[256,128]{1,0:T(8,128)S(1)}, u32[]{:S(2)}, u32[]{:S(2)}) collective-permute-start(f32[256,128]{1,0:T(8,128)S(1)} %collective-permute-done.6.refs_10_), channel_id=1, source_target_pairs={{0,2},{2,0},{1,3},{3,1},{4,6},{6,4},{5,7},{7,5},{8,10},{10,8},{9,1... | collective-permute-start | bytes 393224 | tf_op jit(solution)/shard_map/ppermute | solution.py:770
  44.0 5.8 %collective-permute-start.11 = (f32[8,32,128]{2,1,0:T(8,128)S(1)}, f32[8,32,128]{2,1,0:T(8,128)S(1)}, u32[]{:S(2)}, u32[]{:S(2)}) collective-permute-start(f32[8,32,128]{2,1,0:T(8,128)S(1)} %get-tuple-element.33), channel_id=1, source_target_pairs={{0,1},{1,0},{2,3},{3,2},{4,5},{5,4},{6,7},{7,6},{8,9},{9,8},{10,11... | collective-permute-start | bytes 393224 | tf_op jit(solution)/shard_map/ppermute | solution.py:821

commit v17 on v16

--- a/solution.py
+++ b/solution.py
@@ -665,7 +665,7 @@
             body(pl.ds(electrode, 1), pl.ds(cells_ref[0, electrode], 1))
             return carry
 
-        lax.fori_loop(0, electrodes, one, 0, unroll=64)
+        lax.fori_loop(0, electrodes, one, 0, unroll=128)
 
     def put(electrode, cell):
         fine.base.ref[cell, :] = (2.0 * gathered[electrode, :]) * fine.weight.ref[cell, :]
@@ -792,11 +792,11 @@
     count_x = lax.axis_size("gx")
     diagonal = [(2 * i + j, 2 * (i ^ 1) + 1 - j) for i in range(count_x) for j in range(2)]
     crossed, relayed = lax.ppermute(far, "shot", swap), partner(far, 1)
-    slanted = lax.ppermute(far, ("gx", "shot"), diagonal)
+    slanted = with_mate(lax.ppermute(far, ("gx", "shot"), diagonal))
     parts = [piece for own in (mine, near) for piece in with_mate(own)]
-    halved = [piece for own in (far, crossed, relayed) for piece in with_mate(own)]
-    slanted, halved[3] = lax.optimization_barrier((slanted, halved[3]))
-    halved += with_mate(slanted)
+    halved = [piece for own in (far, crossed) for piece in with_mate(own)]
+    relayed, slanted[1] = lax.optimization_barrier((relayed, slanted[1]))
+    halved += with_mate(relayed) + slanted
     chunk = cols // 2
     levels = [shape for index in range(LEVELS - 2) for shape in Level.scratch(index)]
     levels += HeldLevel.scratch(LEVELS - 2)

time: 50.6 us -> 51 us (level)
  waiting for transfers between devices: 13.3 us -> 14.3 us
    ppermute x1, waiting for transfers between devices: 1.8 us -> 4.8 us  [replicated(): slanted = with_mate(lax.ppermute(far, ('gx', 'shot'), diagonal))]
    ppermute x3, waiting for transfers between devices: 5.85 us -> 3.55 us  [partner(): return lax.ppermute(part, 'gx', [(i, i ^ k) for i in range(count)])]
    ppermute x1, starting transfers between devices: 1.54 us -> 0.49 us  [replicated(): crossed, relayed = (lax.ppermute(far, 'shot', swap), partner(far, 1))]
    ppermute x3, starting transfers between devices: 6.29 us -> 7.09 us  [partner(): return lax.ppermute(part, 'gx', [(i, i ^ k) for i in range(count)])]
    ppermute x1, waiting for transfers between devices: 3.17 us -> 3.8 us  [replicated(): arrived = lax.ppermute(theirs, 'shot', swap)]
    ppermute x1, starting transfers between devices: 1.25 us -> 0.62 us  [replicated(): arrived = lax.ppermute(theirs, 'shot', swap)]
  transfers between devices with their start and end apart: 12 -> 12, of which waited for: 7 -> 6; matrix products, arithmetic and copies ran while one was open for 0% -> 0% of each run, Pallas kernels for 4% -> 4%
where the time goes in v17:
time: 51 us; the launch traced here: 50.8 us
  Pallas kernels  22.5 us (44%)
  waiting for transfers between devices  14.3 us (28%)
  starting transfers between devices  10.9 us (21%)
  local copies, waits for them, and re-layouts  1.76 us (3%)
  between operations  0.7 us (1%)
  other arithmetic  0.67 us (1%)
    pallas_call x1, Pallas kernels, replicated(): pl.pallas_call(functools.partial(replicated_kernel, len(parts), len(halve...  20.1 us
    ppermute x3, starting transfers between devices, partner(): return lax.ppermute(part, 'gx', [(i, i ^ k) for i in range(count)])  7.09 us
    ppermute x1, waiting for transfers between devices, replicated(): slanted = with_mate(lax.ppermute(far, ('gx', 'shot'), diagonal))  4.8 us
    ppermute x1, waiting for transfers between devices, replicated(): arrived = lax.ppermute(theirs, 'shot', swap)  3.8 us
    ppermute x3, waiting for transfers between devices, partner(): return lax.ppermute(part, 'gx', [(i, i ^ k) for i in range(count)])  3.55 us
    unnamed x11, local copies, waits for them, and re-layouts  1.76 us
    ppermute x1, starting transfers between devices, replicated(): slanted = with_mate(lax.ppermute(far, ('gx', 'shot'), diagonal))  1.59 us
    pallas_call x1, Pallas kernels, replicated(): pl.pallas_call(potentials_kernel, out_shape=jax.ShapeDtypeStruct((rows, c...  1.37 us
  transfers between devices with their start and end apart: 12, of which 6 were waited for; matrix products, arithmetic and copies ran while one was open for 0% of the time, Pallas kernels for 4%

profile of v17, /device:TPU:0, one launch (start us, length us, event | category | flops | bytes accessed | tf_op | source)
XLA Modules:
  0.0 50.8 jit_solution(17049915082814869299)
XLA Ops:
  0.6 0.9 %copy-done = f32[8,64,128]{2,1,0:T(8,128)S(1)} copy-done((f32[8,64,128]{2,1,0:T(8,128)S(1)}, f32[8,64,128]{2,1,0:T(8,128)}, u32[]{:S(2)}) %copy-start) | copy-done | bytes 262168
  1.6 0.6 %shard_map.69 = (f32[512,128]{1,0:T(8,128)S(1)}, f32[256,128]{1,0:T(8,128)S(1)}) custom-call(f32[8,64,128]{2,1,0:T(8,128)S(1)} %copy-done), custom_call_target="tpu_custom_call" | custom-call | tf_op jit(solution)/shard_map/pallas_call | solution.py:753
  2.2 4.1 %collective-permute-start.3 = (f32[256,128]{1,0:T(8,128)S(1)}, f32[256,128]{1,0:T(8,128)S(1)}, u32[]{:S(2)}, u32[]{:S(2)}) collective-permute-start(f32[256,128]{1,0:T(8,128)S(1)} %get-tuple-element.20), channel_id=1, source_target_pairs={{0,8},{4,12},{8,0},{12,4},{1,9},{5,13},{9,1},{13,5},{2,10},{6,14},... | collective-permute-start | bytes 393224 | tf_op jit(solution)/shard_map/ppermute | solution.py:767
  6.3 1.6 %collective-permute-start.1 = (f32[512,128]{1,0:T(8,128)S(1)}, f32[512,128]{1,0:T(8,128)S(1)}, u32[]{:S(2)}, u32[]{:S(2)}) collective-permute-start(f32[512,128]{1,0:T(8,128)S(1)} %get-tuple-element.19.refs_0_), channel_id=1, source_target_pairs={{0,4},{4,0},{8,12},{12,8},{1,5},{5,1},{9,13},{13,9},{2,6},{6,2},{1... | collective-permute-start | bytes 786440 | tf_op jit(solution)/shard_map/ppermute | solution.py:767
  7.9 0.1 copy.7.receivers_ref
  8.0 0.0 copy-start.2
  8.0 0.5 copy-done.3
  8.5 0.2 copy-done.2
  8.7 0.4 shard_map.68
  9.1 3.5 %collective-permute-done.3.refs_4_ = f32[256,128]{1,0:T(8,128)S(1)} collective-permute-done((f32[256,128]{1,0:T(8,128)S(1)}, f32[256,128]{1,0:T(8,128)S(1)}, u32[]{:S(2)}, u32[]{:S(2)}) %collective-permute-start.3) | collective-permute-done | bytes 131104 | tf_op jit(solution)/shard_map/ppermute | solution.py:767
  12.7 1.6 %collective-permute-start.8 = (f32[256,128]{1,0:T(8,128)S(1)}, f32[256,128]{1,0:T(8,128)S(1)}, u32[]{:S(2)}, u32[]{:S(2)}) collective-permute-start(f32[256,128]{1,0:T(8,128)S(1)} %collective-permute-done.3.refs_4_), channel_id=1, source_target_pairs={{0,5},{1,4},{4,1},{5,0},{8,13},{9,12},{12,9},{13,8},{2,7},{3,6},{6... | collective-permute-start | bytes 393224 | tf_op jit(solution)/shard_map/ppermute | solution.py:795
  14.3 1.4 %collective-permute-start.7 = (f32[256,128]{1,0:T(8,128)S(1)}, f32[256,128]{1,0:T(8,128)S(1)}, u32[]{:S(2)}, u32[]{:S(2)}) collective-permute-start(f32[256,128]{1,0:T(8,128)S(1)} %collective-permute-done.3.refs_4_), channel_id=1, source_target_pairs={{0,4},{4,0},{8,12},{12,8},{1,5},{5,1},{9,13},{13,9},{2,6},{6,2},{1... | collective-permute-start | bytes 393224 | tf_op jit(solution)/shard_map/ppermute | solution.py:767
  15.7 0.0 collective-permute-start
  15.7 0.5 collective-permute-start.5
  16.2 4.8 %collective-permute-done.8.refs_10_ = f32[256,128]{1,0:T(8,128)S(1)} collective-permute-done((f32[256,128]{1,0:T(8,128)S(1)}, f32[256,128]{1,0:T(8,128)S(1)}, u32[]{:S(2)}, u32[]{:S(2)}) %collective-permute-start.8) | collective-permute-done | bytes 131104 | tf_op jit(solution)/shard_map/ppermute | solution.py:795
  21.0 0.0 collective-permute-start.9
  21.0 0.0 collective-permute-done.1.refs_2_
  21.0 0.5 collective-permute-start.2
  21.5 0.0 collective-permute-done.7.refs_8_
  21.5 0.1 collective-permute-start.4
  21.6 1.1 %collective-permute-done.5.refs_6_ = f32[256,128]{1,0:T(8,128)S(1)} collective-permute-done((f32[256,128]{1,0:T(8,128)S(1)}, f32[256,128]{1,0:T(8,128)S(1)}, u32[]{:S(2)}, u32[]{:S(2)}) %collective-permute-start.5) | collective-permute-done | bytes 131104 | tf_op jit(solution)/shard_map/ppermute | solution.py:794
  22.7 0.0 collective-permute-start.6
  22.7 0.0 collective-permute-done.9.refs_11_
  22.7 0.5 collective-permute-start.10
  23.2 0.0 collective-permute-done.refs_1_
  23.2 0.8 %collective-permute-done.6.refs_7_ = f32[256,128]{1,0:T(8,128)S(1)} collective-permute-done((f32[256,128]{1,0:T(8,128)S(1)}, f32[256,128]{1,0:T(8,128)S(1)}, u32[]{:S(2)}, u32[]{:S(2)}) %collective-permute-start.6) | collective-permute-done | bytes 131104 | tf_op jit(solution)/shard_map/ppermute | solution.py:770
  24.0 0.2 collective-permute-done.10.refs_9_
  24.2 20.1 %shard_map.70 = (f32[512,128]{1,0:T(8,128)S(1)}, f32[8,32,128]{2,1,0:T(8,128)S(1)}, f32[8,32,128]{2,1,0:T(8,128)S(1)}) custom-call(s32[1,256]{1,0:T(1,128)S(1)} %get-tuple-element.18.cells_ref, f32[512,128]{1,0:T(8,128)S(1)} %get-tuple-element.19.refs_0_, f32[512,128]{1,0:T(8,128)S(1)} %collective-permute-done.refs_1_, ...), custom_call_target="tpu_custom_call" | custom-call | flops 200000000 | bytes 4000000 | tf_op jit(solution)/shard_map/pallas_call | solution.py:803
  44.4 0.6 %collective-permute-start.11 = (f32[8,32,128]{2,1,0:T(8,128)S(1)}, f32[8,32,128]{2,1,0:T(8,128)S(1)}, u32[]{:S(2)}, u32[]{:S(2)}) collective-permute-start(f32[8,32,128]{2,1,0:T(8,128)S(1)} %get-tuple-element.33), channel_id=1, source_target_pairs={{0,1},{1,0},{2,3},{3,2},{4,5},{5,4},{6,7},{7,6},{8,9},{9,8},{10,11... | collective-permute-start | bytes 393224 | tf_op jit(solution)/shard_map/ppermute | solution.py:821
  45.0 1.4 %shard_map.71 = f32[8,64,128]{2,1,0:T(8,128)} custom-call(f32[512,128]{1,0:T(8,128)S(1)} %get-tuple-element.31.rows_ref), custom_call_target="tpu_custom_call" | custom-call | flops 50000000 | bytes 500000 | tf_op jit(solution)/shard_map/pallas_call | solution.py:822
  46.3 3.8 %collective-permute-done.11 = f32[8,32,128]{2,1,0:T(8,128)S(1)} collective-permute-done((f32[8,32,128]{2,1,0:T(8,128)S(1)}, f32[8,32,128]{2,1,0:T(8,128)S(1)}, u32[]{:S(2)}, u32[]{:S(2)}) %collective-permute-start.11) | collective-permute-done | bytes 131104 | tf_op jit(solution)/shard_map/ppermute | solution.py:821
  50.1 0.7 %add.3 = f32[8,32,128]{2,1,0:T(8,128)} add(f32[8,32,128]{2,1,0:T(8,128)S(1)} %get-tuple-element.32, f32[8,32,128]{2,1,0:T(8,128)S(1)} %collective-permute-done.11) | non-fusion elementwise | flops 32768 | bytes 393216 | tf_op jit(solution)/shard_map/add | solution.py:830
  (8 shorter events, 0.0 us)
Async XLA Ops:
  0.6 1.0 %copy-start = (f32[8,64,128]{2,1,0:T(8,128)S(1)}, f32[8,64,128]{2,1,0:T(8,128)}, u32[]{:S(2)}) copy-start(f32[8,64,128]{2,1,0:T(8,128)} %natural_ref.1) | copy-start | bytes 786436
  1.6 6.3 %copy-start.4 = (s32[512,2]{0,1:T(2,128)S(1)}, s32[512,2]{0,1:T(2,128)}, u32[]{:S(2)}) copy-start(s32[512,2]{0,1:T(2,128)} %param.8) | copy-start | bytes 12292
  2.2 10.5 %collective-permute-start.3 = (f32[256,128]{1,0:T(8,128)S(1)}, f32[256,128]{1,0:T(8,128)S(1)}, u32[]{:S(2)}, u32[]{:S(2)}) collective-permute-start(f32[256,128]{1,0:T(8,128)S(1)} %get-tuple-element.20), channel_id=1, source_target_pairs={{0,8},{4,12},{8,0},{12,4},{1,9},{5,13},{9,1},{13,5},{2,10},{6,14},... | collective-permute-start | bytes 393224 | tf_op jit(solution)/shard_map/ppermute | solution.py:767
  6.3 1.7 %copy-start.1 = (f32[1,512]{1,0:T(1,128)S(1)}, f32[1,512]{1,0:T(1,128)}, u32[]{:S(2)}) copy-start(f32[1,512]{1,0:T(1,128)} %observed_ref.1) | copy-start | bytes 6148
  6.3 14.7 %collective-permute-start.1 = (f32[512,128]{1,0:T(8,128)S(1)}, f32[512,128]{1,0:T(8,128)S(1)}, u32[]{:S(2)}, u32[]{:S(2)}) collective-permute-start(f32[512,128]{1,0:T(8,128)S(1)} %get-tuple-element.19.refs_0_), channel_id=1, source_target_pairs={{0,4},{4,0},{8,12},{12,8},{1,5},{5,1},{9,13},{13,9},{2,6},{6,2},{1... | collective-permute-start | bytes 786440 | tf_op jit(solution)/shard_map/ppermute | solution.py:767
  7.9 0.7 %copy-start.3 = (f32[1,256]{1,0:T(1,128)S(1)}, f32[1,256]{1,0:T(1,128)}, u32[]{:S(2)}) copy-start(f32[1,256]{1,0:T(1,128)} %currents_ref.1) | copy-start | bytes 3076
  8.0 0.7 %copy-start.2 = (s32[256]{0:T(256)S(1)}, s32[256]{0:T(256)}, u32[]{:S(2)}) copy-start(s32[256]{0:T(256)} %param.6) | copy-start | bytes 3076
  12.7 8.3 %collective-permute-start.8 = (f32[256,128]{1,0:T(8,128)S(1)}, f32[256,128]{1,0:T(8,128)S(1)}, u32[]{:S(2)}, u32[]{:S(2)}) collective-permute-start(f32[256,128]{1,0:T(8,128)S(1)} %collective-permute-done.3.refs_4_), channel_id=1, source_target_pairs={{0,5},{1,4},{4,1},{5,0},{8,13},{9,12},{12,9},{13,8},{2,7},{3,6},{6... | collective-permute-start | bytes 393224 | tf_op jit(solution)/shard_map/ppermute | solution.py:795
  14.3 7.2 %collective-permute-start.7 = (f32[256,128]{1,0:T(8,128)S(1)}, f32[256,128]{1,0:T(8,128)S(1)}, u32[]{:S(2)}, u32[]{:S(2)}) collective-permute-start(f32[256,128]{1,0:T(8,128)S(1)} %collective-permute-done.3.refs_4_), channel_id=1, source_target_pairs={{0,4},{4,0},{8,12},{12,8},{1,5},{5,1},{9,13},{13,9},{2,6},{6,2},{1... | collective-permute-start | bytes 393224 | tf_op jit(solution)/shard_map/ppermute | solution.py:767
  15.7 7.5 %collective-permute-start = (f32[512,128]{1,0:T(8,128)S(1)}, f32[512,128]{1,0:T(8,128)S(1)}, u32[]{:S(2)}, u32[]{:S(2)}) collective-permute-start(f32[512,128]{1,0:T(8,128)S(1)} %get-tuple-element.19.refs_0_), channel_id=1, source_target_pairs={{0,2},{2,0},{1,3},{3,1},{4,6},{6,4},{5,7},{7,5},{8,10},{10,8},{9,1... | collective-permute-start | bytes 786440 | tf_op jit(solution)/shard_map/ppermute | solution.py:770
  15.7 7.0 %collective-permute-start.5 = (f32[256,128]{1,0:T(8,128)S(1)}, f32[256,128]{1,0:T(8,128)S(1)}, u32[]{:S(2)}, u32[]{:S(2)}) collective-permute-start(f32[256,128]{1,0:T(8,128)S(1)} %collective-permute-done.3.refs_4_), channel_id=1, source_target_pairs={{0,1},{1,0},{2,3},{3,2},{4,5},{5,4},{6,7},{7,6},{8,9},{9,8},{10,11... | collective-permute-start | bytes 393224 | tf_op jit(solution)/shard_map/ppermute | solution.py:794
  21.0 1.7 %collective-permute-start.9 = (f32[256,128]{1,0:T(8,128)S(1)}, f32[256,128]{1,0:T(8,128)S(1)}, u32[]{:S(2)}, u32[]{:S(2)}) collective-permute-start(f32[256,128]{1,0:T(8,128)S(1)} %collective-permute-done.8.refs_10_), channel_id=1, source_target_pairs={{0,2},{2,0},{1,3},{3,1},{4,6},{6,4},{5,7},{7,5},{8,10},{10,8},{9,1... | collective-permute-start | bytes 393224 | tf_op jit(solution)/shard_map/ppermute | solution.py:770
  21.0 3.0 %collective-permute-start.2 = (f32[512,128]{1,0:T(8,128)S(1)}, f32[512,128]{1,0:T(8,128)S(1)}, u32[]{:S(2)}, u32[]{:S(2)}) collective-permute-start(f32[512,128]{1,0:T(8,128)S(1)} %collective-permute-done.1.refs_2_), channel_id=1, source_target_pairs={{0,2},{2,0},{1,3},{3,1},{4,6},{6,4},{5,7},{7,5},{8,10},{10,8},{9,1... | collective-permute-start | bytes 786440 | tf_op jit(solution)/shard_map/ppermute | solution.py:770
  21.5 1.7 %collective-permute-start.4 = (f32[256,128]{1,0:T(8,128)S(1)}, f32[256,128]{1,0:T(8,128)S(1)}, u32[]{:S(2)}, u32[]{:S(2)}) collective-permute-start(f32[256,128]{1,0:T(8,128)S(1)} %collective-permute-done.3.refs_4_), channel_id=1, source_target_pairs={{0,2},{2,0},{1,3},{3,1},{4,6},{6,4},{5,7},{7,5},{8,10},{10,8},{9,1... | collective-permute-start | bytes 393224 | tf_op jit(solution)/shard_map/ppermute | solution.py:770
  22.7 1.3 %collective-permute-start.6 = (f32[256,128]{1,0:T(8,128)S(1)}, f32[256,128]{1,0:T(8,128)S(1)}, u32[]{:S(2)}, u32[]{:S(2)}) collective-permute-start(f32[256,128]{1,0:T(8,128)S(1)} %collective-permute-done.5.refs_6_), channel_id=1, source_target_pairs={{0,2},{2,0},{1,3},{3,1},{4,6},{6,4},{5,7},{7,5},{8,10},{10,8},{9,1... | collective-permute-start | bytes 393224 | tf_op jit(solution)/shard_map/ppermute | solution.py:770
  22.7 1.5 %collective-permute-start.10 = (f32[256,128]{1,0:T(8,128)S(1)}, f32[256,128]{1,0:T(8,128)S(1)}, u32[]{:S(2)}, u32[]{:S(2)}) collective-permute-start(f32[256,128]{1,0:T(8,128)S(1)} %collective-permute-done.7.refs_8_), channel_id=1, source_target_pairs={{0,2},{2,0},{1,3},{3,1},{4,6},{6,4},{5,7},{7,5},{8,10},{10,8},{9,1... | collective-permute-start | bytes 393224 | tf_op jit(solution)/shard_map/ppermute | solution.py:770
  44.4 5.8 %collective-permute-start.11 = (f32[8,32,128]{2,1,0:T(8,128)S(1)}, f32[8,32,128]{2,1,0:T(8,128)S(1)}, u32[]{:S(2)}, u32[]{:S(2)}) collective-permute-start(f32[8,32,128]{2,1,0:T(8,128)S(1)} %get-tuple-element.33), channel_id=1, source_target_pairs={{0,1},{1,0},{2,3},{3,2},{4,5},{5,4},{6,7},{7,6},{8,9},{9,8},{10,11... | collective-permute-start | bytes 393224 | tf_op jit(solution)/shard_map/ppermute | solution.py:821

commit v18 on v17

--- a/solution.py
+++ b/solution.py
@@ -770,7 +770,7 @@
         return [part, lax.ppermute(part, "gy", swap)]
 
     far = partner(half, 2)
-    near = partner(mine, 1)
+    near = partner(half, 1)
     line = jax.ShapeDtypeStruct((1, electrodes), jnp.int32)
     cells, spot, rows_of, same, pairs, turned, held = pl.pallas_call(
         electrode_kernel,
@@ -789,12 +789,14 @@
         cost_estimate=pl.CostEstimate(flops=100_000_000, bytes_accessed=1_000_000, transcendentals=0),
     )(station_row, currents, receivers, observed)
     far, rows_of = lax.optimization_barrier((far, rows_of))
+    parts = with_mate(mine)
+    far, parts[1] = lax.optimization_barrier((far, parts[1]))
     count_x = lax.axis_size("gx")
     diagonal = [(2 * i + j, 2 * (i ^ 1) + 1 - j) for i in range(count_x) for j in range(2)]
+    near_crossed = lax.ppermute(near, "shot", swap)
     crossed, relayed = lax.ppermute(far, "shot", swap), partner(far, 1)
     slanted = with_mate(lax.ppermute(far, ("gx", "shot"), diagonal))
-    parts = [piece for own in (mine, near) for piece in with_mate(own)]
-    halved = [piece for own in (far, crossed) for piece in with_mate(own)]
+    halved = [piece for own in (near, near_crossed, far, crossed) for piece in with_mate(own)]
     relayed, slanted[1] = lax.optimization_barrier((relayed, slanted[1]))
     halved += with_mate(relayed) + slanted
     chunk = cols // 2

time: 51 us -> 53.3 us (1.045)
  starting transfers between devices: 10.9 us -> 13.7 us
    ppermute x1, waiting for transfers between devices: 4.8 us -> 1.94 us  [replicated(): slanted = with_mate(lax.ppermute(far, ('gx', 'shot'), diagonal))]
    ppermute x0 -> x1, waiting for transfers between devices: none -> 1.44 us  [replicated(): near_crossed = lax.ppermute(near, 'shot', swap)]
    ppermute x1, waiting for transfers between devices: 1.11 us -> 2.2 us  [replicated(): crossed, relayed = (lax.ppermute(far, 'shot', swap), partner(far, 1))]
    ppermute x1, starting transfers between devices: 0.49 us -> 1.56 us  [replicated(): crossed, relayed = (lax.ppermute(far, 'shot', swap), partner(far, 1))]
    ppermute x6 -> x7, starting transfers between devices: 1.09 us -> 2.05 us  [with_mate(): return [part, lax.ppermute(part, 'gy', swap)]]
    ppermute x1, waiting for transfers between devices: 3.8 us -> 3.11 us  [replicated(): arrived = lax.ppermute(theirs, 'shot', swap)]
    ppermute x1, starting transfers between devices: 0.62 us -> 1.32 us  [replicated(): arrived = lax.ppermute(theirs, 'shot', swap)]
    ppermute x3, waiting for transfers between devices: 3.55 us -> 4.13 us  [partner(): return lax.ppermute(part, 'gx', [(i, i ^ k) for i in range(count)])]
  transfers between devices with their start and end apart: 12 -> 14, of which waited for: 6 -> 7; matrix products, arithmetic and copies ran while one was open for 0% -> 0% of each run, Pallas kernels for 4% -> 3%
where the time goes in v18:
time: 53.3 us; the launch traced here: 53.2 us
  Pallas kernels  22.5 us (42%)
  waiting for transfers between devices  13.8 us (26%)
  starting transfers between devices  13.7 us (26%)
  local copies, waits for them, and re-layouts  1.76 us (3%)
  between operations  0.71 us (1%)
  other arithmetic  0.67 us (1%)
    pallas_call x1, Pallas kernels, replicated(): pl.pallas_call(functools.partial(replicated_kernel, len(parts), len(halve...  20.1 us
    ppermute x3, starting transfers between devices, partner(): return lax.ppermute(part, 'gx', [(i, i ^ k) for i in range(count)])  6.62 us
    ppermute x3, waiting for transfers between devices, partner(): return lax.ppermute(part, 'gx', [(i, i ^ k) for i in range(count)])  4.13 us
    ppermute x1, waiting for transfers between devices, replicated(): arrived = lax.ppermute(theirs, 'shot', swap)  3.11 us
    ppermute x1, waiting for transfers between devices, replicated(): crossed, relayed = (lax.ppermute(far, 'shot', swap), partner(far, 1))  2.2 us
    ppermute x7, starting transfers between devices, with_mate(): return [part, lax.ppermute(part, 'gy', swap)]  2.05 us
    ppermute x1, waiting for transfers between devices, replicated(): slanted = with_mate(lax.ppermute(far, ('gx', 'shot'), diagonal))  1.94 us
    unnamed x11, local copies, waits for them, and re-layouts  1.76 us
  transfers between devices with their start and end apart: 14, of which 7 were waited for; matrix products, arithmetic and copies ran while one was open for 0% of the time, Pallas kernels for 3%

profile of v18, /device:TPU:0, one launch (start us, length us, event | category | flops | bytes accessed | tf_op | source)
XLA Modules:
  0.0 53.2 jit_solution(1799422975512075759)
XLA Ops:
  0.6 0.9 %copy-done = f32[8,64,128]{2,1,0:T(8,128)S(1)} copy-done((f32[8,64,128]{2,1,0:T(8,128)S(1)}, f32[8,64,128]{2,1,0:T(8,128)}, u32[]{:S(2)}) %copy-start) | copy-done | bytes 262168
  1.6 0.6 %shard_map.69 = (f32[512,128]{1,0:T(8,128)S(1)}, f32[256,128]{1,0:T(8,128)S(1)}) custom-call(f32[8,64,128]{2,1,0:T(8,128)S(1)} %copy-done), custom_call_target="tpu_custom_call" | custom-call | tf_op jit(solution)/shard_map/pallas_call | solution.py:753
  2.2 0.5 collective-permute-start.1
  2.7 3.7 %collective-permute-start = (f32[256,128]{1,0:T(8,128)S(1)}, f32[256,128]{1,0:T(8,128)S(1)}, u32[]{:S(2)}, u32[]{:S(2)}) collective-permute-start(f32[256,128]{1,0:T(8,128)S(1)} %get-tuple-element.22), channel_id=1, source_target_pairs={{0,8},{4,12},{8,0},{12,4},{1,9},{5,13},{9,1},{13,5},{2,10},{6,14},... | collective-permute-start | bytes 393224 | tf_op jit(solution)/shard_map/ppermute | solution.py:767
  6.4 1.6 %collective-permute-start.2 = (f32[256,128]{1,0:T(8,128)S(1)}, f32[256,128]{1,0:T(8,128)S(1)}, u32[]{:S(2)}, u32[]{:S(2)}) collective-permute-start(f32[256,128]{1,0:T(8,128)S(1)} %get-tuple-element.22), channel_id=1, source_target_pairs={{0,4},{4,0},{8,12},{12,8},{1,5},{5,1},{9,13},{13,9},{2,6},{6,2},{1... | collective-permute-start | bytes 393224 | tf_op jit(solution)/shard_map/ppermute | solution.py:767
  7.9 0.1 copy.7.receivers_ref
  8.1 0.0 copy-start.2
  8.1 0.5 copy-done.3
  8.6 0.2 copy-done.2
  8.8 0.4 shard_map.68
  9.2 4.1 %collective-permute-done.refs_6_ = f32[256,128]{1,0:T(8,128)S(1)} collective-permute-done((f32[256,128]{1,0:T(8,128)S(1)}, f32[256,128]{1,0:T(8,128)S(1)}, u32[]{:S(2)}, u32[]{:S(2)}) %collective-permute-start) | collective-permute-done | bytes 131104 | tf_op jit(solution)/shard_map/ppermute | solution.py:767
  13.4 0.0 collective-permute-done.1.refs_1_
  13.4 1.6 %collective-permute-start.10 = (f32[256,128]{1,0:T(8,128)S(1)}, f32[256,128]{1,0:T(8,128)S(1)}, u32[]{:S(2)}, u32[]{:S(2)}) collective-permute-start(f32[256,128]{1,0:T(8,128)S(1)} %collective-permute-done.refs_6_), channel_id=1, source_target_pairs={{0,5},{1,4},{4,1},{5,0},{8,13},{9,12},{12,9},{13,8},{2,7},{3,6},{6... | collective-permute-start | bytes 393224 | tf_op jit(solution)/shard_map/ppermute | solution.py:798
  14.9 0.0 collective-permute-done.2.refs_2_
  14.9 0.5 %collective-permute-start.4 = (f32[256,128]{1,0:T(8,128)S(1)}, f32[256,128]{1,0:T(8,128)S(1)}, u32[]{:S(2)}, u32[]{:S(2)}) collective-permute-start(f32[256,128]{1,0:T(8,128)S(1)} %collective-permute-done.2.refs_2_), channel_id=1, source_target_pairs={{0,1},{1,0},{2,3},{3,2},{4,5},{5,4},{6,7},{7,6},{8,9},{9,8},{10,11... | collective-permute-start | bytes 393224 | tf_op jit(solution)/shard_map/ppermute | solution.py:796
  15.5 1.4 %collective-permute-start.9 = (f32[256,128]{1,0:T(8,128)S(1)}, f32[256,128]{1,0:T(8,128)S(1)}, u32[]{:S(2)}, u32[]{:S(2)}) collective-permute-start(f32[256,128]{1,0:T(8,128)S(1)} %collective-permute-done.refs_6_), channel_id=1, source_target_pairs={{0,4},{4,0},{8,12},{12,8},{1,5},{5,1},{9,13},{13,9},{2,6},{6,2},{1... | collective-permute-start | bytes 393224 | tf_op jit(solution)/shard_map/ppermute | solution.py:767
  16.9 1.6 %collective-permute-start.7 = (f32[256,128]{1,0:T(8,128)S(1)}, f32[256,128]{1,0:T(8,128)S(1)}, u32[]{:S(2)}, u32[]{:S(2)}) collective-permute-start(f32[256,128]{1,0:T(8,128)S(1)} %collective-permute-done.refs_6_), channel_id=1, source_target_pairs={{0,1},{1,0},{2,3},{3,2},{4,5},{5,4},{6,7},{7,6},{8,9},{9,8},{10,11... | collective-permute-start | bytes 393224 | tf_op jit(solution)/shard_map/ppermute | solution.py:797
  18.4 1.9 %collective-permute-done.10.refs_12_ = f32[256,128]{1,0:T(8,128)S(1)} collective-permute-done((f32[256,128]{1,0:T(8,128)S(1)}, f32[256,128]{1,0:T(8,128)S(1)}, u32[]{:S(2)}, u32[]{:S(2)}) %collective-permute-start.10) | collective-permute-done | bytes 131104 | tf_op jit(solution)/shard_map/ppermute | solution.py:798
  20.4 0.5 collective-permute-start.3
  20.9 1.4 %collective-permute-done.4.refs_4_ = f32[256,128]{1,0:T(8,128)S(1)} collective-permute-done((f32[256,128]{1,0:T(8,128)S(1)}, f32[256,128]{1,0:T(8,128)S(1)}, u32[]{:S(2)}, u32[]{:S(2)}) %collective-permute-start.4) | collective-permute-done | bytes 131104 | tf_op jit(solution)/shard_map/ppermute | solution.py:796
  22.3 0.0 collective-permute-start.6
  22.3 0.5 collective-permute-start.5
  22.8 2.2 %collective-permute-done.7.refs_8_ = f32[256,128]{1,0:T(8,128)S(1)} collective-permute-done((f32[256,128]{1,0:T(8,128)S(1)}, f32[256,128]{1,0:T(8,128)S(1)}, u32[]{:S(2)}, u32[]{:S(2)}) %collective-permute-start.7) | collective-permute-done | bytes 131104 | tf_op jit(solution)/shard_map/ppermute | solution.py:797
  25.0 0.0 collective-permute-start.8
  25.0 0.5 collective-permute-start.12
  25.5 0.8 %collective-permute-done.8.refs_9_ = f32[256,128]{1,0:T(8,128)S(1)} collective-permute-done((f32[256,128]{1,0:T(8,128)S(1)}, f32[256,128]{1,0:T(8,128)S(1)}, u32[]{:S(2)}, u32[]{:S(2)}) %collective-permute-start.8) | collective-permute-done | bytes 131104 | tf_op jit(solution)/shard_map/ppermute | solution.py:770
  26.4 0.2 collective-permute-done.12.refs_11_
  26.6 20.1 %shard_map.70 = (f32[512,128]{1,0:T(8,128)S(1)}, f32[8,32,128]{2,1,0:T(8,128)S(1)}, f32[8,32,128]{2,1,0:T(8,128)S(1)}) custom-call(s32[1,256]{1,0:T(1,128)S(1)} %get-tuple-element.20.cells_ref, f32[512,128]{1,0:T(8,128)S(1)} %get-tuple-element.21.refs_0_, f32[512,128]{1,0:T(8,128)S(1)} %collective-permute-done.1.refs_1_, ...), custom_call_target="tpu_custom_call" | custom-call | flops 200000000 | bytes 4000000 | tf_op jit(solution)/shard_map/pallas_call | solution.py:805
  46.7 1.3 %collective-permute-start.13 = (f32[8,32,128]{2,1,0:T(8,128)S(1)}, f32[8,32,128]{2,1,0:T(8,128)S(1)}, u32[]{:S(2)}, u32[]{:S(2)}) collective-permute-start(f32[8,32,128]{2,1,0:T(8,128)S(1)} %get-tuple-element.37), channel_id=1, source_target_pairs={{0,1},{1,0},{2,3},{3,2},{4,5},{5,4},{6,7},{7,6},{8,9},{9,8},{10,11... | collective-permute-start | bytes 393224 | tf_op jit(solution)/shard_map/ppermute | solution.py:823
  48.0 1.4 %shard_map.71 = f32[8,64,128]{2,1,0:T(8,128)} custom-call(f32[512,128]{1,0:T(8,128)S(1)} %get-tuple-element.35.rows_ref), custom_call_target="tpu_custom_call" | custom-call | flops 50000000 | bytes 500000 | tf_op jit(solution)/shard_map/pallas_call | solution.py:824
  49.4 3.1 %collective-permute-done.13 = f32[8,32,128]{2,1,0:T(8,128)S(1)} collective-permute-done((f32[8,32,128]{2,1,0:T(8,128)S(1)}, f32[8,32,128]{2,1,0:T(8,128)S(1)}, u32[]{:S(2)}, u32[]{:S(2)}) %collective-permute-start.13) | collective-permute-done | bytes 131104 | tf_op jit(solution)/shard_map/ppermute | solution.py:823
  52.5 0.7 %add.3 = f32[8,32,128]{2,1,0:T(8,128)} add(f32[8,32,128]{2,1,0:T(8,128)S(1)} %get-tuple-element.36, f32[8,32,128]{2,1,0:T(8,128)S(1)} %collective-permute-done.13) | non-fusion elementwise | flops 32768 | bytes 393216 | tf_op jit(solution)/shard_map/add | solution.py:832
  (12 shorter events, 0.0 us)
Async XLA Ops:
  0.6 1.0 %copy-start = (f32[8,64,128]{2,1,0:T(8,128)S(1)}, f32[8,64,128]{2,1,0:T(8,128)}, u32[]{:S(2)}) copy-start(f32[8,64,128]{2,1,0:T(8,128)} %natural_ref.1) | copy-start | bytes 786436
  1.6 6.4 %copy-start.4 = (s32[512,2]{0,1:T(2,128)S(1)}, s32[512,2]{0,1:T(2,128)}, u32[]{:S(2)}) copy-start(s32[512,2]{0,1:T(2,128)} %param.8) | copy-start | bytes 12292
  2.2 11.2 %collective-permute-start.1 = (f32[512,128]{1,0:T(8,128)S(1)}, f32[512,128]{1,0:T(8,128)S(1)}, u32[]{:S(2)}, u32[]{:S(2)}) collective-permute-start(f32[512,128]{1,0:T(8,128)S(1)} %get-tuple-element.21.refs_0_), channel_id=1, source_target_pairs={{0,2},{2,0},{1,3},{3,1},{4,6},{6,4},{5,7},{7,5},{8,10},{10,8},{9,1... | collective-permute-start | bytes 786440 | tf_op jit(solution)/shard_map/ppermute | solution.py:770
  2.7 5.4 %copy-start.1 = (f32[1,512]{1,0:T(1,128)S(1)}, f32[1,512]{1,0:T(1,128)}, u32[]{:S(2)}) copy-start(f32[1,512]{1,0:T(1,128)} %observed_ref.1) | copy-start | bytes 6148
  2.7 10.7 %collective-permute-start = (f32[256,128]{1,0:T(8,128)S(1)}, f32[256,128]{1,0:T(8,128)S(1)}, u32[]{:S(2)}, u32[]{:S(2)}) collective-permute-start(f32[256,128]{1,0:T(8,128)S(1)} %get-tuple-element.22), channel_id=1, source_target_pairs={{0,8},{4,12},{8,0},{12,4},{1,9},{5,13},{9,1},{13,5},{2,10},{6,14},... | collective-permute-start | bytes 393224 | tf_op jit(solution)/shard_map/ppermute | solution.py:767
  6.4 8.6 %collective-permute-start.2 = (f32[256,128]{1,0:T(8,128)S(1)}, f32[256,128]{1,0:T(8,128)S(1)}, u32[]{:S(2)}, u32[]{:S(2)}) collective-permute-start(f32[256,128]{1,0:T(8,128)S(1)} %get-tuple-element.22), channel_id=1, source_target_pairs={{0,4},{4,0},{8,12},{12,8},{1,5},{5,1},{9,13},{13,9},{2,6},{6,2},{1... | collective-permute-start | bytes 393224 | tf_op jit(solution)/shard_map/ppermute | solution.py:767
  7.9 0.7 %copy-start.3 = (f32[1,256]{1,0:T(1,128)S(1)}, f32[1,256]{1,0:T(1,128)}, u32[]{:S(2)}) copy-start(f32[1,256]{1,0:T(1,128)} %currents_ref.1) | copy-start | bytes 3076
  8.1 0.7 %copy-start.2 = (s32[256]{0:T(256)S(1)}, s32[256]{0:T(256)}, u32[]{:S(2)}) copy-start(s32[256]{0:T(256)} %param.6) | copy-start | bytes 3076
  13.4 7.0 %collective-permute-start.10 = (f32[256,128]{1,0:T(8,128)S(1)}, f32[256,128]{1,0:T(8,128)S(1)}, u32[]{:S(2)}, u32[]{:S(2)}) collective-permute-start(f32[256,128]{1,0:T(8,128)S(1)} %collective-permute-done.refs_6_), channel_id=1, source_target_pairs={{0,5},{1,4},{4,1},{5,0},{8,13},{9,12},{12,9},{13,8},{2,7},{3,6},{6... | collective-permute-start | bytes 393224 | tf_op jit(solution)/shard_map/ppermute | solution.py:798
  14.9 7.4 %collective-permute-start.4 = (f32[256,128]{1,0:T(8,128)S(1)}, f32[256,128]{1,0:T(8,128)S(1)}, u32[]{:S(2)}, u32[]{:S(2)}) collective-permute-start(f32[256,128]{1,0:T(8,128)S(1)} %collective-permute-done.2.refs_2_), channel_id=1, source_target_pairs={{0,1},{1,0},{2,3},{3,2},{4,5},{5,4},{6,7},{7,6},{8,9},{9,8},{10,11... | collective-permute-start | bytes 393224 | tf_op jit(solution)/shard_map/ppermute | solution.py:796
  15.5 6.8 %collective-permute-start.9 = (f32[256,128]{1,0:T(8,128)S(1)}, f32[256,128]{1,0:T(8,128)S(1)}, u32[]{:S(2)}, u32[]{:S(2)}) collective-permute-start(f32[256,128]{1,0:T(8,128)S(1)} %collective-permute-done.refs_6_), channel_id=1, source_target_pairs={{0,4},{4,0},{8,12},{12,8},{1,5},{5,1},{9,13},{13,9},{2,6},{6,2},{1... | collective-permute-start | bytes 393224 | tf_op jit(solution)/shard_map/ppermute | solution.py:767
  16.9 8.2 %collective-permute-start.7 = (f32[256,128]{1,0:T(8,128)S(1)}, f32[256,128]{1,0:T(8,128)S(1)}, u32[]{:S(2)}, u32[]{:S(2)}) collective-permute-start(f32[256,128]{1,0:T(8,128)S(1)} %collective-permute-done.refs_6_), channel_id=1, source_target_pairs={{0,1},{1,0},{2,3},{3,2},{4,5},{5,4},{6,7},{7,6},{8,9},{9,8},{10,11... | collective-permute-start | bytes 393224 | tf_op jit(solution)/shard_map/ppermute | solution.py:797
  20.4 4.7 %collective-permute-start.11 = (f32[256,128]{1,0:T(8,128)S(1)}, f32[256,128]{1,0:T(8,128)S(1)}, u32[]{:S(2)}, u32[]{:S(2)}) collective-permute-start(f32[256,128]{1,0:T(8,128)S(1)} %collective-permute-done.10.refs_12_), channel_id=1, source_target_pairs={{0,2},{2,0},{1,3},{3,1},{4,6},{6,4},{5,7},{7,5},{8,10},{10,8},{9,1... | collective-permute-start | bytes 393224 | tf_op jit(solution)/shard_map/ppermute | solution.py:770
  20.4 5.2 %collective-permute-start.3 = (f32[256,128]{1,0:T(8,128)S(1)}, f32[256,128]{1,0:T(8,128)S(1)}, u32[]{:S(2)}, u32[]{:S(2)}) collective-permute-start(f32[256,128]{1,0:T(8,128)S(1)} %collective-permute-done.2.refs_2_), channel_id=1, source_target_pairs={{0,2},{2,0},{1,3},{3,1},{4,6},{6,4},{5,7},{7,5},{8,10},{10,8},{9,1... | collective-permute-start | bytes 393224 | tf_op jit(solution)/shard_map/ppermute | solution.py:770
  22.3 3.2 %collective-permute-start.6 = (f32[256,128]{1,0:T(8,128)S(1)}, f32[256,128]{1,0:T(8,128)S(1)}, u32[]{:S(2)}, u32[]{:S(2)}) collective-permute-start(f32[256,128]{1,0:T(8,128)S(1)} %collective-permute-done.refs_6_), channel_id=1, source_target_pairs={{0,2},{2,0},{1,3},{3,1},{4,6},{6,4},{5,7},{7,5},{8,10},{10,8},{9,1... | collective-permute-start | bytes 393224 | tf_op jit(solution)/shard_map/ppermute | solution.py:770
  22.3 3.2 %collective-permute-start.5 = (f32[256,128]{1,0:T(8,128)S(1)}, f32[256,128]{1,0:T(8,128)S(1)}, u32[]{:S(2)}, u32[]{:S(2)}) collective-permute-start(f32[256,128]{1,0:T(8,128)S(1)} %collective-permute-done.4.refs_4_), channel_id=1, source_target_pairs={{0,2},{2,0},{1,3},{3,1},{4,6},{6,4},{5,7},{7,5},{8,10},{10,8},{9,1... | collective-permute-start | bytes 393224 | tf_op jit(solution)/shard_map/ppermute | solution.py:770
  25.0 1.3 %collective-permute-start.8 = (f32[256,128]{1,0:T(8,128)S(1)}, f32[256,128]{1,0:T(8,128)S(1)}, u32[]{:S(2)}, u32[]{:S(2)}) collective-permute-start(f32[256,128]{1,0:T(8,128)S(1)} %collective-permute-done.7.refs_8_), channel_id=1, source_target_pairs={{0,2},{2,0},{1,3},{3,1},{4,6},{6,4},{5,7},{7,5},{8,10},{10,8},{9,1... | collective-permute-start | bytes 393224 | tf_op jit(solution)/shard_map/ppermute | solution.py:770
  25.0 1.5 %collective-permute-start.12 = (f32[256,128]{1,0:T(8,128)S(1)}, f32[256,128]{1,0:T(8,128)S(1)}, u32[]{:S(2)}, u32[]{:S(2)}) collective-permute-start(f32[256,128]{1,0:T(8,128)S(1)} %collective-permute-done.9.refs_10_), channel_id=1, source_target_pairs={{0,2},{2,0},{1,3},{3,1},{4,6},{6,4},{5,7},{7,5},{8,10},{10,8},{9,1... | collective-permute-start | bytes 393224 | tf_op jit(solution)/shard_map/ppermute | solution.py:770
  46.7 5.8 %collective-permute-start.13 = (f32[8,32,128]{2,1,0:T(8,128)S(1)}, f32[8,32,128]{2,1,0:T(8,128)S(1)}, u32[]{:S(2)}, u32[]{:S(2)}) collective-permute-start(f32[8,32,128]{2,1,0:T(8,128)S(1)} %get-tuple-element.37), channel_id=1, source_target_pairs={{0,1},{1,0},{2,3},{3,2},{4,5},{5,4},{6,7},{7,6},{8,9},{9,8},{10,11... | collective-permute-start | bytes 393224 | tf_op jit(solution)/shard_map/ppermute | solution.py:823

commit v19 on v16

--- a/solution.py
+++ b/solution.py
@@ -205,13 +205,13 @@
         x, z = at
         self.ref[pl.ds(self.start(x, z), self.side * SIDE), :] = value.reshape(-1, LANES)
 
-    def put(self, x, z, value, exact=False):
+    def put(self, x, z, value, exact=False, along_z=True):
         self[x, z] = value
         n = self.side
-        if z == 0:
+        if z == 0 and along_z:
             edge = block_up(value, 2)
             self[x, n] = inside_up(edge, 2) if exact else edge
-        if z == n - 1:
+        if z == n - 1 and along_z:
             edge = block_down(value, 2)
             self[x, -1] = inside_down(edge, 2) if exact else edge
         if x == 0:
@@ -308,7 +308,7 @@
                 last_y = jnp.concatenate([before, here[:-1]])
                 total = (next_x + cond[x - 1, z]) + (ahead + cond[x, z - 1]) + (next_y + last_y)
                 total = 6.0 * here + total
-                self.weight[x, z] = DAMPING / total
+                self.weight[x, z] = DAMPING * reciprocal(total)
                 if n == SIDE:
                     self.base[x, z] = jnp.zeros_like(here)
                 self.back[x, z] = total * (0.5 * self.scale / DAMPING)
@@ -363,7 +363,7 @@
                         value = (2.0 - DAMPING) * here[p] + sums[p]
                     else:
                         value = (1.0 - DAMPING) * here[p] + (self.base[x + p, z] + sums[p])
-                    out.put(x + p, z, value, exact)
+                    out.put(x + p, z, value, exact, along_z=not exact)
 
         self.pairs(pair)
 
@@ -410,6 +410,13 @@
 
         self.pairs(pair)
         self.sweep(self.second, out, exact)
+
+
+def reciprocal(value):
+    result = pl.reciprocal(value, approx=True)
+    for _ in range(2):
+        result = result * (2.0 - value * result)
+    return result
 
 
 class HeldLevel:

time: 50.6 us -> 50.3 us (level)
  no operation moved by 1% of the time
where the time goes in v19:
time: 50.3 us; the launch traced here: 50.2 us
  Pallas kernels  22.3 us (44%)
  waiting for transfers between devices  13.3 us (26%)
  starting transfers between devices  11.4 us (23%)
  local copies, waits for them, and re-layouts  1.76 us (3%)
  between operations  0.7 us (1%)
  other arithmetic  0.67 us (1%)
    pallas_call x1, Pallas kernels, replicated(): pl.pallas_call(functools.partial(replicated_kernel, len(parts), len(halve...  19.9 us
    ppermute x3, starting transfers between devices, partner(): return lax.ppermute(part, 'gx', [(i, i ^ k) for i in range(count)])  6.29 us
    ppermute x3, waiting for transfers between devices, partner(): return lax.ppermute(part, 'gx', [(i, i ^ k) for i in range(count)])  5.85 us
    ppermute x1, waiting for transfers between devices, replicated(): arrived = lax.ppermute(theirs, 'shot', swap)  3.17 us
    ppermute x1, waiting for transfers between devices, replicated(): slanted = lax.ppermute(far, ('gx', 'shot'), diagonal)  1.8 us
    unnamed x11, local copies, waits for them, and re-layouts  1.76 us
    ppermute x1, starting transfers between devices, replicated(): crossed, relayed = (lax.ppermute(far, 'shot', swap), partner(far, 1))  1.54 us
    ppermute x1, waiting for transfers between devices, replicated(): crossed, relayed = (lax.ppermute(far, 'shot', swap), partner(far, 1))  1.48 us
  transfers between devices with their start and end apart: 12, of which 7 were waited for; matrix products, arithmetic and copies ran while one was open for 0% of the time, Pallas kernels for 4%

profile of v19, /device:TPU:0, one launch (start us, length us, event | category | flops | bytes accessed | tf_op | source)
XLA Modules:
  0.0 50.2 jit_solution(7601755319799249977)
XLA Ops:
  0.6 0.9 %copy-done = f32[8,64,128]{2,1,0:T(8,128)S(1)} copy-done((f32[8,64,128]{2,1,0:T(8,128)S(1)}, f32[8,64,128]{2,1,0:T(8,128)}, u32[]{:S(2)}) %copy-start) | copy-done | bytes 262168
  1.6 0.6 %shard_map.69 = (f32[512,128]{1,0:T(8,128)S(1)}, f32[256,128]{1,0:T(8,128)S(1)}) custom-call(f32[8,64,128]{2,1,0:T(8,128)S(1)} %copy-done), custom_call_target="tpu_custom_call" | custom-call | tf_op jit(solution)/shard_map/pallas_call | solution.py:760
  2.2 4.1 %collective-permute-start.3 = (f32[256,128]{1,0:T(8,128)S(1)}, f32[256,128]{1,0:T(8,128)S(1)}, u32[]{:S(2)}, u32[]{:S(2)}) collective-permute-start(f32[256,128]{1,0:T(8,128)S(1)} %get-tuple-element.20), channel_id=1, source_target_pairs={{0,8},{4,12},{8,0},{12,4},{1,9},{5,13},{9,1},{13,5},{2,10},{6,14},... | collective-permute-start | bytes 393224 | tf_op jit(solution)/shard_map/ppermute | solution.py:774
  6.3 1.6 %collective-permute-start.1 = (f32[512,128]{1,0:T(8,128)S(1)}, f32[512,128]{1,0:T(8,128)S(1)}, u32[]{:S(2)}, u32[]{:S(2)}) collective-permute-start(f32[512,128]{1,0:T(8,128)S(1)} %get-tuple-element.19.refs_0_), channel_id=1, source_target_pairs={{0,4},{4,0},{8,12},{12,8},{1,5},{5,1},{9,13},{13,9},{2,6},{6,2},{1... | collective-permute-start | bytes 786440 | tf_op jit(solution)/shard_map/ppermute | solution.py:774
  7.9 0.1 copy.7.receivers_ref
  8.0 0.0 copy-start.2
  8.0 0.5 %copy-done.3 = f32[1,256]{1,0:T(1,128)S(1)} copy-done((f32[1,256]{1,0:T(1,128)S(1)}, f32[1,256]{1,0:T(1,128)}, u32[]{:S(2)}) %copy-start.3) | copy-done | bytes 1048
  8.5 0.2 copy-done.2
  8.7 0.4 shard_map.68
  9.1 3.5 %collective-permute-done.3.refs_4_ = f32[256,128]{1,0:T(8,128)S(1)} collective-permute-done((f32[256,128]{1,0:T(8,128)S(1)}, f32[256,128]{1,0:T(8,128)S(1)}, u32[]{:S(2)}, u32[]{:S(2)}) %collective-permute-start.3) | collective-permute-done | bytes 131104 | tf_op jit(solution)/shard_map/ppermute | solution.py:774
  12.7 1.5 %collective-permute-start.5 = (f32[256,128]{1,0:T(8,128)S(1)}, f32[256,128]{1,0:T(8,128)S(1)}, u32[]{:S(2)}, u32[]{:S(2)}) collective-permute-start(f32[256,128]{1,0:T(8,128)S(1)} %collective-permute-done.3.refs_4_), channel_id=1, source_target_pairs={{0,1},{1,0},{2,3},{3,2},{4,5},{5,4},{6,7},{7,6},{8,9},{9,8},{10,11... | collective-permute-start | bytes 393224 | tf_op jit(solution)/shard_map/ppermute | solution.py:801
  14.2 0.6 %collective-permute-start.8 = (f32[256,128]{1,0:T(8,128)S(1)}, f32[256,128]{1,0:T(8,128)S(1)}, u32[]{:S(2)}, u32[]{:S(2)}) collective-permute-start(f32[256,128]{1,0:T(8,128)S(1)} %collective-permute-done.3.refs_4_), channel_id=1, source_target_pairs={{0,4},{4,0},{8,12},{12,8},{1,5},{5,1},{9,13},{13,9},{2,6},{6,2},{1... | collective-permute-start | bytes 393224 | tf_op jit(solution)/shard_map/ppermute | solution.py:774
  14.8 0.0 collective-permute-start
  14.8 1.3 %collective-permute-start.6 = (f32[256,128]{1,0:T(8,128)S(1)}, f32[256,128]{1,0:T(8,128)S(1)}, u32[]{:S(2)}, u32[]{:S(2)}) collective-permute-start(f32[256,128]{1,0:T(8,128)S(1)} %collective-permute-done.3.refs_4_), channel_id=1, source_target_pairs={{0,5},{1,4},{4,1},{5,0},{8,13},{9,12},{12,9},{13,8},{2,7},{3,6},{6... | collective-permute-start | bytes 393224 | tf_op jit(solution)/shard_map/ppermute | solution.py:802
  16.2 1.5 %collective-permute-done.5.refs_6_ = f32[256,128]{1,0:T(8,128)S(1)} collective-permute-done((f32[256,128]{1,0:T(8,128)S(1)}, f32[256,128]{1,0:T(8,128)S(1)}, u32[]{:S(2)}, u32[]{:S(2)}) %collective-permute-start.5) | collective-permute-done | bytes 131104 | tf_op jit(solution)/shard_map/ppermute | solution.py:801
  17.7 0.0 collective-permute-start.7
  17.7 0.0 collective-permute-done.1.refs_2_
  17.7 0.5 %collective-permute-start.2 = (f32[512,128]{1,0:T(8,128)S(1)}, f32[512,128]{1,0:T(8,128)S(1)}, u32[]{:S(2)}, u32[]{:S(2)}) collective-permute-start(f32[512,128]{1,0:T(8,128)S(1)} %collective-permute-done.1.refs_2_), channel_id=1, source_target_pairs={{0,2},{2,0},{1,3},{3,1},{4,6},{6,4},{5,7},{7,5},{8,10},{10,8},{9,1... | collective-permute-start | bytes 786440 | tf_op jit(solution)/shard_map/ppermute | solution.py:777
  18.2 2.3 %collective-permute-done.8.refs_8_ = f32[256,128]{1,0:T(8,128)S(1)} collective-permute-done((f32[256,128]{1,0:T(8,128)S(1)}, f32[256,128]{1,0:T(8,128)S(1)}, u32[]{:S(2)}, u32[]{:S(2)}) %collective-permute-start.8) | collective-permute-done | bytes 131104 | tf_op jit(solution)/shard_map/ppermute | solution.py:774
  20.5 0.0 collective-permute-start.4
  20.5 1.8 %collective-permute-done.6.refs_10_ = f32[256,128]{1,0:T(8,128)S(1)} collective-permute-done((f32[256,128]{1,0:T(8,128)S(1)}, f32[256,128]{1,0:T(8,128)S(1)}, u32[]{:S(2)}, u32[]{:S(2)}) %collective-permute-start.6) | collective-permute-done | bytes 131104 | tf_op jit(solution)/shard_map/ppermute | solution.py:802
  22.3 0.0 collective-permute-start.9
  22.3 0.0 collective-permute-done.7.refs_7_
  22.3 0.5 %collective-permute-start.10 = (f32[256,128]{1,0:T(8,128)S(1)}, f32[256,128]{1,0:T(8,128)S(1)}, u32[]{:S(2)}, u32[]{:S(2)}) collective-permute-start(f32[256,128]{1,0:T(8,128)S(1)} %collective-permute-done.6.refs_10_), channel_id=1, source_target_pairs={{0,2},{2,0},{1,3},{3,1},{4,6},{6,4},{5,7},{7,5},{8,10},{10,8},{9,1... | collective-permute-start | bytes 393224 | tf_op jit(solution)/shard_map/ppermute | solution.py:777
  22.8 0.8 %collective-permute-done.9.refs_9_ = f32[256,128]{1,0:T(8,128)S(1)} collective-permute-done((f32[256,128]{1,0:T(8,128)S(1)}, f32[256,128]{1,0:T(8,128)S(1)}, u32[]{:S(2)}, u32[]{:S(2)}) %collective-permute-start.9) | collective-permute-done | bytes 131104 | tf_op jit(solution)/shard_map/ppermute | solution.py:777
  23.6 0.0 collective-permute-done.2.refs_3_
  23.6 0.2 collective-permute-done.10.refs_11_
  23.8 19.9 %shard_map.70 = (f32[512,128]{1,0:T(8,128)S(1)}, f32[8,32,128]{2,1,0:T(8,128)S(1)}, f32[8,32,128]{2,1,0:T(8,128)S(1)}) custom-call(s32[1,256]{1,0:T(1,128)S(1)} %get-tuple-element.18.cells_ref, f32[512,128]{1,0:T(8,128)S(1)} %get-tuple-element.19.refs_0_, f32[512,128]{1,0:T(8,128)S(1)} %collective-permute-done.refs_1_, ...), custom_call_target="tpu_custom_call" | custom-call | flops 200000000 | bytes 4000000 | tf_op jit(solution)/shard_map/pallas_call | solution.py:810
  43.7 1.3 %collective-permute-start.11 = (f32[8,32,128]{2,1,0:T(8,128)S(1)}, f32[8,32,128]{2,1,0:T(8,128)S(1)}, u32[]{:S(2)}, u32[]{:S(2)}) collective-permute-start(f32[8,32,128]{2,1,0:T(8,128)S(1)} %get-tuple-element.33), channel_id=1, source_target_pairs={{0,1},{1,0},{2,3},{3,2},{4,5},{5,4},{6,7},{7,6},{8,9},{9,8},{10,11... | collective-permute-start | bytes 393224 | tf_op jit(solution)/shard_map/ppermute | solution.py:828
  44.9 1.4 %shard_map.71 = f32[8,64,128]{2,1,0:T(8,128)} custom-call(f32[512,128]{1,0:T(8,128)S(1)} %get-tuple-element.31.rows_ref), custom_call_target="tpu_custom_call" | custom-call | flops 50000000 | bytes 500000 | tf_op jit(solution)/shard_map/pallas_call | solution.py:829
  46.3 3.2 %collective-permute-done.11 = f32[8,32,128]{2,1,0:T(8,128)S(1)} collective-permute-done((f32[8,32,128]{2,1,0:T(8,128)S(1)}, f32[8,32,128]{2,1,0:T(8,128)S(1)}, u32[]{:S(2)}, u32[]{:S(2)}) %collective-permute-start.11) | collective-permute-done | bytes 131104 | tf_op jit(solution)/shard_map/ppermute | solution.py:828
  49.5 0.7 %add.3 = f32[8,32,128]{2,1,0:T(8,128)} add(f32[8,32,128]{2,1,0:T(8,128)S(1)} %get-tuple-element.32, f32[8,32,128]{2,1,0:T(8,128)S(1)} %collective-permute-done.11) | non-fusion elementwise | flops 32768 | bytes 393216 | tf_op jit(solution)/shard_map/add | solution.py:837
  (8 shorter events, 0.0 us)
Async XLA Ops:
  0.6 1.0 %copy-start = (f32[8,64,128]{2,1,0:T(8,128)S(1)}, f32[8,64,128]{2,1,0:T(8,128)}, u32[]{:S(2)}) copy-start(f32[8,64,128]{2,1,0:T(8,128)} %natural_ref.1) | copy-start | bytes 786436
  1.6 6.3 %copy-start.4 = (s32[512,2]{0,1:T(2,128)S(1)}, s32[512,2]{0,1:T(2,128)}, u32[]{:S(2)}) copy-start(s32[512,2]{0,1:T(2,128)} %param.8) | copy-start | bytes 12292
  2.2 10.5 %collective-permute-start.3 = (f32[256,128]{1,0:T(8,128)S(1)}, f32[256,128]{1,0:T(8,128)S(1)}, u32[]{:S(2)}, u32[]{:S(2)}) collective-permute-start(f32[256,128]{1,0:T(8,128)S(1)} %get-tuple-element.20), channel_id=1, source_target_pairs={{0,8},{4,12},{8,0},{12,4},{1,9},{5,13},{9,1},{13,5},{2,10},{6,14},... | collective-permute-start | bytes 393224 | tf_op jit(solution)/shard_map/ppermute | solution.py:774
  6.3 1.7 %copy-start.1 = (f32[1,512]{1,0:T(1,128)S(1)}, f32[1,512]{1,0:T(1,128)}, u32[]{:S(2)}) copy-start(f32[1,512]{1,0:T(1,128)} %observed_ref.1) | copy-start | bytes 6148
  6.3 11.4 %collective-permute-start.1 = (f32[512,128]{1,0:T(8,128)S(1)}, f32[512,128]{1,0:T(8,128)S(1)}, u32[]{:S(2)}, u32[]{:S(2)}) collective-permute-start(f32[512,128]{1,0:T(8,128)S(1)} %get-tuple-element.19.refs_0_), channel_id=1, source_target_pairs={{0,4},{4,0},{8,12},{12,8},{1,5},{5,1},{9,13},{13,9},{2,6},{6,2},{1... | collective-permute-start | bytes 786440 | tf_op jit(solution)/shard_map/ppermute | solution.py:774
  7.9 0.7 %copy-start.3 = (f32[1,256]{1,0:T(1,128)S(1)}, f32[1,256]{1,0:T(1,128)}, u32[]{:S(2)}) copy-start(f32[1,256]{1,0:T(1,128)} %currents_ref.1) | copy-start | bytes 3076
  8.0 0.7 %copy-start.2 = (s32[256]{0:T(256)S(1)}, s32[256]{0:T(256)}, u32[]{:S(2)}) copy-start(s32[256]{0:T(256)} %param.6) | copy-start | bytes 3076
  12.7 5.0 %collective-permute-start.5 = (f32[256,128]{1,0:T(8,128)S(1)}, f32[256,128]{1,0:T(8,128)S(1)}, u32[]{:S(2)}, u32[]{:S(2)}) collective-permute-start(f32[256,128]{1,0:T(8,128)S(1)} %collective-permute-done.3.refs_4_), channel_id=1, source_target_pairs={{0,1},{1,0},{2,3},{3,2},{4,5},{5,4},{6,7},{7,6},{8,9},{9,8},{10,11... | collective-permute-start | bytes 393224 | tf_op jit(solution)/shard_map/ppermute | solution.py:801
  14.2 6.2 %collective-permute-start.8 = (f32[256,128]{1,0:T(8,128)S(1)}, f32[256,128]{1,0:T(8,128)S(1)}, u32[]{:S(2)}, u32[]{:S(2)}) collective-permute-start(f32[256,128]{1,0:T(8,128)S(1)} %collective-permute-done.3.refs_4_), channel_id=1, source_target_pairs={{0,4},{4,0},{8,12},{12,8},{1,5},{5,1},{9,13},{13,9},{2,6},{6,2},{1... | collective-permute-start | bytes 393224 | tf_op jit(solution)/shard_map/ppermute | solution.py:774
  14.8 8.0 %collective-permute-start = (f32[512,128]{1,0:T(8,128)S(1)}, f32[512,128]{1,0:T(8,128)S(1)}, u32[]{:S(2)}, u32[]{:S(2)}) collective-permute-start(f32[512,128]{1,0:T(8,128)S(1)} %get-tuple-element.19.refs_0_), channel_id=1, source_target_pairs={{0,2},{2,0},{1,3},{3,1},{4,6},{6,4},{5,7},{7,5},{8,10},{10,8},{9,1... | collective-permute-start | bytes 786440 | tf_op jit(solution)/shard_map/ppermute | solution.py:777
  14.8 7.4 %collective-permute-start.6 = (f32[256,128]{1,0:T(8,128)S(1)}, f32[256,128]{1,0:T(8,128)S(1)}, u32[]{:S(2)}, u32[]{:S(2)}) collective-permute-start(f32[256,128]{1,0:T(8,128)S(1)} %collective-permute-done.3.refs_4_), channel_id=1, source_target_pairs={{0,5},{1,4},{4,1},{5,0},{8,13},{9,12},{12,9},{13,8},{2,7},{3,6},{6... | collective-permute-start | bytes 393224 | tf_op jit(solution)/shard_map/ppermute | solution.py:802
  17.7 4.6 %collective-permute-start.7 = (f32[256,128]{1,0:T(8,128)S(1)}, f32[256,128]{1,0:T(8,128)S(1)}, u32[]{:S(2)}, u32[]{:S(2)}) collective-permute-start(f32[256,128]{1,0:T(8,128)S(1)} %collective-permute-done.5.refs_6_), channel_id=1, source_target_pairs={{0,2},{2,0},{1,3},{3,1},{4,6},{6,4},{5,7},{7,5},{8,10},{10,8},{9,1... | collective-permute-start | bytes 393224 | tf_op jit(solution)/shard_map/ppermute | solution.py:777
  17.7 6.0 %collective-permute-start.2 = (f32[512,128]{1,0:T(8,128)S(1)}, f32[512,128]{1,0:T(8,128)S(1)}, u32[]{:S(2)}, u32[]{:S(2)}) collective-permute-start(f32[512,128]{1,0:T(8,128)S(1)} %collective-permute-done.1.refs_2_), channel_id=1, source_target_pairs={{0,2},{2,0},{1,3},{3,1},{4,6},{6,4},{5,7},{7,5},{8,10},{10,8},{9,1... | collective-permute-start | bytes 786440 | tf_op jit(solution)/shard_map/ppermute | solution.py:777
  20.5 2.3 %collective-permute-start.4 = (f32[256,128]{1,0:T(8,128)S(1)}, f32[256,128]{1,0:T(8,128)S(1)}, u32[]{:S(2)}, u32[]{:S(2)}) collective-permute-start(f32[256,128]{1,0:T(8,128)S(1)} %collective-permute-done.3.refs_4_), channel_id=1, source_target_pairs={{0,2},{2,0},{1,3},{3,1},{4,6},{6,4},{5,7},{7,5},{8,10},{10,8},{9,1... | collective-permute-start | bytes 393224 | tf_op jit(solution)/shard_map/ppermute | solution.py:777
  22.3 1.3 %collective-permute-start.9 = (f32[256,128]{1,0:T(8,128)S(1)}, f32[256,128]{1,0:T(8,128)S(1)}, u32[]{:S(2)}, u32[]{:S(2)}) collective-permute-start(f32[256,128]{1,0:T(8,128)S(1)} %collective-permute-done.8.refs_8_), channel_id=1, source_target_pairs={{0,2},{2,0},{1,3},{3,1},{4,6},{6,4},{5,7},{7,5},{8,10},{10,8},{9,1... | collective-permute-start | bytes 393224 | tf_op jit(solution)/shard_map/ppermute | solution.py:777
  22.3 1.5 %collective-permute-start.10 = (f32[256,128]{1,0:T(8,128)S(1)}, f32[256,128]{1,0:T(8,128)S(1)}, u32[]{:S(2)}, u32[]{:S(2)}) collective-permute-start(f32[256,128]{1,0:T(8,128)S(1)} %collective-permute-done.6.refs_10_), channel_id=1, source_target_pairs={{0,2},{2,0},{1,3},{3,1},{4,6},{6,4},{5,7},{7,5},{8,10},{10,8},{9,1... | collective-permute-start | bytes 393224 | tf_op jit(solution)/shard_map/ppermute | solution.py:777
  43.7 5.8 %collective-permute-start.11 = (f32[8,32,128]{2,1,0:T(8,128)S(1)}, f32[8,32,128]{2,1,0:T(8,128)S(1)}, u32[]{:S(2)}, u32[]{:S(2)}) collective-permute-start(f32[8,32,128]{2,1,0:T(8,128)S(1)} %get-tuple-element.33), channel_id=1, source_target_pairs={{0,1},{1,0},{2,3},{3,2},{4,5},{5,4},{6,7},{7,6},{8,9},{9,8},{10,11... | collective-permute-start | bytes 393224 | tf_op jit(solution)/shard_map/ppermute | solution.py:828

commit v20 on v19

--- a/solution.py
+++ b/solution.py
@@ -584,63 +584,36 @@
             coarse,
         )
 
-    keep = iota((1, SIDE, LANES), 1) % 2 == 0
-    lane = iota((1, SIDE, LANES), 2)
-
-    def split(value):
-        return [jnp.where(keep, part, 0.0) for part in (value, pltpu.roll(value, SIDE - 1, 1))]
-
-    def around(value):
-        low, high = value
-        low_up, high_up = [pltpu.roll(part, LANES - GROUP, 2) for part in value]
-        low_down, high_down = [pltpu.roll(part, GROUP, 2) for part in value]
-        along = [[move(part, axis) for part in value] for axis in (0, 2) for move in (block_up, block_down)]
-        return along + [
-            [jnp.where(lane < LANES - GROUP, low_up, high_up), high_up],
-            [low_down, jnp.where(lane >= GROUP, high_down, low_down)],
-        ]
-
-    sub = iota((1, SIDE, LANES), 1)
-    inside_last = [
-        [sub < 6] * 2,
-        [sub >= 2] * 2,
-        [lane % GROUP < GROUP - 1] * 2,
-        [lane % GROUP > 0] * 2,
-        [keep, lane < LANES - GROUP],
-        [lane >= GROUP, keep],
+    here = coarsest[0]
+    moves = [(axis, up) for axis in range(3) for up in (True, False)]
+
+    def moved(value, axis, up):
+        return block_up(value, axis) if up else block_down(value, axis)
+
+    def inside(value, axis, up):
+        return inside_up(value, axis) if up else inside_down(value, axis)
+
+    others = [inside(moved(here, axis, up), axis, up) for axis, up in moves]
+    total = 6.0 * here
+    for other in others:
+        total = total + other
+    inverse = DAMPING / total
+    last_weight = inverse * (2.0 / 0.25 ** (LEVELS - 1))
+    last_links = [
+        inside(inverse * (here + other), axis, up) for other, (axis, up) in zip(others, moves)
     ]
-    last_scale = 0.25 ** (LEVELS - 1)
-    here = split(coarsest[0])
-    others = [
-        [jnp.where(inside & keep, part, 0.0) for inside, part in zip(pair, moved)]
-        for pair, moved in zip(inside_last, around(here))
-    ]
-    last_weight, last_links = [], []
-    for half, part in enumerate(here):
-        total = 3.0 * part
-        for other in others:
-            total = total + 0.5 * other[half]
-        inverse = jnp.where(keep, DAMPING / jnp.where(keep, total, 1.0), 0.0)
-        last_weight.append(inverse * (1.0 / last_scale))
-        last_links.append(
-            [
-                jnp.where(pair[half] & keep, 0.5 * inverse * (part + other[half]), 0.0)
-                for pair, other in zip(inside_last, others)
-            ]
-        )
 
     def solve_last(rhs):
-        base = [weight * part for weight, part in zip(last_weight, split(rhs))]
+        base = last_weight * rhs
         value = base
         for _ in range(COARSE_SWEEPS - 1):
-            moved = around(value)
-            fresh = []
-            for half in range(2):
-                parts = [link * other[half] for link, other in zip(last_links[half], moved)]
-                start = base[half] + (1.0 - DAMPING) * value[half]
-                fresh.append(((start + parts[0]) + (parts[1] + parts[2])) + (parts[3] + (parts[4] + parts[5])))
-            value = fresh
-        return value[0] + pltpu.roll(value[1], 1, 1)
+            parts = [
+                link * moved(value, axis, up) for link, (axis, up) in zip(last_links, moves)
+            ]
+            start = base + (1.0 - DAMPING) * value
+            value = ((start + parts[0]) + (parts[1] + parts[4])) + parts[5]
+            value = value + (parts[2] + parts[3])
+        return value
 
     def cycle(index, out, exact=False):
         level = levels[index]

time: 50.3 us -> 50.3 us (level)
  no operation moved by 1% of the time
where the time goes in v20:
time: 50.3 us; the launch traced here: 50.1 us
  Pallas kernels  22.2 us (44%)
  waiting for transfers between devices  13.3 us (26%)
  starting transfers between devices  11.4 us (23%)
  local copies, waits for them, and re-layouts  1.76 us (3%)
  between operations  0.7 us (1%)
  other arithmetic  0.67 us (1%)
    pallas_call x1, Pallas kernels, replicated(): pl.pallas_call(functools.partial(replicated_kernel, len(parts), len(halve...  19.8 us
    ppermute x3, starting transfers between devices, partner(): return lax.ppermute(part, 'gx', [(i, i ^ k) for i in range(count)])  6.29 us
    ppermute x3, waiting for transfers between devices, partner(): return lax.ppermute(part, 'gx', [(i, i ^ k) for i in range(count)])  5.85 us
    ppermute x1, waiting for transfers between devices, replicated(): arrived = lax.ppermute(theirs, 'shot', swap)  3.17 us
    ppermute x1, waiting for transfers between devices, replicated(): slanted = lax.ppermute(far, ('gx', 'shot'), diagonal)  1.8 us
    unnamed x11, local copies, waits for them, and re-layouts  1.76 us
    ppermute x1, starting transfers between devices, replicated(): crossed, relayed = (lax.ppermute(far, 'shot', swap), partner(far, 1))  1.54 us
    ppermute x1, waiting for transfers between devices, replicated(): crossed, relayed = (lax.ppermute(far, 'shot', swap), partner(far, 1))  1.48 us
  transfers between devices with their start and end apart: 12, of which 7 were waited for; matrix products, arithmetic and copies ran while one was open for 0% of the time, Pallas kernels for 4%

profile of v20, /device:TPU:0, one launch (start us, length us, event | category | flops | bytes accessed | tf_op | source)
XLA Modules:
  0.0 50.1 jit_solution(14901281097406905018)
XLA Ops:
  0.6 0.9 %copy-done = f32[8,64,128]{2,1,0:T(8,128)S(1)} copy-done((f32[8,64,128]{2,1,0:T(8,128)S(1)}, f32[8,64,128]{2,1,0:T(8,128)}, u32[]{:S(2)}) %copy-start) | copy-done | bytes 262168
  1.6 0.6 %shard_map.69 = (f32[512,128]{1,0:T(8,128)S(1)}, f32[256,128]{1,0:T(8,128)S(1)}) custom-call(f32[8,64,128]{2,1,0:T(8,128)S(1)} %copy-done), custom_call_target="tpu_custom_call" | custom-call | tf_op jit(solution)/shard_map/pallas_call | solution.py:733
  2.2 4.1 %collective-permute-start.3 = (f32[256,128]{1,0:T(8,128)S(1)}, f32[256,128]{1,0:T(8,128)S(1)}, u32[]{:S(2)}, u32[]{:S(2)}) collective-permute-start(f32[256,128]{1,0:T(8,128)S(1)} %get-tuple-element.20), channel_id=1, source_target_pairs={{0,8},{4,12},{8,0},{12,4},{1,9},{5,13},{9,1},{13,5},{2,10},{6,14},... | collective-permute-start | bytes 393224 | tf_op jit(solution)/shard_map/ppermute | solution.py:747
  6.3 1.6 %collective-permute-start.1 = (f32[512,128]{1,0:T(8,128)S(1)}, f32[512,128]{1,0:T(8,128)S(1)}, u32[]{:S(2)}, u32[]{:S(2)}) collective-permute-start(f32[512,128]{1,0:T(8,128)S(1)} %get-tuple-element.19.refs_0_), channel_id=1, source_target_pairs={{0,4},{4,0},{8,12},{12,8},{1,5},{5,1},{9,13},{13,9},{2,6},{6,2},{1... | collective-permute-start | bytes 786440 | tf_op jit(solution)/shard_map/ppermute | solution.py:747
  7.9 0.1 copy.7.receivers_ref
  8.0 0.0 copy-start.2
  8.0 0.5 %copy-done.3 = f32[1,256]{1,0:T(1,128)S(1)} copy-done((f32[1,256]{1,0:T(1,128)S(1)}, f32[1,256]{1,0:T(1,128)}, u32[]{:S(2)}) %copy-start.3) | copy-done | bytes 1048
  8.5 0.2 copy-done.2
  8.7 0.4 shard_map.68
  9.1 3.5 %collective-permute-done.3.refs_4_ = f32[256,128]{1,0:T(8,128)S(1)} collective-permute-done((f32[256,128]{1,0:T(8,128)S(1)}, f32[256,128]{1,0:T(8,128)S(1)}, u32[]{:S(2)}, u32[]{:S(2)}) %collective-permute-start.3) | collective-permute-done | bytes 131104 | tf_op jit(solution)/shard_map/ppermute | solution.py:747
  12.7 1.5 %collective-permute-start.5 = (f32[256,128]{1,0:T(8,128)S(1)}, f32[256,128]{1,0:T(8,128)S(1)}, u32[]{:S(2)}, u32[]{:S(2)}) collective-permute-start(f32[256,128]{1,0:T(8,128)S(1)} %collective-permute-done.3.refs_4_), channel_id=1, source_target_pairs={{0,1},{1,0},{2,3},{3,2},{4,5},{5,4},{6,7},{7,6},{8,9},{9,8},{10,11... | collective-permute-start | bytes 393224 | tf_op jit(solution)/shard_map/ppermute | solution.py:774
  14.2 0.6 %collective-permute-start.8 = (f32[256,128]{1,0:T(8,128)S(1)}, f32[256,128]{1,0:T(8,128)S(1)}, u32[]{:S(2)}, u32[]{:S(2)}) collective-permute-start(f32[256,128]{1,0:T(8,128)S(1)} %collective-permute-done.3.refs_4_), channel_id=1, source_target_pairs={{0,4},{4,0},{8,12},{12,8},{1,5},{5,1},{9,13},{13,9},{2,6},{6,2},{1... | collective-permute-start | bytes 393224 | tf_op jit(solution)/shard_map/ppermute | solution.py:747
  14.8 0.0 collective-permute-start
  14.8 1.3 %collective-permute-start.6 = (f32[256,128]{1,0:T(8,128)S(1)}, f32[256,128]{1,0:T(8,128)S(1)}, u32[]{:S(2)}, u32[]{:S(2)}) collective-permute-start(f32[256,128]{1,0:T(8,128)S(1)} %collective-permute-done.3.refs_4_), channel_id=1, source_target_pairs={{0,5},{1,4},{4,1},{5,0},{8,13},{9,12},{12,9},{13,8},{2,7},{3,6},{6... | collective-permute-start | bytes 393224 | tf_op jit(solution)/shard_map/ppermute | solution.py:775
  16.2 1.5 %collective-permute-done.5.refs_6_ = f32[256,128]{1,0:T(8,128)S(1)} collective-permute-done((f32[256,128]{1,0:T(8,128)S(1)}, f32[256,128]{1,0:T(8,128)S(1)}, u32[]{:S(2)}, u32[]{:S(2)}) %collective-permute-start.5) | collective-permute-done | bytes 131104 | tf_op jit(solution)/shard_map/ppermute | solution.py:774
  17.7 0.0 collective-permute-start.7
  17.7 0.5 %collective-permute-start.2 = (f32[512,128]{1,0:T(8,128)S(1)}, f32[512,128]{1,0:T(8,128)S(1)}, u32[]{:S(2)}, u32[]{:S(2)}) collective-permute-start(f32[512,128]{1,0:T(8,128)S(1)} %collective-permute-done.1.refs_2_), channel_id=1, source_target_pairs={{0,2},{2,0},{1,3},{3,1},{4,6},{6,4},{5,7},{7,5},{8,10},{10,8},{9,1... | collective-permute-start | bytes 786440 | tf_op jit(solution)/shard_map/ppermute | solution.py:750
  18.2 2.3 %collective-permute-done.8.refs_8_ = f32[256,128]{1,0:T(8,128)S(1)} collective-permute-done((f32[256,128]{1,0:T(8,128)S(1)}, f32[256,128]{1,0:T(8,128)S(1)}, u32[]{:S(2)}, u32[]{:S(2)}) %collective-permute-start.8) | collective-permute-done | bytes 131104 | tf_op jit(solution)/shard_map/ppermute | solution.py:747
  20.5 0.0 collective-permute-start.4
  20.5 1.8 %collective-permute-done.6.refs_10_ = f32[256,128]{1,0:T(8,128)S(1)} collective-permute-done((f32[256,128]{1,0:T(8,128)S(1)}, f32[256,128]{1,0:T(8,128)S(1)}, u32[]{:S(2)}, u32[]{:S(2)}) %collective-permute-start.6) | collective-permute-done | bytes 131104 | tf_op jit(solution)/shard_map/ppermute | solution.py:775
  22.3 0.0 collective-permute-start.9
  22.3 0.0 collective-permute-done.7.refs_7_
  22.3 0.5 %collective-permute-start.10 = (f32[256,128]{1,0:T(8,128)S(1)}, f32[256,128]{1,0:T(8,128)S(1)}, u32[]{:S(2)}, u32[]{:S(2)}) collective-permute-start(f32[256,128]{1,0:T(8,128)S(1)} %collective-permute-done.6.refs_10_), channel_id=1, source_target_pairs={{0,2},{2,0},{1,3},{3,1},{4,6},{6,4},{5,7},{7,5},{8,10},{10,8},{9,1... | collective-permute-start | bytes 393224 | tf_op jit(solution)/shard_map/ppermute | solution.py:750
  22.8 0.0 collective-permute-done.refs_1_
  22.8 0.0 collective-permute-done.4.refs_5_
  22.8 0.8 %collective-permute-done.9.refs_9_ = f32[256,128]{1,0:T(8,128)S(1)} collective-permute-done((f32[256,128]{1,0:T(8,128)S(1)}, f32[256,128]{1,0:T(8,128)S(1)}, u32[]{:S(2)}, u32[]{:S(2)}) %collective-permute-start.9) | collective-permute-done | bytes 131104 | tf_op jit(solution)/shard_map/ppermute | solution.py:750
  23.6 0.2 collective-permute-done.10.refs_11_
  23.8 19.8 %shard_map.70 = (f32[512,128]{1,0:T(8,128)S(1)}, f32[8,32,128]{2,1,0:T(8,128)S(1)}, f32[8,32,128]{2,1,0:T(8,128)S(1)}) custom-call(s32[1,256]{1,0:T(1,128)S(1)} %get-tuple-element.18.cells_ref, f32[512,128]{1,0:T(8,128)S(1)} %get-tuple-element.19.refs_0_, f32[512,128]{1,0:T(8,128)S(1)} %collective-permute-done.refs_1_, ...), custom_call_target="tpu_custom_call" | custom-call | flops 200000000 | bytes 4000000 | tf_op jit(solution)/shard_map/pallas_call | solution.py:783
  43.6 1.3 %collective-permute-start.11 = (f32[8,32,128]{2,1,0:T(8,128)S(1)}, f32[8,32,128]{2,1,0:T(8,128)S(1)}, u32[]{:S(2)}, u32[]{:S(2)}) collective-permute-start(f32[8,32,128]{2,1,0:T(8,128)S(1)} %get-tuple-element.33), channel_id=1, source_target_pairs={{0,1},{1,0},{2,3},{3,2},{4,5},{5,4},{6,7},{7,6},{8,9},{9,8},{10,11... | collective-permute-start | bytes 393224 | tf_op jit(solution)/shard_map/ppermute | solution.py:801
  44.9 1.4 %shard_map.71 = f32[8,64,128]{2,1,0:T(8,128)} custom-call(f32[512,128]{1,0:T(8,128)S(1)} %get-tuple-element.31.rows_ref), custom_call_target="tpu_custom_call" | custom-call | flops 50000000 | bytes 500000 | tf_op jit(solution)/shard_map/pallas_call | solution.py:802
  46.3 3.2 %collective-permute-done.11 = f32[8,32,128]{2,1,0:T(8,128)S(1)} collective-permute-done((f32[8,32,128]{2,1,0:T(8,128)S(1)}, f32[8,32,128]{2,1,0:T(8,128)S(1)}, u32[]{:S(2)}, u32[]{:S(2)}) %collective-permute-start.11) | collective-permute-done | bytes 131104 | tf_op jit(solution)/shard_map/ppermute | solution.py:801
  49.4 0.7 %add.3 = f32[8,32,128]{2,1,0:T(8,128)} add(f32[8,32,128]{2,1,0:T(8,128)S(1)} %get-tuple-element.32, f32[8,32,128]{2,1,0:T(8,128)S(1)} %collective-permute-done.11) | non-fusion elementwise | flops 32768 | bytes 393216 | tf_op jit(solution)/shard_map/add | solution.py:810
  (8 shorter events, 0.0 us)
Async XLA Ops:
  0.6 1.0 %copy-start = (f32[8,64,128]{2,1,0:T(8,128)S(1)}, f32[8,64,128]{2,1,0:T(8,128)}, u32[]{:S(2)}) copy-start(f32[8,64,128]{2,1,0:T(8,128)} %natural_ref.1) | copy-start | bytes 786436
  1.6 6.3 %copy-start.4 = (s32[512,2]{0,1:T(2,128)S(1)}, s32[512,2]{0,1:T(2,128)}, u32[]{:S(2)}) copy-start(s32[512,2]{0,1:T(2,128)} %param.8) | copy-start | bytes 12292
  2.2 10.5 %collective-permute-start.3 = (f32[256,128]{1,0:T(8,128)S(1)}, f32[256,128]{1,0:T(8,128)S(1)}, u32[]{:S(2)}, u32[]{:S(2)}) collective-permute-start(f32[256,128]{1,0:T(8,128)S(1)} %get-tuple-element.20), channel_id=1, source_target_pairs={{0,8},{4,12},{8,0},{12,4},{1,9},{5,13},{9,1},{13,5},{2,10},{6,14},... | collective-permute-start | bytes 393224 | tf_op jit(solution)/shard_map/ppermute | solution.py:747
  6.3 1.7 %copy-start.1 = (f32[1,512]{1,0:T(1,128)S(1)}, f32[1,512]{1,0:T(1,128)}, u32[]{:S(2)}) copy-start(f32[1,512]{1,0:T(1,128)} %observed_ref.1) | copy-start | bytes 6148
  6.3 11.4 %collective-permute-start.1 = (f32[512,128]{1,0:T(8,128)S(1)}, f32[512,128]{1,0:T(8,128)S(1)}, u32[]{:S(2)}, u32[]{:S(2)}) collective-permute-start(f32[512,128]{1,0:T(8,128)S(1)} %get-tuple-element.19.refs_0_), channel_id=1, source_target_pairs={{0,4},{4,0},{8,12},{12,8},{1,5},{5,1},{9,13},{13,9},{2,6},{6,2},{1... | collective-permute-start | bytes 786440 | tf_op jit(solution)/shard_map/ppermute | solution.py:747
  7.9 0.7 %copy-start.3 = (f32[1,256]{1,0:T(1,128)S(1)}, f32[1,256]{1,0:T(1,128)}, u32[]{:S(2)}) copy-start(f32[1,256]{1,0:T(1,128)} %currents_ref.1) | copy-start | bytes 3076
  8.0 0.7 %copy-start.2 = (s32[256]{0:T(256)S(1)}, s32[256]{0:T(256)}, u32[]{:S(2)}) copy-start(s32[256]{0:T(256)} %param.6) | copy-start | bytes 3076
  12.7 5.0 %collective-permute-start.5 = (f32[256,128]{1,0:T(8,128)S(1)}, f32[256,128]{1,0:T(8,128)S(1)}, u32[]{:S(2)}, u32[]{:S(2)}) collective-permute-start(f32[256,128]{1,0:T(8,128)S(1)} %collective-permute-done.3.refs_4_), channel_id=1, source_target_pairs={{0,1},{1,0},{2,3},{3,2},{4,5},{5,4},{6,7},{7,6},{8,9},{9,8},{10,11... | collective-permute-start | bytes 393224 | tf_op jit(solution)/shard_map/ppermute | solution.py:774
  14.2 6.2 %collective-permute-start.8 = (f32[256,128]{1,0:T(8,128)S(1)}, f32[256,128]{1,0:T(8,128)S(1)}, u32[]{:S(2)}, u32[]{:S(2)}) collective-permute-start(f32[256,128]{1,0:T(8,128)S(1)} %collective-permute-done.3.refs_4_), channel_id=1, source_target_pairs={{0,4},{4,0},{8,12},{12,8},{1,5},{5,1},{9,13},{13,9},{2,6},{6,2},{1... | collective-permute-start | bytes 393224 | tf_op jit(solution)/shard_map/ppermute | solution.py:747
  14.8 8.0 %collective-permute-start = (f32[512,128]{1,0:T(8,128)S(1)}, f32[512,128]{1,0:T(8,128)S(1)}, u32[]{:S(2)}, u32[]{:S(2)}) collective-permute-start(f32[512,128]{1,0:T(8,128)S(1)} %get-tuple-element.19.refs_0_), channel_id=1, source_target_pairs={{0,2},{2,0},{1,3},{3,1},{4,6},{6,4},{5,7},{7,5},{8,10},{10,8},{9,1... | collective-permute-start | bytes 786440 | tf_op jit(solution)/shard_map/ppermute | solution.py:750
  14.8 7.4 %collective-permute-start.6 = (f32[256,128]{1,0:T(8,128)S(1)}, f32[256,128]{1,0:T(8,128)S(1)}, u32[]{:S(2)}, u32[]{:S(2)}) collective-permute-start(f32[256,128]{1,0:T(8,128)S(1)} %collective-permute-done.3.refs_4_), channel_id=1, source_target_pairs={{0,5},{1,4},{4,1},{5,0},{8,13},{9,12},{12,9},{13,8},{2,7},{3,6},{6... | collective-permute-start | bytes 393224 | tf_op jit(solution)/shard_map/ppermute | solution.py:775
  17.7 4.6 %collective-permute-start.7 = (f32[256,128]{1,0:T(8,128)S(1)}, f32[256,128]{1,0:T(8,128)S(1)}, u32[]{:S(2)}, u32[]{:S(2)}) collective-permute-start(f32[256,128]{1,0:T(8,128)S(1)} %collective-permute-done.5.refs_6_), channel_id=1, source_target_pairs={{0,2},{2,0},{1,3},{3,1},{4,6},{6,4},{5,7},{7,5},{8,10},{10,8},{9,1... | collective-permute-start | bytes 393224 | tf_op jit(solution)/shard_map/ppermute | solution.py:750
  17.7 6.0 %collective-permute-start.2 = (f32[512,128]{1,0:T(8,128)S(1)}, f32[512,128]{1,0:T(8,128)S(1)}, u32[]{:S(2)}, u32[]{:S(2)}) collective-permute-start(f32[512,128]{1,0:T(8,128)S(1)} %collective-permute-done.1.refs_2_), channel_id=1, source_target_pairs={{0,2},{2,0},{1,3},{3,1},{4,6},{6,4},{5,7},{7,5},{8,10},{10,8},{9,1... | collective-permute-start | bytes 786440 | tf_op jit(solution)/shard_map/ppermute | solution.py:750
  20.5 2.3 %collective-permute-start.4 = (f32[256,128]{1,0:T(8,128)S(1)}, f32[256,128]{1,0:T(8,128)S(1)}, u32[]{:S(2)}, u32[]{:S(2)}) collective-permute-start(f32[256,128]{1,0:T(8,128)S(1)} %collective-permute-done.3.refs_4_), channel_id=1, source_target_pairs={{0,2},{2,0},{1,3},{3,1},{4,6},{6,4},{5,7},{7,5},{8,10},{10,8},{9,1... | collective-permute-start | bytes 393224 | tf_op jit(solution)/shard_map/ppermute | solution.py:750
  22.3 1.3 %collective-permute-start.9 = (f32[256,128]{1,0:T(8,128)S(1)}, f32[256,128]{1,0:T(8,128)S(1)}, u32[]{:S(2)}, u32[]{:S(2)}) collective-permute-start(f32[256,128]{1,0:T(8,128)S(1)} %collective-permute-done.8.refs_8_), channel_id=1, source_target_pairs={{0,2},{2,0},{1,3},{3,1},{4,6},{6,4},{5,7},{7,5},{8,10},{10,8},{9,1... | collective-permute-start | bytes 393224 | tf_op jit(solution)/shard_map/ppermute | solution.py:750
  22.3 1.5 %collective-permute-start.10 = (f32[256,128]{1,0:T(8,128)S(1)}, f32[256,128]{1,0:T(8,128)S(1)}, u32[]{:S(2)}, u32[]{:S(2)}) collective-permute-start(f32[256,128]{1,0:T(8,128)S(1)} %collective-permute-done.6.refs_10_), channel_id=1, source_target_pairs={{0,2},{2,0},{1,3},{3,1},{4,6},{6,4},{5,7},{7,5},{8,10},{10,8},{9,1... | collective-permute-start | bytes 393224 | tf_op jit(solution)/shard_map/ppermute | solution.py:750
  43.6 5.8 %collective-permute-start.11 = (f32[8,32,128]{2,1,0:T(8,128)S(1)}, f32[8,32,128]{2,1,0:T(8,128)S(1)}, u32[]{:S(2)}, u32[]{:S(2)}) collective-permute-start(f32[8,32,128]{2,1,0:T(8,128)S(1)} %get-tuple-element.33), channel_id=1, source_target_pairs={{0,1},{1,0},{2,3},{3,2},{4,5},{5,4},{6,7},{7,6},{8,9},{9,8},{10,11... | collective-permute-start | bytes 393224 | tf_op jit(solution)/shard_map/ppermute | solution.py:801
